TPU v7x, 32 devices: a whole 2x2x4 slice. The times are simulated.
32 devices in a mesh: row: 8 (over y, x, core), col: 4 (over z).
Axes of the slice: x: 2, y: 2, z: 4, core: 2. Of those that a mesh axis runs over, the one named last changes fastest.
Arguments:
- tokens: bfloat16 [64, 8192], P('row', 'col'), may hold values from -6 to 6
- gate_weight: bfloat16 [8192, 24576], P('col', 'row'), may hold values from -0.0625 to 0.0625
- up_weight: bfloat16 [8192, 24576], P('col', 'row'), may hold values from -0.0625 to 0.0625
- down_weight: bfloat16 [24576, 8192], P('row', 'col'), may hold values from -0.0390625 to 0.0390625
- out_grad: bfloat16 [64, 8192], P('row', 'col'), may hold values from -1.5 to 1.5
Outputs:
- mixed: bfloat16 [64, 8192], P('row', 'col')
- input_grad: bfloat16 [64, 8192], P('row', 'col')
- gate_grad: bfloat16 [8192, 24576], P('col', 'row')
- up_grad: bfloat16 [8192, 24576], P('col', 'row')
- down_grad: bfloat16 [24576, 8192], P('row', 'col')
All inputs are finite; a program needn't handle non-finite values.
Results may differ from a plain program's by a relative error of at most 0.0049.
Values may be sent and summed in bfloat16 or wider, within the bound.
No kernel may reach another device: no remote copies, remote signals or barrier semaphores. Data moves between devices by JAX's collectives and lax.ppermute only.
A program may use at most 192 MiB of HBM per device.

v0:
```python
import jax
import jax.numpy as jnp
from jax import lax
from jax.sharding import PartitionSpec as P


def reduce_rows(term_fn, total_rows, rows):
    summed = lax.psum(term_fn(0, total_rows), "row")
    return lax.dynamic_slice_in_dim(summed, lax.axis_index("row") * rows, rows, 0)


def shards(tokens, gate_weight, up_weight, down_weight, out_grad):
    rows = tokens.shape[0]
    all_tokens, all_grads = (
        lax.all_gather(tokens, "row", axis=0, tiled=True),
        lax.all_gather(out_grad, "row", axis=0, tiled=True),
    )
    total_rows = all_tokens.shape[0]
    units = gate_weight.shape[1]
    joined_weight = jnp.concatenate([gate_weight, up_weight], axis=1)
    back = (((1,), (1,)), ((), ()))
    contract = (((0,), (0,)), ((), ()))
    block = all_tokens
    gate_up = lax.psum_scatter(
        jnp.dot(block, joined_weight, preferred_element_type=jnp.float32),
        "col",
        scatter_dimension=0,
        tiled=True,
    )
    gate = gate_up[:, :units]
    up_value = gate_up[:, units:]
    sigmoid = jax.nn.sigmoid(gate)
    swish = gate * sigmoid
    hidden_mine = (swish * up_value).astype(jnp.bfloat16)
    hidden = lax.all_gather(hidden_mine, "col", axis=0, tiled=True)

    def output_term(start, count):
        return jnp.dot(hidden, down_weight, preferred_element_type=jnp.float32)

    mixed = reduce_rows(output_term, total_rows, rows).astype(jnp.bfloat16)
    down_grad = lax.dot_general(
        hidden, all_grads, contract, preferred_element_type=jnp.float32
    ).astype(jnp.bfloat16)
    block = all_grads
    hidden_grad = lax.psum_scatter(
        lax.dot_general(block, down_weight, back, preferred_element_type=jnp.float32),
        "col",
        scatter_dimension=0,
        tiled=True,
    )
    gate_delta = (hidden_grad * up_value * sigmoid * (1.0 + gate * (1.0 - sigmoid))).astype(
        jnp.bfloat16
    )
    up_delta = (hidden_grad * swish).astype(jnp.bfloat16)
    gate_rows, up_rows = (
        lax.all_gather(gate_delta, "col", axis=0, tiled=True),
        lax.all_gather(up_delta, "col", axis=0, tiled=True),
    )
    deltas = jnp.concatenate([gate_rows, up_rows], axis=1)
    weight_grads = lax.dot_general(all_tokens, deltas, contract, preferred_element_type=jnp.float32)
    gate_grad = weight_grads[:, :units].astype(jnp.bfloat16)
    up_grad = weight_grads[:, units:].astype(jnp.bfloat16)

    def input_term(start, count):
        return lax.dot_general(deltas, joined_weight, back, preferred_element_type=jnp.float32)

    input_grad = reduce_rows(input_term, total_rows, rows).astype(jnp.bfloat16)
    return (mixed, input_grad, gate_grad, up_grad, down_grad)


def solution(mesh):
    return jax.shard_map(
        shards,
        mesh=mesh,
        in_specs=(
            P("row", "col"),
            P("col", "row"),
            P("col", "row"),
            P("row", "col"),
            P("row", "col"),
        ),
        out_specs=(
            P("row", "col"),
            P("row", "col"),
            P("col", "row"),
            P("col", "row"),
            P("row", "col"),
        ),
        check_vma=False,
    )
```

profile of v0, /device:TPU:0, one launch (start us, length us, event | category | flops | bytes accessed | tf_op | source)
XLA Modules:
  0.0 297.6 jit_solution(9741312480381712812)
XLA Ops:
  7.2 0.0 reduce-scatter.5.cloned.1.call-start
  7.2 11.0 %all_gather.17 = bf16[64,2048]{1,0:T(8,128)(2,1)S(1)} all-gather(bf16[8,2048]{1,0:T(8,128)(2,1)} %param.9), channel_id=1, replica_groups=mesh['row'=8,'col'=4] {'row'}, dimensions={0}, use_global_device_ids=true | all-gather | bytes 294912 | tf_op jit(solution)/shard_map/all_gather | solution.py:16
  18.2 9.4 %fusion.3 = f32[64,3072]{1,0:T(8,128)} fusion(bf16[64,2048]{1,0:T(8,128)(2,1)S(1)} %all_gather.17, bf16[3072,2048]{1,0:T(8,128)(2,1)} %param.8), kind=kOutput, calls=%fused_computation.16 | convolution fusion | flops 805306368 | bytes 13631488 | tf_op jit(solution)/shard_map/dot_general | solution.py:46
  27.6 0.0 reduce-scatter.5.cloned.1.call-update
  27.6 0.0 copy-start
  27.6 0.0 reduce-scatter.3.cloned.1.call-start
  27.6 10.6 %constant_dynamic-update-slice_fusion.1 = bf16[2048,6144]{1,0:T(8,128)(2,1)} fusion(bf16[2048,3072]{1,0:T(8,128)(2,1)} %param.6), kind=kLoop, calls=%fused_computation.11 | loop fusion | bytes 25165824
  38.3 0.0 copy-done
  38.3 9.1 %all_gather.15 = bf16[64,2048]{1,0:T(8,128)(2,1)S(1)} all-gather(bf16[8,2048]{1,0:T(8,128)(2,1)S(1)} %copy-done), channel_id=1, replica_groups=mesh['row'=8,'col'=4] {'row'}, dimensions={0}, use_global_device_ids=true | all-gather | bytes 294912 | tf_op jit(solution)/shard_map/all_gather | solution.py:15
  47.3 10.6 %constant_dynamic-update-slice_fusion = bf16[2048,6144]{1,0:T(8,128)(2,1)} fusion(bf16[2048,6144]{1,0:T(8,128)(2,1)} %constant_dynamic-update-slice_fusion.1, bf16[2048,3072]{1,0:T(8,128)(2,1)} %param.7), kind=kLoop, calls=%fused_computation.10 | loop fusion | bytes 25165824 | tf_op jit(solution)/shard_map/concatenate | solution.py:20
  58.0 11.6 %convolution_bitcast_fusion = f32[64,6144]{1,0:T(8,128)} fusion(bf16[64,2048]{1,0:T(8,128)(2,1)S(1)} %all_gather.15, bf16[2048,6144]{1,0:T(8,128)(2,1)} %constant_dynamic-update-slice_fusion), kind=kOutput, calls=%fused_computation.2 | convolution fusion | flops 1610612736 | bytes 27000832 | tf_op jit(solution)/shard_map/dot_general | solution.py:25
  69.6 0.0 reduce-scatter.3.cloned.1.call-update
  69.6 0.0 reduce-scatter.5.cloned.1.call-done
  69.6 35.7 %reduce-scatter.3.cloned.1.call-done = f32[16,6144]{1,0:T(8,128)} async-done(((f32[64,6144]{1,0:T(8,128)}), f32[16,6144]{1,0:T(8,128)}) %reduce-scatter.3.cloned.1.call-update) | async-done | bytes 393232 | tf_op jit(solution)/shard_map/reduce_scatter | solution.py:24
  105.4 1.2 multiply_convert_fusion
  106.6 15.1 %all_gather.18 = bf16[64,3072]{1,0:T(8,128)(2,1)S(1)} all-gather(bf16[16,3072]{1,0:T(8,128)(2,1)S(1)} %get-tuple-element.15), channel_id=1, replica_groups=mesh['row'=8,'col'=4] {'col'}, dimensions={0}, use_global_device_ids=true | all-gather | bytes 491520 | tf_op jit(solution)/shard_map/all_gather | solution.py:56
  121.8 14.9 %all_gather.19 = bf16[64,3072]{1,0:T(8,128)(2,1)S(1)} all-gather(bf16[16,3072]{1,0:T(8,128)(2,1)S(1)} %get-tuple-element.14), channel_id=1, replica_groups=mesh['row'=8,'col'=4] {'col'}, dimensions={0}, use_global_device_ids=true | all-gather | bytes 491520 | tf_op jit(solution)/shard_map/all_gather | solution.py:57
  136.7 12.5 %fusion.4 = f32[64,2048]{1,0:T(8,128)S(1)} fusion(bf16[64,6144]{1,0:T(8,128)(2,1)S(1)} %constant_dynamic-update-slice_fusion.2, bf16[2048,6144]{1,0:T(8,128)(2,1)} %constant_dynamic-update-slice_fusion), kind=kOutput, calls=%fused_computation.17 | convolution fusion | flops 1610612736 | bytes 26476544 | tf_op jit(solution)/shard_map/dot_general | solution.py:65
  149.2 11.7 %convert_bitcast_fusion = bf16[2048,6144]{0,1:T(8,128)(2,1)} fusion(bf16[64,6144]{1,0:T(8,128)(2,1)S(1)} %constant_dynamic-update-slice_fusion.2, bf16[64,2048]{1,0:T(8,128)(2,1)S(1)} %all_gather.15), kind=kOutput, calls=%fused_computation | convolution fusion | flops 1623195648 | bytes 26214400 | tf_op jit(solution)/shard_map/dot_general | solution.py:60
  160.9 14.3 %all_gather.16 = bf16[64,3072]{1,0:T(8,128)(2,1)S(1)} all-gather(bf16[16,3072]{1,0:T(8,128)(2,1)S(1)} %get-tuple-element.16), channel_id=1, replica_groups=mesh['row'=8,'col'=4] {'col'}, dimensions={0}, use_global_device_ids=true | all-gather | bytes 491520 | tf_op jit(solution)/shard_map/all_gather | solution.py:35
  175.3 6.9 %fusion.2 = f32[64,2048]{1,0:T(8,128)S(1)} fusion(bf16[64,3072]{1,0:T(8,128)(2,1)S(1)} %all_gather.16, bf16[3072,2048]{1,0:T(8,128)(2,1)} %param.8), kind=kOutput, calls=%fused_computation.15 | convolution fusion | flops 805306368 | bytes 13500416 | tf_op jit(solution)/shard_map/dot_general | solution.py:38
  182.2 6.6 %convolution_convert_fusion = bf16[3072,2048]{1,0:T(8,128)(2,1)} fusion(bf16[64,3072]{1,0:T(8,128)(2,1)S(1)} %all_gather.16, bf16[64,2048]{1,0:T(8,128)(2,1)S(1)} %all_gather.17), kind=kOutput, calls=%fused_computation.1 | convolution fusion | flops 811597824 | bytes 13238272 | tf_op jit(solution)/shard_map/dot_general | solution.py:41
  188.8 17.8 %fusion.1 = (bf16[2048,3072]{0,1:T(8,128)(2,1)}, bf16[2048,3072]{0,1:T(8,128)(2,1)}) fusion(bf16[2048,6144]{0,1:T(8,128)(2,1)} %convert_bitcast_fusion), kind=kLoop, calls=%fused_computation.14 | loop fusion | bytes 50331648 | tf_op jit(solution)/shard_map/slice | solution.py:62
  206.5 16.6 %copy.10 = bf16[2048,3072]{1,0:T(8,128)(2,1)} copy(bf16[2048,3072]{0,1:T(8,128)(2,1)} %get-tuple-element.13) | data formatting | bytes 25165824
  223.1 16.6 %copy.11 = bf16[2048,3072]{1,0:T(8,128)(2,1)} copy(bf16[2048,3072]{0,1:T(8,128)(2,1)} %get-tuple-element.12) | data formatting | bytes 25165824
  239.7 50.4 %all-reduce.2 = (bf16[64,2048]{1,0:T(8,128)(2,1)S(1)}, bf16[64,2048]{1,0:T(8,128)(2,1)S(1)}) all-reduce(f32[64,2048]{1,0:T(8,128)S(1)} %fusion.2, f32[64,2048]{1,0:T(8,128)S(1)} %fusion.4), channel_id=1, replica_groups=mesh['row'=8,'col'=4] {'row'}, use_global_device_ids=true, to_apply=%region_1.0 | all-reduce | flops 262144 | bytes 1572864 | tf_op jit(solution)/shard_map/psum | solution.py:8
  290.1 0.6 dynamic-slice_convert_fusion
  (2 shorter events, 0.1 us)
Async XLA Ops:
  7.2 62.5 %reduce-scatter.5.cloned.1.call-start = ((), (), s32[]{:S(2)}) async-start(), calls=%async_computation.3 | async-start | bytes 983040 | tf_op jit(solution)/shard_map/reduce_scatter | solution.py:45
  27.6 10.7 %copy-start = (bf16[8,2048]{1,0:T(8,128)(2,1)S(1)}, bf16[8,2048]{1,0:T(8,128)(2,1)}, u32[]{:S(2)}) copy-start(bf16[8,2048]{1,0:T(8,128)(2,1)} %param.5) | copy-start | bytes 98308
  27.6 77.8 %reduce-scatter.3.cloned.1.call-start = ((), (), s32[]{:S(2)}) async-start(), calls=%async_computation.2 | async-start | bytes 1966080 | tf_op jit(solution)/shard_map/reduce_scatter | solution.py:24
Sparse Core Ops, SparseCore 0:
  27.7 23.5 reduce-scatter.4
  69.7 35.5 reduce-scatter.2
where the time goes:
time: 299 us; the launch traced here: 298 us
  blocking collectives  115 us (38%)
  local copies, waits for them, and re-layouts  72.9 us (24%)
  matrix products  58.7 us (20%)
  waiting for transfers between devices  35.8 us (12%)
  between operations  14.1 us (5%)
    psum x1, blocking collectives, reduce_rows(): summed = lax.psum(term_fn(0, total_rows), 'row')  50.4 us
    unnamed x6, local copies, waits for them, and re-layouts  43.8 us
    reduce_scatter x1, waiting for transfers between devices, shards(): lax.psum_scatter(jnp.dot(block, joined_weight, preferred_element_type=jnp...  35.7 us
    slice x1, local copies, waits for them, and re-layouts, shards(): up_grad = weight_grads[:, units:].astype(jnp.bfloat16)  17.8 us
    all_gather x1, blocking collectives, shards(): lax.all_gather(gate_delta, 'col', axis=0, tiled=True)  15.1 us
    all_gather x1, blocking collectives, shards(): lax.all_gather(up_delta, 'col', axis=0, tiled=True)  14.9 us
    all_gather x1, blocking collectives, shards(): hidden = lax.all_gather(hidden_mine, 'col', axis=0, tiled=True)  14.3 us
    dot_general x1, matrix products, input_term(): lax.dot_general(deltas, joined_weight, back, preferred_element_type=jnp.f...  12.5 us
  transfers between devices with their start and end apart: 2, of which 1 were waited for; matrix products, arithmetic and copies ran while one was open for 11% of the time, Pallas kernels for 0%

commit v1 on v0

v1 whole, which is shorter than its diff:
```python
import functools

import jax
import jax.numpy as jnp
from jax import lax
from jax.experimental import pallas as pl
from jax.experimental.pallas import tpu as pltpu
from jax.sharding import PartitionSpec as P

BF16 = jnp.bfloat16
F32 = jnp.float32
VMEM_LIMIT = 48 * 1024 * 1024
BACK = (((1,), (1,)), ((), ()))
CONTRACT = (((0,), (0,)), ((), ()))


def dot(a, b):
    return jnp.dot(a, b, preferred_element_type=F32)


def swap(x, axis, size, k):
    return lax.ppermute(x, axis, [(i, i ^ k) for i in range(size)])


def estimate(flops, num_bytes):
    return pl.CostEstimate(flops=flops, bytes_accessed=num_bytes, transcendentals=0)


def assemble_kernel(rows, *refs):
    pieces, (tok, grad, tok_t, grad_t) = refs[:-4], refs[-4:]
    both = [p[...].astype(F32) for p in pieces]
    all_tok = jnp.concatenate([b[:rows] for b in both], axis=0)
    all_grad = jnp.concatenate([b[rows:] for b in both], axis=0)
    tok[...] = all_tok.astype(BF16)
    grad[...] = all_grad.astype(BF16)
    tok_t[...] = all_tok.T.astype(BF16)
    grad_t[...] = all_grad.T.astype(BF16)


def assemble(pieces, rows):
    total, width = rows * len(pieces), pieces[0].shape[1]
    flat, turned = (total, width), (width, total)
    return pl.pallas_call(
        functools.partial(assemble_kernel, rows),
        out_shape=[jax.ShapeDtypeStruct(s, BF16) for s in (flat, flat, turned, turned)],
        compiler_params=pltpu.CompilerParams(vmem_limit_bytes=VMEM_LIMIT),
        cost_estimate=estimate(0, 12 * total * width),
        name="assemble",
    )(*pieces)


def sums_kernel(where, tok, grad_t, gate_w, up_w, down_w, out):
    out[0] = dot(tok[...], gate_w[...]).astype(out.dtype)
    out[1] = dot(tok[...], up_w[...]).astype(out.dtype)
    out[2] = dot(down_w[...], grad_t[...]).T.astype(out.dtype)


def partial_sums(where, tok, grad_t, gate_w, up_w, down_w, units, block, dtype):
    total, width = tok.shape
    steps = units // block
    return pl.pallas_call(
        sums_kernel,
        grid_spec=pltpu.PrefetchScalarGridSpec(
            num_scalar_prefetch=1,
            grid=(steps,),
            in_specs=[
                pl.BlockSpec((total, width), lambda i, w: (0, 0)),
                pl.BlockSpec((width, total), lambda i, w: (0, 0)),
                pl.BlockSpec((width, block), lambda i, w: (0, w[0] * steps + i)),
                pl.BlockSpec((width, block), lambda i, w: (0, w[0] * steps + i)),
                pl.BlockSpec((block, width), lambda i, w: (w[0] * steps + i, 0)),
            ],
            out_specs=pl.BlockSpec((3, total, block), lambda i, w: (0, 0, i)),
        ),
        out_shape=jax.ShapeDtypeStruct((3, total, units), dtype),
        compiler_params=pltpu.CompilerParams(vmem_limit_bytes=VMEM_LIMIT),
        cost_estimate=estimate(6 * total * width * units, 6 * width * units),
        name="partial_sums",
    )(where, tok, grad_t, gate_w, up_w, down_w)


def activate_kernel(own, *refs):
    others, out = refs[:-1], refs[-1]
    gate, up, hidden_grad = (
        functools.reduce(lambda s, o: s + o[j].astype(F32), others, own[j]) for j in range(3)
    )
    sig = jax.nn.sigmoid(gate)
    swish = gate * sig
    out[0] = (swish * up).astype(BF16)
    out[1] = (hidden_grad * up * sig * (1.0 + gate * (1.0 - sig))).astype(BF16)
    out[2] = (hidden_grad * swish).astype(BF16)


def activate(own, others):
    size = own.size
    return pl.pallas_call(
        activate_kernel,
        out_shape=jax.ShapeDtypeStruct(own.shape, BF16),
        compiler_params=pltpu.CompilerParams(vmem_limit_bytes=VMEM_LIMIT),
        cost_estimate=estimate(8 * size, 12 * size),
        name="activate",
    )(own, *others)


def products_kernel(first, where, act, gate_w, up_w, down_w, *refs):
    before, (mixed, back, back_t) = refs[:2], refs[-3:]
    step = pl.program_id(0)

    @pl.when(step == 0)
    def _():
        mixed[...] = jnp.zeros_like(mixed) if first else before[0][...]
        back_t[...] = jnp.zeros_like(back_t)

    gate_delta = act[1].astype(F32).T.astype(BF16)
    up_delta = act[2].astype(F32).T.astype(BF16)
    mixed[...] += dot(act[0], down_w[...])
    back_t[...] += dot(gate_w[...], gate_delta) + dot(up_w[...], up_delta)

    @pl.when(step == pl.num_programs(0) - 1)
    def _():
        turned = back_t[...].T
        back[...] = turned if first else before[1][...] + turned


def products(where, act, gate_w, up_w, down_w, before, after, block):
    _, total, units = act.shape
    width = gate_w.shape[0]
    steps = units // block
    whole = pl.BlockSpec((total, width), lambda i, w: (0, 0))
    return pl.pallas_call(
        functools.partial(products_kernel, not before),
        grid_spec=pltpu.PrefetchScalarGridSpec(
            num_scalar_prefetch=1,
            grid=(steps,),
            in_specs=[
                pl.BlockSpec((3, total, block), lambda i, w: (0, 0, i)),
                pl.BlockSpec((width, block), lambda i, w: (0, w[0] * steps + i)),
                pl.BlockSpec((width, block), lambda i, w: (0, w[0] * steps + i)),
                pl.BlockSpec((block, width), lambda i, w: (w[0] * steps + i, 0)),
            ]
            + [whole] * len(before)
            + [pl.BlockSpec(memory_space=pl.ANY)] * len(after),
            out_specs=[whole, whole],
            scratch_shapes=[pltpu.VMEM((width, total), F32)],
        ),
        out_shape=[jax.ShapeDtypeStruct((total, width), F32)] * 2,
        compiler_params=pltpu.CompilerParams(vmem_limit_bytes=VMEM_LIMIT),
        cost_estimate=estimate(6 * total * width * units, 6 * width * units),
        name="products",
    )(where, act, gate_w, up_w, down_w, *before, *after)


def grads_kernel(where, act, tok_t, grad, *refs):
    gate_g, up_g, down_g = refs[-3:]
    gate_g[...] = dot(tok_t[...], act[1]).astype(BF16)
    up_g[...] = dot(tok_t[...], act[2]).astype(BF16)
    down_g[...] = dot(act[0].astype(F32).T.astype(BF16), grad[...]).astype(BF16)


def weight_grads(where, act, tok_t, grad, before, after, all_units, block):
    _, total, units = act.shape
    width = grad.shape[1]
    steps = units // block
    hold = [pl.BlockSpec(memory_space=pl.ANY)]
    extra = list(before) + list(after)
    return pl.pallas_call(
        grads_kernel,
        grid_spec=pltpu.PrefetchScalarGridSpec(
            num_scalar_prefetch=1,
            grid=(steps,),
            in_specs=[
                pl.BlockSpec((3, total, block), lambda i, w: (0, 0, i)),
                pl.BlockSpec((width, total), lambda i, w: (0, 0)),
                pl.BlockSpec((total, width), lambda i, w: (0, 0)),
            ]
            + hold * len(extra),
            out_specs=[
                pl.BlockSpec((width, block), lambda i, w: (0, w[0] * steps + i)),
                pl.BlockSpec((width, block), lambda i, w: (0, w[0] * steps + i)),
                pl.BlockSpec((block, width), lambda i, w: (w[0] * steps + i, 0)),
            ],
        ),
        out_shape=[
            jax.ShapeDtypeStruct((width, all_units), BF16),
            jax.ShapeDtypeStruct((width, all_units), BF16),
            jax.ShapeDtypeStruct((all_units, width), BF16),
        ],
        input_output_aliases={4 + i: i for i in range(len(before))},
        compiler_params=pltpu.CompilerParams(vmem_limit_bytes=VMEM_LIMIT),
        cost_estimate=estimate(6 * total * width * units, 6 * width * units),
        name="weight_grads",
    )(where, act, tok_t, grad, *extra)


def pairwise(n_row, n_col, tokens, gate_weight, up_weight, down_weight, out_grad):
    rows, width = tokens.shape
    all_units = gate_weight.shape[1]
    units = all_units // n_col
    block = 256
    col = lax.axis_index("col")

    mine = jnp.concatenate([tokens, out_grad], axis=0)
    even = [mine] + [swap(mine, "row", n_row, k) for k in range(2, n_row, 2)]
    odd = [swap(piece, "row", n_row, 1) for piece in even]
    order = list(range(0, n_row, 2)) + list(range(1, n_row, 2))
    tok, grad, tok_t, grad_t = assemble(even + odd, rows)

    far_first = sorted(range(1, n_col), reverse=True)
    where = {k: jnp.bitwise_xor(col, k).reshape(1) for k in range(n_col)}

    def sums_of(k, dtype):
        return partial_sums(
            where[k], tok, grad_t, gate_weight, up_weight, down_weight, units, block, dtype
        )

    arrived = [swap(sums_of(k, BF16), "col", n_col, k) for k in far_first]
    own = activate(sums_of(0, F32), arrived)

    acts = {0: own}
    for k in (1 << b for b in range(n_col.bit_length() - 1)):
        acts[k] = swap(own, "col", n_col, k)
    terms, grads, late = (), (), []
    for k in range(n_col):
        terms = products(
            where[k], acts[k], gate_weight, up_weight, down_weight, terms, grads, block
        )
        if k < n_col // 2:
            grads = weight_grads(where[k], acts[k], tok_t, grad, grads, (), all_units, block)
        else:
            late.append(k)
        if k == 0:
            for j in range(n_col):
                if j not in acts:
                    low = j & -j
                    held, _ = lax.optimization_barrier((acts[j ^ low], (terms, grads)))
                    acts[j] = swap(held, "col", n_col, low)
    both = jnp.stack(terms).reshape(2, n_row, rows, width)
    sent = both.astype(BF16)
    parts = [
        swap(sent[:, i], "row", n_row, k).astype(F32) for i, k in enumerate(order) if k
    ]
    for k in late:
        grads = weight_grads(where[k], acts[k], tok_t, grad, grads, terms, all_units, block)
    mixed, input_grad = functools.reduce(jnp.add, parts, both[:, 0]).astype(BF16)
    return (mixed, input_grad, *grads)


def gathered(tokens, gate_weight, up_weight, down_weight, out_grad):
    tok = lax.all_gather(tokens, "row", axis=0, tiled=True)
    grad = lax.all_gather(out_grad, "row", axis=0, tiled=True)

    def total(x):
        return lax.psum_scatter(x, "col", scatter_dimension=0, tiled=True)

    def back_dot(a, b):
        return lax.dot_general(a, b, BACK, preferred_element_type=F32)

    def outer(a, b):
        return lax.dot_general(a, b, CONTRACT, preferred_element_type=F32).astype(BF16)

    gate, up = total(dot(tok, gate_weight)), total(dot(tok, up_weight))
    hidden_grad = total(back_dot(grad, down_weight))
    sig = jax.nn.sigmoid(gate)
    swish = gate * sig
    hidden = (swish * up).astype(BF16)
    gate_delta = (hidden_grad * up * sig * (1.0 + gate * (1.0 - sig))).astype(BF16)
    up_delta = (hidden_grad * swish).astype(BF16)
    hidden, gate_delta, up_delta = (
        lax.all_gather(x, "col", axis=0, tiled=True) for x in (hidden, gate_delta, up_delta)
    )
    mixed = dot(hidden, down_weight)
    input_grad = back_dot(gate_delta, gate_weight) + back_dot(up_delta, up_weight)
    mixed, input_grad = (
        lax.psum_scatter(x, "row", scatter_dimension=0, tiled=True).astype(BF16)
        for x in (mixed, input_grad)
    )
    return (
        mixed,
        input_grad,
        outer(tok, gate_delta),
        outer(tok, up_delta),
        outer(hidden, grad),
    )


def solution(mesh):
    n_row, n_col = mesh.shape["row"], mesh.shape["col"]

    def shards(*args):
        tokens, gate_weight = args[:2]
        fits = (
            n_row & (n_row - 1) == 0
            and n_col & (n_col - 1) == 0
            and n_row > 1
            and n_col > 1
            and tokens.shape[0] % 8 == 0
            and tokens.shape[1] % 128 == 0
            and gate_weight.shape[1] % (256 * n_col) == 0
        )
        if fits:
            return pairwise(n_row, n_col, *args)
        return gathered(*args)

    return jax.shard_map(
        shards,
        mesh=mesh,
        in_specs=(
            P("row", "col"),
            P("col", "row"),
            P("col", "row"),
            P("row", "col"),
            P("row", "col"),
        ),
        out_specs=(
            P("row", "col"),
            P("row", "col"),
            P("col", "row"),
            P("col", "row"),
            P("row", "col"),
        ),
        check_vma=False,
    )
```

time: 299 us -> 110 us (0.37)
  blocking collectives: 115 us -> 0 us
  local copies, waits for them, and re-layouts: 72.9 us -> 2.18 us
  Pallas kernels: 0 us -> 65.9 us
  matrix products: 58.7 us -> 0 us
  starting transfers between devices: 0.08 us -> 23 us
  waiting for transfers between devices: 35.8 us -> 17.7 us
  between operations: 14.1 us -> 0.79 us
    pallas_call x0 -> x14, Pallas kernels: none -> 65.9 us  [the longest x4 24.2 us: products(): pl.pallas_call(functools.partial(products_kernel, not before), grid_spec=...]
    all_gather x5 -> x0, blocking collectives: 64.4 us -> none  [the longest x1 15.1 us: shards(): lax.all_gather(gate_delta, 'col', axis=0, tiled=True)]
    dot_general x6 -> x0, matrix products: 58.7 us -> none  [the longest x1 12.5 us: input_term(): lax.dot_general(deltas, joined_weight, back, preferred_element_type=jnp.f...]
    psum x1 -> x0, blocking collectives: 50.4 us -> none  [reduce_rows(): summed = lax.psum(term_fn(0, total_rows), 'row')]
    unnamed x6 -> x1, local copies, waits for them, and re-layouts: 43.8 us -> 0.76 us
    reduce_scatter x2 -> x0, waiting for transfers between devices: 35.7 us -> none  [the longest x1 35.7 us: shards(): lax.psum_scatter(jnp.dot(block, joined_weight, preferred_element_type=jnp...]
    ppermute x0 -> x20, starting transfers between devices: none -> 23 us  [swap(): return lax.ppermute(x, axis, [(i, i ^ k) for i in range(size)])]
    slice x1 -> x0, local copies, waits for them, and re-layouts: 17.8 us -> none  [shards(): up_grad = weight_grads[:, units:].astype(jnp.bfloat16)]
  transfers between devices with their start and end apart: 2 -> 20, of which waited for: 1 -> 8; matrix products, arithmetic and copies ran while one was open for 11% -> 0% of each run, Pallas kernels for 0% -> 49%
where the time goes in v1:
time: 110 us
  Pallas kernels  65.9 us (60%)
  starting transfers between devices  23 us (21%)
  waiting for transfers between devices  17.7 us (16%)
  local copies, waits for them, and re-layouts  2.18 us (2%)
    pallas_call x4, Pallas kernels, products(): pl.pallas_call(functools.partial(products_kernel, not before), grid_spec=...  24.2 us
    ppermute x20, starting transfers between devices, swap(): return lax.ppermute(x, axis, [(i, i ^ k) for i in range(size)])  23 us
    pallas_call x4, Pallas kernels, partial_sums(): pl.pallas_call(sums_kernel, grid_spec=pltpu.PrefetchScalarGridSpec(num_sc...  22.1 us
    pallas_call x4, Pallas kernels, weight_grads(): pl.pallas_call(grads_kernel, grid_spec=pltpu.PrefetchScalarGridSpec(num_s...  19 us
    ppermute x20, waiting for transfers between devices, swap(): return lax.ppermute(x, axis, [(i, i ^ k) for i in range(size)])  17.7 us
  transfers between devices with their start and end apart: 20, of which 8 were waited for; matrix products, arithmetic and copies ran while one was open for 0% of the time, Pallas kernels for 49%

profile of v1, /device:TPU:0, one launch (start us, length us, event | category | flops | bytes accessed | tf_op | source)
XLA Modules:
  0.0 109.7 jit_solution(5465237949447060147)
XLA Ops:
  0.6 0.8 constant_dynamic-update-slice_fusion.1
  1.4 0.8 constant_dynamic-update-slice_fusion.refs_0_
  2.2 2.9 %collective-permute-start = (bf16[16,2048]{1,0:T(8,128)(2,1)S(1)}, bf16[16,2048]{1,0:T(8,128)(2,1)S(1)}, u32[]{:S(2)}, u32[]{:S(2)}) collective-permute-start(bf16[16,2048]{1,0:T(8,128)(2,1)S(1)} %constant_dynamic-update-slice_fusion.refs_0_), channel_id=1, source_target_pairs={{0,8},{4,12},{8,0},{12,4},{16,24},{20,28},{24,16},{28,20},{1,9},{5... | collective-permute-start | bytes 196616 | tf_op jit(solution)/shard_map/ppermute | solution.py:22
  5.1 1.5 %collective-permute-start.1 = (bf16[16,2048]{1,0:T(8,128)(2,1)S(1)}, bf16[16,2048]{1,0:T(8,128)(2,1)S(1)}, u32[]{:S(2)}, u32[]{:S(2)}) collective-permute-start(bf16[16,2048]{1,0:T(8,128)(2,1)S(1)} %constant_dynamic-update-slice_fusion.refs_0_), channel_id=1, source_target_pairs={{0,16},{4,20},{8,24},{12,28},{16,0},{20,4},{24,8},{28,12},{1,17},{... | collective-permute-start | bytes 196616 | tf_op jit(solution)/shard_map/ppermute | solution.py:22
  6.6 0.0 collective-permute-start.2
  6.6 0.8 collective-permute-done.refs_1_
  7.5 0.0 collective-permute-start.4
  7.5 1.9 %collective-permute-done.1.refs_2_ = bf16[16,2048]{1,0:T(8,128)(2,1)S(1)} collective-permute-done((bf16[16,2048]{1,0:T(8,128)(2,1)S(1)}, bf16[16,2048]{1,0:T(8,128)(2,1)S(1)}, u32[]{:S(2)}, u32[]{:S(2)}) %collective-permute-start.1) | collective-permute-done | bytes 65568 | tf_op jit(solution)/shard_map/ppermute | solution.py:22
  9.4 2.4 %collective-permute-done.2.refs_3_ = bf16[16,2048]{1,0:T(8,128)(2,1)S(1)} collective-permute-done((bf16[16,2048]{1,0:T(8,128)(2,1)S(1)}, bf16[16,2048]{1,0:T(8,128)(2,1)S(1)}, u32[]{:S(2)}, u32[]{:S(2)}) %collective-permute-start.2) | collective-permute-done | bytes 65568 | tf_op jit(solution)/shard_map/ppermute | solution.py:22
  11.8 0.0 collective-permute-start.6
  11.8 0.0 collective-permute-done.3.refs_4_
  11.8 0.0 collective-permute-done.4.refs_5_
  11.8 1.2 %collective-permute-done.6.refs_7_ = bf16[16,2048]{1,0:T(8,128)(2,1)S(1)} collective-permute-done((bf16[16,2048]{1,0:T(8,128)(2,1)S(1)}, bf16[16,2048]{1,0:T(8,128)(2,1)S(1)}, u32[]{:S(2)}, u32[]{:S(2)}) %collective-permute-start.6) | collective-permute-done | bytes 65568 | tf_op jit(solution)/shard_map/ppermute | solution.py:22
  13.0 0.3 assemble.1
  13.4 5.5 %partial_sums.7 = bf16[3,64,768]{2,1,0:T(8,128)(2,1)S(1)} custom-call(s32[1]{0:T(128)} %bitcast.3.where, bf16[64,2048]{1,0:T(8,128)(2,1)S(1)} %get-tuple-element.30.tok, bf16[2048,64]{1,0:T(8,128)(2,1)S(1)} %get-tuple-element.31.grad_t, bf16[2048,3072]{1,0:T(8,128)(2,1)} %gate_w.15, bf16[2048,3072]{1,0:T(8,128)(2,1)} %up_w.15, bf16[3072,2048]{1,0:T(8,128)(2,1)} %down_w.15), custom_call_target="tpu_custom_call" | custom-call | flops 603979776 | bytes 9437184 | tf_op jit(solution)/shard_map/partial_sums/pallas_call | solution.py:61
  18.9 1.7 %collective-permute-start.9 = (bf16[3,64,768]{2,1,0:T(8,128)(2,1)S(1)}, bf16[3,64,768]{2,1,0:T(8,128)(2,1)S(1)}, u32[]{:S(2)}, u32[]{:S(2)}) collective-permute-start(bf16[3,64,768]{2,1,0:T(8,128)(2,1)S(1)} %partial_sums.7), channel_id=1, source_target_pairs={{0,1},{1,0},{2,3},{3,2},{4,5},{5,4},{6,7},{7,6},{8,9},{9,8},{10,11... | collective-permute-start | bytes 884744 | tf_op jit(solution)/shard_map/ppermute | solution.py:22
  20.6 5.5 %partial_sums.6 = bf16[3,64,768]{2,1,0:T(8,128)(2,1)S(1)} custom-call(s32[1]{0:T(128)} %bitcast.2.where, bf16[64,2048]{1,0:T(8,128)(2,1)S(1)} %get-tuple-element.30.tok, bf16[2048,64]{1,0:T(8,128)(2,1)S(1)} %get-tuple-element.31.grad_t, bf16[2048,3072]{1,0:T(8,128)(2,1)} %gate_w.15, bf16[2048,3072]{1,0:T(8,128)(2,1)} %up_w.15, bf16[3072,2048]{1,0:T(8,128)(2,1)} %down_w.15), custom_call_target="tpu_custom_call" | custom-call | flops 603979776 | bytes 9437184 | tf_op jit(solution)/shard_map/partial_sums/pallas_call | solution.py:61
  26.1 2.7 %collective-permute-start.8 = (bf16[3,64,768]{2,1,0:T(8,128)(2,1)S(1)}, bf16[3,64,768]{2,1,0:T(8,128)(2,1)S(1)}, u32[]{:S(2)}, u32[]{:S(2)}) collective-permute-start(bf16[3,64,768]{2,1,0:T(8,128)(2,1)S(1)} %partial_sums.6), channel_id=1, source_target_pairs={{0,2},{1,3},{2,0},{3,1},{4,6},{5,7},{6,4},{7,5},{8,10},{9,11},{10,... | collective-permute-start | bytes 884744 | tf_op jit(solution)/shard_map/ppermute | solution.py:22
  28.8 5.5 %partial_sums.5 = bf16[3,64,768]{2,1,0:T(8,128)(2,1)S(1)} custom-call(s32[1]{0:T(128)} %bitcast.where, bf16[64,2048]{1,0:T(8,128)(2,1)S(1)} %get-tuple-element.30.tok, bf16[2048,64]{1,0:T(8,128)(2,1)S(1)} %get-tuple-element.31.grad_t, bf16[2048,3072]{1,0:T(8,128)(2,1)} %gate_w.15, bf16[2048,3072]{1,0:T(8,128)(2,1)} %up_w.15, bf16[3072,2048]{1,0:T(8,128)(2,1)} %down_w.15), custom_call_target="tpu_custom_call" | custom-call | flops 603979776 | bytes 9437184 | tf_op jit(solution)/shard_map/partial_sums/pallas_call | solution.py:61
  34.3 0.3 collective-permute-start.7
  34.6 5.5 %partial_sums.4.own = f32[3,64,768]{2,1,0:T(8,128)S(1)} custom-call(s32[1]{0:T(128)} %bitcast.1.where, bf16[64,2048]{1,0:T(8,128)(2,1)S(1)} %get-tuple-element.30.tok, bf16[2048,64]{1,0:T(8,128)(2,1)S(1)} %get-tuple-element.31.grad_t, bf16[2048,3072]{1,0:T(8,128)(2,1)} %gate_w.15, bf16[2048,3072]{1,0:T(8,128)(2,1)} %up_w.15, bf16[3072,2048]{1,0:T(8,128)(2,1)} %down_w.15), custom_call_target="tpu_custom_call" | custom-call | flops 603979776 | bytes 9437184 | tf_op jit(solution)/shard_map/partial_sums/pallas_call | solution.py:61
  40.1 0.0 collective-permute-done.9.refs_2_
  40.1 8.9 %collective-permute-done.8.refs_1_ = bf16[3,64,768]{2,1,0:T(8,128)(2,1)S(1)} collective-permute-done((bf16[3,64,768]{2,1,0:T(8,128)(2,1)S(1)}, bf16[3,64,768]{2,1,0:T(8,128)(2,1)S(1)}, u32[]{:S(2)}, u32[]{:S(2)}) %collective-permute-start.8) | collective-permute-done | bytes 294944 | tf_op jit(solution)/shard_map/ppermute | solution.py:22
  49.0 0.2 activate.1.act
  49.3 7.4 %collective-permute-start.10 = (bf16[3,64,768]{2,1,0:T(8,128)(2,1)S(1)}, bf16[3,64,768]{2,1,0:T(8,128)(2,1)S(1)}, u32[]{:S(2)}, u32[]{:S(2)}) collective-permute-start(bf16[3,64,768]{2,1,0:T(8,128)(2,1)S(1)} %activate.1.act), channel_id=1, source_target_pairs={{0,2},{1,3},{2,0},{3,1},{4,6},{5,7},{6,4},{7,5},{8,10},{9,11},{10,... | collective-permute-start | bytes 884744 | tf_op jit(solution)/shard_map/ppermute | solution.py:22
  56.7 6.0 %products.4 = (f32[64,2048]{1,0:T(8,128)S(1)}, f32[64,2048]{1,0:T(8,128)S(1)}) custom-call(s32[1]{0:T(128)} %bitcast.1.where, bf16[3,64,768]{2,1,0:T(8,128)(2,1)S(1)} %activate.1.act, bf16[2048,3072]{1,0:T(8,128)(2,1)} %gate_w.15, bf16[2048,3072]{1,0:T(8,128)(2,1)} %up_w.15, bf16[3072,2048]{1,0:T(8,128)(2,1)} %down_w.15), custom_call_target="tpu_custom_call" | custom-call | flops 603979776 | bytes 9437184 | tf_op jit(solution)/shard_map/products/pallas_call | solution.py:130
  62.7 4.8 %weight_grads.4 = (bf16[2048,3072]{1,0:T(8,128)(2,1)}, bf16[2048,3072]{1,0:T(8,128)(2,1)}, bf16[3072,2048]{1,0:T(8,128)(2,1)}) custom-call(s32[1]{0:T(128)} %bitcast.1.where, bf16[3,64,768]{2,1,0:T(8,128)(2,1)S(1)} %activate.1.act, bf16[2048,64]{1,0:T(8,128)(2,1)S(1)} %get-tuple-element.34.tok_t, bf16[64,2048]{1,0:T(8,128)(2,1)S(1)} %get-tuple-element.35.grad), custom_call_target="tpu_custom_call" | custom-call | flops 603979776 | bytes 9437184 | tf_op jit(solution)/shard_map/weight_grads/pallas_call | solution.py:166
  67.5 1.7 %collective-permute-done.10.act = bf16[3,64,768]{2,1,0:T(8,128)(2,1)S(1)} collective-permute-done((bf16[3,64,768]{2,1,0:T(8,128)(2,1)S(1)}, bf16[3,64,768]{2,1,0:T(8,128)(2,1)S(1)}, u32[]{:S(2)}, u32[]{:S(2)}) %collective-permute-start.10) | collective-permute-done | bytes 294944 | tf_op jit(solution)/shard_map/ppermute | solution.py:22
  69.2 0.3 collective-permute-start.11
  69.5 0.0 collective-permute-done.12.act
  69.5 6.0 %products.5 = (f32[64,2048]{1,0:T(8,128)S(1)}, f32[64,2048]{1,0:T(8,128)S(1)}) custom-call(s32[1]{0:T(128)} %bitcast.3.where, bf16[3,64,768]{2,1,0:T(8,128)(2,1)S(1)} %collective-permute-done.12.act, bf16[2048,3072]{1,0:T(8,128)(2,1)} %gate_w.15, bf16[2048,3072]{1,0:T(8,128)(2,1)} %up_w.15, bf16[3072,2048]{1,0:T(8,128)(2,1)} %down_w.15, ...), custom_call_target="tpu_custom_call" | custom-call | flops 603979776 | bytes 9437184 | tf_op jit(solution)/shard_map/products/pallas_call | solution.py:130
  75.6 4.8 %weight_grads.5 = (bf16[2048,3072]{1,0:T(8,128)(2,1)}, bf16[2048,3072]{1,0:T(8,128)(2,1)}, bf16[3072,2048]{1,0:T(8,128)(2,1)}) custom-call(s32[1]{0:T(128)} %bitcast.3.where, bf16[3,64,768]{2,1,0:T(8,128)(2,1)S(1)} %collective-permute-done.12.act, ...), custom_call_target="tpu_custom_call", output_to_operand_aliasing={{0}: (4, {}), {1}: (5, {}), {2}: (6, {})} | custom-call | flops 603979776 | bytes 9437184 | tf_op jit(solution)/shard_map/weight_grads/pallas_call | solution.py:166
  80.3 6.1 %products.6 = (f32[64,2048]{1,0:T(8,128)S(1)}, f32[64,2048]{1,0:T(8,128)S(1)}) custom-call(s32[1]{0:T(128)} %bitcast.2.where, bf16[3,64,768]{2,1,0:T(8,128)(2,1)S(1)} %collective-permute-done.10.act, bf16[2048,3072]{1,0:T(8,128)(2,1)} %gate_w.15, bf16[2048,3072]{1,0:T(8,128)(2,1)} %up_w.15, bf16[3072,2048]{1,0:T(8,128)(2,1)} %down_w.15, ...), custom_call_target="tpu_custom_call" | custom-call | flops 603979776 | bytes 9437184 | tf_op jit(solution)/shard_map/products/pallas_call | solution.py:130
  86.4 0.0 collective-permute-done.11.act
  86.4 6.1 %products.7 = (f32[64,2048]{1,0:T(8,128)S(1)}, f32[64,2048]{1,0:T(8,128)S(1)}) custom-call(s32[1]{0:T(128)} %bitcast.where, bf16[3,64,768]{2,1,0:T(8,128)(2,1)S(1)} %collective-permute-done.11.act, bf16[2048,3072]{1,0:T(8,128)(2,1)} %gate_w.15, bf16[2048,3072]{1,0:T(8,128)(2,1)} %up_w.15, bf16[3072,2048]{1,0:T(8,128)(2,1)} %down_w.15, ...), custom_call_target="tpu_custom_call" | custom-call | flops 603979776 | bytes 9437184 | tf_op jit(solution)/shard_map/products/pallas_call | solution.py:130
  92.5 0.1 fusion
  92.6 0.6 collective-permute-start.13
  93.2 0.5 collective-permute-start.14
  93.7 2.4 %collective-permute-start.15 = (bf16[2,8,2048]{2,1,0:T(8,128)(2,1)S(1)}, bf16[2,8,2048]{2,1,0:T(8,128)(2,1)S(1)}, u32[]{:S(2)}, u32[]{:S(2)}) collective-permute-start(bf16[2,8,2048]{2,1,0:T(8,128)(2,1)S(1)} %get-tuple-element.60), channel_id=1, source_target_pairs={{0,24},{4,28},{8,16},{12,20},{16,8},{20,12},{24,0},{28,4},{1,25},{... | collective-permute-start | bytes 196616 | tf_op jit(solution)/shard_map/ppermute | solution.py:22
  96.2 0.7 collective-permute-start.17
  96.8 0.1 collective-permute-done.13
  97.0 0.0 collective-permute-start.18
  97.0 0.5 collective-permute-done.14
  97.5 2.0 %collective-permute-start.19 = (bf16[2,8,2048]{2,1,0:T(8,128)(2,1)S(1)}, bf16[2,8,2048]{2,1,0:T(8,128)(2,1)S(1)}, u32[]{:S(2)}, u32[]{:S(2)}) collective-permute-start(bf16[2,8,2048]{2,1,0:T(8,128)(2,1)S(1)} %get-tuple-element.56), channel_id=1, source_target_pairs={{0,28},{4,24},{8,20},{12,16},{16,12},{20,8},{24,4},{28,0},{1,29},{... | collective-permute-start | bytes 196616 | tf_op jit(solution)/shard_map/ppermute | solution.py:22
  99.5 4.7 %weight_grads.6 = (bf16[2048,3072]{1,0:T(8,128)(2,1)}, bf16[2048,3072]{1,0:T(8,128)(2,1)}, bf16[3072,2048]{1,0:T(8,128)(2,1)}) custom-call(s32[1]{0:T(128)} %bitcast.2.where, bf16[3,64,768]{2,1,0:T(8,128)(2,1)S(1)} %collective-permute-done.10.act, ...), custom_call_target="tpu_custom_call", output_to_operand_aliasing={{0}: (4, {}), {1}: (5, {}), {2}: (6, {})} | custom-call | flops 603979776 | bytes 9437184 | tf_op jit(solution)/shard_map/weight_grads/pallas_call | solution.py:166
  104.2 4.7 %weight_grads.7 = (bf16[2048,3072]{1,0:T(8,128)(2,1)}, bf16[2048,3072]{1,0:T(8,128)(2,1)}, bf16[3072,2048]{1,0:T(8,128)(2,1)}) custom-call(s32[1]{0:T(128)} %bitcast.where, bf16[3,64,768]{2,1,0:T(8,128)(2,1)S(1)} %collective-permute-done.11.act, ...), custom_call_target="tpu_custom_call", output_to_operand_aliasing={{0}: (4, {}), {1}: (5, {}), {2}: (6, {})} | custom-call | flops 603979776 | bytes 9437184 | tf_op jit(solution)/shard_map/weight_grads/pallas_call | solution.py:166
  109.0 0.1 fusion.10
  109.1 0.6 slice_bitcast_fusion.7
  (12 shorter events, 0.1 us)
Async XLA Ops:
  2.2 5.3 %collective-permute-start = (bf16[16,2048]{1,0:T(8,128)(2,1)S(1)}, bf16[16,2048]{1,0:T(8,128)(2,1)S(1)}, u32[]{:S(2)}, u32[]{:S(2)}) collective-permute-start(bf16[16,2048]{1,0:T(8,128)(2,1)S(1)} %constant_dynamic-update-slice_fusion.refs_0_), channel_id=1, source_target_pairs={{0,8},{4,12},{8,0},{12,4},{16,24},{20,28},{24,16},{28,20},{1,9},{5... | collective-permute-start | bytes 196616 | tf_op jit(solution)/shard_map/ppermute | solution.py:22
  5.1 4.3 %collective-permute-start.1 = (bf16[16,2048]{1,0:T(8,128)(2,1)S(1)}, bf16[16,2048]{1,0:T(8,128)(2,1)S(1)}, u32[]{:S(2)}, u32[]{:S(2)}) collective-permute-start(bf16[16,2048]{1,0:T(8,128)(2,1)S(1)} %constant_dynamic-update-slice_fusion.refs_0_), channel_id=1, source_target_pairs={{0,16},{4,20},{8,24},{12,28},{16,0},{20,4},{24,8},{28,12},{1,17},{... | collective-permute-start | bytes 196616 | tf_op jit(solution)/shard_map/ppermute | solution.py:22
  6.6 5.2 %collective-permute-start.2 = (bf16[16,2048]{1,0:T(8,128)(2,1)S(1)}, bf16[16,2048]{1,0:T(8,128)(2,1)S(1)}, u32[]{:S(2)}, u32[]{:S(2)}) collective-permute-start(bf16[16,2048]{1,0:T(8,128)(2,1)S(1)} %constant_dynamic-update-slice_fusion.refs_0_), channel_id=1, source_target_pairs={{0,24},{4,28},{8,16},{12,20},{16,8},{20,12},{24,0},{28,4},{1,25},{... | collective-permute-start | bytes 196616 | tf_op jit(solution)/shard_map/ppermute | solution.py:22
  6.6 5.2 %collective-permute-start.3 = (bf16[16,2048]{1,0:T(8,128)(2,1)S(1)}, bf16[16,2048]{1,0:T(8,128)(2,1)S(1)}, u32[]{:S(2)}, u32[]{:S(2)}) collective-permute-start(bf16[16,2048]{1,0:T(8,128)(2,1)S(1)} %constant_dynamic-update-slice_fusion.refs_0_), channel_id=1, source_target_pairs={{0,4},{4,0},{8,12},{12,8},{16,20},{20,16},{24,28},{28,24},{1,5},{5... | collective-permute-start | bytes 196616 | tf_op jit(solution)/shard_map/ppermute | solution.py:22
  7.5 4.3 %collective-permute-start.4 = (bf16[16,2048]{1,0:T(8,128)(2,1)S(1)}, bf16[16,2048]{1,0:T(8,128)(2,1)S(1)}, u32[]{:S(2)}, u32[]{:S(2)}) collective-permute-start(bf16[16,2048]{1,0:T(8,128)(2,1)S(1)} %collective-permute-done.refs_1_), channel_id=1, source_target_pairs={{0,4},{4,0},{8,12},{12,8},{16,20},{20,16},{24,28},{28,24},{1,5},{5... | collective-permute-start | bytes 196616 | tf_op jit(solution)/shard_map/ppermute | solution.py:22
  9.4 2.4 %collective-permute-start.5 = (bf16[16,2048]{1,0:T(8,128)(2,1)S(1)}, bf16[16,2048]{1,0:T(8,128)(2,1)S(1)}, u32[]{:S(2)}, u32[]{:S(2)}) collective-permute-start(bf16[16,2048]{1,0:T(8,128)(2,1)S(1)} %collective-permute-done.1.refs_2_), channel_id=1, source_target_pairs={{0,4},{4,0},{8,12},{12,8},{16,20},{20,16},{24,28},{28,24},{1,5},{5... | collective-permute-start | bytes 196616 | tf_op jit(solution)/shard_map/ppermute | solution.py:22
  11.8 1.3 %collective-permute-start.6 = (bf16[16,2048]{1,0:T(8,128)(2,1)S(1)}, bf16[16,2048]{1,0:T(8,128)(2,1)S(1)}, u32[]{:S(2)}, u32[]{:S(2)}) collective-permute-start(bf16[16,2048]{1,0:T(8,128)(2,1)S(1)} %collective-permute-done.2.refs_3_), channel_id=1, source_target_pairs={{0,4},{4,0},{8,12},{12,8},{16,20},{20,16},{24,28},{28,24},{1,5},{5... | collective-permute-start | bytes 196616 | tf_op jit(solution)/shard_map/ppermute | solution.py:22
  18.9 21.2 %collective-permute-start.9 = (bf16[3,64,768]{2,1,0:T(8,128)(2,1)S(1)}, bf16[3,64,768]{2,1,0:T(8,128)(2,1)S(1)}, u32[]{:S(2)}, u32[]{:S(2)}) collective-permute-start(bf16[3,64,768]{2,1,0:T(8,128)(2,1)S(1)} %partial_sums.7), channel_id=1, source_target_pairs={{0,1},{1,0},{2,3},{3,2},{4,5},{5,4},{6,7},{7,6},{8,9},{9,8},{10,11... | collective-permute-start | bytes 884744 | tf_op jit(solution)/shard_map/ppermute | solution.py:22
  26.1 22.9 %collective-permute-start.8 = (bf16[3,64,768]{2,1,0:T(8,128)(2,1)S(1)}, bf16[3,64,768]{2,1,0:T(8,128)(2,1)S(1)}, u32[]{:S(2)}, u32[]{:S(2)}) collective-permute-start(bf16[3,64,768]{2,1,0:T(8,128)(2,1)S(1)} %partial_sums.6), channel_id=1, source_target_pairs={{0,2},{1,3},{2,0},{3,1},{4,6},{5,7},{6,4},{7,5},{8,10},{9,11},{10,... | collective-permute-start | bytes 884744 | tf_op jit(solution)/shard_map/ppermute | solution.py:22
  34.3 14.7 %collective-permute-start.7 = (bf16[3,64,768]{2,1,0:T(8,128)(2,1)S(1)}, bf16[3,64,768]{2,1,0:T(8,128)(2,1)S(1)}, u32[]{:S(2)}, u32[]{:S(2)}) collective-permute-start(bf16[3,64,768]{2,1,0:T(8,128)(2,1)S(1)} %partial_sums.5), channel_id=1, source_target_pairs={{0,3},{1,2},{2,1},{3,0},{4,7},{5,6},{6,5},{7,4},{8,11},{9,10},{10,... | collective-permute-start | bytes 884744 | tf_op jit(solution)/shard_map/ppermute | solution.py:22
  49.3 19.9 %collective-permute-start.10 = (bf16[3,64,768]{2,1,0:T(8,128)(2,1)S(1)}, bf16[3,64,768]{2,1,0:T(8,128)(2,1)S(1)}, u32[]{:S(2)}, u32[]{:S(2)}) collective-permute-start(bf16[3,64,768]{2,1,0:T(8,128)(2,1)S(1)} %activate.1.act), channel_id=1, source_target_pairs={{0,2},{1,3},{2,0},{3,1},{4,6},{5,7},{6,4},{7,5},{8,10},{9,11},{10,... | collective-permute-start | bytes 884744 | tf_op jit(solution)/shard_map/ppermute | solution.py:22
  56.7 12.9 %collective-permute-start.12 = (bf16[3,64,768]{2,1,0:T(8,128)(2,1)S(1)}, bf16[3,64,768]{2,1,0:T(8,128)(2,1)S(1)}, u32[]{:S(2)}, u32[]{:S(2)}) collective-permute-start(bf16[3,64,768]{2,1,0:T(8,128)(2,1)S(1)} %activate.1.act), channel_id=1, source_target_pairs={{0,1},{1,0},{2,3},{3,2},{4,5},{5,4},{6,7},{7,6},{8,9},{9,8},{10,11... | collective-permute-start | bytes 884744 | tf_op jit(solution)/shard_map/ppermute | solution.py:22
  69.2 17.2 %collective-permute-start.11 = (bf16[3,64,768]{2,1,0:T(8,128)(2,1)S(1)}, bf16[3,64,768]{2,1,0:T(8,128)(2,1)S(1)}, u32[]{:S(2)}, u32[]{:S(2)}) collective-permute-start(bf16[3,64,768]{2,1,0:T(8,128)(2,1)S(1)} %collective-permute-done.10.act), channel_id=1, source_target_pairs={{0,1},{1,0},{2,3},{3,2},{4,5},{5,4},{6,7},{7,6},{8,9},{9,8},{10,11... | collective-permute-start | bytes 884744 | tf_op jit(solution)/shard_map/ppermute | solution.py:22
  92.6 4.3 %collective-permute-start.13 = (bf16[2,8,2048]{2,1,0:T(8,128)(2,1)S(1)}, bf16[2,8,2048]{2,1,0:T(8,128)(2,1)S(1)}, u32[]{:S(2)}, u32[]{:S(2)}) collective-permute-start(bf16[2,8,2048]{2,1,0:T(8,128)(2,1)S(1)} %get-tuple-element.55), channel_id=1, source_target_pairs={{0,8},{4,12},{8,0},{12,4},{16,24},{20,28},{24,16},{28,20},{1,9},{5... | collective-permute-start | bytes 196616 | tf_op jit(solution)/shard_map/ppermute | solution.py:22
  93.2 4.3 %collective-permute-start.14 = (bf16[2,8,2048]{2,1,0:T(8,128)(2,1)S(1)}, bf16[2,8,2048]{2,1,0:T(8,128)(2,1)S(1)}, u32[]{:S(2)}, u32[]{:S(2)}) collective-permute-start(bf16[2,8,2048]{2,1,0:T(8,128)(2,1)S(1)} %get-tuple-element.61), channel_id=1, source_target_pairs={{0,16},{4,20},{8,24},{12,28},{16,0},{20,4},{24,8},{28,12},{1,17},{... | collective-permute-start | bytes 196616 | tf_op jit(solution)/shard_map/ppermute | solution.py:22
  93.7 15.2 %collective-permute-start.15 = (bf16[2,8,2048]{2,1,0:T(8,128)(2,1)S(1)}, bf16[2,8,2048]{2,1,0:T(8,128)(2,1)S(1)}, u32[]{:S(2)}, u32[]{:S(2)}) collective-permute-start(bf16[2,8,2048]{2,1,0:T(8,128)(2,1)S(1)} %get-tuple-element.60), channel_id=1, source_target_pairs={{0,24},{4,28},{8,16},{12,20},{16,8},{20,12},{24,0},{28,4},{1,25},{... | collective-permute-start | bytes 196616 | tf_op jit(solution)/shard_map/ppermute | solution.py:22
  96.2 12.8 %collective-permute-start.16 = (bf16[2,8,2048]{2,1,0:T(8,128)(2,1)S(1)}, bf16[2,8,2048]{2,1,0:T(8,128)(2,1)S(1)}, u32[]{:S(2)}, u32[]{:S(2)}) collective-permute-start(bf16[2,8,2048]{2,1,0:T(8,128)(2,1)S(1)} %get-tuple-element.59), channel_id=1, source_target_pairs={{0,4},{4,0},{8,12},{12,8},{16,20},{20,16},{24,28},{28,24},{1,5},{5... | collective-permute-start | bytes 196616 | tf_op jit(solution)/shard_map/ppermute | solution.py:22
  96.2 12.8 %collective-permute-start.17 = (bf16[2,8,2048]{2,1,0:T(8,128)(2,1)S(1)}, bf16[2,8,2048]{2,1,0:T(8,128)(2,1)S(1)}, u32[]{:S(2)}, u32[]{:S(2)}) collective-permute-start(bf16[2,8,2048]{2,1,0:T(8,128)(2,1)S(1)} %get-tuple-element.58), channel_id=1, source_target_pairs={{0,12},{4,8},{8,4},{12,0},{16,28},{20,24},{24,20},{28,16},{1,13},{... | collective-permute-start | bytes 196616 | tf_op jit(solution)/shard_map/ppermute | solution.py:22
  97.0 12.0 %collective-permute-start.18 = (bf16[2,8,2048]{2,1,0:T(8,128)(2,1)S(1)}, bf16[2,8,2048]{2,1,0:T(8,128)(2,1)S(1)}, u32[]{:S(2)}, u32[]{:S(2)}) collective-permute-start(bf16[2,8,2048]{2,1,0:T(8,128)(2,1)S(1)} %get-tuple-element.57), channel_id=1, source_target_pairs={{0,20},{4,16},{8,28},{12,24},{16,4},{20,0},{24,12},{28,8},{1,21},{... | collective-permute-start | bytes 196616 | tf_op jit(solution)/shard_map/ppermute | solution.py:22
  97.5 11.5 %collective-permute-start.19 = (bf16[2,8,2048]{2,1,0:T(8,128)(2,1)S(1)}, bf16[2,8,2048]{2,1,0:T(8,128)(2,1)S(1)}, u32[]{:S(2)}, u32[]{:S(2)}) collective-permute-start(bf16[2,8,2048]{2,1,0:T(8,128)(2,1)S(1)} %get-tuple-element.56), channel_id=1, source_target_pairs={{0,28},{4,24},{8,20},{12,16},{16,12},{20,8},{24,4},{28,0},{1,29},{... | collective-permute-start | bytes 196616 | tf_op jit(solution)/shard_map/ppermute | solution.py:22

commit v2 on v1

v2 whole, which is shorter than its diff:
```python
import functools

import jax
import jax.numpy as jnp
from jax import lax
from jax.experimental import pallas as pl
from jax.experimental.pallas import tpu as pltpu
from jax.sharding import PartitionSpec as P

BF16 = jnp.bfloat16
F32 = jnp.float32
VMEM_LIMIT = 48 * 1024 * 1024
CHUNK = 256
BACK = (((1,), (1,)), ((), ()))
CONTRACT = (((0,), (0,)), ((), ()))
PARAMS = pltpu.CompilerParams(vmem_limit_bytes=VMEM_LIMIT)
HOLD = pl.BlockSpec(memory_space=pl.ANY)


def dot(a, b):
    return jnp.dot(a, b, preferred_element_type=F32)


def swap(x, axis, size, k):
    return lax.ppermute(x, axis, [(i, i ^ k) for i in range(size)])


def estimate(flops, num_bytes):
    return pl.CostEstimate(flops=flops, bytes_accessed=num_bytes, transcendentals=0)


def array(shape, dtype):
    return jax.ShapeDtypeStruct(shape, dtype)


def pack_kernel(tokens, out_grad, out):
    joined = jnp.concatenate([tokens[...].astype(F32), out_grad[...].astype(F32)], axis=0)
    out[...] = joined.astype(BF16)


def pack(tokens, out_grad):
    rows, width = tokens.shape
    return pl.pallas_call(
        pack_kernel,
        out_shape=array((2 * rows, width), BF16),
        compiler_params=PARAMS,
        cost_estimate=estimate(0, 8 * rows * width),
        name="pack",
    )(tokens, out_grad)


def assemble_kernel(rows, *refs):
    pieces, (tok, grad, tok_t, grad_t) = refs[:-4], refs[-4:]
    both = [p[...].astype(F32) for p in pieces]
    all_tok = jnp.concatenate([b[:rows] for b in both], axis=0)
    all_grad = jnp.concatenate([b[rows:] for b in both], axis=0)
    tok[...] = all_tok.astype(BF16)
    grad[...] = all_grad.astype(BF16)
    tok_t[...] = all_tok.T.astype(BF16)
    grad_t[...] = all_grad.T.astype(BF16)


def assemble(pieces, rows):
    total, width = rows * len(pieces), pieces[0].shape[1]
    flat, turned = (total, width), (width, total)
    return pl.pallas_call(
        functools.partial(assemble_kernel, rows),
        out_shape=[array(shape, BF16) for shape in (flat, flat, turned, turned)],
        compiler_params=PARAMS,
        cost_estimate=estimate(0, 12 * total * width),
        name="assemble",
    )(*pieces)


def weight_specs(units):
    wide = pl.BlockSpec((CHUNK, units), lambda i, w: (i, w[0]))
    tall = pl.BlockSpec((units, CHUNK), lambda i, w: (w[0], i))
    return [wide, wide, tall]


def sums_kernel(where, tok, grad_t, gate_w, up_w, down_w, *refs):
    out, gate, up, back = refs[-4:]
    step = pl.program_id(0)

    @pl.when(step == 0)
    def _():
        for acc in (gate, up, back):
            acc[...] = jnp.zeros_like(acc)

    gate[...] += dot(tok[...], gate_w[...])
    up[...] += dot(tok[...], up_w[...])
    back[...] += dot(down_w[...], grad_t[...])

    @pl.when(step == pl.num_programs(0) - 1)
    def _():
        out[0] = gate[...].astype(out.dtype)
        out[1] = up[...].astype(out.dtype)
        out[2] = back[...].T.astype(out.dtype)


def partial_sums(where, tok, grad_t, weights, units, dtype, after=()):
    total, width = tok.shape
    return pl.pallas_call(
        sums_kernel,
        grid_spec=pltpu.PrefetchScalarGridSpec(
            num_scalar_prefetch=1,
            grid=(width // CHUNK,),
            in_specs=[
                pl.BlockSpec((total, CHUNK), lambda i, w: (0, i)),
                pl.BlockSpec((CHUNK, total), lambda i, w: (i, 0)),
                *weight_specs(units),
                *[HOLD] * len(after),
            ],
            out_specs=pl.BlockSpec((3, total, units), lambda i, w: (0, 0, 0)),
            scratch_shapes=[
                pltpu.VMEM((total, units), F32),
                pltpu.VMEM((total, units), F32),
                pltpu.VMEM((units, total), F32),
            ],
        ),
        out_shape=array((3, total, units), dtype),
        compiler_params=PARAMS,
        cost_estimate=estimate(6 * total * width * units, 6 * width * units),
        name="partial_sums",
    )(where, tok, grad_t, *weights, *after)


def combine_kernel(own, other, out):
    out[...] = (own[...] + other[...].astype(F32)).astype(BF16)


def combine(own, other):
    return pl.pallas_call(
        combine_kernel,
        out_shape=array(own.shape, BF16),
        compiler_params=PARAMS,
        cost_estimate=estimate(own.size, 8 * own.size),
        name="combine",
    )(own, other)


def activate_kernel(own, *refs):
    others, out = refs[:-1], refs[-1]
    gate, up, hidden_grad = (
        functools.reduce(lambda s, o: s + o[j].astype(F32), others, own[j]) for j in range(3)
    )
    sig = jax.nn.sigmoid(gate)
    swish = gate * sig
    out[0] = (swish * up).astype(BF16)
    out[1] = (hidden_grad * up * sig * (1.0 + gate * (1.0 - sig))).astype(BF16)
    out[2] = (hidden_grad * swish).astype(BF16)


def activate(own, others):
    return pl.pallas_call(
        activate_kernel,
        out_shape=array(own.shape, BF16),
        compiler_params=PARAMS,
        cost_estimate=estimate(8 * own.size, 12 * own.size),
        name="activate",
    )(own, *others)


def turned(x):
    return x.astype(F32).T.astype(BF16)


def use_kernel(first, last, with_products, with_grads, where, act, *refs):
    refs = list(refs)
    step = pl.program_id(0)
    if with_products:
        gate_w, up_w, down_w = (refs.pop(0) for _ in range(3))
        before = None if first else refs.pop(0)
    if with_grads:
        tok_t, grad = refs.pop(0), refs.pop(0)
    gate_t, up_t, hidden_t = refs[-3:]
    outs = refs[-3 - (1 + last) * with_products - 3 * with_grads : -3]

    @pl.when(step == 0)
    def _():
        gate_t[...] = turned(act[1])
        up_t[...] = turned(act[2])
        hidden_t[...] = turned(act[0])

    if with_products:
        back = dot(gate_w[...], gate_t[...]) + dot(up_w[...], up_t[...])
        for j, term in enumerate((dot(act[0], down_w[...]), back.T)):
            term = term if first else before[j] + term
            if last:
                half = term.shape[0] // 2
                outs[0][j] = term[:half]
                outs[1][j] = term[half:]
            else:
                outs[0][j] = term
    if with_grads:
        gate_g, up_g, down_g = outs[-3:]
        gate_g[...] = dot(tok_t[...], act[1]).astype(BF16)
        up_g[...] = dot(tok_t[...], act[2]).astype(BF16)
        rows = down_g.shape[0]
        start = pl.multiple_of(step * rows, rows)
        down_g[...] = dot(hidden_t[pl.ds(start, rows)], grad[...]).astype(BF16)


def use(where, act, weights=None, terms=None, last=False, sides=None, grads=(), after=()):
    _, total, units = act.shape
    first = terms is None
    specs = [pl.BlockSpec((3, total, units), lambda i, w: (0, 0, 0))]
    args, out_specs, out_shape, aliases = [act], [], [], {}
    moved = 0
    if weights is not None:
        all_units, width = weights[2].shape
        specs += weight_specs(units)
        args += weights
        if not first:
            specs.append(pl.BlockSpec((2, total, CHUNK), lambda i, w: (0, 0, i)))
            args.append(terms)
        held = total // 2 if last else total
        out_specs += [pl.BlockSpec((2, held, CHUNK), lambda i, w: (0, 0, i))] * (1 + last)
        out_shape += [array((2, held, width), F32)] * (1 + last)
        moved += 6 * width * units
    if sides is not None:
        tok_t, grad, all_units = sides
        width = grad.shape[1]
        steps = width // CHUNK
        rows = units // steps
        specs += [
            pl.BlockSpec((CHUNK, total), lambda i, w: (i, 0)),
            pl.BlockSpec((total, width), lambda i, w: (0, 0)),
        ]
        args += [tok_t, grad]
        for j, grad_before in enumerate(grads):
            aliases[1 + len(args)] = len(out_shape) + j
            specs.append(HOLD)
            args.append(grad_before)
        wide = pl.BlockSpec((CHUNK, units), lambda i, w: (i, w[0]))
        out_specs += [wide, wide, pl.BlockSpec((rows, width), lambda i, w: (w[0] * steps + i, 0))]
        out_shape += [array((width, all_units), BF16)] * 2 + [array((all_units, width), BF16)]
        moved += 6 * width * units
    return pl.pallas_call(
        functools.partial(use_kernel, first, last, weights is not None, sides is not None),
        grid_spec=pltpu.PrefetchScalarGridSpec(
            num_scalar_prefetch=1,
            grid=(width // CHUNK,),
            in_specs=specs + [HOLD] * len(after),
            out_specs=out_specs,
            scratch_shapes=[pltpu.VMEM((units, total), BF16)] * 3,
        ),
        out_shape=out_shape,
        input_output_aliases=aliases,
        compiler_params=PARAMS,
        cost_estimate=estimate(total * moved, moved),
        name=("products" if weights else "") + ("grads" if sides else ""),
    )(where, *args, *after)


def fold_kernel(rows, own, other, keep, *sent):
    total = own[...] + other[...]
    keep[...] = total[:, :rows]
    for i, out in enumerate(sent, 1):
        out[...] = total[:, i * rows : (i + 1) * rows].astype(BF16)


def fold(own, other, rows):
    _, total, width = own.shape
    others = total // rows - 1
    return pl.pallas_call(
        functools.partial(fold_kernel, rows),
        out_shape=[array((2, rows, width), F32)] + [array((2, rows, width), BF16)] * others,
        compiler_params=PARAMS,
        cost_estimate=estimate(own.size, 12 * own.size),
        name="fold",
    )(own, other)


def finish_kernel(own, *refs):
    others, outs = refs[:-2], refs[-2:]
    for j, out in enumerate(outs):
        total = functools.reduce(lambda s, o: s + o[j].astype(F32), others, own[j])
        out[...] = total.astype(BF16)


def finish(own, others):
    return pl.pallas_call(
        finish_kernel,
        out_shape=[array(own.shape[1:], BF16)] * 2,
        compiler_params=PARAMS,
        cost_estimate=estimate(own.size, 12 * own.size),
        name="finish",
    )(own, *others)


def pairwise(n_row, n_col, tokens, gate_weight, up_weight, down_weight, out_grad):
    rows = tokens.shape[0]
    all_units = gate_weight.shape[1]
    units = all_units // n_col
    weights = (gate_weight, up_weight, down_weight)
    col = lax.axis_index("col")
    where = {k: jnp.bitwise_xor(col, k).reshape(1) for k in range(n_col)}
    along_row = functools.partial(swap, axis="row", size=n_row)
    along_col = functools.partial(swap, axis="col", size=n_col)

    mine = pack(tokens, out_grad)
    even = [mine] + [along_row(mine, k=k) for k in range(2, n_row, 2)]
    odd = [along_row(piece, k=1) for piece in even]
    tok, grad, tok_t, grad_t = assemble(even + odd, rows)
    sides = (tok_t, grad, all_units)

    sums = functools.partial(partial_sums, tok=tok, grad_t=grad_t, weights=weights, units=units)
    near = along_col(sums(where[3], dtype=BF16), k=1)
    pair = combine(sums(where[2], dtype=F32), near)
    from_far = along_col(pair, k=2)
    from_near = along_col(sums(where[1], dtype=BF16, after=(pair,)), k=1)
    own = activate(sums(where[0], dtype=F32), [from_near, from_far])

    far_act = along_col(own, k=2)
    near_act = along_col(own, k=1)
    terms, *grads = use(where[0], own, weights, sides=sides)
    held, _ = lax.optimization_barrier((far_act, (terms, grads)))
    last_act = along_col(held, k=1)
    terms, *grads = use(where[1], near_act, weights, terms, sides=sides, grads=grads)
    (terms,) = use(where[2], far_act, weights, terms)
    kept, given = use(where[3], last_act, weights, terms, last=True)

    other = along_row(given, k=1)
    grads = use(where[2], far_act, sides=sides, grads=grads, after=(given,))
    other, _ = lax.optimization_barrier((other, grads))
    mine, *sent = fold(kept, other, rows)
    parts = [along_row(piece, k=2 * i) for i, piece in enumerate(sent, 1)]
    grads = use(where[3], last_act, sides=sides, grads=grads, after=(mine,))
    mixed, input_grad = finish(mine, parts)
    return (mixed, input_grad, *grads)


def gathered(tokens, gate_weight, up_weight, down_weight, out_grad):
    tok = lax.all_gather(tokens, "row", axis=0, tiled=True)
    grad = lax.all_gather(out_grad, "row", axis=0, tiled=True)

    def total(x):
        return lax.psum_scatter(x, "col", scatter_dimension=0, tiled=True)

    def back_dot(a, b):
        return lax.dot_general(a, b, BACK, preferred_element_type=F32)

    def outer(a, b):
        return lax.dot_general(a, b, CONTRACT, preferred_element_type=F32).astype(BF16)

    gate, up = total(dot(tok, gate_weight)), total(dot(tok, up_weight))
    hidden_grad = total(back_dot(grad, down_weight))
    sig = jax.nn.sigmoid(gate)
    swish = gate * sig
    hidden = (swish * up).astype(BF16)
    gate_delta = (hidden_grad * up * sig * (1.0 + gate * (1.0 - sig))).astype(BF16)
    up_delta = (hidden_grad * swish).astype(BF16)
    hidden, gate_delta, up_delta = (
        lax.all_gather(x, "col", axis=0, tiled=True) for x in (hidden, gate_delta, up_delta)
    )
    mixed = dot(hidden, down_weight)
    input_grad = back_dot(gate_delta, gate_weight) + back_dot(up_delta, up_weight)
    mixed, input_grad = (
        lax.psum_scatter(x, "row", scatter_dimension=0, tiled=True).astype(BF16)
        for x in (mixed, input_grad)
    )
    return (
        mixed,
        input_grad,
        outer(tok, gate_delta),
        outer(tok, up_delta),
        outer(hidden, grad),
    )


def solution(mesh):
    n_row, n_col = mesh.shape["row"], mesh.shape["col"]

    def shards(*args):
        tokens, gate_weight = args[:2]
        fits = (
            n_row & (n_row - 1) == 0
            and n_row > 1
            and n_col == 4
            and tokens.shape[0] % 8 == 0
            and tokens.shape[1] % CHUNK == 0
            and gate_weight.shape[1] % (128 * n_col) == 0
            and gate_weight.shape[1] % (16 * n_col * (tokens.shape[1] // CHUNK)) == 0
        )
        if fits:
            return pairwise(n_row, n_col, *args)
        return gathered(*args)

    return jax.shard_map(
        shards,
        mesh=mesh,
        in_specs=(
            P("row", "col"),
            P("col", "row"),
            P("col", "row"),
            P("row", "col"),
            P("row", "col"),
        ),
        out_specs=(
            P("row", "col"),
            P("row", "col"),
            P("col", "row"),
            P("col", "row"),
            P("row", "col"),
        ),
        check_vma=False,
    )
```

time: 110 us -> 116 us (1.055); the launches traced: 110 us -> 114 us
  Pallas kernels: 65.9 us -> 83 us
  waiting for transfers between devices: 17.7 us -> 9.87 us
  starting transfers between devices: 23 us -> 19.2 us
    pallas_call x10 -> x12, Pallas kernels: 43.8 us -> 52.5 us  [the longest x6 51.2 us: use(): pl.pallas_call(functools.partial(use_kernel, first, last, weights is not...]
    pallas_call x4, Pallas kernels: 22.1 us -> 30.5 us  [partial_sums(): pl.pallas_call(sums_kernel, grid_spec=pltpu.PrefetchScalarGridSpec(num_sc...]
    ppermute x20 -> x17, waiting for transfers between devices: 17.7 us -> 9.87 us  [swap(): return lax.ppermute(x, axis, [(i, i ^ k) for i in range(size)])]
    ppermute x20 -> x17, starting transfers between devices: 23 us -> 19.2 us  [swap(): return lax.ppermute(x, axis, [(i, i ^ k) for i in range(size)])]
  transfers between devices with their start and end apart: 20 -> 17, of which waited for: 8 -> 5; matrix products, arithmetic and copies ran while one was open for 0% -> 0% of each run, Pallas kernels for 49% -> 51%
where the time goes in v2:
time: 116 us; the launch traced here: 114 us
  Pallas kernels  83 us (72%)
  starting transfers between devices  19.2 us (17%)
  waiting for transfers between devices  9.87 us (9%)
  local copies, waits for them, and re-layouts  1.51 us (1%)
    pallas_call x6, Pallas kernels, use(): pl.pallas_call(functools.partial(use_kernel, first, last, weights is not...  51.2 us
    pallas_call x4, Pallas kernels, partial_sums(): pl.pallas_call(sums_kernel, grid_spec=pltpu.PrefetchScalarGridSpec(num_sc...  30.5 us
    ppermute x17, starting transfers between devices, swap(): return lax.ppermute(x, axis, [(i, i ^ k) for i in range(size)])  19.2 us
    ppermute x17, waiting for transfers between devices, swap(): return lax.ppermute(x, axis, [(i, i ^ k) for i in range(size)])  9.87 us
  transfers between devices with their start and end apart: 17, of which 5 were waited for; matrix products, arithmetic and copies ran while one was open for 0% of the time, Pallas kernels for 51%

profile of v2, /device:TPU:0, one launch (start us, length us, event | category | flops | bytes accessed | tf_op | source)
XLA Modules:
  0.0 114.3 jit_solution(13110696682160406758)
XLA Ops:
  0.6 0.7 copy-done
  1.4 0.8 copy-done.1
  2.2 2.9 %collective-permute-start = (bf16[16,2048]{1,0:T(8,128)(2,1)S(1)}, bf16[16,2048]{1,0:T(8,128)(2,1)S(1)}, u32[]{:S(2)}, u32[]{:S(2)}) collective-permute-start(bf16[16,2048]{1,0:T(8,128)(2,1)S(1)} %pack.1.refs_0_), channel_id=1, source_target_pairs={{0,8},{4,12},{8,0},{12,4},{16,24},{20,28},{24,16},{28,20},{1,9},{5... | collective-permute-start | bytes 196616 | tf_op jit(solution)/shard_map/ppermute | solution.py:25
  5.1 1.5 %collective-permute-start.1 = (bf16[16,2048]{1,0:T(8,128)(2,1)S(1)}, bf16[16,2048]{1,0:T(8,128)(2,1)S(1)}, u32[]{:S(2)}, u32[]{:S(2)}) collective-permute-start(bf16[16,2048]{1,0:T(8,128)(2,1)S(1)} %pack.1.refs_0_), channel_id=1, source_target_pairs={{0,16},{4,20},{8,24},{12,28},{16,0},{20,4},{24,8},{28,12},{1,17},{... | collective-permute-start | bytes 196616 | tf_op jit(solution)/shard_map/ppermute | solution.py:25
  6.6 0.0 collective-permute-start.2
  6.6 0.0 collective-permute-start.3
  6.6 0.8 collective-permute-done.refs_1_
  7.5 0.0 collective-permute-start.4
  7.5 1.9 %collective-permute-done.1.refs_2_ = bf16[16,2048]{1,0:T(8,128)(2,1)S(1)} collective-permute-done((bf16[16,2048]{1,0:T(8,128)(2,1)S(1)}, bf16[16,2048]{1,0:T(8,128)(2,1)S(1)}, u32[]{:S(2)}, u32[]{:S(2)}) %collective-permute-start.1) | collective-permute-done | bytes 65568 | tf_op jit(solution)/shard_map/ppermute | solution.py:25
  9.4 0.0 collective-permute-start.5
  9.4 2.4 %collective-permute-done.2.refs_3_ = bf16[16,2048]{1,0:T(8,128)(2,1)S(1)} collective-permute-done((bf16[16,2048]{1,0:T(8,128)(2,1)S(1)}, bf16[16,2048]{1,0:T(8,128)(2,1)S(1)}, u32[]{:S(2)}, u32[]{:S(2)}) %collective-permute-start.2) | collective-permute-done | bytes 65568 | tf_op jit(solution)/shard_map/ppermute | solution.py:25
  11.8 0.0 collective-permute-start.6
  11.8 0.0 collective-permute-done.3.refs_4_
  11.8 0.0 collective-permute-done.4.refs_5_
  11.8 1.2 %collective-permute-done.6.refs_7_ = bf16[16,2048]{1,0:T(8,128)(2,1)S(1)} collective-permute-done((bf16[16,2048]{1,0:T(8,128)(2,1)S(1)}, bf16[16,2048]{1,0:T(8,128)(2,1)S(1)}, u32[]{:S(2)}, u32[]{:S(2)}) %collective-permute-start.6) | collective-permute-done | bytes 65568 | tf_op jit(solution)/shard_map/ppermute | solution.py:25
  13.0 0.3 assemble.1
  13.4 7.6 %partial_sums.6 = bf16[3,64,768]{2,1,0:T(8,128)(2,1)S(1)} custom-call(s32[1]{0:T(128)} %bitcast.where, bf16[64,2048]{1,0:T(8,128)(2,1)S(1)} %get-tuple-element.33.tok, bf16[2048,64]{1,0:T(8,128)(2,1)S(1)} %get-tuple-element.34.grad_t, bf16[2048,3072]{1,0:T(8,128)(2,1)} %refs_0_.7, bf16[2048,3072]{1,0:T(8,128)(2,1)} %refs_1_.7, bf16[3072,2048]{1,0:T(8,128)(2,1)} %refs_2_.7), custom_call_target="tpu_custom_call" | custom-call | flops 603979776 | bytes 9437184 | tf_op jit(solution)/shard_map/partial_sums/pallas_call | solution.py:103
  21.0 1.6 %collective-permute-start.7 = (bf16[3,64,768]{2,1,0:T(8,128)(2,1)S(1)}, bf16[3,64,768]{2,1,0:T(8,128)(2,1)S(1)}, u32[]{:S(2)}, u32[]{:S(2)}) collective-permute-start(bf16[3,64,768]{2,1,0:T(8,128)(2,1)S(1)} %partial_sums.6), channel_id=1, source_target_pairs={{0,1},{1,0},{2,3},{3,2},{4,5},{5,4},{6,7},{7,6},{8,9},{9,8},{10,11... | collective-permute-start | bytes 884744 | tf_op jit(solution)/shard_map/ppermute | solution.py:25
  22.7 7.6 %partial_sums.5.own = f32[3,64,768]{2,1,0:T(8,128)S(1)} custom-call(s32[1]{0:T(128)} %bitcast.3.where, bf16[64,2048]{1,0:T(8,128)(2,1)S(1)} %get-tuple-element.33.tok, bf16[2048,64]{1,0:T(8,128)(2,1)S(1)} %get-tuple-element.34.grad_t, bf16[2048,3072]{1,0:T(8,128)(2,1)} %refs_0_.7, bf16[2048,3072]{1,0:T(8,128)(2,1)} %refs_1_.7, bf16[3072,2048]{1,0:T(8,128)(2,1)} %refs_2_.7), custom_call_target="tpu_custom_call" | custom-call | flops 603979776 | bytes 9437184 | tf_op jit(solution)/shard_map/partial_sums/pallas_call | solution.py:103
  30.3 0.1 combine.1.refs_0_
  30.3 7.6 %partial_sums.7 = bf16[3,64,768]{2,1,0:T(8,128)(2,1)S(1)} custom-call(s32[1]{0:T(128)} %bitcast.2.where, bf16[64,2048]{1,0:T(8,128)(2,1)S(1)} %get-tuple-element.33.tok, bf16[2048,64]{1,0:T(8,128)(2,1)S(1)} %get-tuple-element.34.grad_t, bf16[2048,3072]{1,0:T(8,128)(2,1)} %refs_0_.7, bf16[2048,3072]{1,0:T(8,128)(2,1)} %refs_1_.7, bf16[3072,2048]{1,0:T(8,128)(2,1)} %refs_2_.7, ...), custom_call_target="tpu_custom_call" | custom-call | flops 603979776 | bytes 9437184 | tf_op jit(solution)/shard_map/partial_sums/pallas_call | solution.py:103
  38.0 1.5 %collective-permute-start.8 = (bf16[3,64,768]{2,1,0:T(8,128)(2,1)S(1)}, bf16[3,64,768]{2,1,0:T(8,128)(2,1)S(1)}, u32[]{:S(2)}, u32[]{:S(2)}) collective-permute-start(bf16[3,64,768]{2,1,0:T(8,128)(2,1)S(1)} %partial_sums.7), channel_id=1, source_target_pairs={{0,1},{1,0},{2,3},{3,2},{4,5},{5,4},{6,7},{7,6},{8,9},{9,8},{10,11... | collective-permute-start | bytes 884744 | tf_op jit(solution)/shard_map/ppermute | solution.py:25
  39.5 2.6 %collective-permute-start.9 = (bf16[3,64,768]{2,1,0:T(8,128)(2,1)S(1)}, bf16[3,64,768]{2,1,0:T(8,128)(2,1)S(1)}, u32[]{:S(2)}, u32[]{:S(2)}) collective-permute-start(bf16[3,64,768]{2,1,0:T(8,128)(2,1)S(1)} %combine.1.refs_0_), channel_id=1, source_target_pairs={{0,2},{1,3},{2,0},{3,1},{4,6},{5,7},{6,4},{7,5},{8,10},{9,11},{10,... | collective-permute-start | bytes 884744 | tf_op jit(solution)/shard_map/ppermute | solution.py:25
  42.1 7.6 %partial_sums.4.own = f32[3,64,768]{2,1,0:T(8,128)S(1)} custom-call(s32[1]{0:T(128)} %bitcast.1.where, bf16[64,2048]{1,0:T(8,128)(2,1)S(1)} %get-tuple-element.33.tok, bf16[2048,64]{1,0:T(8,128)(2,1)S(1)} %get-tuple-element.34.grad_t, bf16[2048,3072]{1,0:T(8,128)(2,1)} %refs_0_.7, bf16[2048,3072]{1,0:T(8,128)(2,1)} %refs_1_.7, bf16[3072,2048]{1,0:T(8,128)(2,1)} %refs_2_.7), custom_call_target="tpu_custom_call" | custom-call | flops 603979776 | bytes 9437184 | tf_op jit(solution)/shard_map/partial_sums/pallas_call | solution.py:103
  49.7 3.5 %collective-permute-done.8.refs_0_ = bf16[3,64,768]{2,1,0:T(8,128)(2,1)S(1)} collective-permute-done((bf16[3,64,768]{2,1,0:T(8,128)(2,1)S(1)}, bf16[3,64,768]{2,1,0:T(8,128)(2,1)S(1)}, u32[]{:S(2)}, u32[]{:S(2)}) %collective-permute-start.8) | collective-permute-done | bytes 294944 | tf_op jit(solution)/shard_map/ppermute | solution.py:25
  53.2 0.0 collective-permute-done.9.refs_1_
  53.2 0.2 activate.1.act
  53.3 1.9 %collective-permute-start.10 = (bf16[3,64,768]{2,1,0:T(8,128)(2,1)S(1)}, bf16[3,64,768]{2,1,0:T(8,128)(2,1)S(1)}, u32[]{:S(2)}, u32[]{:S(2)}) collective-permute-start(bf16[3,64,768]{2,1,0:T(8,128)(2,1)S(1)} %activate.1.act), channel_id=1, source_target_pairs={{0,2},{1,3},{2,0},{3,1},{4,6},{5,7},{6,4},{7,5},{8,10},{9,11},{10,... | collective-permute-start | bytes 884744 | tf_op jit(solution)/shard_map/ppermute | solution.py:25
  55.3 3.4 %collective-permute-start.12 = (bf16[3,64,768]{2,1,0:T(8,128)(2,1)S(1)}, bf16[3,64,768]{2,1,0:T(8,128)(2,1)S(1)}, u32[]{:S(2)}, u32[]{:S(2)}) collective-permute-start(bf16[3,64,768]{2,1,0:T(8,128)(2,1)S(1)} %activate.1.act), channel_id=1, source_target_pairs={{0,1},{1,0},{2,3},{3,2},{4,5},{5,4},{6,7},{7,6},{8,9},{9,8},{10,11... | collective-permute-start | bytes 884744 | tf_op jit(solution)/shard_map/ppermute | solution.py:25
  58.7 11.5 %productsgrads.2 = (f32[2,64,2048]{2,1,0:T(8,128)S(1)}, bf16[2048,3072]{1,0:T(8,128)(2,1)}, bf16[2048,3072]{1,0:T(8,128)(2,1)}, bf16[3072,2048]{1,0:T(8,128)(2,1)}) custom-call(s32[1]{0:T(128)} %bitcast.1.where, bf16[3,64,768]{2,1,0:T(8,128)(2,1)S(1)} %activate.1.act, bf16[2048,3072]{1,0:T(8,128)(2,1)} %refs_0_.7, bf16[2048,3072]{1,0:T(8,128)(2,1)} %refs_1_.7, ...), custom_call_target="tpu_custom_call" | custom-call | flops 1207959552 | bytes 18874368 | tf_op jit(solution)/shard_map/productsgrads/pallas_call | solution.py:239
  70.2 0.0 collective-permute-done.10.act
  70.2 0.0 collective-permute-start.11
  70.2 0.0 collective-permute-done.12.act
  70.2 11.5 %productsgrads.3 = (f32[2,64,2048]{2,1,0:T(8,128)S(1)}, bf16[2048,3072]{1,0:T(8,128)(2,1)}, bf16[2048,3072]{1,0:T(8,128)(2,1)}, bf16[3072,2048]{1,0:T(8,128)(2,1)}) custom-call(s32[1]{0:T(128)} %bitcast.2.where, bf16[3,64,768]{2,1,0:T(8,128)(2,1)S(1)} %collective-permute-done.12.act, ...), custom_call_target="tpu_custom_call", output_to_operand_aliasing={{1}: (8, {}), {2}: (9, {}), {3}: (10, {})} | custom-call | flops 1207959552 | bytes 18874368 | tf_op jit(solution)/shard_map/productsgrads/pallas_call | solution.py:239
  81.7 8.0 %products.2.refs_3_ = f32[2,64,2048]{2,1,0:T(8,128)S(1)} custom-call(s32[1]{0:T(128)} %bitcast.3.where, bf16[3,64,768]{2,1,0:T(8,128)(2,1)S(1)} %collective-permute-done.10.act, bf16[2048,3072]{1,0:T(8,128)(2,1)} %refs_0_.7, bf16[2048,3072]{1,0:T(8,128)(2,1)} %refs_1_.7, bf16[3072,2048]{1,0:T(8,128)(2,1)} %refs_2_.7, ...), custom_call_target="tpu_custom_call" | custom-call | flops 603979776 | bytes 9437184 | tf_op jit(solution)/shard_map/products/pallas_call | solution.py:239
  89.8 8.0 %products.3 = (f32[2,32,2048]{2,1,0:T(8,128)S(1)}, f32[2,32,2048]{2,1,0:T(8,128)S(1)}) custom-call(s32[1]{0:T(128)} %bitcast.where, bf16[3,64,768]{2,1,0:T(8,128)(2,1)S(1)} %collective-permute-done.11.act, bf16[2048,3072]{1,0:T(8,128)(2,1)} %refs_0_.7, bf16[2048,3072]{1,0:T(8,128)(2,1)} %refs_1_.7, bf16[3072,2048]{1,0:T(8,128)(2,1)} %refs_2_.7, ...), custom_call_target="tpu_custom_call" | custom-call | flops 603979776 | bytes 9437184 | tf_op jit(solution)/shard_map/products/pallas_call | solution.py:239
  97.8 0.1 collective-permute-start.13
  97.9 6.1 %grads.2 = (bf16[2048,3072]{1,0:T(8,128)(2,1)}, bf16[2048,3072]{1,0:T(8,128)(2,1)}, bf16[3072,2048]{1,0:T(8,128)(2,1)}) custom-call(s32[1]{0:T(128)} %bitcast.3.where, bf16[3,64,768]{2,1,0:T(8,128)(2,1)S(1)} %collective-permute-done.10.act, ...), custom_call_target="tpu_custom_call", output_to_operand_aliasing={{0}: (4, {}), {1}: (5, {}), {2}: (6, {})} | custom-call | flops 603979776 | bytes 9437184 | tf_op jit(solution)/shard_map/grads/pallas_call | solution.py:239
  104.0 0.0 collective-permute-done.13.other
  104.0 0.1 fold.1
  104.1 0.6 collective-permute-start.14
  104.6 0.5 collective-permute-start.15
  105.1 2.5 %collective-permute-start.16 = (bf16[2,8,2048]{2,1,0:T(8,128)(2,1)S(1)}, bf16[2,8,2048]{2,1,0:T(8,128)(2,1)S(1)}, u32[]{:S(2)}, u32[]{:S(2)}) collective-permute-start(bf16[2,8,2048]{2,1,0:T(8,128)(2,1)S(1)} %get-tuple-element.55), channel_id=1, source_target_pairs={{0,24},{4,28},{8,16},{12,20},{16,8},{20,12},{24,0},{28,4},{1,25},{... | collective-permute-start | bytes 196616 | tf_op jit(solution)/shard_map/ppermute | solution.py:25
  107.6 6.0 %grads.3 = (bf16[2048,3072]{1,0:T(8,128)(2,1)}, bf16[2048,3072]{1,0:T(8,128)(2,1)}, bf16[3072,2048]{1,0:T(8,128)(2,1)}) custom-call(s32[1]{0:T(128)} %bitcast.where, bf16[3,64,768]{2,1,0:T(8,128)(2,1)S(1)} %collective-permute-done.11.act, ...), custom_call_target="tpu_custom_call", output_to_operand_aliasing={{0}: (4, {}), {1}: (5, {}), {2}: (6, {})} | custom-call | flops 603979776 | bytes 9437184 | tf_op jit(solution)/shard_map/grads/pallas_call | solution.py:239
  113.7 0.0 collective-permute-done.14.refs_0_
  113.7 0.0 collective-permute-done.15.refs_1_
  113.7 0.0 collective-permute-done.16.refs_2_
  113.7 0.6 finish.1
  (6 shorter events, 0.0 us)
Async XLA Ops:
  0.6 0.8 copy-start
  1.4 0.8 copy-start.1
  2.2 5.3 %collective-permute-start = (bf16[16,2048]{1,0:T(8,128)(2,1)S(1)}, bf16[16,2048]{1,0:T(8,128)(2,1)S(1)}, u32[]{:S(2)}, u32[]{:S(2)}) collective-permute-start(bf16[16,2048]{1,0:T(8,128)(2,1)S(1)} %pack.1.refs_0_), channel_id=1, source_target_pairs={{0,8},{4,12},{8,0},{12,4},{16,24},{20,28},{24,16},{28,20},{1,9},{5... | collective-permute-start | bytes 196616 | tf_op jit(solution)/shard_map/ppermute | solution.py:25
  5.1 4.3 %collective-permute-start.1 = (bf16[16,2048]{1,0:T(8,128)(2,1)S(1)}, bf16[16,2048]{1,0:T(8,128)(2,1)S(1)}, u32[]{:S(2)}, u32[]{:S(2)}) collective-permute-start(bf16[16,2048]{1,0:T(8,128)(2,1)S(1)} %pack.1.refs_0_), channel_id=1, source_target_pairs={{0,16},{4,20},{8,24},{12,28},{16,0},{20,4},{24,8},{28,12},{1,17},{... | collective-permute-start | bytes 196616 | tf_op jit(solution)/shard_map/ppermute | solution.py:25
  6.6 5.2 %collective-permute-start.2 = (bf16[16,2048]{1,0:T(8,128)(2,1)S(1)}, bf16[16,2048]{1,0:T(8,128)(2,1)S(1)}, u32[]{:S(2)}, u32[]{:S(2)}) collective-permute-start(bf16[16,2048]{1,0:T(8,128)(2,1)S(1)} %pack.1.refs_0_), channel_id=1, source_target_pairs={{0,24},{4,28},{8,16},{12,20},{16,8},{20,12},{24,0},{28,4},{1,25},{... | collective-permute-start | bytes 196616 | tf_op jit(solution)/shard_map/ppermute | solution.py:25
  6.6 5.2 %collective-permute-start.3 = (bf16[16,2048]{1,0:T(8,128)(2,1)S(1)}, bf16[16,2048]{1,0:T(8,128)(2,1)S(1)}, u32[]{:S(2)}, u32[]{:S(2)}) collective-permute-start(bf16[16,2048]{1,0:T(8,128)(2,1)S(1)} %pack.1.refs_0_), channel_id=1, source_target_pairs={{0,4},{4,0},{8,12},{12,8},{16,20},{20,16},{24,28},{28,24},{1,5},{5... | collective-permute-start | bytes 196616 | tf_op jit(solution)/shard_map/ppermute | solution.py:25
  7.5 4.3 %collective-permute-start.4 = (bf16[16,2048]{1,0:T(8,128)(2,1)S(1)}, bf16[16,2048]{1,0:T(8,128)(2,1)S(1)}, u32[]{:S(2)}, u32[]{:S(2)}) collective-permute-start(bf16[16,2048]{1,0:T(8,128)(2,1)S(1)} %collective-permute-done.refs_1_), channel_id=1, source_target_pairs={{0,4},{4,0},{8,12},{12,8},{16,20},{20,16},{24,28},{28,24},{1,5},{5... | collective-permute-start | bytes 196616 | tf_op jit(solution)/shard_map/ppermute | solution.py:25
  9.4 2.4 %collective-permute-start.5 = (bf16[16,2048]{1,0:T(8,128)(2,1)S(1)}, bf16[16,2048]{1,0:T(8,128)(2,1)S(1)}, u32[]{:S(2)}, u32[]{:S(2)}) collective-permute-start(bf16[16,2048]{1,0:T(8,128)(2,1)S(1)} %collective-permute-done.1.refs_2_), channel_id=1, source_target_pairs={{0,4},{4,0},{8,12},{12,8},{16,20},{20,16},{24,28},{28,24},{1,5},{5... | collective-permute-start | bytes 196616 | tf_op jit(solution)/shard_map/ppermute | solution.py:25
  11.8 1.3 %collective-permute-start.6 = (bf16[16,2048]{1,0:T(8,128)(2,1)S(1)}, bf16[16,2048]{1,0:T(8,128)(2,1)S(1)}, u32[]{:S(2)}, u32[]{:S(2)}) collective-permute-start(bf16[16,2048]{1,0:T(8,128)(2,1)S(1)} %collective-permute-done.2.refs_3_), channel_id=1, source_target_pairs={{0,4},{4,0},{8,12},{12,8},{16,20},{20,16},{24,28},{28,24},{1,5},{5... | collective-permute-start | bytes 196616 | tf_op jit(solution)/shard_map/ppermute | solution.py:25
  21.0 9.3 %collective-permute-start.7 = (bf16[3,64,768]{2,1,0:T(8,128)(2,1)S(1)}, bf16[3,64,768]{2,1,0:T(8,128)(2,1)S(1)}, u32[]{:S(2)}, u32[]{:S(2)}) collective-permute-start(bf16[3,64,768]{2,1,0:T(8,128)(2,1)S(1)} %partial_sums.6), channel_id=1, source_target_pairs={{0,1},{1,0},{2,3},{3,2},{4,5},{5,4},{6,7},{7,6},{8,9},{9,8},{10,11... | collective-permute-start | bytes 884744 | tf_op jit(solution)/shard_map/ppermute | solution.py:25
  38.0 15.2 %collective-permute-start.8 = (bf16[3,64,768]{2,1,0:T(8,128)(2,1)S(1)}, bf16[3,64,768]{2,1,0:T(8,128)(2,1)S(1)}, u32[]{:S(2)}, u32[]{:S(2)}) collective-permute-start(bf16[3,64,768]{2,1,0:T(8,128)(2,1)S(1)} %partial_sums.7), channel_id=1, source_target_pairs={{0,1},{1,0},{2,3},{3,2},{4,5},{5,4},{6,7},{7,6},{8,9},{9,8},{10,11... | collective-permute-start | bytes 884744 | tf_op jit(solution)/shard_map/ppermute | solution.py:25
  39.5 13.7 %collective-permute-start.9 = (bf16[3,64,768]{2,1,0:T(8,128)(2,1)S(1)}, bf16[3,64,768]{2,1,0:T(8,128)(2,1)S(1)}, u32[]{:S(2)}, u32[]{:S(2)}) collective-permute-start(bf16[3,64,768]{2,1,0:T(8,128)(2,1)S(1)} %combine.1.refs_0_), channel_id=1, source_target_pairs={{0,2},{1,3},{2,0},{3,1},{4,6},{5,7},{6,4},{7,5},{8,10},{9,11},{10,... | collective-permute-start | bytes 884744 | tf_op jit(solution)/shard_map/ppermute | solution.py:25
  53.3 16.8 %collective-permute-start.10 = (bf16[3,64,768]{2,1,0:T(8,128)(2,1)S(1)}, bf16[3,64,768]{2,1,0:T(8,128)(2,1)S(1)}, u32[]{:S(2)}, u32[]{:S(2)}) collective-permute-start(bf16[3,64,768]{2,1,0:T(8,128)(2,1)S(1)} %activate.1.act), channel_id=1, source_target_pairs={{0,2},{1,3},{2,0},{3,1},{4,6},{5,7},{6,4},{7,5},{8,10},{9,11},{10,... | collective-permute-start | bytes 884744 | tf_op jit(solution)/shard_map/ppermute | solution.py:25
  55.3 14.9 %collective-permute-start.12 = (bf16[3,64,768]{2,1,0:T(8,128)(2,1)S(1)}, bf16[3,64,768]{2,1,0:T(8,128)(2,1)S(1)}, u32[]{:S(2)}, u32[]{:S(2)}) collective-permute-start(bf16[3,64,768]{2,1,0:T(8,128)(2,1)S(1)} %activate.1.act), channel_id=1, source_target_pairs={{0,1},{1,0},{2,3},{3,2},{4,5},{5,4},{6,7},{7,6},{8,9},{9,8},{10,11... | collective-permute-start | bytes 884744 | tf_op jit(solution)/shard_map/ppermute | solution.py:25
  70.2 19.6 %collective-permute-start.11 = (bf16[3,64,768]{2,1,0:T(8,128)(2,1)S(1)}, bf16[3,64,768]{2,1,0:T(8,128)(2,1)S(1)}, u32[]{:S(2)}, u32[]{:S(2)}) collective-permute-start(bf16[3,64,768]{2,1,0:T(8,128)(2,1)S(1)} %collective-permute-done.10.act), channel_id=1, source_target_pairs={{0,1},{1,0},{2,3},{3,2},{4,5},{5,4},{6,7},{7,6},{8,9},{9,8},{10,11... | collective-permute-start | bytes 884744 | tf_op jit(solution)/shard_map/ppermute | solution.py:25
  97.8 6.2 %collective-permute-start.13 = (f32[2,32,2048]{2,1,0:T(8,128)S(1)}, f32[2,32,2048]{2,1,0:T(8,128)S(1)}, u32[]{:S(2)}, u32[]{:S(2)}) collective-permute-start(f32[2,32,2048]{2,1,0:T(8,128)S(1)} %get-tuple-element.44.refs_5_), channel_id=1, source_target_pairs={{0,4},{4,0},{8,12},{12,8},{16,20},{20,16},{24,28},{28,24},{1,5},{5... | collective-permute-start | bytes 1572872 | tf_op jit(solution)/shard_map/ppermute | solution.py:25
  104.1 9.6 %collective-permute-start.14 = (bf16[2,8,2048]{2,1,0:T(8,128)(2,1)S(1)}, bf16[2,8,2048]{2,1,0:T(8,128)(2,1)S(1)}, u32[]{:S(2)}, u32[]{:S(2)}) collective-permute-start(bf16[2,8,2048]{2,1,0:T(8,128)(2,1)S(1)} %get-tuple-element.53), channel_id=1, source_target_pairs={{0,8},{4,12},{8,0},{12,4},{16,24},{20,28},{24,16},{28,20},{1,9},{5... | collective-permute-start | bytes 196616 | tf_op jit(solution)/shard_map/ppermute | solution.py:25
  104.6 9.0 %collective-permute-start.15 = (bf16[2,8,2048]{2,1,0:T(8,128)(2,1)S(1)}, bf16[2,8,2048]{2,1,0:T(8,128)(2,1)S(1)}, u32[]{:S(2)}, u32[]{:S(2)}) collective-permute-start(bf16[2,8,2048]{2,1,0:T(8,128)(2,1)S(1)} %get-tuple-element.54), channel_id=1, source_target_pairs={{0,16},{4,20},{8,24},{12,28},{16,0},{20,4},{24,8},{28,12},{1,17},{... | collective-permute-start | bytes 196616 | tf_op jit(solution)/shard_map/ppermute | solution.py:25
  105.1 8.5 %collective-permute-start.16 = (bf16[2,8,2048]{2,1,0:T(8,128)(2,1)S(1)}, bf16[2,8,2048]{2,1,0:T(8,128)(2,1)S(1)}, u32[]{:S(2)}, u32[]{:S(2)}) collective-permute-start(bf16[2,8,2048]{2,1,0:T(8,128)(2,1)S(1)} %get-tuple-element.55), channel_id=1, source_target_pairs={{0,24},{4,28},{8,16},{12,20},{16,8},{20,12},{24,0},{28,4},{1,25},{... | collective-permute-start | bytes 196616 | tf_op jit(solution)/shard_map/ppermute | solution.py:25

commit v3 on v2

--- a/solution.py
+++ b/solution.py
@@ -10,11 +10,12 @@
 BF16 = jnp.bfloat16
 F32 = jnp.float32
 VMEM_LIMIT = 48 * 1024 * 1024
-CHUNK = 256
+CHUNKS = 4
 BACK = (((1,), (1,)), ((), ()))
 CONTRACT = (((0,), (0,)), ((), ()))
 PARAMS = pltpu.CompilerParams(vmem_limit_bytes=VMEM_LIMIT)
 HOLD = pl.BlockSpec(memory_space=pl.ANY)
+WHOLE = pl.BlockSpec(memory_space=pltpu.VMEM)
 
 
 def dot(a, b):
@@ -26,7 +27,11 @@
 
 
 def estimate(flops, num_bytes):
-    return pl.CostEstimate(flops=flops, bytes_accessed=num_bytes, transcendentals=0)
+    return pl.CostEstimate(flops=flops // 8, bytes_accessed=num_bytes // 8, transcendentals=0)
+
+
+def in_hbm(arrays):
+    return [pltpu.with_memory_space_constraint(x, pltpu.HBM) for x in arrays]
 
 
 def array(shape, dtype):
@@ -46,7 +51,7 @@
         compiler_params=PARAMS,
         cost_estimate=estimate(0, 8 * rows * width),
         name="pack",
-    )(tokens, out_grad)
+    )(*in_hbm((tokens, out_grad)))
 
 
 def assemble_kernel(rows, *refs):
@@ -72,57 +77,85 @@
     )(*pieces)
 
 
-def weight_specs(units):
-    wide = pl.BlockSpec((CHUNK, units), lambda i, w: (i, w[0]))
-    tall = pl.BlockSpec((units, CHUNK), lambda i, w: (w[0], i))
-    return [wide, wide, tall]
-
-
-def sums_kernel(where, tok, grad_t, gate_w, up_w, down_w, *refs):
-    out, gate, up, back = refs[-4:]
-    step = pl.program_id(0)
-
-    @pl.when(step == 0)
-    def _():
-        for acc in (gate, up, back):
-            acc[...] = jnp.zeros_like(acc)
-
-    gate[...] += dot(tok[...], gate_w[...])
-    up[...] += dot(tok[...], up_w[...])
-    back[...] += dot(down_w[...], grad_t[...])
-
-    @pl.when(step == pl.num_programs(0) - 1)
-    def _():
-        out[0] = gate[...].astype(out.dtype)
-        out[1] = up[...].astype(out.dtype)
-        out[2] = back[...].T.astype(out.dtype)
-
-
-def partial_sums(where, tok, grad_t, weights, units, dtype, after=()):
+def unit_block(k, units):
+    start = jnp.bitwise_xor(lax.axis_index("col"), k) * units
+    return pl.ds(pl.multiple_of(start, units), units)
+
+
+def span(i, size):
+    return slice(i * size, (i + 1) * size)
+
+
+def fetches(k, hbm, vmem, sems):
+    units, width = vmem[2].shape
+    mine = unit_block(k, units)
+    part = width // CHUNKS
+    copies = []
+    for i in range(CHUNKS):
+        rows = pl.ds(i * part, part)
+        ends = [
+            (hbm[0].at[rows, mine], vmem[0].at[rows]),
+            (hbm[1].at[rows, mine], vmem[1].at[rows]),
+            (hbm[2].at[mine, rows], vmem[2].at[:, rows]),
+        ]
+        copies.append(
+            [pltpu.make_async_copy(*ends[j], sems.at[i, j]) for j in range(len(ends))]
+        )
+    return copies
+
+
+def weight_scratch(units, width):
+    return [
+        pltpu.VMEM((width, units), BF16),
+        pltpu.VMEM((width, units), BF16),
+        pltpu.VMEM((units, width), BF16),
+        pltpu.SemaphoreType.DMA((CHUNKS, 3)),
+    ]
+
+
+def sums_kernel(k, tok, grad_t, gate_w, up_w, down_w, *refs):
+    out, gate_b, up_b, down_b, sems, gate, up, back = refs[-8:]
+    copies = fetches(k, (gate_w, up_w, down_w), (gate_b, up_b, down_b), sems)
+    for chunk in copies:
+        for copy in chunk:
+            copy.start()
+    part = grad_t.shape[0] // CHUNKS
+    for i, chunk in enumerate(copies):
+        here = span(i, part)
+        for copy in chunk:
+            copy.wait()
+        terms = (
+            (gate, dot(tok[:, here], gate_b[here])),
+            (up, dot(tok[:, here], up_b[here])),
+            (back, dot(down_b[:, here], grad_t[here])),
+        )
+        for acc, term in terms:
+            if i == 0:
+                acc[...] = term
+            else:
+                acc[...] += term
+    out[0] = gate[...].astype(out.dtype)
+    out[1] = up[...].astype(out.dtype)
+    out[2] = back[...].T.astype(out.dtype)
+
+
+def partial_sums(k, tok, grad_t, weights, units, dtype, after=()):
     total, width = tok.shape
     return pl.pallas_call(
-        sums_kernel,
-        grid_spec=pltpu.PrefetchScalarGridSpec(
-            num_scalar_prefetch=1,
-            grid=(width // CHUNK,),
-            in_specs=[
-                pl.BlockSpec((total, CHUNK), lambda i, w: (0, i)),
-                pl.BlockSpec((CHUNK, total), lambda i, w: (i, 0)),
-                *weight_specs(units),
-                *[HOLD] * len(after),
-            ],
-            out_specs=pl.BlockSpec((3, total, units), lambda i, w: (0, 0, 0)),
-            scratch_shapes=[
-                pltpu.VMEM((total, units), F32),
-                pltpu.VMEM((total, units), F32),
-                pltpu.VMEM((units, total), F32),
-            ],
-        ),
+        functools.partial(sums_kernel, k),
+        in_specs=[WHOLE, WHOLE] + [HOLD] * (3 + len(after)),
+        out_specs=WHOLE,
+        scratch_shapes=weight_scratch(units, width)
+        + [
+            pltpu.VMEM((total, units), F32),
+            pltpu.VMEM((total, units), F32),
+            pltpu.VMEM((units, total), F32),
+        ],
         out_shape=array((3, total, units), dtype),
         compiler_params=PARAMS,
         cost_estimate=estimate(6 * total * width * units, 6 * width * units),
         name="partial_sums",
-    )(where, tok, grad_t, *weights, *after)
+    )(tok, grad_t, *in_hbm(weights), *after)
 
 
 def combine_kernel(own, other, out):
@@ -165,92 +198,115 @@
     return x.astype(F32).T.astype(BF16)
 
 
-def use_kernel(first, last, with_products, with_grads, where, act, *refs):
+def use_kernel(k, first, last, with_products, with_grads, act, *refs):
     refs = list(refs)
-    step = pl.program_id(0)
+    width = 0
     if with_products:
-        gate_w, up_w, down_w = (refs.pop(0) for _ in range(3))
+        weights = [refs.pop(0) for _ in range(3)]
         before = None if first else refs.pop(0)
+        width = weights[2].shape[1]
     if with_grads:
         tok_t, grad = refs.pop(0), refs.pop(0)
-    gate_t, up_t, hidden_t = refs[-3:]
-    outs = refs[-3 - (1 + last) * with_products - 3 * with_grads : -3]
-
-    @pl.when(step == 0)
-    def _():
-        gate_t[...] = turned(act[1])
-        up_t[...] = turned(act[2])
-        hidden_t[...] = turned(act[0])
-
+        width = grad.shape[1]
+    units = act.shape[2]
+    if with_grads:
+        gate_s, up_s, down_s, out_sems = refs[-4:]
+        refs = refs[:-4]
     if with_products:
-        back = dot(gate_w[...], gate_t[...]) + dot(up_w[...], up_t[...])
-        for j, term in enumerate((dot(act[0], down_w[...]), back.T)):
-            term = term if first else before[j] + term
-            if last:
-                half = term.shape[0] // 2
-                outs[0][j] = term[:half]
-                outs[1][j] = term[half:]
-            else:
-                outs[0][j] = term
+        gate_b, up_b, down_b, sems = refs[-4:]
+        refs = refs[:-4]
+    outs = refs[-(1 + last) * with_products - 3 * with_grads :]
+    part, rows = width // CHUNKS, units // CHUNKS
+
+    arriving, leaving = [], []
+    if with_products:
+        arriving = fetches(k, weights, (gate_b, up_b, down_b), sems)
+        for chunk in arriving:
+            for copy in chunk:
+                copy.start()
+        gate_t, up_t = turned(act[1]), turned(act[2])
     if with_grads:
-        gate_g, up_g, down_g = outs[-3:]
-        gate_g[...] = dot(tok_t[...], act[1]).astype(BF16)
-        up_g[...] = dot(tok_t[...], act[2]).astype(BF16)
-        rows = down_g.shape[0]
-        start = pl.multiple_of(step * rows, rows)
-        down_g[...] = dot(hidden_t[pl.ds(start, rows)], grad[...]).astype(BF16)
-
-
-def use(where, act, weights=None, terms=None, last=False, sides=None, grads=(), after=()):
+        hidden_t = turned(act[0])
+        mine = unit_block(k, units)
+        start = jnp.bitwise_xor(lax.axis_index("col"), k) * units
+    for i in range(CHUNKS):
+        here = span(i, part)
+        if with_grads:
+            gate_g, up_g, down_g = outs[-3:]
+            gate_s[here] = dot(tok_t[here], act[1]).astype(BF16)
+            up_s[here] = dot(tok_t[here], act[2]).astype(BF16)
+            some = span(i, rows)
+            down_s[some] = dot(hidden_t[some], grad[...]).astype(BF16)
+            there = pl.ds(i * part, part)
+            below = pl.ds(pl.multiple_of(start + i * rows, rows), rows)
+            ends = (
+                (gate_s.at[there], gate_g.at[there, mine]),
+                (up_s.at[there], up_g.at[there, mine]),
+                (down_s.at[pl.ds(i * rows, rows)], down_g.at[below]),
+            )
+            for j, (source, target) in enumerate(ends):
+                copy = pltpu.make_async_copy(source, target, out_sems.at[i, j])
+                copy.start()
+                leaving.append(copy)
+        if with_products:
+            for copy in arriving[i]:
+                copy.wait()
+            back = dot(gate_b[here], gate_t) + dot(up_b[here], up_t)
+            for j, term in enumerate((dot(act[0], down_b[:, here]), back.T)):
+                term = term if first else before[j, :, here] + term
+                if last:
+                    half = term.shape[0] // 2
+                    outs[0][j, :, here] = term[:half]
+                    outs[1][j, :, here] = term[half:]
+                else:
+                    outs[0][j, :, here] = term
+    for copy in leaving:
+        copy.wait()
+
+
+def use(k, act, weights=None, terms=None, last=False, sides=None, grads=(), after=()):
     _, total, units = act.shape
     first = terms is None
-    specs = [pl.BlockSpec((3, total, units), lambda i, w: (0, 0, 0))]
-    args, out_specs, out_shape, aliases = [act], [], [], {}
+    specs, args = [WHOLE], [act]
+    out_specs, out_shape, scratch, aliases = [], [], [], {}
     moved = 0
     if weights is not None:
-        all_units, width = weights[2].shape
-        specs += weight_specs(units)
-        args += weights
+        width = weights[2].shape[1]
+        specs += [HOLD] * 3
+        args += in_hbm(weights)
         if not first:
-            specs.append(pl.BlockSpec((2, total, CHUNK), lambda i, w: (0, 0, i)))
+            specs.append(WHOLE)
             args.append(terms)
         held = total // 2 if last else total
-        out_specs += [pl.BlockSpec((2, held, CHUNK), lambda i, w: (0, 0, i))] * (1 + last)
+        out_specs += [WHOLE] * (1 + last)
         out_shape += [array((2, held, width), F32)] * (1 + last)
+        scratch += weight_scratch(units, width)
         moved += 6 * width * units
     if sides is not None:
         tok_t, grad, all_units = sides
         width = grad.shape[1]
-        steps = width // CHUNK
-        rows = units // steps
-        specs += [
-            pl.BlockSpec((CHUNK, total), lambda i, w: (i, 0)),
-            pl.BlockSpec((total, width), lambda i, w: (0, 0)),
-        ]
+        specs += [WHOLE, WHOLE]
         args += [tok_t, grad]
         for j, grad_before in enumerate(grads):
-            aliases[1 + len(args)] = len(out_shape) + j
+            aliases[len(args)] = len(out_shape) + j
             specs.append(HOLD)
             args.append(grad_before)
-        wide = pl.BlockSpec((CHUNK, units), lambda i, w: (i, w[0]))
-        out_specs += [wide, wide, pl.BlockSpec((rows, width), lambda i, w: (w[0] * steps + i, 0))]
-        out_shape += [array((width, all_units), BF16)] * 2 + [array((all_units, width), BF16)]
+        out_specs += [HOLD] * 3
+        out_shape += [pltpu.HBM((width, all_units), BF16)] * 2
+        out_shape.append(pltpu.HBM((all_units, width), BF16))
+        scratch += weight_scratch(units, width)
         moved += 6 * width * units
     return pl.pallas_call(
-        functools.partial(use_kernel, first, last, weights is not None, sides is not None),
-        grid_spec=pltpu.PrefetchScalarGridSpec(
-            num_scalar_prefetch=1,
-            grid=(width // CHUNK,),
-            in_specs=specs + [HOLD] * len(after),
-            out_specs=out_specs,
-            scratch_shapes=[pltpu.VMEM((units, total), BF16)] * 3,
-        ),
+        functools.partial(use_kernel, k, first, last, weights is not None, sides is not None),
+        in_specs=specs + [HOLD] * len(after),
+        out_specs=out_specs,
+        scratch_shapes=scratch,
         out_shape=out_shape,
         input_output_aliases=aliases,
         compiler_params=PARAMS,
         cost_estimate=estimate(total * moved, moved),
         name=("products" if weights else "") + ("grads" if sides else ""),
-    )(where, *args, *after)
+    )(*args, *after)
 
 
 def fold_kernel(rows, own, other, keep, *sent):
@@ -294,8 +350,6 @@
     all_units = gate_weight.shape[1]
     units = all_units // n_col
     weights = (gate_weight, up_weight, down_weight)
-    col = lax.axis_index("col")
-    where = {k: jnp.bitwise_xor(col, k).reshape(1) for k in range(n_col)}
     along_row = functools.partial(swap, axis="row", size=n_row)
     along_col = functools.partial(swap, axis="col", size=n_col)
 
@@ -306,27 +360,27 @@
     sides = (tok_t, grad, all_units)
 
     sums = functools.partial(partial_sums, tok=tok, grad_t=grad_t, weights=weights, units=units)
-    near = along_col(sums(where[3], dtype=BF16), k=1)
-    pair = combine(sums(where[2], dtype=F32), near)
+    near = along_col(sums(3, dtype=BF16), k=1)
+    pair = combine(sums(2, dtype=F32), near)
     from_far = along_col(pair, k=2)
-    from_near = along_col(sums(where[1], dtype=BF16, after=(pair,)), k=1)
-    own = activate(sums(where[0], dtype=F32), [from_near, from_far])
+    from_near = along_col(sums(1, dtype=BF16), k=1)
+    own = activate(sums(0, dtype=F32), [from_near, from_far])
 
     far_act = along_col(own, k=2)
     near_act = along_col(own, k=1)
-    terms, *grads = use(where[0], own, weights, sides=sides)
+    terms, *grads = use(0, own, weights, sides=sides)
     held, _ = lax.optimization_barrier((far_act, (terms, grads)))
     last_act = along_col(held, k=1)
-    terms, *grads = use(where[1], near_act, weights, terms, sides=sides, grads=grads)
-    (terms,) = use(where[2], far_act, weights, terms)
-    kept, given = use(where[3], last_act, weights, terms, last=True)
+    terms, *grads = use(1, near_act, weights, terms, sides=sides, grads=grads)
+    (terms,) = use(2, far_act, weights, terms)
+    kept, given = use(3, last_act, weights, terms, last=True)
 
     other = along_row(given, k=1)
-    grads = use(where[2], far_act, sides=sides, grads=grads, after=(given,))
+    grads = use(2, far_act, sides=sides, grads=grads, after=(given,))
     other, _ = lax.optimization_barrier((other, grads))
     mine, *sent = fold(kept, other, rows)
     parts = [along_row(piece, k=2 * i) for i, piece in enumerate(sent, 1)]
-    grads = use(where[3], last_act, sides=sides, grads=grads, after=(mine,))
+    grads = use(3, last_act, sides=sides, grads=grads, after=(mine,))
     mixed, input_grad = finish(mine, parts)
     return (mixed, input_grad, *grads)
 
@@ -379,9 +433,10 @@
             and n_row > 1
             and n_col == 4
             and tokens.shape[0] % 8 == 0
-            and tokens.shape[1] % CHUNK == 0
+            and tokens.shape[1] % (128 * CHUNKS) == 0
             and gate_weight.shape[1] % (128 * n_col) == 0
-            and gate_weight.shape[1] % (16 * n_col * (tokens.shape[1] // CHUNK)) == 0
+            and gate_weight.shape[1] % (16 * CHUNKS * n_col) == 0
+            and 3 * gate_weight.size <= 24 * 1024 * 1024
         )
         if fits:
             return pairwise(n_row, n_col, *args)

time: 116 us -> 92.6 us (0.80); the launches traced: 114 us -> 92.4 us
  Pallas kernels: 83 us -> 56.2 us
  waiting for transfers between devices: 9.87 us -> 18.2 us
  starting transfers between devices: 19.2 us -> 17.2 us
  local copies, waits for them, and re-layouts: 1.51 us -> 0 us
    pallas_call x10, Pallas kernels: 81.7 us -> 54.2 us  [the longest x6 35.2 us: use(): pl.pallas_call(functools.partial(use_kernel, k, first, last, weights is n...]
    ppermute x17, waiting for transfers between devices: 9.87 us -> 18.2 us  [swap(): return lax.ppermute(x, axis, [(i, i ^ k) for i in range(size)])]
    ppermute x17, starting transfers between devices: 19.2 us -> 17.2 us  [swap(): return lax.ppermute(x, axis, [(i, i ^ k) for i in range(size)])]
    unnamed x4 -> x0, local copies, waits for them, and re-layouts: 1.51 us -> none
  transfers between devices with their start and end apart: 17 -> 17, of which waited for: 5 -> 7; matrix products, arithmetic and copies ran while one was open for 0% -> 0% of each run, Pallas kernels for 51% -> 47%
where the time goes in v3:
time: 92.6 us; the launch traced here: 92.4 us
  Pallas kernels  56.2 us (61%)
  waiting for transfers between devices  18.2 us (20%)
  starting transfers between devices  17.2 us (19%)
    pallas_call x6, Pallas kernels, use(): pl.pallas_call(functools.partial(use_kernel, k, first, last, weights is n...  35.2 us
    pallas_call x4, Pallas kernels, partial_sums(): pl.pallas_call(functools.partial(sums_kernel, k), in_specs=[WHOLE, WHOLE]...  19 us
    ppermute x17, waiting for transfers between devices, swap(): return lax.ppermute(x, axis, [(i, i ^ k) for i in range(size)])  18.2 us
    ppermute x17, starting transfers between devices, swap(): return lax.ppermute(x, axis, [(i, i ^ k) for i in range(size)])  17.2 us
  transfers between devices with their start and end apart: 17, of which 7 were waited for; matrix products, arithmetic and copies ran while one was open for 0% of the time, Pallas kernels for 47%

profile of v3, /device:TPU:0, one launch (start us, length us, event | category | flops | bytes accessed | tf_op | source)
XLA Modules:
  0.0 92.4 jit_solution(12085561739933878057)
XLA Ops:
  0.6 0.8 pack.1.refs_0_
  1.4 2.9 %collective-permute-start = (bf16[16,2048]{1,0:T(8,128)(2,1)S(1)}, bf16[16,2048]{1,0:T(8,128)(2,1)S(1)}, u32[]{:S(2)}, u32[]{:S(2)}) collective-permute-start(bf16[16,2048]{1,0:T(8,128)(2,1)S(1)} %pack.1.refs_0_), channel_id=1, source_target_pairs={{0,8},{4,12},{8,0},{12,4},{16,24},{20,28},{24,16},{28,20},{1,9},{5... | collective-permute-start | bytes 196616 | tf_op jit(solution)/shard_map/ppermute | solution.py:26
  4.4 1.5 %collective-permute-start.1 = (bf16[16,2048]{1,0:T(8,128)(2,1)S(1)}, bf16[16,2048]{1,0:T(8,128)(2,1)S(1)}, u32[]{:S(2)}, u32[]{:S(2)}) collective-permute-start(bf16[16,2048]{1,0:T(8,128)(2,1)S(1)} %pack.1.refs_0_), channel_id=1, source_target_pairs={{0,16},{4,20},{8,24},{12,28},{16,0},{20,4},{24,8},{28,12},{1,17},{... | collective-permute-start | bytes 196616 | tf_op jit(solution)/shard_map/ppermute | solution.py:26
  5.9 0.0 collective-permute-start.2
  5.9 0.0 collective-permute-start.3
  5.9 0.8 collective-permute-done.refs_1_
  6.7 0.0 collective-permute-start.4
  6.7 1.9 %collective-permute-done.1.refs_2_ = bf16[16,2048]{1,0:T(8,128)(2,1)S(1)} collective-permute-done((bf16[16,2048]{1,0:T(8,128)(2,1)S(1)}, bf16[16,2048]{1,0:T(8,128)(2,1)S(1)}, u32[]{:S(2)}, u32[]{:S(2)}) %collective-permute-start.1) | collective-permute-done | bytes 65568 | tf_op jit(solution)/shard_map/ppermute | solution.py:26
  8.6 0.0 collective-permute-start.5
  8.6 2.4 %collective-permute-done.2.refs_3_ = bf16[16,2048]{1,0:T(8,128)(2,1)S(1)} collective-permute-done((bf16[16,2048]{1,0:T(8,128)(2,1)S(1)}, bf16[16,2048]{1,0:T(8,128)(2,1)S(1)}, u32[]{:S(2)}, u32[]{:S(2)}) %collective-permute-start.2) | collective-permute-done | bytes 65568 | tf_op jit(solution)/shard_map/ppermute | solution.py:26
  11.0 0.0 collective-permute-start.6
  11.0 0.0 collective-permute-done.3.refs_4_
  11.0 0.0 collective-permute-done.4.refs_5_
  11.0 0.0 collective-permute-done.5.refs_6_
  11.1 1.2 %collective-permute-done.6.refs_7_ = bf16[16,2048]{1,0:T(8,128)(2,1)S(1)} collective-permute-done((bf16[16,2048]{1,0:T(8,128)(2,1)S(1)}, bf16[16,2048]{1,0:T(8,128)(2,1)S(1)}, u32[]{:S(2)}, u32[]{:S(2)}) %collective-permute-start.6) | collective-permute-done | bytes 65568 | tf_op jit(solution)/shard_map/ppermute | solution.py:26
  12.3 0.3 assemble.1
  12.6 4.7 %partial_sums.7 = bf16[3,64,768]{2,1,0:T(8,128)(2,1)S(1)} custom-call(bf16[64,2048]{1,0:T(8,128)(2,1)S(1)} %get-tuple-element.33.tok, bf16[2048,64]{1,0:T(8,128)(2,1)S(1)} %get-tuple-element.34.grad_t, bf16[2048,3072]{1,0:T(8,128)(2,1)} %refs_0_.7, bf16[2048,3072]{1,0:T(8,128)(2,1)} %refs_1_.7, bf16[3072,2048]{1,0:T(8,128)(2,1)} %refs_2_.7), custom_call_target="tpu_custom_call" | custom-call | flops 75497472 | bytes 1179648 | tf_op jit(solution)/shard_map/partial_sums/pallas_call | solution.py:144
  17.4 1.6 %collective-permute-start.8 = (bf16[3,64,768]{2,1,0:T(8,128)(2,1)S(1)}, bf16[3,64,768]{2,1,0:T(8,128)(2,1)S(1)}, u32[]{:S(2)}, u32[]{:S(2)}) collective-permute-start(bf16[3,64,768]{2,1,0:T(8,128)(2,1)S(1)} %partial_sums.7), channel_id=1, source_target_pairs={{0,1},{1,0},{2,3},{3,2},{4,5},{5,4},{6,7},{7,6},{8,9},{9,8},{10,11... | collective-permute-start | bytes 884744 | tf_op jit(solution)/shard_map/ppermute | solution.py:26
  19.0 4.7 %partial_sums.5 = bf16[3,64,768]{2,1,0:T(8,128)(2,1)S(1)} custom-call(bf16[64,2048]{1,0:T(8,128)(2,1)S(1)} %get-tuple-element.33.tok, bf16[2048,64]{1,0:T(8,128)(2,1)S(1)} %get-tuple-element.34.grad_t, bf16[2048,3072]{1,0:T(8,128)(2,1)} %refs_0_.7, bf16[2048,3072]{1,0:T(8,128)(2,1)} %refs_1_.7, bf16[3072,2048]{1,0:T(8,128)(2,1)} %refs_2_.7), custom_call_target="tpu_custom_call" | custom-call | flops 75497472 | bytes 1179648 | tf_op jit(solution)/shard_map/partial_sums/pallas_call | solution.py:144
  23.7 0.6 collective-permute-start.7
  24.3 4.8 %partial_sums.6.own = f32[3,64,768]{2,1,0:T(8,128)S(1)} custom-call(bf16[64,2048]{1,0:T(8,128)(2,1)S(1)} %get-tuple-element.33.tok, bf16[2048,64]{1,0:T(8,128)(2,1)S(1)} %get-tuple-element.34.grad_t, bf16[2048,3072]{1,0:T(8,128)(2,1)} %refs_0_.7, bf16[2048,3072]{1,0:T(8,128)(2,1)} %refs_1_.7, bf16[3072,2048]{1,0:T(8,128)(2,1)} %refs_2_.7), custom_call_target="tpu_custom_call" | custom-call | flops 75497472 | bytes 1179648 | tf_op jit(solution)/shard_map/partial_sums/pallas_call | solution.py:144
  29.1 0.0 collective-permute-done.8.other
  29.1 0.1 combine.1
  29.2 2.7 %collective-permute-start.9 = (bf16[3,64,768]{2,1,0:T(8,128)(2,1)S(1)}, bf16[3,64,768]{2,1,0:T(8,128)(2,1)S(1)}, u32[]{:S(2)}, u32[]{:S(2)}) collective-permute-start(bf16[3,64,768]{2,1,0:T(8,128)(2,1)S(1)} %combine.1), channel_id=1, source_target_pairs={{0,2},{1,3},{2,0},{3,1},{4,6},{5,7},{6,4},{7,5},{8,10},{9,11},{10,... | collective-permute-start | bytes 884744 | tf_op jit(solution)/shard_map/ppermute | solution.py:26
  31.8 4.8 %partial_sums.4.own = f32[3,64,768]{2,1,0:T(8,128)S(1)} custom-call(bf16[64,2048]{1,0:T(8,128)(2,1)S(1)} %get-tuple-element.33.tok, bf16[2048,64]{1,0:T(8,128)(2,1)S(1)} %get-tuple-element.34.grad_t, bf16[2048,3072]{1,0:T(8,128)(2,1)} %refs_0_.7, bf16[2048,3072]{1,0:T(8,128)(2,1)} %refs_1_.7, bf16[3072,2048]{1,0:T(8,128)(2,1)} %refs_2_.7), custom_call_target="tpu_custom_call" | custom-call | flops 75497472 | bytes 1179648 | tf_op jit(solution)/shard_map/partial_sums/pallas_call | solution.py:144
  36.7 0.0 collective-permute-done.7.refs_0_
  36.7 8.3 %collective-permute-done.9.refs_1_ = bf16[3,64,768]{2,1,0:T(8,128)(2,1)S(1)} collective-permute-done((bf16[3,64,768]{2,1,0:T(8,128)(2,1)S(1)}, bf16[3,64,768]{2,1,0:T(8,128)(2,1)S(1)}, u32[]{:S(2)}, u32[]{:S(2)}) %collective-permute-start.9) | collective-permute-done | bytes 294944 | tf_op jit(solution)/shard_map/ppermute | solution.py:26
  45.0 0.2 activate.1.act
  45.2 0.1 collective-permute-start.10
  45.3 4.1 %collective-permute-start.12 = (bf16[3,64,768]{2,1,0:T(8,128)(2,1)S(1)}, bf16[3,64,768]{2,1,0:T(8,128)(2,1)S(1)}, u32[]{:S(2)}, u32[]{:S(2)}) collective-permute-start(bf16[3,64,768]{2,1,0:T(8,128)(2,1)S(1)} %activate.1.act), channel_id=1, source_target_pairs={{0,1},{1,0},{2,3},{3,2},{4,5},{5,4},{6,7},{7,6},{8,9},{9,8},{10,11... | collective-permute-start | bytes 884744 | tf_op jit(solution)/shard_map/ppermute | solution.py:26
  49.4 7.5 %productsgrads.2 = (f32[2,64,2048]{2,1,0:T(8,128)S(1)}, bf16[2048,3072]{1,0:T(8,128)(2,1)}, bf16[2048,3072]{1,0:T(8,128)(2,1)}, bf16[3072,2048]{1,0:T(8,128)(2,1)}) custom-call(bf16[3,64,768]{2,1,0:T(8,128)(2,1)S(1)} %activate.1.act, bf16[2048,3072]{1,0:T(8,128)(2,1)} %refs_0_.7, bf16[2048,3072]{1,0:T(8,128)(2,1)} %refs_1_.7, bf16[3072,2048]{1,0:T(8,128)(2,1)} %refs_2_.7, ...), custom_call_target="tpu_custom_call" | custom-call | flops 150994944 | bytes 2359296 | tf_op jit(solution)/shard_map/productsgrads/pallas_call | solution.py:299
  56.9 3.4 %collective-permute-done.10.act = bf16[3,64,768]{2,1,0:T(8,128)(2,1)S(1)} collective-permute-done((bf16[3,64,768]{2,1,0:T(8,128)(2,1)S(1)}, bf16[3,64,768]{2,1,0:T(8,128)(2,1)S(1)}, u32[]{:S(2)}, u32[]{:S(2)}) %collective-permute-start.10) | collective-permute-done | bytes 294944 | tf_op jit(solution)/shard_map/ppermute | solution.py:26
  60.2 0.0 collective-permute-start.11
  60.2 0.1 collective-permute-done.12.act
  60.3 7.6 %productsgrads.3 = (f32[2,64,2048]{2,1,0:T(8,128)S(1)}, bf16[2048,3072]{1,0:T(8,128)(2,1)}, bf16[2048,3072]{1,0:T(8,128)(2,1)}, bf16[3072,2048]{1,0:T(8,128)(2,1)}) custom-call(bf16[3,64,768]{2,1,0:T(8,128)(2,1)S(1)} %collective-permute-done.12.act, bf16[2048,3072]{1,0:T(8,128)(2,1)} %refs_0_.7, ...), custom_call_target="tpu_custom_call", output_to_operand_aliasing={{1}: (7, {}), {2}: (8, {}), {3}: (9, {})} | custom-call | flops 150994944 | bytes 2359296 | tf_op jit(solution)/shard_map/productsgrads/pallas_call | solution.py:299
  67.9 5.8 %products.2.refs_3_ = f32[2,64,2048]{2,1,0:T(8,128)S(1)} custom-call(bf16[3,64,768]{2,1,0:T(8,128)(2,1)S(1)} %collective-permute-done.10.act, bf16[2048,3072]{1,0:T(8,128)(2,1)} %refs_0_.7, bf16[2048,3072]{1,0:T(8,128)(2,1)} %refs_1_.7, bf16[3072,2048]{1,0:T(8,128)(2,1)} %refs_2_.7, f32[2,64,2048]{2,1,0:T(8,128)S(1)} %get-tuple-element.42.refs_3_), custom_call_target="tpu_custom_call" | custom-call | flops 75497472 | bytes 1179648 | tf_op jit(solution)/shard_map/products/pallas_call | solution.py:299
  73.7 0.0 collective-permute-done.11.act
  73.7 6.0 %products.3 = (f32[2,32,2048]{2,1,0:T(8,128)S(1)}, f32[2,32,2048]{2,1,0:T(8,128)S(1)}) custom-call(bf16[3,64,768]{2,1,0:T(8,128)(2,1)S(1)} %collective-permute-done.11.act, bf16[2048,3072]{1,0:T(8,128)(2,1)} %refs_0_.7, bf16[2048,3072]{1,0:T(8,128)(2,1)} %refs_1_.7, bf16[3072,2048]{1,0:T(8,128)(2,1)} %refs_2_.7, f32[2,64,2048]{2,1,0:T(8,128)S(1)} %products.2.refs_3_), custom_call_target="tpu_custom_call" | custom-call | flops 75497472 | bytes 1179648 | tf_op jit(solution)/shard_map/products/pallas_call | solution.py:299
  79.8 0.1 collective-permute-start.13
  79.8 4.1 %grads.2 = (bf16[2048,3072]{1,0:T(8,128)(2,1)}, bf16[2048,3072]{1,0:T(8,128)(2,1)}, bf16[3072,2048]{1,0:T(8,128)(2,1)}) custom-call(bf16[3,64,768]{2,1,0:T(8,128)(2,1)S(1)} %collective-permute-done.10.act, bf16[2048,64]{1,0:T(8,128)(2,1)S(1)} %get-tuple-element.35.refs_3_.refs_4_.refs_0_, ...), custom_call_target="tpu_custom_call", output_to_operand_aliasing={{0}: (3, {}), {1}: (4, {}), {2}: (5, {})} | custom-call | flops 75497472 | bytes 1179648 | tf_op jit(solution)/shard_map/grads/pallas_call | solution.py:299
  84.0 0.0 collective-permute-done.13.other
  84.0 0.1 fold.1
  84.0 0.6 collective-permute-start.14
  84.7 0.9 collective-permute-start.15
  85.5 2.1 %collective-permute-start.16 = (bf16[2,8,2048]{2,1,0:T(8,128)(2,1)S(1)}, bf16[2,8,2048]{2,1,0:T(8,128)(2,1)S(1)}, u32[]{:S(2)}, u32[]{:S(2)}) collective-permute-start(bf16[2,8,2048]{2,1,0:T(8,128)(2,1)S(1)} %get-tuple-element.55), channel_id=1, source_target_pairs={{0,24},{4,28},{8,16},{12,20},{16,8},{20,12},{24,0},{28,4},{1,25},{... | collective-permute-start | bytes 196616 | tf_op jit(solution)/shard_map/ppermute | solution.py:26
  87.6 4.1 %grads.3 = (bf16[2048,3072]{1,0:T(8,128)(2,1)}, bf16[2048,3072]{1,0:T(8,128)(2,1)}, bf16[3072,2048]{1,0:T(8,128)(2,1)}) custom-call(bf16[3,64,768]{2,1,0:T(8,128)(2,1)S(1)} %collective-permute-done.11.act, bf16[2048,64]{1,0:T(8,128)(2,1)S(1)} %get-tuple-element.35.refs_3_.refs_4_.refs_0_, ...), custom_call_target="tpu_custom_call", output_to_operand_aliasing={{0}: (3, {}), {1}: (4, {}), {2}: (5, {})} | custom-call | flops 75497472 | bytes 1179648 | tf_op jit(solution)/shard_map/grads/pallas_call | solution.py:299
  91.7 0.0 collective-permute-done.15.refs_1_
  91.8 0.6 finish.1
  (2 shorter events, 0.0 us)
Async XLA Ops:
  1.4 5.3 %collective-permute-start = (bf16[16,2048]{1,0:T(8,128)(2,1)S(1)}, bf16[16,2048]{1,0:T(8,128)(2,1)S(1)}, u32[]{:S(2)}, u32[]{:S(2)}) collective-permute-start(bf16[16,2048]{1,0:T(8,128)(2,1)S(1)} %pack.1.refs_0_), channel_id=1, source_target_pairs={{0,8},{4,12},{8,0},{12,4},{16,24},{20,28},{24,16},{28,20},{1,9},{5... | collective-permute-start | bytes 196616 | tf_op jit(solution)/shard_map/ppermute | solution.py:26
  4.4 4.3 %collective-permute-start.1 = (bf16[16,2048]{1,0:T(8,128)(2,1)S(1)}, bf16[16,2048]{1,0:T(8,128)(2,1)S(1)}, u32[]{:S(2)}, u32[]{:S(2)}) collective-permute-start(bf16[16,2048]{1,0:T(8,128)(2,1)S(1)} %pack.1.refs_0_), channel_id=1, source_target_pairs={{0,16},{4,20},{8,24},{12,28},{16,0},{20,4},{24,8},{28,12},{1,17},{... | collective-permute-start | bytes 196616 | tf_op jit(solution)/shard_map/ppermute | solution.py:26
  5.9 5.2 %collective-permute-start.2 = (bf16[16,2048]{1,0:T(8,128)(2,1)S(1)}, bf16[16,2048]{1,0:T(8,128)(2,1)S(1)}, u32[]{:S(2)}, u32[]{:S(2)}) collective-permute-start(bf16[16,2048]{1,0:T(8,128)(2,1)S(1)} %pack.1.refs_0_), channel_id=1, source_target_pairs={{0,24},{4,28},{8,16},{12,20},{16,8},{20,12},{24,0},{28,4},{1,25},{... | collective-permute-start | bytes 196616 | tf_op jit(solution)/shard_map/ppermute | solution.py:26
  5.9 5.2 %collective-permute-start.3 = (bf16[16,2048]{1,0:T(8,128)(2,1)S(1)}, bf16[16,2048]{1,0:T(8,128)(2,1)S(1)}, u32[]{:S(2)}, u32[]{:S(2)}) collective-permute-start(bf16[16,2048]{1,0:T(8,128)(2,1)S(1)} %pack.1.refs_0_), channel_id=1, source_target_pairs={{0,4},{4,0},{8,12},{12,8},{16,20},{20,16},{24,28},{28,24},{1,5},{5... | collective-permute-start | bytes 196616 | tf_op jit(solution)/shard_map/ppermute | solution.py:26
  6.7 4.3 %collective-permute-start.4 = (bf16[16,2048]{1,0:T(8,128)(2,1)S(1)}, bf16[16,2048]{1,0:T(8,128)(2,1)S(1)}, u32[]{:S(2)}, u32[]{:S(2)}) collective-permute-start(bf16[16,2048]{1,0:T(8,128)(2,1)S(1)} %collective-permute-done.refs_1_), channel_id=1, source_target_pairs={{0,4},{4,0},{8,12},{12,8},{16,20},{20,16},{24,28},{28,24},{1,5},{5... | collective-permute-start | bytes 196616 | tf_op jit(solution)/shard_map/ppermute | solution.py:26
  8.6 2.4 %collective-permute-start.5 = (bf16[16,2048]{1,0:T(8,128)(2,1)S(1)}, bf16[16,2048]{1,0:T(8,128)(2,1)S(1)}, u32[]{:S(2)}, u32[]{:S(2)}) collective-permute-start(bf16[16,2048]{1,0:T(8,128)(2,1)S(1)} %collective-permute-done.1.refs_2_), channel_id=1, source_target_pairs={{0,4},{4,0},{8,12},{12,8},{16,20},{20,16},{24,28},{28,24},{1,5},{5... | collective-permute-start | bytes 196616 | tf_op jit(solution)/shard_map/ppermute | solution.py:26
  11.0 1.3 %collective-permute-start.6 = (bf16[16,2048]{1,0:T(8,128)(2,1)S(1)}, bf16[16,2048]{1,0:T(8,128)(2,1)S(1)}, u32[]{:S(2)}, u32[]{:S(2)}) collective-permute-start(bf16[16,2048]{1,0:T(8,128)(2,1)S(1)} %collective-permute-done.2.refs_3_), channel_id=1, source_target_pairs={{0,4},{4,0},{8,12},{12,8},{16,20},{20,16},{24,28},{28,24},{1,5},{5... | collective-permute-start | bytes 196616 | tf_op jit(solution)/shard_map/ppermute | solution.py:26
  17.4 11.7 %collective-permute-start.8 = (bf16[3,64,768]{2,1,0:T(8,128)(2,1)S(1)}, bf16[3,64,768]{2,1,0:T(8,128)(2,1)S(1)}, u32[]{:S(2)}, u32[]{:S(2)}) collective-permute-start(bf16[3,64,768]{2,1,0:T(8,128)(2,1)S(1)} %partial_sums.7), channel_id=1, source_target_pairs={{0,1},{1,0},{2,3},{3,2},{4,5},{5,4},{6,7},{7,6},{8,9},{9,8},{10,11... | collective-permute-start | bytes 884744 | tf_op jit(solution)/shard_map/ppermute | solution.py:26
  23.7 12.9 %collective-permute-start.7 = (bf16[3,64,768]{2,1,0:T(8,128)(2,1)S(1)}, bf16[3,64,768]{2,1,0:T(8,128)(2,1)S(1)}, u32[]{:S(2)}, u32[]{:S(2)}) collective-permute-start(bf16[3,64,768]{2,1,0:T(8,128)(2,1)S(1)} %partial_sums.5), channel_id=1, source_target_pairs={{0,1},{1,0},{2,3},{3,2},{4,5},{5,4},{6,7},{7,6},{8,9},{9,8},{10,11... | collective-permute-start | bytes 884744 | tf_op jit(solution)/shard_map/ppermute | solution.py:26
  29.2 15.8 %collective-permute-start.9 = (bf16[3,64,768]{2,1,0:T(8,128)(2,1)S(1)}, bf16[3,64,768]{2,1,0:T(8,128)(2,1)S(1)}, u32[]{:S(2)}, u32[]{:S(2)}) collective-permute-start(bf16[3,64,768]{2,1,0:T(8,128)(2,1)S(1)} %combine.1), channel_id=1, source_target_pairs={{0,2},{1,3},{2,0},{3,1},{4,6},{5,7},{6,4},{7,5},{8,10},{9,11},{10,... | collective-permute-start | bytes 884744 | tf_op jit(solution)/shard_map/ppermute | solution.py:26
  45.2 15.0 %collective-permute-start.10 = (bf16[3,64,768]{2,1,0:T(8,128)(2,1)S(1)}, bf16[3,64,768]{2,1,0:T(8,128)(2,1)S(1)}, u32[]{:S(2)}, u32[]{:S(2)}) collective-permute-start(bf16[3,64,768]{2,1,0:T(8,128)(2,1)S(1)} %activate.1.act), channel_id=1, source_target_pairs={{0,2},{1,3},{2,0},{3,1},{4,6},{5,7},{6,4},{7,5},{8,10},{9,11},{10,... | collective-permute-start | bytes 884744 | tf_op jit(solution)/shard_map/ppermute | solution.py:26
  45.3 15.0 %collective-permute-start.12 = (bf16[3,64,768]{2,1,0:T(8,128)(2,1)S(1)}, bf16[3,64,768]{2,1,0:T(8,128)(2,1)S(1)}, u32[]{:S(2)}, u32[]{:S(2)}) collective-permute-start(bf16[3,64,768]{2,1,0:T(8,128)(2,1)S(1)} %activate.1.act), channel_id=1, source_target_pairs={{0,1},{1,0},{2,3},{3,2},{4,5},{5,4},{6,7},{7,6},{8,9},{9,8},{10,11... | collective-permute-start | bytes 884744 | tf_op jit(solution)/shard_map/ppermute | solution.py:26
  60.2 13.5 %collective-permute-start.11 = (bf16[3,64,768]{2,1,0:T(8,128)(2,1)S(1)}, bf16[3,64,768]{2,1,0:T(8,128)(2,1)S(1)}, u32[]{:S(2)}, u32[]{:S(2)}) collective-permute-start(bf16[3,64,768]{2,1,0:T(8,128)(2,1)S(1)} %collective-permute-done.10.act), channel_id=1, source_target_pairs={{0,1},{1,0},{2,3},{3,2},{4,5},{5,4},{6,7},{7,6},{8,9},{9,8},{10,11... | collective-permute-start | bytes 884744 | tf_op jit(solution)/shard_map/ppermute | solution.py:26
  79.8 4.2 %collective-permute-start.13 = (f32[2,32,2048]{2,1,0:T(8,128)S(1)}, f32[2,32,2048]{2,1,0:T(8,128)S(1)}, u32[]{:S(2)}, u32[]{:S(2)}) collective-permute-start(f32[2,32,2048]{2,1,0:T(8,128)S(1)} %get-tuple-element.44.refs_5_), channel_id=1, source_target_pairs={{0,4},{4,0},{8,12},{12,8},{16,20},{20,16},{24,28},{28,24},{1,5},{5... | collective-permute-start | bytes 1572872 | tf_op jit(solution)/shard_map/ppermute | solution.py:26
  84.0 7.7 %collective-permute-start.14 = (bf16[2,8,2048]{2,1,0:T(8,128)(2,1)S(1)}, bf16[2,8,2048]{2,1,0:T(8,128)(2,1)S(1)}, u32[]{:S(2)}, u32[]{:S(2)}) collective-permute-start(bf16[2,8,2048]{2,1,0:T(8,128)(2,1)S(1)} %get-tuple-element.53), channel_id=1, source_target_pairs={{0,8},{4,12},{8,0},{12,4},{16,24},{20,28},{24,16},{28,20},{1,9},{5... | collective-permute-start | bytes 196616 | tf_op jit(solution)/shard_map/ppermute | solution.py:26
  84.7 7.1 %collective-permute-start.15 = (bf16[2,8,2048]{2,1,0:T(8,128)(2,1)S(1)}, bf16[2,8,2048]{2,1,0:T(8,128)(2,1)S(1)}, u32[]{:S(2)}, u32[]{:S(2)}) collective-permute-start(bf16[2,8,2048]{2,1,0:T(8,128)(2,1)S(1)} %get-tuple-element.54), channel_id=1, source_target_pairs={{0,16},{4,20},{8,24},{12,28},{16,0},{20,4},{24,8},{28,12},{1,17},{... | collective-permute-start | bytes 196616 | tf_op jit(solution)/shard_map/ppermute | solution.py:26
  85.5 6.2 %collective-permute-start.16 = (bf16[2,8,2048]{2,1,0:T(8,128)(2,1)S(1)}, bf16[2,8,2048]{2,1,0:T(8,128)(2,1)S(1)}, u32[]{:S(2)}, u32[]{:S(2)}) collective-permute-start(bf16[2,8,2048]{2,1,0:T(8,128)(2,1)S(1)} %get-tuple-element.55), channel_id=1, source_target_pairs={{0,24},{4,28},{8,16},{12,20},{16,8},{20,12},{24,0},{28,4},{1,25},{... | collective-permute-start | bytes 196616 | tf_op jit(solution)/shard_map/ppermute | solution.py:26

commit v4 on v3

--- a/solution.py
+++ b/solution.py
@@ -10,7 +10,7 @@
 BF16 = jnp.bfloat16
 F32 = jnp.float32
 VMEM_LIMIT = 48 * 1024 * 1024
-CHUNKS = 4
+CHUNKS = 8
 BACK = (((1,), (1,)), ((), ()))
 CONTRACT = (((0,), (0,)), ((), ()))
 PARAMS = pltpu.CompilerParams(vmem_limit_bytes=VMEM_LIMIT)
@@ -22,6 +22,10 @@
     return jnp.dot(a, b, preferred_element_type=F32)
 
 
+def back_dot(a, b):
+    return lax.dot_general(a, b, BACK, preferred_element_type=F32)
+
+
 def swap(x, axis, size, k):
     return lax.ppermute(x, axis, [(i, i ^ k) for i in range(size)])
 
@@ -55,22 +59,21 @@
 
 
 def assemble_kernel(rows, *refs):
-    pieces, (tok, grad, tok_t, grad_t) = refs[:-4], refs[-4:]
+    pieces, (tok, grad, tok_t) = refs[:-3], refs[-3:]
     both = [p[...].astype(F32) for p in pieces]
     all_tok = jnp.concatenate([b[:rows] for b in both], axis=0)
     all_grad = jnp.concatenate([b[rows:] for b in both], axis=0)
     tok[...] = all_tok.astype(BF16)
     grad[...] = all_grad.astype(BF16)
     tok_t[...] = all_tok.T.astype(BF16)
-    grad_t[...] = all_grad.T.astype(BF16)
 
 
 def assemble(pieces, rows):
     total, width = rows * len(pieces), pieces[0].shape[1]
-    flat, turned = (total, width), (width, total)
+    flat = (total, width)
     return pl.pallas_call(
         functools.partial(assemble_kernel, rows),
-        out_shape=[array(shape, BF16) for shape in (flat, flat, turned, turned)],
+        out_shape=[array(shape, BF16) for shape in (flat, flat, (width, total))],
         compiler_params=PARAMS,
         cost_estimate=estimate(0, 12 * total * width),
         name="assemble",
@@ -113,13 +116,13 @@
     ]
 
 
-def sums_kernel(k, tok, grad_t, gate_w, up_w, down_w, *refs):
+def sums_kernel(k, tok, grad, gate_w, up_w, down_w, *refs):
     out, gate_b, up_b, down_b, sems, gate, up, back = refs[-8:]
     copies = fetches(k, (gate_w, up_w, down_w), (gate_b, up_b, down_b), sems)
     for chunk in copies:
         for copy in chunk:
             copy.start()
-    part = grad_t.shape[0] // CHUNKS
+    part = grad.shape[1] // CHUNKS
     for i, chunk in enumerate(copies):
         here = span(i, part)
         for copy in chunk:
@@ -127,7 +130,7 @@
         terms = (
             (gate, dot(tok[:, here], gate_b[here])),
             (up, dot(tok[:, here], up_b[here])),
-            (back, dot(down_b[:, here], grad_t[here])),
+            (back, back_dot(grad[:, here], down_b[:, here])),
         )
         for acc, term in terms:
             if i == 0:
@@ -136,26 +139,22 @@
                 acc[...] += term
     out[0] = gate[...].astype(out.dtype)
     out[1] = up[...].astype(out.dtype)
-    out[2] = back[...].T.astype(out.dtype)
-
-
-def partial_sums(k, tok, grad_t, weights, units, dtype, after=()):
+    out[2] = back[...].astype(out.dtype)
+
+
+def partial_sums(k, tok, grad, weights, units, dtype, after=()):
     total, width = tok.shape
     return pl.pallas_call(
         functools.partial(sums_kernel, k),
         in_specs=[WHOLE, WHOLE] + [HOLD] * (3 + len(after)),
         out_specs=WHOLE,
         scratch_shapes=weight_scratch(units, width)
-        + [
-            pltpu.VMEM((total, units), F32),
-            pltpu.VMEM((total, units), F32),
-            pltpu.VMEM((units, total), F32),
-        ],
+        + [pltpu.VMEM((total, units), F32)] * 3,
         out_shape=array((3, total, units), dtype),
         compiler_params=PARAMS,
         cost_estimate=estimate(6 * total * width * units, 6 * width * units),
         name="partial_sums",
-    )(tok, grad_t, *in_hbm(weights), *after)
+    )(tok, grad, *in_hbm(weights), *after)
 
 
 def combine_kernel(own, other, out):
@@ -194,11 +193,7 @@
     )(own, *others)
 
 
-def turned(x):
-    return x.astype(F32).T.astype(BF16)
-
-
-def use_kernel(k, first, last, with_products, with_grads, act, *refs):
+def use_kernel(k, chunks, first, last, with_products, with_grads, act, *refs):
     refs = list(refs)
     width = 0
     if with_products:
@@ -224,12 +219,11 @@
         for chunk in arriving:
             for copy in chunk:
                 copy.start()
-        gate_t, up_t = turned(act[1]), turned(act[2])
     if with_grads:
-        hidden_t = turned(act[0])
+        hidden_t = act[0].astype(F32).T.astype(BF16)
         mine = unit_block(k, units)
         start = jnp.bitwise_xor(lax.axis_index("col"), k) * units
-    for i in range(CHUNKS):
+    for i in chunks:
         here = span(i, part)
         if with_grads:
             gate_g, up_g, down_g = outs[-3:]
@@ -251,8 +245,8 @@
         if with_products:
             for copy in arriving[i]:
                 copy.wait()
-            back = dot(gate_b[here], gate_t) + dot(up_b[here], up_t)
-            for j, term in enumerate((dot(act[0], down_b[:, here]), back.T)):
+            back = back_dot(act[1], gate_b[here]) + back_dot(act[2], up_b[here])
+            for j, term in enumerate((dot(act[0], down_b[:, here]), back)):
                 term = term if first else before[j, :, here] + term
                 if last:
                     half = term.shape[0] // 2
@@ -264,7 +258,17 @@
         copy.wait()
 
 
-def use(k, act, weights=None, terms=None, last=False, sides=None, grads=(), after=()):
+def use(
+    k,
+    act,
+    weights=None,
+    terms=None,
+    last=False,
+    sides=None,
+    grads=(),
+    after=(),
+    chunks=range(CHUNKS),
+):
     _, total, units = act.shape
     first = terms is None
     specs, args = [WHOLE], [act]
@@ -297,7 +301,9 @@
         scratch += weight_scratch(units, width)
         moved += 6 * width * units
     return pl.pallas_call(
-        functools.partial(use_kernel, k, first, last, weights is not None, sides is not None),
+        functools.partial(
+            use_kernel, k, chunks, first, last, weights is not None, sides is not None
+        ),
         in_specs=specs + [HOLD] * len(after),
         out_specs=out_specs,
         scratch_shapes=scratch,
@@ -356,31 +362,32 @@
     mine = pack(tokens, out_grad)
     even = [mine] + [along_row(mine, k=k) for k in range(2, n_row, 2)]
     odd = [along_row(piece, k=1) for piece in even]
-    tok, grad, tok_t, grad_t = assemble(even + odd, rows)
+    tok, grad, tok_t = assemble(even + odd, rows)
     sides = (tok_t, grad, all_units)
 
-    sums = functools.partial(partial_sums, tok=tok, grad_t=grad_t, weights=weights, units=units)
+    sums = functools.partial(partial_sums, tok=tok, grad=grad, weights=weights, units=units)
     near = along_col(sums(3, dtype=BF16), k=1)
     pair = combine(sums(2, dtype=F32), near)
     from_far = along_col(pair, k=2)
     from_near = along_col(sums(1, dtype=BF16), k=1)
     own = activate(sums(0, dtype=F32), [from_near, from_far])
 
+    near_act = along_col(own, k=1)
     far_act = along_col(own, k=2)
-    near_act = along_col(own, k=1)
     terms, *grads = use(0, own, weights, sides=sides)
+    terms, *grads = use(1, near_act, weights, terms, sides=sides, grads=grads)
     held, _ = lax.optimization_barrier((far_act, (terms, grads)))
     last_act = along_col(held, k=1)
-    terms, *grads = use(1, near_act, weights, terms, sides=sides, grads=grads)
-    (terms,) = use(2, far_act, weights, terms)
+    terms, *grads = use(2, far_act, weights, terms, sides=sides, grads=grads)
     kept, given = use(3, last_act, weights, terms, last=True)
 
     other = along_row(given, k=1)
-    grads = use(2, far_act, sides=sides, grads=grads, after=(given,))
+    halves = range(CHUNKS // 2), range(CHUNKS // 2, CHUNKS)
+    grads = use(3, last_act, sides=sides, grads=grads, after=(given,), chunks=halves[0])
     other, _ = lax.optimization_barrier((other, grads))
     mine, *sent = fold(kept, other, rows)
     parts = [along_row(piece, k=2 * i) for i, piece in enumerate(sent, 1)]
-    grads = use(3, last_act, sides=sides, grads=grads, after=(mine,))
+    grads = use(3, last_act, sides=sides, grads=grads, after=(mine,), chunks=halves[1])
     mixed, input_grad = finish(mine, parts)
     return (mixed, input_grad, *grads)
 
@@ -391,9 +398,6 @@
 
     def total(x):
         return lax.psum_scatter(x, "col", scatter_dimension=0, tiled=True)
-
-    def back_dot(a, b):
-        return lax.dot_general(a, b, BACK, preferred_element_type=F32)
 
     def outer(a, b):
         return lax.dot_general(a, b, CONTRACT, preferred_element_type=F32).astype(BF16)

time: 92.6 us -> 89.2 us (0.963)
  Pallas kernels: 56.2 us -> 54 us
  waiting for transfers between devices: 18.2 us -> 16.9 us
    pallas_call x4, Pallas kernels: 19 us -> 17.4 us  [partial_sums(): pl.pallas_call(functools.partial(sums_kernel, k), in_specs=[WHOLE, WHOLE]...]
    ppermute x17, waiting for transfers between devices: 18.2 us -> 16.9 us  [swap(): return lax.ppermute(x, axis, [(i, i ^ k) for i in range(size)])]
  transfers between devices with their start and end apart: 17 -> 17, of which waited for: 7 -> 9; matrix products, arithmetic and copies ran while one was open for 0% -> 0% of each run, Pallas kernels for 47% -> 47%
where the time goes in v4:
time: 89.2 us; the launch traced here: 89 us
  Pallas kernels  54 us (61%)
  starting transfers between devices  17.3 us (19%)
  waiting for transfers between devices  16.9 us (19%)
    pallas_call x6, Pallas kernels, use(): pl.pallas_call(functools.partial(use_kernel, k, chunks, first, last, weig...  34.7 us
    pallas_call x4, Pallas kernels, partial_sums(): pl.pallas_call(functools.partial(sums_kernel, k), in_specs=[WHOLE, WHOLE]...  17.4 us
    ppermute x17, starting transfers between devices, swap(): return lax.ppermute(x, axis, [(i, i ^ k) for i in range(size)])  17.3 us
    ppermute x17, waiting for transfers between devices, swap(): return lax.ppermute(x, axis, [(i, i ^ k) for i in range(size)])  16.9 us
  transfers between devices with their start and end apart: 17, of which 9 were waited for; matrix products, arithmetic and copies ran while one was open for 0% of the time, Pallas kernels for 47%

profile of v4, /device:TPU:0, one launch (start us, length us, event | category | flops | bytes accessed | tf_op | source)
XLA Modules:
  0.0 89.0 jit_solution(16225680958132320213)
XLA Ops:
  0.6 0.8 pack.1.refs_0_
  1.4 3.9 %collective-permute-start.2 = (bf16[16,2048]{1,0:T(8,128)(2,1)S(1)}, bf16[16,2048]{1,0:T(8,128)(2,1)S(1)}, u32[]{:S(2)}, u32[]{:S(2)}) collective-permute-start(bf16[16,2048]{1,0:T(8,128)(2,1)S(1)} %pack.1.refs_0_), channel_id=1, source_target_pairs={{0,24},{4,28},{8,16},{12,20},{16,8},{20,12},{24,0},{28,4},{1,25},{... | collective-permute-start | bytes 196616 | tf_op jit(solution)/shard_map/ppermute | solution.py:30
  5.3 0.5 collective-permute-start.1
  5.8 0.1 collective-permute-start
  5.9 0.0 collective-permute-start.3
  5.9 1.6 %collective-permute-done.2.refs_3_ = bf16[16,2048]{1,0:T(8,128)(2,1)S(1)} collective-permute-done((bf16[16,2048]{1,0:T(8,128)(2,1)S(1)}, bf16[16,2048]{1,0:T(8,128)(2,1)S(1)}, u32[]{:S(2)}, u32[]{:S(2)}) %collective-permute-start.2) | collective-permute-done | bytes 65568 | tf_op jit(solution)/shard_map/ppermute | solution.py:30
  7.6 0.0 collective-permute-start.6
  7.6 2.0 %collective-permute-done.1.refs_2_ = bf16[16,2048]{1,0:T(8,128)(2,1)S(1)} collective-permute-done((bf16[16,2048]{1,0:T(8,128)(2,1)S(1)}, bf16[16,2048]{1,0:T(8,128)(2,1)S(1)}, u32[]{:S(2)}, u32[]{:S(2)}) %collective-permute-start.1) | collective-permute-done | bytes 65568 | tf_op jit(solution)/shard_map/ppermute | solution.py:30
  9.6 0.0 collective-permute-start.5
  9.6 0.5 collective-permute-done.refs_1_
  10.1 0.0 collective-permute-start.4
  10.1 0.0 collective-permute-done.3.refs_4_
  10.1 0.0 collective-permute-done.6.refs_7_
  10.1 0.7 collective-permute-done.5.refs_6_
  10.8 0.5 collective-permute-done.4.refs_5_
  11.3 0.2 assemble.1
  11.6 4.3 %partial_sums.7 = bf16[3,64,768]{2,1,0:T(8,128)(2,1)S(1)} custom-call(bf16[64,2048]{1,0:T(8,128)(2,1)S(1)} %get-tuple-element.36.tok, bf16[64,2048]{1,0:T(8,128)(2,1)S(1)} %get-tuple-element.37.grad.refs_4_.refs_5_.refs_1_, bf16[2048,3072]{1,0:T(8,128)(2,1)} %refs_0_.7, bf16[2048,3072]{1,0:T(8,128)(2,1)} %refs_1_.7, bf16[3072,2048]{1,0:T(8,128)(2,1)} %refs_2_.7), custom_call_target="tpu_custom_call" | custom-call | flops 75497472 | bytes 1179648 | tf_op jit(solution)/shard_map/partial_sums/pallas_call | solution.py:147
  15.9 1.6 %collective-permute-start.8 = (bf16[3,64,768]{2,1,0:T(8,128)(2,1)S(1)}, bf16[3,64,768]{2,1,0:T(8,128)(2,1)S(1)}, u32[]{:S(2)}, u32[]{:S(2)}) collective-permute-start(bf16[3,64,768]{2,1,0:T(8,128)(2,1)S(1)} %partial_sums.7), channel_id=1, source_target_pairs={{0,1},{1,0},{2,3},{3,2},{4,5},{5,4},{6,7},{7,6},{8,9},{9,8},{10,11... | collective-permute-start | bytes 884744 | tf_op jit(solution)/shard_map/ppermute | solution.py:30
  17.5 4.4 %partial_sums.5 = bf16[3,64,768]{2,1,0:T(8,128)(2,1)S(1)} custom-call(bf16[64,2048]{1,0:T(8,128)(2,1)S(1)} %get-tuple-element.36.tok, bf16[64,2048]{1,0:T(8,128)(2,1)S(1)} %get-tuple-element.37.grad.refs_4_.refs_5_.refs_1_, bf16[2048,3072]{1,0:T(8,128)(2,1)} %refs_0_.7, bf16[2048,3072]{1,0:T(8,128)(2,1)} %refs_1_.7, bf16[3072,2048]{1,0:T(8,128)(2,1)} %refs_2_.7), custom_call_target="tpu_custom_call" | custom-call | flops 75497472 | bytes 1179648 | tf_op jit(solution)/shard_map/partial_sums/pallas_call | solution.py:147
  22.0 0.4 collective-permute-start.7
  22.4 4.3 %partial_sums.6.own = f32[3,64,768]{2,1,0:T(8,128)S(1)} custom-call(bf16[64,2048]{1,0:T(8,128)(2,1)S(1)} %get-tuple-element.36.tok, bf16[64,2048]{1,0:T(8,128)(2,1)S(1)} %get-tuple-element.37.grad.refs_4_.refs_5_.refs_1_, bf16[2048,3072]{1,0:T(8,128)(2,1)} %refs_0_.7, bf16[2048,3072]{1,0:T(8,128)(2,1)} %refs_1_.7, bf16[3072,2048]{1,0:T(8,128)(2,1)} %refs_2_.7), custom_call_target="tpu_custom_call" | custom-call | flops 75497472 | bytes 1179648 | tf_op jit(solution)/shard_map/partial_sums/pallas_call | solution.py:147
  26.7 0.0 collective-permute-done.8.other
  26.7 0.1 combine.1
  26.8 2.7 %collective-permute-start.9 = (bf16[3,64,768]{2,1,0:T(8,128)(2,1)S(1)}, bf16[3,64,768]{2,1,0:T(8,128)(2,1)S(1)}, u32[]{:S(2)}, u32[]{:S(2)}) collective-permute-start(bf16[3,64,768]{2,1,0:T(8,128)(2,1)S(1)} %combine.1), channel_id=1, source_target_pairs={{0,2},{1,3},{2,0},{3,1},{4,6},{5,7},{6,4},{7,5},{8,10},{9,11},{10,... | collective-permute-start | bytes 884744 | tf_op jit(solution)/shard_map/ppermute | solution.py:30
  29.5 4.3 %partial_sums.4.own = f32[3,64,768]{2,1,0:T(8,128)S(1)} custom-call(bf16[64,2048]{1,0:T(8,128)(2,1)S(1)} %get-tuple-element.36.tok, bf16[64,2048]{1,0:T(8,128)(2,1)S(1)} %get-tuple-element.37.grad.refs_4_.refs_5_.refs_1_, bf16[2048,3072]{1,0:T(8,128)(2,1)} %refs_0_.7, bf16[2048,3072]{1,0:T(8,128)(2,1)} %refs_1_.7, bf16[3072,2048]{1,0:T(8,128)(2,1)} %refs_2_.7), custom_call_target="tpu_custom_call" | custom-call | flops 75497472 | bytes 1179648 | tf_op jit(solution)/shard_map/partial_sums/pallas_call | solution.py:147
  33.9 1.0 %collective-permute-done.7.refs_0_ = bf16[3,64,768]{2,1,0:T(8,128)(2,1)S(1)} collective-permute-done((bf16[3,64,768]{2,1,0:T(8,128)(2,1)S(1)}, bf16[3,64,768]{2,1,0:T(8,128)(2,1)S(1)}, u32[]{:S(2)}, u32[]{:S(2)}) %collective-permute-start.7) | collective-permute-done | bytes 294944 | tf_op jit(solution)/shard_map/ppermute | solution.py:30
  34.9 7.8 %collective-permute-done.9.refs_1_ = bf16[3,64,768]{2,1,0:T(8,128)(2,1)S(1)} collective-permute-done((bf16[3,64,768]{2,1,0:T(8,128)(2,1)S(1)}, bf16[3,64,768]{2,1,0:T(8,128)(2,1)S(1)}, u32[]{:S(2)}, u32[]{:S(2)}) %collective-permute-start.9) | collective-permute-done | bytes 294944 | tf_op jit(solution)/shard_map/ppermute | solution.py:30
  42.7 0.2 activate.1.act
  42.8 0.9 collective-permute-start.11
  43.7 3.4 %collective-permute-start.10 = (bf16[3,64,768]{2,1,0:T(8,128)(2,1)S(1)}, bf16[3,64,768]{2,1,0:T(8,128)(2,1)S(1)}, u32[]{:S(2)}, u32[]{:S(2)}) collective-permute-start(bf16[3,64,768]{2,1,0:T(8,128)(2,1)S(1)} %activate.1.act), channel_id=1, source_target_pairs={{0,2},{1,3},{2,0},{3,1},{4,6},{5,7},{6,4},{7,5},{8,10},{9,11},{10,... | collective-permute-start | bytes 884744 | tf_op jit(solution)/shard_map/ppermute | solution.py:30
  47.1 8.0 %productsgrads.3 = (f32[2,64,2048]{2,1,0:T(8,128)S(1)}, bf16[2048,3072]{1,0:T(8,128)(2,1)}, bf16[2048,3072]{1,0:T(8,128)(2,1)}, bf16[3072,2048]{1,0:T(8,128)(2,1)}) custom-call(bf16[3,64,768]{2,1,0:T(8,128)(2,1)S(1)} %activate.1.act, bf16[2048,3072]{1,0:T(8,128)(2,1)} %refs_0_.7, bf16[2048,3072]{1,0:T(8,128)(2,1)} %refs_1_.7, bf16[3072,2048]{1,0:T(8,128)(2,1)} %refs_2_.7, ...), custom_call_target="tpu_custom_call" | custom-call | flops 150994944 | bytes 2359296 | tf_op jit(solution)/shard_map/productsgrads/pallas_call | solution.py:303
  55.0 1.6 %collective-permute-done.11.act = bf16[3,64,768]{2,1,0:T(8,128)(2,1)S(1)} collective-permute-done((bf16[3,64,768]{2,1,0:T(8,128)(2,1)S(1)}, bf16[3,64,768]{2,1,0:T(8,128)(2,1)S(1)}, u32[]{:S(2)}, u32[]{:S(2)}) %collective-permute-start.11) | collective-permute-done | bytes 294944 | tf_op jit(solution)/shard_map/ppermute | solution.py:30
  56.7 7.8 %productsgrads.4 = (f32[2,64,2048]{2,1,0:T(8,128)S(1)}, bf16[2048,3072]{1,0:T(8,128)(2,1)}, bf16[2048,3072]{1,0:T(8,128)(2,1)}, bf16[3072,2048]{1,0:T(8,128)(2,1)}) custom-call(bf16[3,64,768]{2,1,0:T(8,128)(2,1)S(1)} %collective-permute-done.11.act, bf16[2048,3072]{1,0:T(8,128)(2,1)} %refs_0_.7, ...), custom_call_target="tpu_custom_call", output_to_operand_aliasing={{1}: (7, {}), {2}: (8, {}), {3}: (9, {})} | custom-call | flops 150994944 | bytes 2359296 | tf_op jit(solution)/shard_map/productsgrads/pallas_call | solution.py:303
  64.5 0.1 collective-permute-start.12
  64.5 7.8 %productsgrads.5 = (f32[2,64,2048]{2,1,0:T(8,128)S(1)}, bf16[2048,3072]{1,0:T(8,128)(2,1)}, bf16[2048,3072]{1,0:T(8,128)(2,1)}, bf16[3072,2048]{1,0:T(8,128)(2,1)}) custom-call(bf16[3,64,768]{2,1,0:T(8,128)(2,1)S(1)} %collective-permute-done.10.act, bf16[2048,3072]{1,0:T(8,128)(2,1)} %refs_0_.7, ...), custom_call_target="tpu_custom_call", output_to_operand_aliasing={{1}: (7, {}), {2}: (8, {}), {3}: (9, {})} | custom-call | flops 150994944 | bytes 2359296 | tf_op jit(solution)/shard_map/productsgrads/pallas_call | solution.py:303
  72.3 0.0 collective-permute-done.12.act
  72.3 5.9 %products.1 = (f32[2,32,2048]{2,1,0:T(8,128)S(1)}, f32[2,32,2048]{2,1,0:T(8,128)S(1)}) custom-call(bf16[3,64,768]{2,1,0:T(8,128)(2,1)S(1)} %collective-permute-done.12.act, bf16[2048,3072]{1,0:T(8,128)(2,1)} %refs_0_.7, bf16[2048,3072]{1,0:T(8,128)(2,1)} %refs_1_.7, bf16[3072,2048]{1,0:T(8,128)(2,1)} %refs_2_.7, f32[2,64,2048]{2,1,0:T(8,128)S(1)} %get-tuple-element.48.refs_3_), custom_call_target="tpu_custom_call" | custom-call | flops 75497472 | bytes 1179648 | tf_op jit(solution)/shard_map/products/pallas_call | solution.py:303
  78.2 0.1 collective-permute-start.13
  78.3 2.7 %grads.2 = (bf16[2048,3072]{1,0:T(8,128)(2,1)}, bf16[2048,3072]{1,0:T(8,128)(2,1)}, bf16[3072,2048]{1,0:T(8,128)(2,1)}) custom-call(bf16[3,64,768]{2,1,0:T(8,128)(2,1)S(1)} %collective-permute-done.12.act, bf16[2048,64]{1,0:T(8,128)(2,1)S(1)} %get-tuple-element.38.refs_3_.refs_4_.refs_0_, ...), custom_call_target="tpu_custom_call", output_to_operand_aliasing={{0}: (3, {}), {1}: (4, {}), {2}: (5, {})} | custom-call | flops 75497472 | bytes 1179648 | tf_op jit(solution)/shard_map/grads/pallas_call | solution.py:303
  81.0 0.0 collective-permute-done.13.other
  81.0 0.1 fold.1
  81.1 1.1 %collective-permute-start.14 = (bf16[2,8,2048]{2,1,0:T(8,128)(2,1)S(1)}, bf16[2,8,2048]{2,1,0:T(8,128)(2,1)S(1)}, u32[]{:S(2)}, u32[]{:S(2)}) collective-permute-start(bf16[2,8,2048]{2,1,0:T(8,128)(2,1)S(1)} %get-tuple-element.59), channel_id=1, source_target_pairs={{0,8},{4,12},{8,0},{12,4},{16,24},{20,28},{24,16},{28,20},{1,9},{5... | collective-permute-start | bytes 196616 | tf_op jit(solution)/shard_map/ppermute | solution.py:30
  82.1 1.1 %collective-permute-start.15 = (bf16[2,8,2048]{2,1,0:T(8,128)(2,1)S(1)}, bf16[2,8,2048]{2,1,0:T(8,128)(2,1)S(1)}, u32[]{:S(2)}, u32[]{:S(2)}) collective-permute-start(bf16[2,8,2048]{2,1,0:T(8,128)(2,1)S(1)} %get-tuple-element.60), channel_id=1, source_target_pairs={{0,16},{4,20},{8,24},{12,28},{16,0},{20,4},{24,8},{28,12},{1,17},{... | collective-permute-start | bytes 196616 | tf_op jit(solution)/shard_map/ppermute | solution.py:30
  83.2 1.4 %collective-permute-start.16 = (bf16[2,8,2048]{2,1,0:T(8,128)(2,1)S(1)}, bf16[2,8,2048]{2,1,0:T(8,128)(2,1)S(1)}, u32[]{:S(2)}, u32[]{:S(2)}) collective-permute-start(bf16[2,8,2048]{2,1,0:T(8,128)(2,1)S(1)} %get-tuple-element.61), channel_id=1, source_target_pairs={{0,24},{4,28},{8,16},{12,20},{16,8},{20,12},{24,0},{28,4},{1,25},{... | collective-permute-start | bytes 196616 | tf_op jit(solution)/shard_map/ppermute | solution.py:30
  84.6 2.7 %grads.3 = (bf16[2048,3072]{1,0:T(8,128)(2,1)}, bf16[2048,3072]{1,0:T(8,128)(2,1)}, bf16[3072,2048]{1,0:T(8,128)(2,1)}) custom-call(bf16[3,64,768]{2,1,0:T(8,128)(2,1)S(1)} %collective-permute-done.12.act, bf16[2048,64]{1,0:T(8,128)(2,1)S(1)} %get-tuple-element.38.refs_3_.refs_4_.refs_0_, ...), custom_call_target="tpu_custom_call", output_to_operand_aliasing={{0}: (3, {}), {1}: (4, {}), {2}: (5, {})} | custom-call | flops 75497472 | bytes 1179648 | tf_op jit(solution)/shard_map/grads/pallas_call | solution.py:303
  87.3 0.0 collective-permute-done.15.refs_1_
  87.3 1.1 %collective-permute-done.16.refs_2_ = bf16[2,8,2048]{2,1,0:T(8,128)(2,1)S(1)} collective-permute-done((bf16[2,8,2048]{2,1,0:T(8,128)(2,1)S(1)}, bf16[2,8,2048]{2,1,0:T(8,128)(2,1)S(1)}, u32[]{:S(2)}, u32[]{:S(2)}) %collective-permute-start.16) | collective-permute-done | bytes 65568 | tf_op jit(solution)/shard_map/ppermute | solution.py:30
  88.3 0.6 finish.1
  (2 shorter events, 0.0 us)
Async XLA Ops:
  1.4 6.1 %collective-permute-start.2 = (bf16[16,2048]{1,0:T(8,128)(2,1)S(1)}, bf16[16,2048]{1,0:T(8,128)(2,1)S(1)}, u32[]{:S(2)}, u32[]{:S(2)}) collective-permute-start(bf16[16,2048]{1,0:T(8,128)(2,1)S(1)} %pack.1.refs_0_), channel_id=1, source_target_pairs={{0,24},{4,28},{8,16},{12,20},{16,8},{20,12},{24,0},{28,4},{1,25},{... | collective-permute-start | bytes 196616 | tf_op jit(solution)/shard_map/ppermute | solution.py:30
  5.3 4.3 %collective-permute-start.1 = (bf16[16,2048]{1,0:T(8,128)(2,1)S(1)}, bf16[16,2048]{1,0:T(8,128)(2,1)S(1)}, u32[]{:S(2)}, u32[]{:S(2)}) collective-permute-start(bf16[16,2048]{1,0:T(8,128)(2,1)S(1)} %pack.1.refs_0_), channel_id=1, source_target_pairs={{0,16},{4,20},{8,24},{12,28},{16,0},{20,4},{24,8},{28,12},{1,17},{... | collective-permute-start | bytes 196616 | tf_op jit(solution)/shard_map/ppermute | solution.py:30
  5.8 4.3 %collective-permute-start = (bf16[16,2048]{1,0:T(8,128)(2,1)S(1)}, bf16[16,2048]{1,0:T(8,128)(2,1)S(1)}, u32[]{:S(2)}, u32[]{:S(2)}) collective-permute-start(bf16[16,2048]{1,0:T(8,128)(2,1)S(1)} %pack.1.refs_0_), channel_id=1, source_target_pairs={{0,8},{4,12},{8,0},{12,4},{16,24},{20,28},{24,16},{28,20},{1,9},{5... | collective-permute-start | bytes 196616 | tf_op jit(solution)/shard_map/ppermute | solution.py:30
  5.9 4.2 %collective-permute-start.3 = (bf16[16,2048]{1,0:T(8,128)(2,1)S(1)}, bf16[16,2048]{1,0:T(8,128)(2,1)S(1)}, u32[]{:S(2)}, u32[]{:S(2)}) collective-permute-start(bf16[16,2048]{1,0:T(8,128)(2,1)S(1)} %pack.1.refs_0_), channel_id=1, source_target_pairs={{0,4},{4,0},{8,12},{12,8},{16,20},{20,16},{24,28},{28,24},{1,5},{5... | collective-permute-start | bytes 196616 | tf_op jit(solution)/shard_map/ppermute | solution.py:30
  7.6 2.5 %collective-permute-start.6 = (bf16[16,2048]{1,0:T(8,128)(2,1)S(1)}, bf16[16,2048]{1,0:T(8,128)(2,1)S(1)}, u32[]{:S(2)}, u32[]{:S(2)}) collective-permute-start(bf16[16,2048]{1,0:T(8,128)(2,1)S(1)} %collective-permute-done.2.refs_3_), channel_id=1, source_target_pairs={{0,4},{4,0},{8,12},{12,8},{16,20},{20,16},{24,28},{28,24},{1,5},{5... | collective-permute-start | bytes 196616 | tf_op jit(solution)/shard_map/ppermute | solution.py:30
  9.6 1.3 %collective-permute-start.5 = (bf16[16,2048]{1,0:T(8,128)(2,1)S(1)}, bf16[16,2048]{1,0:T(8,128)(2,1)S(1)}, u32[]{:S(2)}, u32[]{:S(2)}) collective-permute-start(bf16[16,2048]{1,0:T(8,128)(2,1)S(1)} %collective-permute-done.1.refs_2_), channel_id=1, source_target_pairs={{0,4},{4,0},{8,12},{12,8},{16,20},{20,16},{24,28},{28,24},{1,5},{5... | collective-permute-start | bytes 196616 | tf_op jit(solution)/shard_map/ppermute | solution.py:30
  10.1 1.3 %collective-permute-start.4 = (bf16[16,2048]{1,0:T(8,128)(2,1)S(1)}, bf16[16,2048]{1,0:T(8,128)(2,1)S(1)}, u32[]{:S(2)}, u32[]{:S(2)}) collective-permute-start(bf16[16,2048]{1,0:T(8,128)(2,1)S(1)} %collective-permute-done.refs_1_), channel_id=1, source_target_pairs={{0,4},{4,0},{8,12},{12,8},{16,20},{20,16},{24,28},{28,24},{1,5},{5... | collective-permute-start | bytes 196616 | tf_op jit(solution)/shard_map/ppermute | solution.py:30
  15.9 10.8 %collective-permute-start.8 = (bf16[3,64,768]{2,1,0:T(8,128)(2,1)S(1)}, bf16[3,64,768]{2,1,0:T(8,128)(2,1)S(1)}, u32[]{:S(2)}, u32[]{:S(2)}) collective-permute-start(bf16[3,64,768]{2,1,0:T(8,128)(2,1)S(1)} %partial_sums.7), channel_id=1, source_target_pairs={{0,1},{1,0},{2,3},{3,2},{4,5},{5,4},{6,7},{7,6},{8,9},{9,8},{10,11... | collective-permute-start | bytes 884744 | tf_op jit(solution)/shard_map/ppermute | solution.py:30
  22.0 12.9 %collective-permute-start.7 = (bf16[3,64,768]{2,1,0:T(8,128)(2,1)S(1)}, bf16[3,64,768]{2,1,0:T(8,128)(2,1)S(1)}, u32[]{:S(2)}, u32[]{:S(2)}) collective-permute-start(bf16[3,64,768]{2,1,0:T(8,128)(2,1)S(1)} %partial_sums.5), channel_id=1, source_target_pairs={{0,1},{1,0},{2,3},{3,2},{4,5},{5,4},{6,7},{7,6},{8,9},{9,8},{10,11... | collective-permute-start | bytes 884744 | tf_op jit(solution)/shard_map/ppermute | solution.py:30
  26.8 15.9 %collective-permute-start.9 = (bf16[3,64,768]{2,1,0:T(8,128)(2,1)S(1)}, bf16[3,64,768]{2,1,0:T(8,128)(2,1)S(1)}, u32[]{:S(2)}, u32[]{:S(2)}) collective-permute-start(bf16[3,64,768]{2,1,0:T(8,128)(2,1)S(1)} %combine.1), channel_id=1, source_target_pairs={{0,2},{1,3},{2,0},{3,1},{4,6},{5,7},{6,4},{7,5},{8,10},{9,11},{10,... | collective-permute-start | bytes 884744 | tf_op jit(solution)/shard_map/ppermute | solution.py:30
  42.8 13.8 %collective-permute-start.11 = (bf16[3,64,768]{2,1,0:T(8,128)(2,1)S(1)}, bf16[3,64,768]{2,1,0:T(8,128)(2,1)S(1)}, u32[]{:S(2)}, u32[]{:S(2)}) collective-permute-start(bf16[3,64,768]{2,1,0:T(8,128)(2,1)S(1)} %activate.1.act), channel_id=1, source_target_pairs={{0,1},{1,0},{2,3},{3,2},{4,5},{5,4},{6,7},{7,6},{8,9},{9,8},{10,11... | collective-permute-start | bytes 884744 | tf_op jit(solution)/shard_map/ppermute | solution.py:30
  43.7 20.8 %collective-permute-start.10 = (bf16[3,64,768]{2,1,0:T(8,128)(2,1)S(1)}, bf16[3,64,768]{2,1,0:T(8,128)(2,1)S(1)}, u32[]{:S(2)}, u32[]{:S(2)}) collective-permute-start(bf16[3,64,768]{2,1,0:T(8,128)(2,1)S(1)} %activate.1.act), channel_id=1, source_target_pairs={{0,2},{1,3},{2,0},{3,1},{4,6},{5,7},{6,4},{7,5},{8,10},{9,11},{10,... | collective-permute-start | bytes 884744 | tf_op jit(solution)/shard_map/ppermute | solution.py:30
  64.5 7.9 %collective-permute-start.12 = (bf16[3,64,768]{2,1,0:T(8,128)(2,1)S(1)}, bf16[3,64,768]{2,1,0:T(8,128)(2,1)S(1)}, u32[]{:S(2)}, u32[]{:S(2)}) collective-permute-start(bf16[3,64,768]{2,1,0:T(8,128)(2,1)S(1)} %collective-permute-done.10.act), channel_id=1, source_target_pairs={{0,1},{1,0},{2,3},{3,2},{4,5},{5,4},{6,7},{7,6},{8,9},{9,8},{10,11... | collective-permute-start | bytes 884744 | tf_op jit(solution)/shard_map/ppermute | solution.py:30
  78.2 2.7 %collective-permute-start.13 = (f32[2,32,2048]{2,1,0:T(8,128)S(1)}, f32[2,32,2048]{2,1,0:T(8,128)S(1)}, u32[]{:S(2)}, u32[]{:S(2)}) collective-permute-start(f32[2,32,2048]{2,1,0:T(8,128)S(1)} %get-tuple-element.50.refs_5_), channel_id=1, source_target_pairs={{0,4},{4,0},{8,12},{12,8},{16,20},{20,16},{24,28},{28,24},{1,5},{5... | collective-permute-start | bytes 1572872 | tf_op jit(solution)/shard_map/ppermute | solution.py:30
  81.1 6.2 %collective-permute-start.14 = (bf16[2,8,2048]{2,1,0:T(8,128)(2,1)S(1)}, bf16[2,8,2048]{2,1,0:T(8,128)(2,1)S(1)}, u32[]{:S(2)}, u32[]{:S(2)}) collective-permute-start(bf16[2,8,2048]{2,1,0:T(8,128)(2,1)S(1)} %get-tuple-element.59), channel_id=1, source_target_pairs={{0,8},{4,12},{8,0},{12,4},{16,24},{20,28},{24,16},{28,20},{1,9},{5... | collective-permute-start | bytes 196616 | tf_op jit(solution)/shard_map/ppermute | solution.py:30
  82.1 5.2 %collective-permute-start.15 = (bf16[2,8,2048]{2,1,0:T(8,128)(2,1)S(1)}, bf16[2,8,2048]{2,1,0:T(8,128)(2,1)S(1)}, u32[]{:S(2)}, u32[]{:S(2)}) collective-permute-start(bf16[2,8,2048]{2,1,0:T(8,128)(2,1)S(1)} %get-tuple-element.60), channel_id=1, source_target_pairs={{0,16},{4,20},{8,24},{12,28},{16,0},{20,4},{24,8},{28,12},{1,17},{... | collective-permute-start | bytes 196616 | tf_op jit(solution)/shard_map/ppermute | solution.py:30
  83.2 5.2 %collective-permute-start.16 = (bf16[2,8,2048]{2,1,0:T(8,128)(2,1)S(1)}, bf16[2,8,2048]{2,1,0:T(8,128)(2,1)S(1)}, u32[]{:S(2)}, u32[]{:S(2)}) collective-permute-start(bf16[2,8,2048]{2,1,0:T(8,128)(2,1)S(1)} %get-tuple-element.61), channel_id=1, source_target_pairs={{0,24},{4,28},{8,16},{12,20},{16,8},{20,12},{24,0},{28,4},{1,25},{... | collective-permute-start | bytes 196616 | tf_op jit(solution)/shard_map/ppermute | solution.py:30

commit v5 on v4

--- a/solution.py
+++ b/solution.py
@@ -9,12 +9,13 @@
 
 BF16 = jnp.bfloat16
 F32 = jnp.float32
-VMEM_LIMIT = 48 * 1024 * 1024
+VMEM_LIMIT = 14 * 1024 * 1024
 CHUNKS = 8
 BACK = (((1,), (1,)), ((), ()))
 CONTRACT = (((0,), (0,)), ((), ()))
 PARAMS = pltpu.CompilerParams(vmem_limit_bytes=VMEM_LIMIT)
 HOLD = pl.BlockSpec(memory_space=pl.ANY)
+PIECE = 512
 WHOLE = pl.BlockSpec(memory_space=pltpu.VMEM)
 
 
@@ -32,6 +33,14 @@
 
 def estimate(flops, num_bytes):
     return pl.CostEstimate(flops=flops // 8, bytes_accessed=num_bytes // 8, transcendentals=0)
+
+
+def vmem_array(shape):
+    return pltpu.VMEM(shape, BF16)
+
+
+def in_vmem(arrays):
+    return [pltpu.with_memory_space_constraint(x, pltpu.VMEM) for x in arrays]
 
 
 def in_hbm(arrays):
@@ -107,17 +116,13 @@
     return copies
 
 
-def weight_scratch(units, width):
-    return [
-        pltpu.VMEM((width, units), BF16),
-        pltpu.VMEM((width, units), BF16),
-        pltpu.VMEM((units, width), BF16),
-        pltpu.SemaphoreType.DMA((CHUNKS, 3)),
-    ]
-
-
 def sums_kernel(k, tok, grad, gate_w, up_w, down_w, *refs):
     out, gate_b, up_b, down_b, sems, gate, up, back = refs[-8:]
+    moves = (
+        (gate, lambda here: dot(tok[:, here], gate_b[here])),
+        (up, lambda here: dot(tok[:, here], up_b[here])),
+        (back, lambda here: back_dot(grad[:, here], down_b[:, here])),
+    )
     copies = fetches(k, (gate_w, up_w, down_w), (gate_b, up_b, down_b), sems)
     for chunk in copies:
         for copy in chunk:
@@ -125,36 +130,31 @@
     part = grad.shape[1] // CHUNKS
     for i, chunk in enumerate(copies):
         here = span(i, part)
-        for copy in chunk:
+        for copy, (acc, term) in zip(chunk, moves):
             copy.wait()
-        terms = (
-            (gate, dot(tok[:, here], gate_b[here])),
-            (up, dot(tok[:, here], up_b[here])),
-            (back, back_dot(grad[:, here], down_b[:, here])),
-        )
-        for acc, term in terms:
             if i == 0:
-                acc[...] = term
+                acc[...] = term(here)
             else:
-                acc[...] += term
+                acc[...] += term(here)
     out[0] = gate[...].astype(out.dtype)
     out[1] = up[...].astype(out.dtype)
     out[2] = back[...].astype(out.dtype)
 
 
-def partial_sums(k, tok, grad, weights, units, dtype, after=()):
+def partial_sums(k, tok, grad, weights, units, dtype):
     total, width = tok.shape
+    shapes = [(width, units), (width, units), (units, width)]
     return pl.pallas_call(
         functools.partial(sums_kernel, k),
-        in_specs=[WHOLE, WHOLE] + [HOLD] * (3 + len(after)),
-        out_specs=WHOLE,
-        scratch_shapes=weight_scratch(units, width)
+        in_specs=[WHOLE, WHOLE] + [HOLD] * 3,
+        out_specs=[WHOLE] * 4,
+        scratch_shapes=[pltpu.SemaphoreType.DMA((CHUNKS, 3))]
         + [pltpu.VMEM((total, units), F32)] * 3,
-        out_shape=array((3, total, units), dtype),
+        out_shape=[array((3, total, units), dtype)] + [vmem_array(x) for x in shapes],
         compiler_params=PARAMS,
         cost_estimate=estimate(6 * total * width * units, 6 * width * units),
         name="partial_sums",
-    )(tok, grad, *in_hbm(weights), *after)
+    )(tok, grad, *in_hbm(weights))
 
 
 def combine_kernel(own, other, out):
@@ -193,43 +193,27 @@
     )(own, *others)
 
 
-def use_kernel(k, chunks, first, last, with_products, with_grads, act, *refs):
+def use_kernel(k, first, last, with_products, with_grads, act, *refs):
     refs = list(refs)
-    width = 0
+    leaving = []
     if with_products:
-        weights = [refs.pop(0) for _ in range(3)]
+        gate_w, up_w, down_w = (refs.pop(0) for _ in range(3))
         before = None if first else refs.pop(0)
-        width = weights[2].shape[1]
     if with_grads:
         tok_t, grad = refs.pop(0), refs.pop(0)
-        width = grad.shape[1]
-    units = act.shape[2]
-    if with_grads:
-        gate_s, up_s, down_s, out_sems = refs[-4:]
+        gate_s, up_s, down_s, sems = refs[-4:]
         refs = refs[:-4]
-    if with_products:
-        gate_b, up_b, down_b, sems = refs[-4:]
-        refs = refs[:-4]
-    outs = refs[-(1 + last) * with_products - 3 * with_grads :]
-    part, rows = width // CHUNKS, units // CHUNKS
-
-    arriving, leaving = [], []
-    if with_products:
-        arriving = fetches(k, weights, (gate_b, up_b, down_b), sems)
-        for chunk in arriving:
-            for copy in chunk:
-                copy.start()
-    if with_grads:
+        gate_g, up_g, down_g = refs[-3:]
+        refs = refs[:-3]
+        units, width = down_s.shape
+        part, rows = width // CHUNKS, units // CHUNKS
         hidden_t = act[0].astype(F32).T.astype(BF16)
         mine = unit_block(k, units)
         start = jnp.bitwise_xor(lax.axis_index("col"), k) * units
-    for i in chunks:
-        here = span(i, part)
-        if with_grads:
-            gate_g, up_g, down_g = outs[-3:]
+        for i in range(CHUNKS):
+            here, some = span(i, part), span(i, rows)
             gate_s[here] = dot(tok_t[here], act[1]).astype(BF16)
             up_s[here] = dot(tok_t[here], act[2]).astype(BF16)
-            some = span(i, rows)
             down_s[some] = dot(hidden_t[some], grad[...]).astype(BF16)
             there = pl.ds(i * part, part)
             below = pl.ds(pl.multiple_of(start + i * rows, rows), rows)
@@ -239,14 +223,15 @@
                 (down_s.at[pl.ds(i * rows, rows)], down_g.at[below]),
             )
             for j, (source, target) in enumerate(ends):
-                copy = pltpu.make_async_copy(source, target, out_sems.at[i, j])
+                copy = pltpu.make_async_copy(source, target, sems.at[i, j])
                 copy.start()
                 leaving.append(copy)
-        if with_products:
-            for copy in arriving[i]:
-                copy.wait()
-            back = back_dot(act[1], gate_b[here]) + back_dot(act[2], up_b[here])
-            for j, term in enumerate((dot(act[0], down_b[:, here]), back)):
+    if with_products:
+        outs = refs[-1 - last :]
+        for i in range(down_w.shape[1] // PIECE):
+            here = span(i, PIECE)
+            back = back_dot(act[1], gate_w[here]) + back_dot(act[2], up_w[here])
+            for j, term in enumerate((dot(act[0], down_w[:, here]), back)):
                 term = term if first else before[j, :, here] + term
                 if last:
                     half = term.shape[0] // 2
@@ -258,17 +243,7 @@
         copy.wait()
 
 
-def use(
-    k,
-    act,
-    weights=None,
-    terms=None,
-    last=False,
-    sides=None,
-    grads=(),
-    after=(),
-    chunks=range(CHUNKS),
-):
+def use(k, act, weights=None, terms=None, last=False, sides=None, grads=(), after=()):
     _, total, units = act.shape
     first = terms is None
     specs, args = [WHOLE], [act]
@@ -276,15 +251,14 @@
     moved = 0
     if weights is not None:
         width = weights[2].shape[1]
-        specs += [HOLD] * 3
-        args += in_hbm(weights)
+        specs += [WHOLE] * 3
+        args += in_vmem(weights)
         if not first:
             specs.append(WHOLE)
             args.append(terms)
         held = total // 2 if last else total
         out_specs += [WHOLE] * (1 + last)
         out_shape += [array((2, held, width), F32)] * (1 + last)
-        scratch += weight_scratch(units, width)
         moved += 6 * width * units
     if sides is not None:
         tok_t, grad, all_units = sides
@@ -298,12 +272,11 @@
         out_specs += [HOLD] * 3
         out_shape += [pltpu.HBM((width, all_units), BF16)] * 2
         out_shape.append(pltpu.HBM((all_units, width), BF16))
-        scratch += weight_scratch(units, width)
+        scratch += [pltpu.VMEM((width, units), BF16)] * 2
+        scratch += [pltpu.VMEM((units, width), BF16), pltpu.SemaphoreType.DMA((CHUNKS, 3))]
         moved += 6 * width * units
     return pl.pallas_call(
-        functools.partial(
-            use_kernel, k, chunks, first, last, weights is not None, sides is not None
-        ),
+        functools.partial(use_kernel, k, first, last, weights is not None, sides is not None),
         in_specs=specs + [HOLD] * len(after),
         out_specs=out_specs,
         scratch_shapes=scratch,
@@ -366,28 +339,28 @@
     sides = (tok_t, grad, all_units)
 
     sums = functools.partial(partial_sums, tok=tok, grad=grad, weights=weights, units=units)
-    near = along_col(sums(3, dtype=BF16), k=1)
-    pair = combine(sums(2, dtype=F32), near)
-    from_far = along_col(pair, k=2)
-    from_near = along_col(sums(1, dtype=BF16), k=1)
-    own = activate(sums(0, dtype=F32), [from_near, from_far])
+    there, *last_weights = sums(3, dtype=BF16)
+    near = along_col(there, k=1)
+    here, *far_weights = sums(2, dtype=F32)
+    from_far = along_col(combine(here, near), k=2)
+    there, *near_weights = sums(1, dtype=BF16)
+    from_near = along_col(there, k=1)
+    here, *own_weights = sums(0, dtype=F32)
+    own = activate(here, [from_near, from_far])
 
     near_act = along_col(own, k=1)
     far_act = along_col(own, k=2)
-    terms, *grads = use(0, own, weights, sides=sides)
-    terms, *grads = use(1, near_act, weights, terms, sides=sides, grads=grads)
+    terms, *grads = use(0, own, own_weights, sides=sides)
+    terms, *grads = use(1, near_act, near_weights, terms, sides=sides, grads=grads)
     held, _ = lax.optimization_barrier((far_act, (terms, grads)))
     last_act = along_col(held, k=1)
-    terms, *grads = use(2, far_act, weights, terms, sides=sides, grads=grads)
-    kept, given = use(3, last_act, weights, terms, last=True)
+    terms, *grads = use(2, far_act, far_weights, terms, sides=sides, grads=grads)
+    kept, given = use(3, last_act, last_weights, terms, last=True)
 
     other = along_row(given, k=1)
-    halves = range(CHUNKS // 2), range(CHUNKS // 2, CHUNKS)
-    grads = use(3, last_act, sides=sides, grads=grads, after=(given,), chunks=halves[0])
-    other, _ = lax.optimization_barrier((other, grads))
     mine, *sent = fold(kept, other, rows)
     parts = [along_row(piece, k=2 * i) for i, piece in enumerate(sent, 1)]
-    grads = use(3, last_act, sides=sides, grads=grads, after=(mine,), chunks=halves[1])
+    grads = use(3, last_act, sides=sides, grads=grads, after=(mine,))
     mixed, input_grad = finish(mine, parts)
     return (mixed, input_grad, *grads)
 
@@ -440,7 +413,8 @@
             and tokens.shape[1] % (128 * CHUNKS) == 0
             and gate_weight.shape[1] % (128 * n_col) == 0
             and gate_weight.shape[1] % (16 * CHUNKS * n_col) == 0
-            and 3 * gate_weight.size <= 24 * 1024 * 1024
+            and tokens.shape[1] % PIECE == 0
+            and 6 * gate_weight.size <= 36 * 1024 * 1024
         )
         if fits:
             return pairwise(n_row, n_col, *args)

time: 89.2 us -> 82.8 us (0.928)
  Pallas kernels: 54 us -> 43.1 us
  waiting for transfers between devices: 16.9 us -> 21.4 us
    pallas_call x6 -> x5, Pallas kernels: 34.7 us -> 22.6 us  [use(): pl.pallas_call(functools.partial(use_kernel, k, first, last, weights is n...]
    ppermute x17, waiting for transfers between devices: 16.9 us -> 21.4 us  [swap(): return lax.ppermute(x, axis, [(i, i ^ k) for i in range(size)])]
    pallas_call x4, Pallas kernels: 17.4 us -> 18.6 us  [partial_sums(): pl.pallas_call(functools.partial(sums_kernel, k), in_specs=[WHOLE, WHOLE]...]
  transfers between devices with their start and end apart: 17 -> 17, of which waited for: 9 -> 9; matrix products, arithmetic and copies ran while one was open for 0% -> 0% of each run, Pallas kernels for 47% -> 41%
where the time goes in v5:
time: 82.8 us; the launch traced here: 82.6 us
  Pallas kernels  43.1 us (52%)
  waiting for transfers between devices  21.4 us (26%)
  starting transfers between devices  17.3 us (21%)
    pallas_call x5, Pallas kernels, use(): pl.pallas_call(functools.partial(use_kernel, k, first, last, weights is n...  22.6 us
    ppermute x17, waiting for transfers between devices, swap(): return lax.ppermute(x, axis, [(i, i ^ k) for i in range(size)])  21.4 us
    pallas_call x4, Pallas kernels, partial_sums(): pl.pallas_call(functools.partial(sums_kernel, k), in_specs=[WHOLE, WHOLE]...  18.6 us
    ppermute x17, starting transfers between devices, swap(): return lax.ppermute(x, axis, [(i, i ^ k) for i in range(size)])  17.3 us
  transfers between devices with their start and end apart: 17, of which 9 were waited for; matrix products, arithmetic and copies ran while one was open for 0% of the time, Pallas kernels for 41%

profile of v5, /device:TPU:0, one launch (start us, length us, event | category | flops | bytes accessed | tf_op | source)
XLA Modules:
  0.0 82.6 jit_solution(10658141652186178472)
XLA Ops:
  0.6 0.8 pack.1.refs_0_
  1.4 3.9 %collective-permute-start.2 = (bf16[16,2048]{1,0:T(8,128)(2,1)S(1)}, bf16[16,2048]{1,0:T(8,128)(2,1)S(1)}, u32[]{:S(2)}, u32[]{:S(2)}) collective-permute-start(bf16[16,2048]{1,0:T(8,128)(2,1)S(1)} %pack.1.refs_0_), channel_id=1, source_target_pairs={{0,24},{4,28},{8,16},{12,20},{16,8},{20,12},{24,0},{28,4},{1,25},{... | collective-permute-start | bytes 196616 | tf_op jit(solution)/shard_map/ppermute | solution.py:31
  5.3 0.5 collective-permute-start.1
  5.8 0.1 collective-permute-start
  5.9 0.0 collective-permute-start.3
  5.9 1.6 %collective-permute-done.2.refs_3_ = bf16[16,2048]{1,0:T(8,128)(2,1)S(1)} collective-permute-done((bf16[16,2048]{1,0:T(8,128)(2,1)S(1)}, bf16[16,2048]{1,0:T(8,128)(2,1)S(1)}, u32[]{:S(2)}, u32[]{:S(2)}) %collective-permute-start.2) | collective-permute-done | bytes 65568 | tf_op jit(solution)/shard_map/ppermute | solution.py:31
  7.6 0.0 collective-permute-start.6
  7.6 2.0 %collective-permute-done.1.refs_2_ = bf16[16,2048]{1,0:T(8,128)(2,1)S(1)} collective-permute-done((bf16[16,2048]{1,0:T(8,128)(2,1)S(1)}, bf16[16,2048]{1,0:T(8,128)(2,1)S(1)}, u32[]{:S(2)}, u32[]{:S(2)}) %collective-permute-start.1) | collective-permute-done | bytes 65568 | tf_op jit(solution)/shard_map/ppermute | solution.py:31
  9.6 0.0 collective-permute-start.5
  9.6 0.5 collective-permute-done.refs_1_
  10.1 0.0 collective-permute-start.4
  10.1 0.0 collective-permute-done.3.refs_4_
  10.1 0.0 collective-permute-done.6.refs_7_
  10.1 0.7 collective-permute-done.5.refs_6_
  10.8 0.5 collective-permute-done.4.refs_5_
  11.3 0.2 assemble.1
  11.6 4.6 %partial_sums.7 = (bf16[3,64,768]{2,1,0:T(8,128)(2,1)S(1)}, bf16[2048,768]{1,0:T(8,128)(2,1)S(1)}, bf16[2048,768]{1,0:T(8,128)(2,1)S(1)}, bf16[768,2048]{1,0:T(8,128)(2,1)S(1)}) custom-call(bf16[64,2048]{1,0:T(8,128)(2,1)S(1)} %get-tuple-element.48.tok, bf16[64,2048]{1,0:T(8,128)(2,1)S(1)} %get-tuple-element.49.grad.refs_4_.refs_5_.refs_1_, ...), custom_call_target="tpu_custom_call" | custom-call | flops 75497472 | bytes 1179648 | tf_op jit(solution)/shard_map/partial_sums/pallas_call | solution.py:147
  16.2 1.6 %collective-permute-start.8 = (bf16[3,64,768]{2,1,0:T(8,128)(2,1)S(1)}, bf16[3,64,768]{2,1,0:T(8,128)(2,1)S(1)}, u32[]{:S(2)}, u32[]{:S(2)}) collective-permute-start(bf16[3,64,768]{2,1,0:T(8,128)(2,1)S(1)} %get-tuple-element.53), channel_id=1, source_target_pairs={{0,1},{1,0},{2,3},{3,2},{4,5},{5,4},{6,7},{7,6},{8,9},{9,8},{10,11... | collective-permute-start | bytes 884744 | tf_op jit(solution)/shard_map/ppermute | solution.py:31
  17.8 4.6 %partial_sums.5 = (bf16[3,64,768]{2,1,0:T(8,128)(2,1)S(1)}, bf16[2048,768]{1,0:T(8,128)(2,1)S(1)}, bf16[2048,768]{1,0:T(8,128)(2,1)S(1)}, bf16[768,2048]{1,0:T(8,128)(2,1)S(1)}) custom-call(bf16[64,2048]{1,0:T(8,128)(2,1)S(1)} %get-tuple-element.48.tok, bf16[64,2048]{1,0:T(8,128)(2,1)S(1)} %get-tuple-element.49.grad.refs_4_.refs_5_.refs_1_, ...), custom_call_target="tpu_custom_call" | custom-call | flops 75497472 | bytes 1179648 | tf_op jit(solution)/shard_map/partial_sums/pallas_call | solution.py:147
  22.5 0.6 collective-permute-start.7
  23.1 4.6 %partial_sums.6 = (f32[3,64,768]{2,1,0:T(8,128)S(1)}, bf16[2048,768]{1,0:T(8,128)(2,1)S(1)}, bf16[2048,768]{1,0:T(8,128)(2,1)S(1)}, bf16[768,2048]{1,0:T(8,128)(2,1)S(1)}) custom-call(bf16[64,2048]{1,0:T(8,128)(2,1)S(1)} %get-tuple-element.48.tok, bf16[64,2048]{1,0:T(8,128)(2,1)S(1)} %get-tuple-element.49.grad.refs_4_.refs_5_.refs_1_, ...), custom_call_target="tpu_custom_call" | custom-call | flops 75497472 | bytes 1179648 | tf_op jit(solution)/shard_map/partial_sums/pallas_call | solution.py:147
  27.7 0.0 collective-permute-done.8.other
  27.7 0.1 combine.1
  27.8 2.7 %collective-permute-start.9 = (bf16[3,64,768]{2,1,0:T(8,128)(2,1)S(1)}, bf16[3,64,768]{2,1,0:T(8,128)(2,1)S(1)}, u32[]{:S(2)}, u32[]{:S(2)}) collective-permute-start(bf16[3,64,768]{2,1,0:T(8,128)(2,1)S(1)} %combine.1), channel_id=1, source_target_pairs={{0,2},{1,3},{2,0},{3,1},{4,6},{5,7},{6,4},{7,5},{8,10},{9,11},{10,... | collective-permute-start | bytes 884744 | tf_op jit(solution)/shard_map/ppermute | solution.py:31
  30.4 4.7 %partial_sums.4 = (f32[3,64,768]{2,1,0:T(8,128)S(1)}, bf16[2048,768]{1,0:T(8,128)(2,1)S(1)}, bf16[2048,768]{1,0:T(8,128)(2,1)S(1)}, bf16[768,2048]{1,0:T(8,128)(2,1)S(1)}) custom-call(bf16[64,2048]{1,0:T(8,128)(2,1)S(1)} %get-tuple-element.48.tok, bf16[64,2048]{1,0:T(8,128)(2,1)S(1)} %get-tuple-element.49.grad.refs_4_.refs_5_.refs_1_, ...), custom_call_target="tpu_custom_call" | custom-call | flops 75497472 | bytes 1179648 | tf_op jit(solution)/shard_map/partial_sums/pallas_call | solution.py:147
  35.1 0.0 collective-permute-done.7.refs_0_
  35.1 8.5 %collective-permute-done.9.refs_1_ = bf16[3,64,768]{2,1,0:T(8,128)(2,1)S(1)} collective-permute-done((bf16[3,64,768]{2,1,0:T(8,128)(2,1)S(1)}, bf16[3,64,768]{2,1,0:T(8,128)(2,1)S(1)}, u32[]{:S(2)}, u32[]{:S(2)}) %collective-permute-start.9) | collective-permute-done | bytes 294944 | tf_op jit(solution)/shard_map/ppermute | solution.py:31
  43.6 0.2 activate.1.act
  43.8 0.8 collective-permute-start.11
  44.6 3.4 %collective-permute-start.10 = (bf16[3,64,768]{2,1,0:T(8,128)(2,1)S(1)}, bf16[3,64,768]{2,1,0:T(8,128)(2,1)S(1)}, u32[]{:S(2)}, u32[]{:S(2)}) collective-permute-start(bf16[3,64,768]{2,1,0:T(8,128)(2,1)S(1)} %activate.1.act), channel_id=1, source_target_pairs={{0,2},{1,3},{2,0},{3,1},{4,6},{5,7},{6,4},{7,5},{8,10},{9,11},{10,... | collective-permute-start | bytes 884744 | tf_op jit(solution)/shard_map/ppermute | solution.py:31
  48.0 5.4 %productsgrads.3 = (f32[2,64,2048]{2,1,0:T(8,128)S(1)}, bf16[2048,3072]{1,0:T(8,128)(2,1)}, bf16[2048,3072]{1,0:T(8,128)(2,1)}, bf16[3072,2048]{1,0:T(8,128)(2,1)}) custom-call(bf16[3,64,768]{2,1,0:T(8,128)(2,1)S(1)} %activate.1.act, bf16[2048,768]{1,0:T(8,128)(2,1)S(1)} %get-tuple-element.57.refs_0_, bf16[2048,768]{1,0:T(8,128)(2,1)S(1)} %get-tuple-element.58.refs_1_, ...), custom_call_target="tpu_custom_call" | custom-call | flops 150994944 | bytes 2359296 | tf_op jit(solution)/shard_map/productsgrads/pallas_call | solution.py:278
  53.4 4.2 %collective-permute-done.11.act = bf16[3,64,768]{2,1,0:T(8,128)(2,1)S(1)} collective-permute-done((bf16[3,64,768]{2,1,0:T(8,128)(2,1)S(1)}, bf16[3,64,768]{2,1,0:T(8,128)(2,1)S(1)}, u32[]{:S(2)}, u32[]{:S(2)}) %collective-permute-start.11) | collective-permute-done | bytes 294944 | tf_op jit(solution)/shard_map/ppermute | solution.py:31
  57.6 5.3 %productsgrads.4 = (f32[2,64,2048]{2,1,0:T(8,128)S(1)}, bf16[2048,3072]{1,0:T(8,128)(2,1)}, bf16[2048,3072]{1,0:T(8,128)(2,1)}, bf16[3072,2048]{1,0:T(8,128)(2,1)}) custom-call(bf16[3,64,768]{2,1,0:T(8,128)(2,1)S(1)} %collective-permute-done.11.act, ...), custom_call_target="tpu_custom_call", output_to_operand_aliasing={{1}: (7, {}), {2}: (8, {}), {3}: (9, {})} | custom-call | flops 150994944 | bytes 2359296 | tf_op jit(solution)/shard_map/productsgrads/pallas_call | solution.py:278
  62.9 0.0 collective-permute-done.10.act
  62.9 0.1 collective-permute-start.12
  63.0 5.3 %productsgrads.5 = (f32[2,64,2048]{2,1,0:T(8,128)S(1)}, bf16[2048,3072]{1,0:T(8,128)(2,1)}, bf16[2048,3072]{1,0:T(8,128)(2,1)}, bf16[3072,2048]{1,0:T(8,128)(2,1)}) custom-call(bf16[3,64,768]{2,1,0:T(8,128)(2,1)S(1)} %collective-permute-done.10.act, ...), custom_call_target="tpu_custom_call", output_to_operand_aliasing={{1}: (7, {}), {2}: (8, {}), {3}: (9, {})} | custom-call | flops 150994944 | bytes 2359296 | tf_op jit(solution)/shard_map/productsgrads/pallas_call | solution.py:278
  68.3 1.4 %collective-permute-done.12.act = bf16[3,64,768]{2,1,0:T(8,128)(2,1)S(1)} collective-permute-done((bf16[3,64,768]{2,1,0:T(8,128)(2,1)S(1)}, bf16[3,64,768]{2,1,0:T(8,128)(2,1)S(1)}, u32[]{:S(2)}, u32[]{:S(2)}) %collective-permute-start.12) | collective-permute-done | bytes 294944 | tf_op jit(solution)/shard_map/ppermute | solution.py:31
  69.7 2.5 %products.1 = (f32[2,32,2048]{2,1,0:T(8,128)S(1)}, f32[2,32,2048]{2,1,0:T(8,128)S(1)}) custom-call(bf16[3,64,768]{2,1,0:T(8,128)(2,1)S(1)} %collective-permute-done.12.act, bf16[2048,768]{1,0:T(8,128)(2,1)S(1)} %get-tuple-element.70.refs_0_, bf16[2048,768]{1,0:T(8,128)(2,1)S(1)} %get-tuple-element.71.refs_1_, ...), custom_call_target="tpu_custom_call" | custom-call | flops 75497472 | bytes 1179648 | tf_op jit(solution)/shard_map/products/pallas_call | solution.py:278
  72.2 0.1 collective-permute-start.13
  72.3 1.9 %collective-permute-done.13.other = f32[2,32,2048]{2,1,0:T(8,128)S(1)} collective-permute-done((f32[2,32,2048]{2,1,0:T(8,128)S(1)}, f32[2,32,2048]{2,1,0:T(8,128)S(1)}, u32[]{:S(2)}, u32[]{:S(2)}) %collective-permute-start.13) | collective-permute-done | bytes 524320 | tf_op jit(solution)/shard_map/ppermute | solution.py:31
  74.2 0.1 fold.1
  74.3 1.3 %collective-permute-start.14 = (bf16[2,8,2048]{2,1,0:T(8,128)(2,1)S(1)}, bf16[2,8,2048]{2,1,0:T(8,128)(2,1)S(1)}, u32[]{:S(2)}, u32[]{:S(2)}) collective-permute-start(bf16[2,8,2048]{2,1,0:T(8,128)(2,1)S(1)} %get-tuple-element.80), channel_id=1, source_target_pairs={{0,8},{4,12},{8,0},{12,4},{16,24},{20,28},{24,16},{28,20},{1,9},{5... | collective-permute-start | bytes 196616 | tf_op jit(solution)/shard_map/ppermute | solution.py:31
  75.5 0.8 %collective-permute-start.15 = (bf16[2,8,2048]{2,1,0:T(8,128)(2,1)S(1)}, bf16[2,8,2048]{2,1,0:T(8,128)(2,1)S(1)}, u32[]{:S(2)}, u32[]{:S(2)}) collective-permute-start(bf16[2,8,2048]{2,1,0:T(8,128)(2,1)S(1)} %get-tuple-element.81), channel_id=1, source_target_pairs={{0,16},{4,20},{8,24},{12,28},{16,0},{20,4},{24,8},{28,12},{1,17},{... | collective-permute-start | bytes 196616 | tf_op jit(solution)/shard_map/ppermute | solution.py:31
  76.4 1.4 %collective-permute-start.16 = (bf16[2,8,2048]{2,1,0:T(8,128)(2,1)S(1)}, bf16[2,8,2048]{2,1,0:T(8,128)(2,1)S(1)}, u32[]{:S(2)}, u32[]{:S(2)}) collective-permute-start(bf16[2,8,2048]{2,1,0:T(8,128)(2,1)S(1)} %get-tuple-element.82), channel_id=1, source_target_pairs={{0,24},{4,28},{8,16},{12,20},{16,8},{20,12},{24,0},{28,4},{1,25},{... | collective-permute-start | bytes 196616 | tf_op jit(solution)/shard_map/ppermute | solution.py:31
  77.8 4.1 %grads.1 = (bf16[2048,3072]{1,0:T(8,128)(2,1)}, bf16[2048,3072]{1,0:T(8,128)(2,1)}, bf16[3072,2048]{1,0:T(8,128)(2,1)}) custom-call(bf16[3,64,768]{2,1,0:T(8,128)(2,1)S(1)} %collective-permute-done.12.act, bf16[2048,64]{1,0:T(8,128)(2,1)S(1)} %get-tuple-element.60.refs_3_.refs_4_.refs_0_, ...), custom_call_target="tpu_custom_call", output_to_operand_aliasing={{0}: (3, {}), {1}: (4, {}), {2}: (5, {})} | custom-call | flops 75497472 | bytes 1179648 | tf_op jit(solution)/shard_map/grads/pallas_call | solution.py:278
  81.9 0.0 collective-permute-done.14.refs_0_
  81.9 0.0 collective-permute-done.16.refs_2_
  81.9 0.6 finish.1
  (1 shorter events, 0.0 us)
Async XLA Ops:
  1.4 6.1 %collective-permute-start.2 = (bf16[16,2048]{1,0:T(8,128)(2,1)S(1)}, bf16[16,2048]{1,0:T(8,128)(2,1)S(1)}, u32[]{:S(2)}, u32[]{:S(2)}) collective-permute-start(bf16[16,2048]{1,0:T(8,128)(2,1)S(1)} %pack.1.refs_0_), channel_id=1, source_target_pairs={{0,24},{4,28},{8,16},{12,20},{16,8},{20,12},{24,0},{28,4},{1,25},{... | collective-permute-start | bytes 196616 | tf_op jit(solution)/shard_map/ppermute | solution.py:31
  5.3 4.3 %collective-permute-start.1 = (bf16[16,2048]{1,0:T(8,128)(2,1)S(1)}, bf16[16,2048]{1,0:T(8,128)(2,1)S(1)}, u32[]{:S(2)}, u32[]{:S(2)}) collective-permute-start(bf16[16,2048]{1,0:T(8,128)(2,1)S(1)} %pack.1.refs_0_), channel_id=1, source_target_pairs={{0,16},{4,20},{8,24},{12,28},{16,0},{20,4},{24,8},{28,12},{1,17},{... | collective-permute-start | bytes 196616 | tf_op jit(solution)/shard_map/ppermute | solution.py:31
  5.8 4.3 %collective-permute-start = (bf16[16,2048]{1,0:T(8,128)(2,1)S(1)}, bf16[16,2048]{1,0:T(8,128)(2,1)S(1)}, u32[]{:S(2)}, u32[]{:S(2)}) collective-permute-start(bf16[16,2048]{1,0:T(8,128)(2,1)S(1)} %pack.1.refs_0_), channel_id=1, source_target_pairs={{0,8},{4,12},{8,0},{12,4},{16,24},{20,28},{24,16},{28,20},{1,9},{5... | collective-permute-start | bytes 196616 | tf_op jit(solution)/shard_map/ppermute | solution.py:31
  5.9 4.2 %collective-permute-start.3 = (bf16[16,2048]{1,0:T(8,128)(2,1)S(1)}, bf16[16,2048]{1,0:T(8,128)(2,1)S(1)}, u32[]{:S(2)}, u32[]{:S(2)}) collective-permute-start(bf16[16,2048]{1,0:T(8,128)(2,1)S(1)} %pack.1.refs_0_), channel_id=1, source_target_pairs={{0,4},{4,0},{8,12},{12,8},{16,20},{20,16},{24,28},{28,24},{1,5},{5... | collective-permute-start | bytes 196616 | tf_op jit(solution)/shard_map/ppermute | solution.py:31
  7.6 2.5 %collective-permute-start.6 = (bf16[16,2048]{1,0:T(8,128)(2,1)S(1)}, bf16[16,2048]{1,0:T(8,128)(2,1)S(1)}, u32[]{:S(2)}, u32[]{:S(2)}) collective-permute-start(bf16[16,2048]{1,0:T(8,128)(2,1)S(1)} %collective-permute-done.2.refs_3_), channel_id=1, source_target_pairs={{0,4},{4,0},{8,12},{12,8},{16,20},{20,16},{24,28},{28,24},{1,5},{5... | collective-permute-start | bytes 196616 | tf_op jit(solution)/shard_map/ppermute | solution.py:31
  9.6 1.3 %collective-permute-start.5 = (bf16[16,2048]{1,0:T(8,128)(2,1)S(1)}, bf16[16,2048]{1,0:T(8,128)(2,1)S(1)}, u32[]{:S(2)}, u32[]{:S(2)}) collective-permute-start(bf16[16,2048]{1,0:T(8,128)(2,1)S(1)} %collective-permute-done.1.refs_2_), channel_id=1, source_target_pairs={{0,4},{4,0},{8,12},{12,8},{16,20},{20,16},{24,28},{28,24},{1,5},{5... | collective-permute-start | bytes 196616 | tf_op jit(solution)/shard_map/ppermute | solution.py:31
  10.1 1.3 %collective-permute-start.4 = (bf16[16,2048]{1,0:T(8,128)(2,1)S(1)}, bf16[16,2048]{1,0:T(8,128)(2,1)S(1)}, u32[]{:S(2)}, u32[]{:S(2)}) collective-permute-start(bf16[16,2048]{1,0:T(8,128)(2,1)S(1)} %collective-permute-done.refs_1_), channel_id=1, source_target_pairs={{0,4},{4,0},{8,12},{12,8},{16,20},{20,16},{24,28},{28,24},{1,5},{5... | collective-permute-start | bytes 196616 | tf_op jit(solution)/shard_map/ppermute | solution.py:31
  16.2 11.5 %collective-permute-start.8 = (bf16[3,64,768]{2,1,0:T(8,128)(2,1)S(1)}, bf16[3,64,768]{2,1,0:T(8,128)(2,1)S(1)}, u32[]{:S(2)}, u32[]{:S(2)}) collective-permute-start(bf16[3,64,768]{2,1,0:T(8,128)(2,1)S(1)} %get-tuple-element.53), channel_id=1, source_target_pairs={{0,1},{1,0},{2,3},{3,2},{4,5},{5,4},{6,7},{7,6},{8,9},{9,8},{10,11... | collective-permute-start | bytes 884744 | tf_op jit(solution)/shard_map/ppermute | solution.py:31
  22.5 12.6 %collective-permute-start.7 = (bf16[3,64,768]{2,1,0:T(8,128)(2,1)S(1)}, bf16[3,64,768]{2,1,0:T(8,128)(2,1)S(1)}, u32[]{:S(2)}, u32[]{:S(2)}) collective-permute-start(bf16[3,64,768]{2,1,0:T(8,128)(2,1)S(1)} %get-tuple-element.51), channel_id=1, source_target_pairs={{0,1},{1,0},{2,3},{3,2},{4,5},{5,4},{6,7},{7,6},{8,9},{9,8},{10,11... | collective-permute-start | bytes 884744 | tf_op jit(solution)/shard_map/ppermute | solution.py:31
  27.8 15.9 %collective-permute-start.9 = (bf16[3,64,768]{2,1,0:T(8,128)(2,1)S(1)}, bf16[3,64,768]{2,1,0:T(8,128)(2,1)S(1)}, u32[]{:S(2)}, u32[]{:S(2)}) collective-permute-start(bf16[3,64,768]{2,1,0:T(8,128)(2,1)S(1)} %combine.1), channel_id=1, source_target_pairs={{0,2},{1,3},{2,0},{3,1},{4,6},{5,7},{6,4},{7,5},{8,10},{9,11},{10,... | collective-permute-start | bytes 884744 | tf_op jit(solution)/shard_map/ppermute | solution.py:31
  43.8 13.8 %collective-permute-start.11 = (bf16[3,64,768]{2,1,0:T(8,128)(2,1)S(1)}, bf16[3,64,768]{2,1,0:T(8,128)(2,1)S(1)}, u32[]{:S(2)}, u32[]{:S(2)}) collective-permute-start(bf16[3,64,768]{2,1,0:T(8,128)(2,1)S(1)} %activate.1.act), channel_id=1, source_target_pairs={{0,1},{1,0},{2,3},{3,2},{4,5},{5,4},{6,7},{7,6},{8,9},{9,8},{10,11... | collective-permute-start | bytes 884744 | tf_op jit(solution)/shard_map/ppermute | solution.py:31
  44.6 18.3 %collective-permute-start.10 = (bf16[3,64,768]{2,1,0:T(8,128)(2,1)S(1)}, bf16[3,64,768]{2,1,0:T(8,128)(2,1)S(1)}, u32[]{:S(2)}, u32[]{:S(2)}) collective-permute-start(bf16[3,64,768]{2,1,0:T(8,128)(2,1)S(1)} %activate.1.act), channel_id=1, source_target_pairs={{0,2},{1,3},{2,0},{3,1},{4,6},{5,7},{6,4},{7,5},{8,10},{9,11},{10,... | collective-permute-start | bytes 884744 | tf_op jit(solution)/shard_map/ppermute | solution.py:31
  62.9 6.8 %collective-permute-start.12 = (bf16[3,64,768]{2,1,0:T(8,128)(2,1)S(1)}, bf16[3,64,768]{2,1,0:T(8,128)(2,1)S(1)}, u32[]{:S(2)}, u32[]{:S(2)}) collective-permute-start(bf16[3,64,768]{2,1,0:T(8,128)(2,1)S(1)} %collective-permute-done.10.act), channel_id=1, source_target_pairs={{0,1},{1,0},{2,3},{3,2},{4,5},{5,4},{6,7},{7,6},{8,9},{9,8},{10,11... | collective-permute-start | bytes 884744 | tf_op jit(solution)/shard_map/ppermute | solution.py:31
  72.2 2.0 %collective-permute-start.13 = (f32[2,32,2048]{2,1,0:T(8,128)S(1)}, f32[2,32,2048]{2,1,0:T(8,128)S(1)}, u32[]{:S(2)}, u32[]{:S(2)}) collective-permute-start(f32[2,32,2048]{2,1,0:T(8,128)S(1)} %get-tuple-element.78), channel_id=1, source_target_pairs={{0,4},{4,0},{8,12},{12,8},{16,20},{20,16},{24,28},{28,24},{1,5},{5... | collective-permute-start | bytes 1572872 | tf_op jit(solution)/shard_map/ppermute | solution.py:31
  74.3 7.6 %collective-permute-start.14 = (bf16[2,8,2048]{2,1,0:T(8,128)(2,1)S(1)}, bf16[2,8,2048]{2,1,0:T(8,128)(2,1)S(1)}, u32[]{:S(2)}, u32[]{:S(2)}) collective-permute-start(bf16[2,8,2048]{2,1,0:T(8,128)(2,1)S(1)} %get-tuple-element.80), channel_id=1, source_target_pairs={{0,8},{4,12},{8,0},{12,4},{16,24},{20,28},{24,16},{28,20},{1,9},{5... | collective-permute-start | bytes 196616 | tf_op jit(solution)/shard_map/ppermute | solution.py:31
  75.5 6.4 %collective-permute-start.15 = (bf16[2,8,2048]{2,1,0:T(8,128)(2,1)S(1)}, bf16[2,8,2048]{2,1,0:T(8,128)(2,1)S(1)}, u32[]{:S(2)}, u32[]{:S(2)}) collective-permute-start(bf16[2,8,2048]{2,1,0:T(8,128)(2,1)S(1)} %get-tuple-element.81), channel_id=1, source_target_pairs={{0,16},{4,20},{8,24},{12,28},{16,0},{20,4},{24,8},{28,12},{1,17},{... | collective-permute-start | bytes 196616 | tf_op jit(solution)/shard_map/ppermute | solution.py:31
  76.4 5.5 %collective-permute-start.16 = (bf16[2,8,2048]{2,1,0:T(8,128)(2,1)S(1)}, bf16[2,8,2048]{2,1,0:T(8,128)(2,1)S(1)}, u32[]{:S(2)}, u32[]{:S(2)}) collective-permute-start(bf16[2,8,2048]{2,1,0:T(8,128)(2,1)S(1)} %get-tuple-element.82), channel_id=1, source_target_pairs={{0,24},{4,28},{8,16},{12,20},{16,8},{20,12},{24,0},{28,4},{1,25},{... | collective-permute-start | bytes 196616 | tf_op jit(solution)/shard_map/ppermute | solution.py:31

commit v6 on v5

--- a/solution.py
+++ b/solution.py
@@ -116,45 +116,63 @@
     return copies
 
 
-def sums_kernel(k, tok, grad, gate_w, up_w, down_w, *refs):
-    out, gate_b, up_b, down_b, sems, gate, up, back = refs[-8:]
-    moves = (
-        (gate, lambda here: dot(tok[:, here], gate_b[here])),
-        (up, lambda here: dot(tok[:, here], up_b[here])),
-        (back, lambda here: back_dot(grad[:, here], down_b[:, here])),
-    )
-    copies = fetches(k, (gate_w, up_w, down_w), (gate_b, up_b, down_b), sems)
-    for chunk in copies:
-        for copy in chunk:
-            copy.start()
-    part = grad.shape[1] // CHUNKS
-    for i, chunk in enumerate(copies):
-        here = span(i, part)
-        for copy, (acc, term) in zip(chunk, moves):
-            copy.wait()
-            if i == 0:
-                acc[...] = term(here)
-            else:
-                acc[...] += term(here)
-    out[0] = gate[...].astype(out.dtype)
-    out[1] = up[...].astype(out.dtype)
-    out[2] = back[...].astype(out.dtype)
-
-
-def partial_sums(k, tok, grad, weights, units, dtype):
+def block_shapes(units, width):
+    return [(width, units), (width, units), (units, width)]
+
+
+def load_kernel(k, *refs):
+    copies = sum(fetches(k, refs[:3], refs[3:6], refs[6]), [])
+    for copy in copies:
+        copy.start()
+    for copy in copies:
+        copy.wait()
+
+
+def load(k, weights, units):
+    shapes = block_shapes(units, weights[0].shape[0])
+    return pl.pallas_call(
+        functools.partial(load_kernel, k),
+        in_specs=[HOLD] * 3,
+        out_specs=[WHOLE] * 3,
+        scratch_shapes=[pltpu.SemaphoreType.DMA((CHUNKS, 3))],
+        out_shape=[vmem_array(x) for x in shapes],
+        compiler_params=PARAMS,
+        cost_estimate=estimate(0, 6 * weights[0].shape[0] * units),
+        name="load",
+    )(*in_hbm(weights))
+
+
+def sums_kernel(following, tok, grad, gate_b, up_b, down_b, *refs):
+    copies = []
+    if following is not None:
+        hbm, out, kept, sems = refs[:3], refs[3], refs[4:7], refs[7]
+        copies = sum(fetches(following, hbm, kept, sems), [])
+    else:
+        (out,) = refs
+    for copy in copies:
+        copy.start()
+    out[0] = dot(tok[...], gate_b[...]).astype(out.dtype)
+    out[1] = dot(tok[...], up_b[...]).astype(out.dtype)
+    out[2] = back_dot(grad[...], down_b[...]).astype(out.dtype)
+    for copy in copies:
+        copy.wait()
+
+
+def partial_sums(block, tok, grad, dtype, weights=None, following=None):
     total, width = tok.shape
-    shapes = [(width, units), (width, units), (units, width)]
-    return pl.pallas_call(
-        functools.partial(sums_kernel, k),
-        in_specs=[WHOLE, WHOLE] + [HOLD] * 3,
-        out_specs=[WHOLE] * 4,
-        scratch_shapes=[pltpu.SemaphoreType.DMA((CHUNKS, 3))]
-        + [pltpu.VMEM((total, units), F32)] * 3,
+    units = block[2].shape[0]
+    more = following is not None
+    shapes = block_shapes(units, width) if more else []
+    return pl.pallas_call(
+        functools.partial(sums_kernel, following),
+        in_specs=[WHOLE] * 5 + [HOLD] * (3 * more),
+        out_specs=[WHOLE] * (1 + 3 * more),
+        scratch_shapes=[pltpu.SemaphoreType.DMA((CHUNKS, 3))] * more,
         out_shape=[array((3, total, units), dtype)] + [vmem_array(x) for x in shapes],
         compiler_params=PARAMS,
         cost_estimate=estimate(6 * total * width * units, 6 * width * units),
         name="partial_sums",
-    )(tok, grad, *in_hbm(weights))
+    )(tok, grad, *in_vmem(block), *(in_hbm(weights) if more else ()))
 
 
 def combine_kernel(own, other, out):
@@ -333,27 +351,29 @@
     along_col = functools.partial(swap, axis="col", size=n_col)
 
     mine = pack(tokens, out_grad)
-    even = [mine] + [along_row(mine, k=k) for k in range(2, n_row, 2)]
+    last_weights = load(3, weights, units)
+    away = [along_row(mine, k=k) for k in range(2, n_row, 2)]
+    away, last_weights = lax.optimization_barrier((away, last_weights))
+    even = [mine, *away]
     odd = [along_row(piece, k=1) for piece in even]
     tok, grad, tok_t = assemble(even + odd, rows)
     sides = (tok_t, grad, all_units)
 
-    sums = functools.partial(partial_sums, tok=tok, grad=grad, weights=weights, units=units)
-    there, *last_weights = sums(3, dtype=BF16)
+    there, *near_weights = partial_sums(last_weights, tok, grad, BF16, weights, 1)
     near = along_col(there, k=1)
-    here, *far_weights = sums(2, dtype=F32)
+    there, *far_weights = partial_sums(near_weights, tok, grad, BF16, weights, 2)
+    from_near = along_col(there, k=1)
+    here, *own_weights = partial_sums(far_weights, tok, grad, F32, weights, 0)
     from_far = along_col(combine(here, near), k=2)
-    there, *near_weights = sums(1, dtype=BF16)
-    from_near = along_col(there, k=1)
-    here, *own_weights = sums(0, dtype=F32)
+    (here,) = partial_sums(own_weights, tok, grad, F32)
     own = activate(here, [from_near, from_far])
 
     near_act = along_col(own, k=1)
     far_act = along_col(own, k=2)
     terms, *grads = use(0, own, own_weights, sides=sides)
-    terms, *grads = use(1, near_act, near_weights, terms, sides=sides, grads=grads)
     held, _ = lax.optimization_barrier((far_act, (terms, grads)))
     last_act = along_col(held, k=1)
+    terms, *grads = use(1, near_act, near_weights, terms, sides=sides, grads=grads)
     terms, *grads = use(2, far_act, far_weights, terms, sides=sides, grads=grads)
     kept, given = use(3, last_act, last_weights, terms, last=True)
 

time: 82.8 us -> 88.7 us (1.071)
  Pallas kernels: 43.1 us -> 48.5 us
    pallas_call x4 -> x5, Pallas kernels: 18.6 us -> 24 us  [the longest x4 20 us: partial_sums(): pl.pallas_call(functools.partial(sums_kernel, following), in_specs=[WHOLE...]
  transfers between devices with their start and end apart: 17 -> 17, of which waited for: 9 -> 9; matrix products, arithmetic and copies ran while one was open for 0% -> 0% of each run, Pallas kernels for 41% -> 43%
where the time goes in v6:
time: 88.7 us; the launch traced here: 88.5 us
  Pallas kernels  48.5 us (55%)
  waiting for transfers between devices  21.6 us (24%)
  starting transfers between devices  17.5 us (20%)
    pallas_call x5, Pallas kernels, use(): pl.pallas_call(functools.partial(use_kernel, k, first, last, weights is n...  22.6 us
    ppermute x17, waiting for transfers between devices, swap(): return lax.ppermute(x, axis, [(i, i ^ k) for i in range(size)])  21.6 us
    pallas_call x4, Pallas kernels, partial_sums(): pl.pallas_call(functools.partial(sums_kernel, following), in_specs=[WHOLE...  20 us
    ppermute x17, starting transfers between devices, swap(): return lax.ppermute(x, axis, [(i, i ^ k) for i in range(size)])  17.5 us
    pallas_call x1, Pallas kernels, load(): pl.pallas_call(functools.partial(load_kernel, k), in_specs=[HOLD] * 3, ou...  3.95 us
  transfers between devices with their start and end apart: 17, of which 9 were waited for; matrix products, arithmetic and copies ran while one was open for 0% of the time, Pallas kernels for 43%

profile of v6, /device:TPU:0, one launch (start us, length us, event | category | flops | bytes accessed | tf_op | source)
XLA Modules:
  0.0 88.5 jit_solution(10627565697770091551)
XLA Ops:
  0.6 0.8 pack.1.refs_0_
  1.4 2.9 %collective-permute-start = (bf16[16,2048]{1,0:T(8,128)(2,1)S(1)}, bf16[16,2048]{1,0:T(8,128)(2,1)S(1)}, u32[]{:S(2)}, u32[]{:S(2)}) collective-permute-start(bf16[16,2048]{1,0:T(8,128)(2,1)S(1)} %pack.1.refs_0_), channel_id=1, source_target_pairs={{0,8},{4,12},{8,0},{12,4},{16,24},{20,28},{24,16},{28,20},{1,9},{5... | collective-permute-start | bytes 196616 | tf_op jit(solution)/shard_map/ppermute | solution.py:31
  4.4 1.5 %collective-permute-start.1 = (bf16[16,2048]{1,0:T(8,128)(2,1)S(1)}, bf16[16,2048]{1,0:T(8,128)(2,1)S(1)}, u32[]{:S(2)}, u32[]{:S(2)}) collective-permute-start(bf16[16,2048]{1,0:T(8,128)(2,1)S(1)} %pack.1.refs_0_), channel_id=1, source_target_pairs={{0,16},{4,20},{8,24},{12,28},{16,0},{20,4},{24,8},{28,12},{1,17},{... | collective-permute-start | bytes 196616 | tf_op jit(solution)/shard_map/ppermute | solution.py:31
  5.9 0.0 collective-permute-start.2
  5.9 0.0 collective-permute-start.3
  5.9 3.9 %load.1 = (bf16[2048,768]{1,0:T(8,128)(2,1)S(1)}, bf16[2048,768]{1,0:T(8,128)(2,1)S(1)}, bf16[768,2048]{1,0:T(8,128)(2,1)S(1)}) custom-call(bf16[2048,3072]{1,0:T(8,128)(2,1)} %refs_0_.7, bf16[2048,3072]{1,0:T(8,128)(2,1)} %refs_1_.7, bf16[3072,2048]{1,0:T(8,128)(2,1)} %refs_2_.7), custom_call_target="tpu_custom_call" | custom-call | bytes 1179648 | tf_op jit(solution)/shard_map/load/pallas_call | solution.py:133
  9.8 0.0 collective-permute-done.refs_1_
  9.8 0.0 collective-permute-done.1.refs_2_
  9.9 1.2 %collective-permute-done.2.refs_3_ = bf16[16,2048]{1,0:T(8,128)(2,1)S(1)} collective-permute-done((bf16[16,2048]{1,0:T(8,128)(2,1)S(1)}, bf16[16,2048]{1,0:T(8,128)(2,1)S(1)}, u32[]{:S(2)}, u32[]{:S(2)}) %collective-permute-start.2) | collective-permute-done | bytes 65568 | tf_op jit(solution)/shard_map/ppermute | solution.py:31
  11.0 0.0 collective-permute-start.4
  11.0 0.5 collective-permute-start.5
  11.5 0.0 collective-permute-start.6
  11.6 0.0 collective-permute-done.3.refs_4_
  11.6 0.7 collective-permute-done.4.refs_5_
  12.3 0.2 collective-permute-done.5.refs_6_
  12.4 0.4 collective-permute-done.6.refs_7_
  12.8 0.2 assemble.1
  13.0 6.0 %partial_sums.4 = (bf16[3,64,768]{2,1,0:T(8,128)(2,1)S(1)}, bf16[2048,768]{1,0:T(8,128)(2,1)S(1)}, bf16[2048,768]{1,0:T(8,128)(2,1)S(1)}, bf16[768,2048]{1,0:T(8,128)(2,1)S(1)}) custom-call(bf16[64,2048]{1,0:T(8,128)(2,1)S(1)} %get-tuple-element.59.tok, bf16[64,2048]{1,0:T(8,128)(2,1)S(1)} %get-tuple-element.60.grad.refs_4_.refs_5_.refs_1_, ...), custom_call_target="tpu_custom_call" | custom-call | flops 75497472 | bytes 1179648 | tf_op jit(solution)/shard_map/partial_sums/pallas_call | solution.py:166
  19.0 1.6 %collective-permute-start.8 = (bf16[3,64,768]{2,1,0:T(8,128)(2,1)S(1)}, bf16[3,64,768]{2,1,0:T(8,128)(2,1)S(1)}, u32[]{:S(2)}, u32[]{:S(2)}) collective-permute-start(bf16[3,64,768]{2,1,0:T(8,128)(2,1)S(1)} %get-tuple-element.75), channel_id=1, source_target_pairs={{0,1},{1,0},{2,3},{3,2},{4,5},{5,4},{6,7},{7,6},{8,9},{9,8},{10,11... | collective-permute-start | bytes 884744 | tf_op jit(solution)/shard_map/ppermute | solution.py:31
  20.6 5.9 %partial_sums.5 = (bf16[3,64,768]{2,1,0:T(8,128)(2,1)S(1)}, bf16[2048,768]{1,0:T(8,128)(2,1)S(1)}, bf16[2048,768]{1,0:T(8,128)(2,1)S(1)}, bf16[768,2048]{1,0:T(8,128)(2,1)S(1)}) custom-call(bf16[64,2048]{1,0:T(8,128)(2,1)S(1)} %get-tuple-element.59.tok, bf16[64,2048]{1,0:T(8,128)(2,1)S(1)} %get-tuple-element.60.grad.refs_4_.refs_5_.refs_1_, ...), custom_call_target="tpu_custom_call" | custom-call | flops 75497472 | bytes 1179648 | tf_op jit(solution)/shard_map/partial_sums/pallas_call | solution.py:166
  26.6 0.6 collective-permute-start.7
  27.1 5.9 %partial_sums.6 = (f32[3,64,768]{2,1,0:T(8,128)S(1)}, bf16[2048,768]{1,0:T(8,128)(2,1)S(1)}, bf16[2048,768]{1,0:T(8,128)(2,1)S(1)}, bf16[768,2048]{1,0:T(8,128)(2,1)S(1)}) custom-call(bf16[64,2048]{1,0:T(8,128)(2,1)S(1)} %get-tuple-element.59.tok, bf16[64,2048]{1,0:T(8,128)(2,1)S(1)} %get-tuple-element.60.grad.refs_4_.refs_5_.refs_1_, ...), custom_call_target="tpu_custom_call" | custom-call | flops 75497472 | bytes 1179648 | tf_op jit(solution)/shard_map/partial_sums/pallas_call | solution.py:166
  33.1 0.0 collective-permute-done.8.other
  33.1 0.1 combine.1
  33.2 2.7 %collective-permute-start.9 = (bf16[3,64,768]{2,1,0:T(8,128)(2,1)S(1)}, bf16[3,64,768]{2,1,0:T(8,128)(2,1)S(1)}, u32[]{:S(2)}, u32[]{:S(2)}) collective-permute-start(bf16[3,64,768]{2,1,0:T(8,128)(2,1)S(1)} %combine.1), channel_id=1, source_target_pairs={{0,2},{1,3},{2,0},{3,1},{4,6},{5,7},{6,4},{7,5},{8,10},{9,11},{10,... | collective-permute-start | bytes 884744 | tf_op jit(solution)/shard_map/ppermute | solution.py:31
  35.8 2.1 %partial_sums.7.own = f32[3,64,768]{2,1,0:T(8,128)S(1)} custom-call(bf16[64,2048]{1,0:T(8,128)(2,1)S(1)} %get-tuple-element.59.tok, bf16[64,2048]{1,0:T(8,128)(2,1)S(1)} %get-tuple-element.60.grad.refs_4_.refs_5_.refs_1_, bf16[2048,768]{1,0:T(8,128)(2,1)S(1)} %get-tuple-element.70.gate_b.refs_0_, bf16[2048,768]{1,0:T(8,128)(2,1)S(1)} %get-tuple-element.71.up_b.refs_1_, ...), custom_call_target="tpu_custom_call" | custom-call | flops 75497472 | bytes 1179648 | tf_op jit(solution)/shard_map/partial_sums/pallas_call | solution.py:166
  38.0 0.0 collective-permute-done.7.refs_0_
  38.0 11.0 %collective-permute-done.9.refs_1_ = bf16[3,64,768]{2,1,0:T(8,128)(2,1)S(1)} collective-permute-done((bf16[3,64,768]{2,1,0:T(8,128)(2,1)S(1)}, bf16[3,64,768]{2,1,0:T(8,128)(2,1)S(1)}, u32[]{:S(2)}, u32[]{:S(2)}) %collective-permute-start.9) | collective-permute-done | bytes 294944 | tf_op jit(solution)/shard_map/ppermute | solution.py:31
  49.0 0.2 activate.1.act
  49.1 0.1 collective-permute-start.10
  49.2 4.0 %collective-permute-start.12 = (bf16[3,64,768]{2,1,0:T(8,128)(2,1)S(1)}, bf16[3,64,768]{2,1,0:T(8,128)(2,1)S(1)}, u32[]{:S(2)}, u32[]{:S(2)}) collective-permute-start(bf16[3,64,768]{2,1,0:T(8,128)(2,1)S(1)} %activate.1.act), channel_id=1, source_target_pairs={{0,1},{1,0},{2,3},{3,2},{4,5},{5,4},{6,7},{7,6},{8,9},{9,8},{10,11... | collective-permute-start | bytes 884744 | tf_op jit(solution)/shard_map/ppermute | solution.py:31
  53.2 5.3 %productsgrads.3 = (f32[2,64,2048]{2,1,0:T(8,128)S(1)}, bf16[2048,3072]{1,0:T(8,128)(2,1)}, bf16[2048,3072]{1,0:T(8,128)(2,1)}, bf16[3072,2048]{1,0:T(8,128)(2,1)}) custom-call(bf16[3,64,768]{2,1,0:T(8,128)(2,1)S(1)} %activate.1.act, bf16[2048,768]{1,0:T(8,128)(2,1)S(1)} %get-tuple-element.70.gate_b.refs_0_, ...), custom_call_target="tpu_custom_call" | custom-call | flops 150994944 | bytes 2359296 | tf_op jit(solution)/shard_map/productsgrads/pallas_call | solution.py:296
  58.5 5.8 %collective-permute-done.10.act = bf16[3,64,768]{2,1,0:T(8,128)(2,1)S(1)} collective-permute-done((bf16[3,64,768]{2,1,0:T(8,128)(2,1)S(1)}, bf16[3,64,768]{2,1,0:T(8,128)(2,1)S(1)}, u32[]{:S(2)}, u32[]{:S(2)}) %collective-permute-start.10) | collective-permute-done | bytes 294944 | tf_op jit(solution)/shard_map/ppermute | solution.py:31
  64.3 0.0 collective-permute-start.11
  64.3 0.1 collective-permute-done.12.act
  64.4 5.5 %productsgrads.4 = (f32[2,64,2048]{2,1,0:T(8,128)S(1)}, bf16[2048,3072]{1,0:T(8,128)(2,1)}, bf16[2048,3072]{1,0:T(8,128)(2,1)}, bf16[3072,2048]{1,0:T(8,128)(2,1)}) custom-call(bf16[3,64,768]{2,1,0:T(8,128)(2,1)S(1)} %collective-permute-done.12.act, ...), custom_call_target="tpu_custom_call", output_to_operand_aliasing={{1}: (7, {}), {2}: (8, {}), {3}: (9, {})} | custom-call | flops 150994944 | bytes 2359296 | tf_op jit(solution)/shard_map/productsgrads/pallas_call | solution.py:296
  69.8 5.3 %productsgrads.5 = (f32[2,64,2048]{2,1,0:T(8,128)S(1)}, bf16[2048,3072]{1,0:T(8,128)(2,1)}, bf16[2048,3072]{1,0:T(8,128)(2,1)}, bf16[3072,2048]{1,0:T(8,128)(2,1)}) custom-call(bf16[3,64,768]{2,1,0:T(8,128)(2,1)S(1)} %collective-permute-done.10.act, ...), custom_call_target="tpu_custom_call", output_to_operand_aliasing={{1}: (7, {}), {2}: (8, {}), {3}: (9, {})} | custom-call | flops 150994944 | bytes 2359296 | tf_op jit(solution)/shard_map/productsgrads/pallas_call | solution.py:296
  75.1 2.5 %products.1 = (f32[2,32,2048]{2,1,0:T(8,128)S(1)}, f32[2,32,2048]{2,1,0:T(8,128)S(1)}) custom-call(bf16[3,64,768]{2,1,0:T(8,128)(2,1)S(1)} %collective-permute-done.11.act, bf16[2048,768]{1,0:T(8,128)(2,1)S(1)} %get-tuple-element.61.gate_b.refs_0_, bf16[2048,768]{1,0:T(8,128)(2,1)S(1)} %get-tuple-element.62.up_b.refs_1_, ...), custom_call_target="tpu_custom_call" | custom-call | flops 75497472 | bytes 1179648 | tf_op jit(solution)/shard_map/products/pallas_call | solution.py:296
  77.7 0.1 collective-permute-start.13
  77.7 1.9 %collective-permute-done.13.other = f32[2,32,2048]{2,1,0:T(8,128)S(1)} collective-permute-done((f32[2,32,2048]{2,1,0:T(8,128)S(1)}, f32[2,32,2048]{2,1,0:T(8,128)S(1)}, u32[]{:S(2)}, u32[]{:S(2)}) %collective-permute-start.13) | collective-permute-done | bytes 524320 | tf_op jit(solution)/shard_map/ppermute | solution.py:31
  79.6 0.1 fold.1
  79.7 1.5 %collective-permute-start.14 = (bf16[2,8,2048]{2,1,0:T(8,128)(2,1)S(1)}, bf16[2,8,2048]{2,1,0:T(8,128)(2,1)S(1)}, u32[]{:S(2)}, u32[]{:S(2)}) collective-permute-start(bf16[2,8,2048]{2,1,0:T(8,128)(2,1)S(1)} %get-tuple-element.90), channel_id=1, source_target_pairs={{0,8},{4,12},{8,0},{12,4},{16,24},{20,28},{24,16},{28,20},{1,9},{5... | collective-permute-start | bytes 196616 | tf_op jit(solution)/shard_map/ppermute | solution.py:31
  81.2 1.5 %collective-permute-start.15 = (bf16[2,8,2048]{2,1,0:T(8,128)(2,1)S(1)}, bf16[2,8,2048]{2,1,0:T(8,128)(2,1)S(1)}, u32[]{:S(2)}, u32[]{:S(2)}) collective-permute-start(bf16[2,8,2048]{2,1,0:T(8,128)(2,1)S(1)} %get-tuple-element.91), channel_id=1, source_target_pairs={{0,16},{4,20},{8,24},{12,28},{16,0},{20,4},{24,8},{28,12},{1,17},{... | collective-permute-start | bytes 196616 | tf_op jit(solution)/shard_map/ppermute | solution.py:31
  82.7 0.6 collective-permute-start.16
  83.3 4.1 %grads.1 = (bf16[2048,3072]{1,0:T(8,128)(2,1)}, bf16[2048,3072]{1,0:T(8,128)(2,1)}, bf16[3072,2048]{1,0:T(8,128)(2,1)}) custom-call(bf16[3,64,768]{2,1,0:T(8,128)(2,1)S(1)} %collective-permute-done.11.act, bf16[2048,64]{1,0:T(8,128)(2,1)S(1)} %get-tuple-element.76.refs_3_.refs_4_.refs_0_, ...), custom_call_target="tpu_custom_call", output_to_operand_aliasing={{0}: (3, {}), {1}: (4, {}), {2}: (5, {})} | custom-call | flops 75497472 | bytes 1179648 | tf_op jit(solution)/shard_map/grads/pallas_call | solution.py:296
  87.3 0.0 collective-permute-done.14.refs_0_
  87.4 0.5 collective-permute-done.16.refs_2_
  87.8 0.6 finish.1
  (2 shorter events, 0.0 us)
Async XLA Ops:
  1.4 8.4 %collective-permute-start = (bf16[16,2048]{1,0:T(8,128)(2,1)S(1)}, bf16[16,2048]{1,0:T(8,128)(2,1)S(1)}, u32[]{:S(2)}, u32[]{:S(2)}) collective-permute-start(bf16[16,2048]{1,0:T(8,128)(2,1)S(1)} %pack.1.refs_0_), channel_id=1, source_target_pairs={{0,8},{4,12},{8,0},{12,4},{16,24},{20,28},{24,16},{28,20},{1,9},{5... | collective-permute-start | bytes 196616 | tf_op jit(solution)/shard_map/ppermute | solution.py:31
  4.4 5.5 %collective-permute-start.1 = (bf16[16,2048]{1,0:T(8,128)(2,1)S(1)}, bf16[16,2048]{1,0:T(8,128)(2,1)S(1)}, u32[]{:S(2)}, u32[]{:S(2)}) collective-permute-start(bf16[16,2048]{1,0:T(8,128)(2,1)S(1)} %pack.1.refs_0_), channel_id=1, source_target_pairs={{0,16},{4,20},{8,24},{12,28},{16,0},{20,4},{24,8},{28,12},{1,17},{... | collective-permute-start | bytes 196616 | tf_op jit(solution)/shard_map/ppermute | solution.py:31
  5.9 5.2 %collective-permute-start.2 = (bf16[16,2048]{1,0:T(8,128)(2,1)S(1)}, bf16[16,2048]{1,0:T(8,128)(2,1)S(1)}, u32[]{:S(2)}, u32[]{:S(2)}) collective-permute-start(bf16[16,2048]{1,0:T(8,128)(2,1)S(1)} %pack.1.refs_0_), channel_id=1, source_target_pairs={{0,24},{4,28},{8,16},{12,20},{16,8},{20,12},{24,0},{28,4},{1,25},{... | collective-permute-start | bytes 196616 | tf_op jit(solution)/shard_map/ppermute | solution.py:31
  5.9 5.7 %collective-permute-start.3 = (bf16[16,2048]{1,0:T(8,128)(2,1)S(1)}, bf16[16,2048]{1,0:T(8,128)(2,1)S(1)}, u32[]{:S(2)}, u32[]{:S(2)}) collective-permute-start(bf16[16,2048]{1,0:T(8,128)(2,1)S(1)} %pack.1.refs_0_), channel_id=1, source_target_pairs={{0,4},{4,0},{8,12},{12,8},{16,20},{20,16},{24,28},{28,24},{1,5},{5... | collective-permute-start | bytes 196616 | tf_op jit(solution)/shard_map/ppermute | solution.py:31
  11.0 1.3 %collective-permute-start.4 = (bf16[16,2048]{1,0:T(8,128)(2,1)S(1)}, bf16[16,2048]{1,0:T(8,128)(2,1)S(1)}, u32[]{:S(2)}, u32[]{:S(2)}) collective-permute-start(bf16[16,2048]{1,0:T(8,128)(2,1)S(1)} %collective-permute-done.refs_1_), channel_id=1, source_target_pairs={{0,4},{4,0},{8,12},{12,8},{16,20},{20,16},{24,28},{28,24},{1,5},{5... | collective-permute-start | bytes 196616 | tf_op jit(solution)/shard_map/ppermute | solution.py:31
  11.0 1.4 %collective-permute-start.5 = (bf16[16,2048]{1,0:T(8,128)(2,1)S(1)}, bf16[16,2048]{1,0:T(8,128)(2,1)S(1)}, u32[]{:S(2)}, u32[]{:S(2)}) collective-permute-start(bf16[16,2048]{1,0:T(8,128)(2,1)S(1)} %collective-permute-done.1.refs_2_), channel_id=1, source_target_pairs={{0,4},{4,0},{8,12},{12,8},{16,20},{20,16},{24,28},{28,24},{1,5},{5... | collective-permute-start | bytes 196616 | tf_op jit(solution)/shard_map/ppermute | solution.py:31
  11.5 1.3 %collective-permute-start.6 = (bf16[16,2048]{1,0:T(8,128)(2,1)S(1)}, bf16[16,2048]{1,0:T(8,128)(2,1)S(1)}, u32[]{:S(2)}, u32[]{:S(2)}) collective-permute-start(bf16[16,2048]{1,0:T(8,128)(2,1)S(1)} %collective-permute-done.2.refs_3_), channel_id=1, source_target_pairs={{0,4},{4,0},{8,12},{12,8},{16,20},{20,16},{24,28},{28,24},{1,5},{5... | collective-permute-start | bytes 196616 | tf_op jit(solution)/shard_map/ppermute | solution.py:31
  19.0 14.0 %collective-permute-start.8 = (bf16[3,64,768]{2,1,0:T(8,128)(2,1)S(1)}, bf16[3,64,768]{2,1,0:T(8,128)(2,1)S(1)}, u32[]{:S(2)}, u32[]{:S(2)}) collective-permute-start(bf16[3,64,768]{2,1,0:T(8,128)(2,1)S(1)} %get-tuple-element.75), channel_id=1, source_target_pairs={{0,1},{1,0},{2,3},{3,2},{4,5},{5,4},{6,7},{7,6},{8,9},{9,8},{10,11... | collective-permute-start | bytes 884744 | tf_op jit(solution)/shard_map/ppermute | solution.py:31
  26.6 11.4 %collective-permute-start.7 = (bf16[3,64,768]{2,1,0:T(8,128)(2,1)S(1)}, bf16[3,64,768]{2,1,0:T(8,128)(2,1)S(1)}, u32[]{:S(2)}, u32[]{:S(2)}) collective-permute-start(bf16[3,64,768]{2,1,0:T(8,128)(2,1)S(1)} %get-tuple-element.73), channel_id=1, source_target_pairs={{0,1},{1,0},{2,3},{3,2},{4,5},{5,4},{6,7},{7,6},{8,9},{9,8},{10,11... | collective-permute-start | bytes 884744 | tf_op jit(solution)/shard_map/ppermute | solution.py:31
  33.2 15.8 %collective-permute-start.9 = (bf16[3,64,768]{2,1,0:T(8,128)(2,1)S(1)}, bf16[3,64,768]{2,1,0:T(8,128)(2,1)S(1)}, u32[]{:S(2)}, u32[]{:S(2)}) collective-permute-start(bf16[3,64,768]{2,1,0:T(8,128)(2,1)S(1)} %combine.1), channel_id=1, source_target_pairs={{0,2},{1,3},{2,0},{3,1},{4,6},{5,7},{6,4},{7,5},{8,10},{9,11},{10,... | collective-permute-start | bytes 884744 | tf_op jit(solution)/shard_map/ppermute | solution.py:31
  49.1 15.1 %collective-permute-start.10 = (bf16[3,64,768]{2,1,0:T(8,128)(2,1)S(1)}, bf16[3,64,768]{2,1,0:T(8,128)(2,1)S(1)}, u32[]{:S(2)}, u32[]{:S(2)}) collective-permute-start(bf16[3,64,768]{2,1,0:T(8,128)(2,1)S(1)} %activate.1.act), channel_id=1, source_target_pairs={{0,2},{1,3},{2,0},{3,1},{4,6},{5,7},{6,4},{7,5},{8,10},{9,11},{10,... | collective-permute-start | bytes 884744 | tf_op jit(solution)/shard_map/ppermute | solution.py:31
  49.2 15.1 %collective-permute-start.12 = (bf16[3,64,768]{2,1,0:T(8,128)(2,1)S(1)}, bf16[3,64,768]{2,1,0:T(8,128)(2,1)S(1)}, u32[]{:S(2)}, u32[]{:S(2)}) collective-permute-start(bf16[3,64,768]{2,1,0:T(8,128)(2,1)S(1)} %activate.1.act), channel_id=1, source_target_pairs={{0,1},{1,0},{2,3},{3,2},{4,5},{5,4},{6,7},{7,6},{8,9},{9,8},{10,11... | collective-permute-start | bytes 884744 | tf_op jit(solution)/shard_map/ppermute | solution.py:31
  64.3 10.8 %collective-permute-start.11 = (bf16[3,64,768]{2,1,0:T(8,128)(2,1)S(1)}, bf16[3,64,768]{2,1,0:T(8,128)(2,1)S(1)}, u32[]{:S(2)}, u32[]{:S(2)}) collective-permute-start(bf16[3,64,768]{2,1,0:T(8,128)(2,1)S(1)} %collective-permute-done.10.act), channel_id=1, source_target_pairs={{0,1},{1,0},{2,3},{3,2},{4,5},{5,4},{6,7},{7,6},{8,9},{9,8},{10,11... | collective-permute-start | bytes 884744 | tf_op jit(solution)/shard_map/ppermute | solution.py:31
  77.7 2.0 %collective-permute-start.13 = (f32[2,32,2048]{2,1,0:T(8,128)S(1)}, f32[2,32,2048]{2,1,0:T(8,128)S(1)}, u32[]{:S(2)}, u32[]{:S(2)}) collective-permute-start(f32[2,32,2048]{2,1,0:T(8,128)S(1)} %get-tuple-element.88), channel_id=1, source_target_pairs={{0,4},{4,0},{8,12},{12,8},{16,20},{20,16},{24,28},{28,24},{1,5},{5... | collective-permute-start | bytes 1572872 | tf_op jit(solution)/shard_map/ppermute | solution.py:31
  79.7 7.6 %collective-permute-start.14 = (bf16[2,8,2048]{2,1,0:T(8,128)(2,1)S(1)}, bf16[2,8,2048]{2,1,0:T(8,128)(2,1)S(1)}, u32[]{:S(2)}, u32[]{:S(2)}) collective-permute-start(bf16[2,8,2048]{2,1,0:T(8,128)(2,1)S(1)} %get-tuple-element.90), channel_id=1, source_target_pairs={{0,8},{4,12},{8,0},{12,4},{16,24},{20,28},{24,16},{28,20},{1,9},{5... | collective-permute-start | bytes 196616 | tf_op jit(solution)/shard_map/ppermute | solution.py:31
  81.2 6.2 %collective-permute-start.15 = (bf16[2,8,2048]{2,1,0:T(8,128)(2,1)S(1)}, bf16[2,8,2048]{2,1,0:T(8,128)(2,1)S(1)}, u32[]{:S(2)}, u32[]{:S(2)}) collective-permute-start(bf16[2,8,2048]{2,1,0:T(8,128)(2,1)S(1)} %get-tuple-element.91), channel_id=1, source_target_pairs={{0,16},{4,20},{8,24},{12,28},{16,0},{20,4},{24,8},{28,12},{1,17},{... | collective-permute-start | bytes 196616 | tf_op jit(solution)/shard_map/ppermute | solution.py:31
  82.7 5.2 %collective-permute-start.16 = (bf16[2,8,2048]{2,1,0:T(8,128)(2,1)S(1)}, bf16[2,8,2048]{2,1,0:T(8,128)(2,1)S(1)}, u32[]{:S(2)}, u32[]{:S(2)}) collective-permute-start(bf16[2,8,2048]{2,1,0:T(8,128)(2,1)S(1)} %get-tuple-element.92), channel_id=1, source_target_pairs={{0,24},{4,28},{8,16},{12,20},{16,8},{20,12},{24,0},{28,4},{1,25},{... | collective-permute-start | bytes 196616 | tf_op jit(solution)/shard_map/ppermute | solution.py:31

commit v7 on v5

--- a/solution.py
+++ b/solution.py
@@ -141,12 +141,12 @@
     out[2] = back[...].astype(out.dtype)
 
 
-def partial_sums(k, tok, grad, weights, units, dtype):
+def partial_sums(k, tok, grad, weights, units, dtype, after=()):
     total, width = tok.shape
     shapes = [(width, units), (width, units), (units, width)]
     return pl.pallas_call(
         functools.partial(sums_kernel, k),
-        in_specs=[WHOLE, WHOLE] + [HOLD] * 3,
+        in_specs=[WHOLE, WHOLE] + [HOLD] * (3 + len(after)),
         out_specs=[WHOLE] * 4,
         scratch_shapes=[pltpu.SemaphoreType.DMA((CHUNKS, 3))]
         + [pltpu.VMEM((total, units), F32)] * 3,
@@ -154,17 +154,18 @@
         compiler_params=PARAMS,
         cost_estimate=estimate(6 * total * width * units, 6 * width * units),
         name="partial_sums",
-    )(tok, grad, *in_hbm(weights))
-
-
-def combine_kernel(own, other, out):
+    )(tok, grad, *in_hbm(weights), *after)
+
+
+def combine_kernel(own, other, out, token):
+    token[...] = jnp.zeros_like(token)
     out[...] = (own[...] + other[...].astype(F32)).astype(BF16)
 
 
 def combine(own, other):
     return pl.pallas_call(
         combine_kernel,
-        out_shape=array(own.shape, BF16),
+        out_shape=[array(own.shape, BF16), array((8, 128), F32)],
         compiler_params=PARAMS,
         cost_estimate=estimate(own.size, 8 * own.size),
         name="combine",
@@ -342,15 +343,18 @@
     there, *last_weights = sums(3, dtype=BF16)
     near = along_col(there, k=1)
     here, *far_weights = sums(2, dtype=F32)
-    from_far = along_col(combine(here, near), k=2)
-    there, *near_weights = sums(1, dtype=BF16)
+    pair, token = combine(here, near)
+    from_far = along_col(pair, k=2)
+    there, *near_weights = sums(1, dtype=BF16, after=(token,))
     from_near = along_col(there, k=1)
     here, *own_weights = sums(0, dtype=F32)
     own = activate(here, [from_near, from_far])
 
     near_act = along_col(own, k=1)
-    far_act = along_col(own, k=2)
-    terms, *grads = use(0, own, own_weights, sides=sides)
+    (terms,) = use(0, own, own_weights)
+    held, _ = lax.optimization_barrier((own, terms))
+    far_act = along_col(held, k=2)
+    grads = use(0, held, sides=sides)
     terms, *grads = use(1, near_act, near_weights, terms, sides=sides, grads=grads)
     held, _ = lax.optimization_barrier((far_act, (terms, grads)))
     last_act = along_col(held, k=1)

time: 82.8 us -> 84.6 us (1.022)
  Pallas kernels: 43.1 us -> 44.3 us
    pallas_call x5 -> x6, Pallas kernels: 22.6 us -> 23.7 us  [use(): pl.pallas_call(functools.partial(use_kernel, k, first, last, weights is n...]
  transfers between devices with their start and end apart: 17 -> 17, of which waited for: 9 -> 12; matrix products, arithmetic and copies ran while one was open for 0% -> 0% of each run, Pallas kernels for 41% -> 42%
where the time goes in v7:
time: 84.6 us; the launch traced here: 84.4 us
  Pallas kernels  44.3 us (52%)
  waiting for transfers between devices  22.1 us (26%)
  starting transfers between devices  17.3 us (20%)
    pallas_call x6, Pallas kernels, use(): pl.pallas_call(functools.partial(use_kernel, k, first, last, weights is n...  23.7 us
    ppermute x17, waiting for transfers between devices, swap(): return lax.ppermute(x, axis, [(i, i ^ k) for i in range(size)])  22.1 us
    pallas_call x4, Pallas kernels, partial_sums(): pl.pallas_call(functools.partial(sums_kernel, k), in_specs=[WHOLE, WHOLE]...  18.6 us
    ppermute x17, starting transfers between devices, swap(): return lax.ppermute(x, axis, [(i, i ^ k) for i in range(size)])  17.3 us
  transfers between devices with their start and end apart: 17, of which 12 were waited for; matrix products, arithmetic and copies ran while one was open for 0% of the time, Pallas kernels for 42%

profile of v7, /device:TPU:0, one launch (start us, length us, event | category | flops | bytes accessed | tf_op | source)
XLA Modules:
  0.0 84.4 jit_solution(5591340784692091349)
XLA Ops:
  0.6 0.8 pack.1.refs_0_
  1.4 3.9 %collective-permute-start.2 = (bf16[16,2048]{1,0:T(8,128)(2,1)S(1)}, bf16[16,2048]{1,0:T(8,128)(2,1)S(1)}, u32[]{:S(2)}, u32[]{:S(2)}) collective-permute-start(bf16[16,2048]{1,0:T(8,128)(2,1)S(1)} %pack.1.refs_0_), channel_id=1, source_target_pairs={{0,24},{4,28},{8,16},{12,20},{16,8},{20,12},{24,0},{28,4},{1,25},{... | collective-permute-start | bytes 196616 | tf_op jit(solution)/shard_map/ppermute | solution.py:31
  5.3 0.5 collective-permute-start.1
  5.8 0.1 collective-permute-start
  5.9 0.0 collective-permute-start.3
  5.9 1.6 %collective-permute-done.2.refs_3_ = bf16[16,2048]{1,0:T(8,128)(2,1)S(1)} collective-permute-done((bf16[16,2048]{1,0:T(8,128)(2,1)S(1)}, bf16[16,2048]{1,0:T(8,128)(2,1)S(1)}, u32[]{:S(2)}, u32[]{:S(2)}) %collective-permute-start.2) | collective-permute-done | bytes 65568 | tf_op jit(solution)/shard_map/ppermute | solution.py:31
  7.6 0.0 collective-permute-start.6
  7.6 2.0 %collective-permute-done.1.refs_2_ = bf16[16,2048]{1,0:T(8,128)(2,1)S(1)} collective-permute-done((bf16[16,2048]{1,0:T(8,128)(2,1)S(1)}, bf16[16,2048]{1,0:T(8,128)(2,1)S(1)}, u32[]{:S(2)}, u32[]{:S(2)}) %collective-permute-start.1) | collective-permute-done | bytes 65568 | tf_op jit(solution)/shard_map/ppermute | solution.py:31
  9.6 0.0 collective-permute-start.5
  9.6 0.5 collective-permute-done.refs_1_
  10.1 0.0 collective-permute-start.4
  10.1 0.0 collective-permute-done.3.refs_4_
  10.1 0.7 collective-permute-done.5.refs_6_
  10.8 0.5 collective-permute-done.4.refs_5_
  11.3 0.2 assemble.1
  11.6 4.6 %partial_sums.6 = (bf16[3,64,768]{2,1,0:T(8,128)(2,1)S(1)}, bf16[2048,768]{1,0:T(8,128)(2,1)S(1)}, bf16[2048,768]{1,0:T(8,128)(2,1)S(1)}, bf16[768,2048]{1,0:T(8,128)(2,1)S(1)}) custom-call(bf16[64,2048]{1,0:T(8,128)(2,1)S(1)} %get-tuple-element.50.tok, bf16[64,2048]{1,0:T(8,128)(2,1)S(1)} %get-tuple-element.51.grad.refs_1_.refs_5_, ...), custom_call_target="tpu_custom_call" | custom-call | flops 75497472 | bytes 1179648 | tf_op jit(solution)/shard_map/partial_sums/pallas_call | solution.py:147
  16.2 1.6 %collective-permute-start.7 = (bf16[3,64,768]{2,1,0:T(8,128)(2,1)S(1)}, bf16[3,64,768]{2,1,0:T(8,128)(2,1)S(1)}, u32[]{:S(2)}, u32[]{:S(2)}) collective-permute-start(bf16[3,64,768]{2,1,0:T(8,128)(2,1)S(1)} %get-tuple-element.54), channel_id=1, source_target_pairs={{0,1},{1,0},{2,3},{3,2},{4,5},{5,4},{6,7},{7,6},{8,9},{9,8},{10,11... | collective-permute-start | bytes 884744 | tf_op jit(solution)/shard_map/ppermute | solution.py:31
  17.8 4.6 %partial_sums.5 = (f32[3,64,768]{2,1,0:T(8,128)S(1)}, bf16[2048,768]{1,0:T(8,128)(2,1)S(1)}, bf16[2048,768]{1,0:T(8,128)(2,1)S(1)}, bf16[768,2048]{1,0:T(8,128)(2,1)S(1)}) custom-call(bf16[64,2048]{1,0:T(8,128)(2,1)S(1)} %get-tuple-element.50.tok, bf16[64,2048]{1,0:T(8,128)(2,1)S(1)} %get-tuple-element.51.grad.refs_1_.refs_5_, bf16[2048,3072]{1,0:T(8,128)(2,1)} %gate_w.7, ...), custom_call_target="tpu_custom_call" | custom-call | flops 75497472 | bytes 1179648 | tf_op jit(solution)/shard_map/partial_sums/pallas_call | solution.py:147
  22.5 2.9 %collective-permute-done.7.other = bf16[3,64,768]{2,1,0:T(8,128)(2,1)S(1)} collective-permute-done((bf16[3,64,768]{2,1,0:T(8,128)(2,1)S(1)}, bf16[3,64,768]{2,1,0:T(8,128)(2,1)S(1)}, u32[]{:S(2)}, u32[]{:S(2)}) %collective-permute-start.7) | collective-permute-done | bytes 294944 | tf_op jit(solution)/shard_map/ppermute | solution.py:31
  25.3 0.1 combine.1
  25.4 2.6 %collective-permute-start.9 = (bf16[3,64,768]{2,1,0:T(8,128)(2,1)S(1)}, bf16[3,64,768]{2,1,0:T(8,128)(2,1)S(1)}, u32[]{:S(2)}, u32[]{:S(2)}) collective-permute-start(bf16[3,64,768]{2,1,0:T(8,128)(2,1)S(1)} %get-tuple-element.57), channel_id=1, source_target_pairs={{0,2},{1,3},{2,0},{3,1},{4,6},{5,7},{6,4},{7,5},{8,10},{9,11},{10,... | collective-permute-start | bytes 884744 | tf_op jit(solution)/shard_map/ppermute | solution.py:31
  28.1 4.6 %partial_sums.7 = (bf16[3,64,768]{2,1,0:T(8,128)(2,1)S(1)}, bf16[2048,768]{1,0:T(8,128)(2,1)S(1)}, bf16[2048,768]{1,0:T(8,128)(2,1)S(1)}, bf16[768,2048]{1,0:T(8,128)(2,1)S(1)}) custom-call(bf16[64,2048]{1,0:T(8,128)(2,1)S(1)} %get-tuple-element.50.tok, bf16[64,2048]{1,0:T(8,128)(2,1)S(1)} %get-tuple-element.51.grad.refs_1_.refs_5_, ...), custom_call_target="tpu_custom_call" | custom-call | flops 75497472 | bytes 1179648 | tf_op jit(solution)/shard_map/partial_sums/pallas_call | solution.py:147
  32.7 1.7 %collective-permute-start.8 = (bf16[3,64,768]{2,1,0:T(8,128)(2,1)S(1)}, bf16[3,64,768]{2,1,0:T(8,128)(2,1)S(1)}, u32[]{:S(2)}, u32[]{:S(2)}) collective-permute-start(bf16[3,64,768]{2,1,0:T(8,128)(2,1)S(1)} %get-tuple-element.56), channel_id=1, source_target_pairs={{0,1},{1,0},{2,3},{3,2},{4,5},{5,4},{6,7},{7,6},{8,9},{9,8},{10,11... | collective-permute-start | bytes 884744 | tf_op jit(solution)/shard_map/ppermute | solution.py:31
  34.4 4.7 %partial_sums.4 = (f32[3,64,768]{2,1,0:T(8,128)S(1)}, bf16[2048,768]{1,0:T(8,128)(2,1)S(1)}, bf16[2048,768]{1,0:T(8,128)(2,1)S(1)}, bf16[768,2048]{1,0:T(8,128)(2,1)S(1)}) custom-call(bf16[64,2048]{1,0:T(8,128)(2,1)S(1)} %get-tuple-element.50.tok, bf16[64,2048]{1,0:T(8,128)(2,1)S(1)} %get-tuple-element.51.grad.refs_1_.refs_5_, bf16[2048,3072]{1,0:T(8,128)(2,1)} %gate_w.7, ...), custom_call_target="tpu_custom_call" | custom-call | flops 75497472 | bytes 1179648 | tf_op jit(solution)/shard_map/partial_sums/pallas_call | solution.py:147
  39.1 1.9 %collective-permute-done.9.refs_1_ = bf16[3,64,768]{2,1,0:T(8,128)(2,1)S(1)} collective-permute-done((bf16[3,64,768]{2,1,0:T(8,128)(2,1)S(1)}, bf16[3,64,768]{2,1,0:T(8,128)(2,1)S(1)}, u32[]{:S(2)}, u32[]{:S(2)}) %collective-permute-start.9) | collective-permute-done | bytes 294944 | tf_op jit(solution)/shard_map/ppermute | solution.py:31
  41.0 4.9 %collective-permute-done.8.refs_0_ = bf16[3,64,768]{2,1,0:T(8,128)(2,1)S(1)} collective-permute-done((bf16[3,64,768]{2,1,0:T(8,128)(2,1)S(1)}, bf16[3,64,768]{2,1,0:T(8,128)(2,1)S(1)}, u32[]{:S(2)}, u32[]{:S(2)}) %collective-permute-start.8) | collective-permute-done | bytes 294944 | tf_op jit(solution)/shard_map/ppermute | solution.py:31
  45.9 0.2 activate.1.act
  46.1 0.1 collective-permute-start.11
  46.2 2.5 %products.2.refs_3_ = f32[2,64,2048]{2,1,0:T(8,128)S(1)} custom-call(bf16[3,64,768]{2,1,0:T(8,128)(2,1)S(1)} %activate.1.act, bf16[2048,768]{1,0:T(8,128)(2,1)S(1)} %get-tuple-element.58.refs_0_, bf16[2048,768]{1,0:T(8,128)(2,1)S(1)} %get-tuple-element.59.refs_1_, bf16[768,2048]{1,0:T(8,128)(2,1)S(1)} %get-tuple-element.60.refs_2_), custom_call_target="tpu_custom_call" | custom-call | flops 75497472 | bytes 1179648 | tf_op jit(solution)/shard_map/products/pallas_call | solution.py:279
  48.7 3.0 %collective-permute-start.10 = (bf16[3,64,768]{2,1,0:T(8,128)(2,1)S(1)}, bf16[3,64,768]{2,1,0:T(8,128)(2,1)S(1)}, u32[]{:S(2)}, u32[]{:S(2)}) collective-permute-start(bf16[3,64,768]{2,1,0:T(8,128)(2,1)S(1)} %activate.1.act), channel_id=1, source_target_pairs={{0,2},{1,3},{2,0},{3,1},{4,6},{5,7},{6,4},{7,5},{8,10},{9,11},{10,... | collective-permute-start | bytes 884744 | tf_op jit(solution)/shard_map/ppermute | solution.py:31
  51.7 4.1 %grads.2 = (bf16[2048,3072]{1,0:T(8,128)(2,1)}, bf16[2048,3072]{1,0:T(8,128)(2,1)}, bf16[3072,2048]{1,0:T(8,128)(2,1)}) custom-call(bf16[3,64,768]{2,1,0:T(8,128)(2,1)S(1)} %activate.1.act, bf16[2048,64]{1,0:T(8,128)(2,1)S(1)} %get-tuple-element.65.refs_0_.refs_4_, bf16[64,2048]{1,0:T(8,128)(2,1)S(1)} %get-tuple-element.51.grad.refs_1_.refs_5_), custom_call_target="tpu_custom_call" | custom-call | flops 75497472 | bytes 1179648 | tf_op jit(solution)/shard_map/grads/pallas_call | solution.py:279
  55.8 0.9 %collective-permute-done.11.act = bf16[3,64,768]{2,1,0:T(8,128)(2,1)S(1)} collective-permute-done((bf16[3,64,768]{2,1,0:T(8,128)(2,1)S(1)}, bf16[3,64,768]{2,1,0:T(8,128)(2,1)S(1)}, u32[]{:S(2)}, u32[]{:S(2)}) %collective-permute-start.11) | collective-permute-done | bytes 294944 | tf_op jit(solution)/shard_map/ppermute | solution.py:31
  56.7 5.3 %productsgrads.2 = (f32[2,64,2048]{2,1,0:T(8,128)S(1)}, bf16[2048,3072]{1,0:T(8,128)(2,1)}, bf16[2048,3072]{1,0:T(8,128)(2,1)}, bf16[3072,2048]{1,0:T(8,128)(2,1)}) custom-call(bf16[3,64,768]{2,1,0:T(8,128)(2,1)S(1)} %collective-permute-done.11.act, ...), custom_call_target="tpu_custom_call", output_to_operand_aliasing={{1}: (7, {}), {2}: (8, {}), {3}: (9, {})} | custom-call | flops 150994944 | bytes 2359296 | tf_op jit(solution)/shard_map/productsgrads/pallas_call | solution.py:279
  62.0 2.1 %collective-permute-done.10.act = bf16[3,64,768]{2,1,0:T(8,128)(2,1)S(1)} collective-permute-done((bf16[3,64,768]{2,1,0:T(8,128)(2,1)S(1)}, bf16[3,64,768]{2,1,0:T(8,128)(2,1)S(1)}, u32[]{:S(2)}, u32[]{:S(2)}) %collective-permute-start.10) | collective-permute-done | bytes 294944 | tf_op jit(solution)/shard_map/ppermute | solution.py:31
  64.1 0.0 collective-permute-start.12
  64.1 5.3 %productsgrads.3 = (f32[2,64,2048]{2,1,0:T(8,128)S(1)}, bf16[2048,3072]{1,0:T(8,128)(2,1)}, bf16[2048,3072]{1,0:T(8,128)(2,1)}, bf16[3072,2048]{1,0:T(8,128)(2,1)}) custom-call(bf16[3,64,768]{2,1,0:T(8,128)(2,1)S(1)} %collective-permute-done.10.act, ...), custom_call_target="tpu_custom_call", output_to_operand_aliasing={{1}: (7, {}), {2}: (8, {}), {3}: (9, {})} | custom-call | flops 150994944 | bytes 2359296 | tf_op jit(solution)/shard_map/productsgrads/pallas_call | solution.py:279
  69.3 2.2 %collective-permute-done.12.act = bf16[3,64,768]{2,1,0:T(8,128)(2,1)S(1)} collective-permute-done((bf16[3,64,768]{2,1,0:T(8,128)(2,1)S(1)}, bf16[3,64,768]{2,1,0:T(8,128)(2,1)S(1)}, u32[]{:S(2)}, u32[]{:S(2)}) %collective-permute-start.12) | collective-permute-done | bytes 294944 | tf_op jit(solution)/shard_map/ppermute | solution.py:31
  71.5 2.5 %products.3 = (f32[2,32,2048]{2,1,0:T(8,128)S(1)}, f32[2,32,2048]{2,1,0:T(8,128)S(1)}) custom-call(bf16[3,64,768]{2,1,0:T(8,128)(2,1)S(1)} %collective-permute-done.12.act, bf16[2048,768]{1,0:T(8,128)(2,1)S(1)} %get-tuple-element.74.refs_0_, bf16[2048,768]{1,0:T(8,128)(2,1)S(1)} %get-tuple-element.75.refs_1_, ...), custom_call_target="tpu_custom_call" | custom-call | flops 75497472 | bytes 1179648 | tf_op jit(solution)/shard_map/products/pallas_call | solution.py:279
  74.0 0.1 collective-permute-start.13
  74.1 1.9 %collective-permute-done.13.other = f32[2,32,2048]{2,1,0:T(8,128)S(1)} collective-permute-done((f32[2,32,2048]{2,1,0:T(8,128)S(1)}, f32[2,32,2048]{2,1,0:T(8,128)S(1)}, u32[]{:S(2)}, u32[]{:S(2)}) %collective-permute-start.13) | collective-permute-done | bytes 524320 | tf_op jit(solution)/shard_map/ppermute | solution.py:31
  76.0 0.1 fold.1
  76.1 1.2 %collective-permute-start.14 = (bf16[2,8,2048]{2,1,0:T(8,128)(2,1)S(1)}, bf16[2,8,2048]{2,1,0:T(8,128)(2,1)S(1)}, u32[]{:S(2)}, u32[]{:S(2)}) collective-permute-start(bf16[2,8,2048]{2,1,0:T(8,128)(2,1)S(1)} %get-tuple-element.84), channel_id=1, source_target_pairs={{0,8},{4,12},{8,0},{12,4},{16,24},{20,28},{24,16},{28,20},{1,9},{5... | collective-permute-start | bytes 196616 | tf_op jit(solution)/shard_map/ppermute | solution.py:31
  77.2 0.9 %collective-permute-start.15 = (bf16[2,8,2048]{2,1,0:T(8,128)(2,1)S(1)}, bf16[2,8,2048]{2,1,0:T(8,128)(2,1)S(1)}, u32[]{:S(2)}, u32[]{:S(2)}) collective-permute-start(bf16[2,8,2048]{2,1,0:T(8,128)(2,1)S(1)} %get-tuple-element.85), channel_id=1, source_target_pairs={{0,16},{4,20},{8,24},{12,28},{16,0},{20,4},{24,8},{28,12},{1,17},{... | collective-permute-start | bytes 196616 | tf_op jit(solution)/shard_map/ppermute | solution.py:31
  78.1 1.5 %collective-permute-start.16 = (bf16[2,8,2048]{2,1,0:T(8,128)(2,1)S(1)}, bf16[2,8,2048]{2,1,0:T(8,128)(2,1)S(1)}, u32[]{:S(2)}, u32[]{:S(2)}) collective-permute-start(bf16[2,8,2048]{2,1,0:T(8,128)(2,1)S(1)} %get-tuple-element.86), channel_id=1, source_target_pairs={{0,24},{4,28},{8,16},{12,20},{16,8},{20,12},{24,0},{28,4},{1,25},{... | collective-permute-start | bytes 196616 | tf_op jit(solution)/shard_map/ppermute | solution.py:31
  79.6 4.1 %grads.3 = (bf16[2048,3072]{1,0:T(8,128)(2,1)}, bf16[2048,3072]{1,0:T(8,128)(2,1)}, bf16[3072,2048]{1,0:T(8,128)(2,1)}) custom-call(bf16[3,64,768]{2,1,0:T(8,128)(2,1)S(1)} %collective-permute-done.12.act, bf16[2048,64]{1,0:T(8,128)(2,1)S(1)} %get-tuple-element.65.refs_0_.refs_4_, ...), custom_call_target="tpu_custom_call", output_to_operand_aliasing={{0}: (3, {}), {1}: (4, {}), {2}: (5, {})} | custom-call | flops 75497472 | bytes 1179648 | tf_op jit(solution)/shard_map/grads/pallas_call | solution.py:279
  83.7 0.0 collective-permute-done.15.refs_1_
  83.7 0.0 collective-permute-done.16.refs_2_
  83.7 0.6 finish.1
  (2 shorter events, 0.0 us)
Async XLA Ops:
  1.4 6.1 %collective-permute-start.2 = (bf16[16,2048]{1,0:T(8,128)(2,1)S(1)}, bf16[16,2048]{1,0:T(8,128)(2,1)S(1)}, u32[]{:S(2)}, u32[]{:S(2)}) collective-permute-start(bf16[16,2048]{1,0:T(8,128)(2,1)S(1)} %pack.1.refs_0_), channel_id=1, source_target_pairs={{0,24},{4,28},{8,16},{12,20},{16,8},{20,12},{24,0},{28,4},{1,25},{... | collective-permute-start | bytes 196616 | tf_op jit(solution)/shard_map/ppermute | solution.py:31
  5.3 4.3 %collective-permute-start.1 = (bf16[16,2048]{1,0:T(8,128)(2,1)S(1)}, bf16[16,2048]{1,0:T(8,128)(2,1)S(1)}, u32[]{:S(2)}, u32[]{:S(2)}) collective-permute-start(bf16[16,2048]{1,0:T(8,128)(2,1)S(1)} %pack.1.refs_0_), channel_id=1, source_target_pairs={{0,16},{4,20},{8,24},{12,28},{16,0},{20,4},{24,8},{28,12},{1,17},{... | collective-permute-start | bytes 196616 | tf_op jit(solution)/shard_map/ppermute | solution.py:31
  5.8 4.3 %collective-permute-start = (bf16[16,2048]{1,0:T(8,128)(2,1)S(1)}, bf16[16,2048]{1,0:T(8,128)(2,1)S(1)}, u32[]{:S(2)}, u32[]{:S(2)}) collective-permute-start(bf16[16,2048]{1,0:T(8,128)(2,1)S(1)} %pack.1.refs_0_), channel_id=1, source_target_pairs={{0,8},{4,12},{8,0},{12,4},{16,24},{20,28},{24,16},{28,20},{1,9},{5... | collective-permute-start | bytes 196616 | tf_op jit(solution)/shard_map/ppermute | solution.py:31
  5.9 4.2 %collective-permute-start.3 = (bf16[16,2048]{1,0:T(8,128)(2,1)S(1)}, bf16[16,2048]{1,0:T(8,128)(2,1)S(1)}, u32[]{:S(2)}, u32[]{:S(2)}) collective-permute-start(bf16[16,2048]{1,0:T(8,128)(2,1)S(1)} %pack.1.refs_0_), channel_id=1, source_target_pairs={{0,4},{4,0},{8,12},{12,8},{16,20},{20,16},{24,28},{28,24},{1,5},{5... | collective-permute-start | bytes 196616 | tf_op jit(solution)/shard_map/ppermute | solution.py:31
  7.6 2.5 %collective-permute-start.6 = (bf16[16,2048]{1,0:T(8,128)(2,1)S(1)}, bf16[16,2048]{1,0:T(8,128)(2,1)S(1)}, u32[]{:S(2)}, u32[]{:S(2)}) collective-permute-start(bf16[16,2048]{1,0:T(8,128)(2,1)S(1)} %collective-permute-done.2.refs_3_), channel_id=1, source_target_pairs={{0,4},{4,0},{8,12},{12,8},{16,20},{20,16},{24,28},{28,24},{1,5},{5... | collective-permute-start | bytes 196616 | tf_op jit(solution)/shard_map/ppermute | solution.py:31
  9.6 1.3 %collective-permute-start.5 = (bf16[16,2048]{1,0:T(8,128)(2,1)S(1)}, bf16[16,2048]{1,0:T(8,128)(2,1)S(1)}, u32[]{:S(2)}, u32[]{:S(2)}) collective-permute-start(bf16[16,2048]{1,0:T(8,128)(2,1)S(1)} %collective-permute-done.1.refs_2_), channel_id=1, source_target_pairs={{0,4},{4,0},{8,12},{12,8},{16,20},{20,16},{24,28},{28,24},{1,5},{5... | collective-permute-start | bytes 196616 | tf_op jit(solution)/shard_map/ppermute | solution.py:31
  10.1 1.3 %collective-permute-start.4 = (bf16[16,2048]{1,0:T(8,128)(2,1)S(1)}, bf16[16,2048]{1,0:T(8,128)(2,1)S(1)}, u32[]{:S(2)}, u32[]{:S(2)}) collective-permute-start(bf16[16,2048]{1,0:T(8,128)(2,1)S(1)} %collective-permute-done.refs_1_), channel_id=1, source_target_pairs={{0,4},{4,0},{8,12},{12,8},{16,20},{20,16},{24,28},{28,24},{1,5},{5... | collective-permute-start | bytes 196616 | tf_op jit(solution)/shard_map/ppermute | solution.py:31
  16.2 9.1 %collective-permute-start.7 = (bf16[3,64,768]{2,1,0:T(8,128)(2,1)S(1)}, bf16[3,64,768]{2,1,0:T(8,128)(2,1)S(1)}, u32[]{:S(2)}, u32[]{:S(2)}) collective-permute-start(bf16[3,64,768]{2,1,0:T(8,128)(2,1)S(1)} %get-tuple-element.54), channel_id=1, source_target_pairs={{0,1},{1,0},{2,3},{3,2},{4,5},{5,4},{6,7},{7,6},{8,9},{9,8},{10,11... | collective-permute-start | bytes 884744 | tf_op jit(solution)/shard_map/ppermute | solution.py:31
  25.4 15.6 %collective-permute-start.9 = (bf16[3,64,768]{2,1,0:T(8,128)(2,1)S(1)}, bf16[3,64,768]{2,1,0:T(8,128)(2,1)S(1)}, u32[]{:S(2)}, u32[]{:S(2)}) collective-permute-start(bf16[3,64,768]{2,1,0:T(8,128)(2,1)S(1)} %get-tuple-element.57), channel_id=1, source_target_pairs={{0,2},{1,3},{2,0},{3,1},{4,6},{5,7},{6,4},{7,5},{8,10},{9,11},{10,... | collective-permute-start | bytes 884744 | tf_op jit(solution)/shard_map/ppermute | solution.py:31
  32.7 13.2 %collective-permute-start.8 = (bf16[3,64,768]{2,1,0:T(8,128)(2,1)S(1)}, bf16[3,64,768]{2,1,0:T(8,128)(2,1)S(1)}, u32[]{:S(2)}, u32[]{:S(2)}) collective-permute-start(bf16[3,64,768]{2,1,0:T(8,128)(2,1)S(1)} %get-tuple-element.56), channel_id=1, source_target_pairs={{0,1},{1,0},{2,3},{3,2},{4,5},{5,4},{6,7},{7,6},{8,9},{9,8},{10,11... | collective-permute-start | bytes 884744 | tf_op jit(solution)/shard_map/ppermute | solution.py:31
  46.1 10.6 %collective-permute-start.11 = (bf16[3,64,768]{2,1,0:T(8,128)(2,1)S(1)}, bf16[3,64,768]{2,1,0:T(8,128)(2,1)S(1)}, u32[]{:S(2)}, u32[]{:S(2)}) collective-permute-start(bf16[3,64,768]{2,1,0:T(8,128)(2,1)S(1)} %activate.1.act), channel_id=1, source_target_pairs={{0,1},{1,0},{2,3},{3,2},{4,5},{5,4},{6,7},{7,6},{8,9},{9,8},{10,11... | collective-permute-start | bytes 884744 | tf_op jit(solution)/shard_map/ppermute | solution.py:31
  48.7 15.3 %collective-permute-start.10 = (bf16[3,64,768]{2,1,0:T(8,128)(2,1)S(1)}, bf16[3,64,768]{2,1,0:T(8,128)(2,1)S(1)}, u32[]{:S(2)}, u32[]{:S(2)}) collective-permute-start(bf16[3,64,768]{2,1,0:T(8,128)(2,1)S(1)} %activate.1.act), channel_id=1, source_target_pairs={{0,2},{1,3},{2,0},{3,1},{4,6},{5,7},{6,4},{7,5},{8,10},{9,11},{10,... | collective-permute-start | bytes 884744 | tf_op jit(solution)/shard_map/ppermute | solution.py:31
  64.1 7.4 %collective-permute-start.12 = (bf16[3,64,768]{2,1,0:T(8,128)(2,1)S(1)}, bf16[3,64,768]{2,1,0:T(8,128)(2,1)S(1)}, u32[]{:S(2)}, u32[]{:S(2)}) collective-permute-start(bf16[3,64,768]{2,1,0:T(8,128)(2,1)S(1)} %collective-permute-done.10.act), channel_id=1, source_target_pairs={{0,1},{1,0},{2,3},{3,2},{4,5},{5,4},{6,7},{7,6},{8,9},{9,8},{10,11... | collective-permute-start | bytes 884744 | tf_op jit(solution)/shard_map/ppermute | solution.py:31
  74.0 2.0 %collective-permute-start.13 = (f32[2,32,2048]{2,1,0:T(8,128)S(1)}, f32[2,32,2048]{2,1,0:T(8,128)S(1)}, u32[]{:S(2)}, u32[]{:S(2)}) collective-permute-start(f32[2,32,2048]{2,1,0:T(8,128)S(1)} %get-tuple-element.82), channel_id=1, source_target_pairs={{0,4},{4,0},{8,12},{12,8},{16,20},{20,16},{24,28},{28,24},{1,5},{5... | collective-permute-start | bytes 1572872 | tf_op jit(solution)/shard_map/ppermute | solution.py:31
  76.1 7.6 %collective-permute-start.14 = (bf16[2,8,2048]{2,1,0:T(8,128)(2,1)S(1)}, bf16[2,8,2048]{2,1,0:T(8,128)(2,1)S(1)}, u32[]{:S(2)}, u32[]{:S(2)}) collective-permute-start(bf16[2,8,2048]{2,1,0:T(8,128)(2,1)S(1)} %get-tuple-element.84), channel_id=1, source_target_pairs={{0,8},{4,12},{8,0},{12,4},{16,24},{20,28},{24,16},{28,20},{1,9},{5... | collective-permute-start | bytes 196616 | tf_op jit(solution)/shard_map/ppermute | solution.py:31
  77.2 6.5 %collective-permute-start.15 = (bf16[2,8,2048]{2,1,0:T(8,128)(2,1)S(1)}, bf16[2,8,2048]{2,1,0:T(8,128)(2,1)S(1)}, u32[]{:S(2)}, u32[]{:S(2)}) collective-permute-start(bf16[2,8,2048]{2,1,0:T(8,128)(2,1)S(1)} %get-tuple-element.85), channel_id=1, source_target_pairs={{0,16},{4,20},{8,24},{12,28},{16,0},{20,4},{24,8},{28,12},{1,17},{... | collective-permute-start | bytes 196616 | tf_op jit(solution)/shard_map/ppermute | solution.py:31
  78.1 5.6 %collective-permute-start.16 = (bf16[2,8,2048]{2,1,0:T(8,128)(2,1)S(1)}, bf16[2,8,2048]{2,1,0:T(8,128)(2,1)S(1)}, u32[]{:S(2)}, u32[]{:S(2)}) collective-permute-start(bf16[2,8,2048]{2,1,0:T(8,128)(2,1)S(1)} %get-tuple-element.86), channel_id=1, source_target_pairs={{0,24},{4,28},{8,16},{12,20},{16,8},{20,12},{24,0},{28,4},{1,25},{... | collective-permute-start | bytes 196616 | tf_op jit(solution)/shard_map/ppermute | solution.py:31

commit v8 on v6

--- a/solution.py
+++ b/solution.py
@@ -11,6 +11,7 @@
 F32 = jnp.float32
 VMEM_LIMIT = 14 * 1024 * 1024
 CHUNKS = 8
+FETCHES = 4
 BACK = (((1,), (1,)), ((), ()))
 CONTRACT = (((0,), (0,)), ((), ()))
 PARAMS = pltpu.CompilerParams(vmem_limit_bytes=VMEM_LIMIT)
@@ -101,18 +102,18 @@
 def fetches(k, hbm, vmem, sems):
     units, width = vmem[2].shape
     mine = unit_block(k, units)
-    part = width // CHUNKS
+    start = jnp.bitwise_xor(lax.axis_index("col"), k) * units
+    tall, wide = width // FETCHES, units // FETCHES
     copies = []
-    for i in range(CHUNKS):
-        rows = pl.ds(i * part, part)
-        ends = [
+    for i in range(FETCHES):
+        rows, some = pl.ds(i * tall, tall), pl.ds(i * wide, wide)
+        below = pl.ds(pl.multiple_of(start + i * wide, wide), wide)
+        ends = (
             (hbm[0].at[rows, mine], vmem[0].at[rows]),
             (hbm[1].at[rows, mine], vmem[1].at[rows]),
-            (hbm[2].at[mine, rows], vmem[2].at[:, rows]),
-        ]
-        copies.append(
-            [pltpu.make_async_copy(*ends[j], sems.at[i, j]) for j in range(len(ends))]
+            (hbm[2].at[below], vmem[2].at[some]),
         )
+        copies += [pltpu.make_async_copy(*ends[j], sems.at[i, j]) for j in range(3)]
     return copies
 
 
@@ -121,7 +122,7 @@
 
 
 def load_kernel(k, *refs):
-    copies = sum(fetches(k, refs[:3], refs[3:6], refs[6]), [])
+    copies = fetches(k, refs[:3], refs[3:6], refs[6])
     for copy in copies:
         copy.start()
     for copy in copies:
@@ -134,7 +135,7 @@
         functools.partial(load_kernel, k),
         in_specs=[HOLD] * 3,
         out_specs=[WHOLE] * 3,
-        scratch_shapes=[pltpu.SemaphoreType.DMA((CHUNKS, 3))],
+        scratch_shapes=[pltpu.SemaphoreType.DMA((FETCHES, 3))],
         out_shape=[vmem_array(x) for x in shapes],
         compiler_params=PARAMS,
         cost_estimate=estimate(0, 6 * weights[0].shape[0] * units),
@@ -146,14 +147,18 @@
     copies = []
     if following is not None:
         hbm, out, kept, sems = refs[:3], refs[3], refs[4:7], refs[7]
-        copies = sum(fetches(following, hbm, kept, sems), [])
+        copies = fetches(following, hbm, kept, sems)
     else:
         (out,) = refs
     for copy in copies:
         copy.start()
-    out[0] = dot(tok[...], gate_b[...]).astype(out.dtype)
-    out[1] = dot(tok[...], up_b[...]).astype(out.dtype)
-    out[2] = back_dot(grad[...], down_b[...]).astype(out.dtype)
+
+    @pl.when(lax.axis_index("col") >= 0)
+    def _():
+        out[0] = dot(tok[...], gate_b[...]).astype(out.dtype)
+        out[1] = dot(tok[...], up_b[...]).astype(out.dtype)
+        out[2] = back_dot(grad[...], down_b[...]).astype(out.dtype)
+
     for copy in copies:
         copy.wait()
 
@@ -167,7 +172,7 @@
         functools.partial(sums_kernel, following),
         in_specs=[WHOLE] * 5 + [HOLD] * (3 * more),
         out_specs=[WHOLE] * (1 + 3 * more),
-        scratch_shapes=[pltpu.SemaphoreType.DMA((CHUNKS, 3))] * more,
+        scratch_shapes=[pltpu.SemaphoreType.DMA((FETCHES, 3))] * more,
         out_shape=[array((3, total, units), dtype)] + [vmem_array(x) for x in shapes],
         compiler_params=PARAMS,
         cost_estimate=estimate(6 * total * width * units, 6 * width * units),
@@ -371,9 +376,9 @@
     near_act = along_col(own, k=1)
     far_act = along_col(own, k=2)
     terms, *grads = use(0, own, own_weights, sides=sides)
+    terms, *grads = use(1, near_act, near_weights, terms, sides=sides, grads=grads)
     held, _ = lax.optimization_barrier((far_act, (terms, grads)))
     last_act = along_col(held, k=1)
-    terms, *grads = use(1, near_act, near_weights, terms, sides=sides, grads=grads)
     terms, *grads = use(2, far_act, far_weights, terms, sides=sides, grads=grads)
     kept, given = use(3, last_act, last_weights, terms, last=True)
 

time: 88.7 us -> 82.5 us (0.930)
  Pallas kernels: 48.5 us -> 42.3 us
    pallas_call x4, Pallas kernels: 20 us -> 13.9 us  [partial_sums(): pl.pallas_call(functools.partial(sums_kernel, following), in_specs=[WHOLE...]
  transfers between devices with their start and end apart: 17 -> 17, of which waited for: 9 -> 11; matrix products, arithmetic and copies ran while one was open for 0% -> 0% of each run, Pallas kernels for 43% -> 41%
where the time goes in v8:
time: 82.5 us; the launch traced here: 82.3 us
  Pallas kernels  42.3 us (51%)
  waiting for transfers between devices  20.9 us (25%)
  starting transfers between devices  18.3 us (22%)
    pallas_call x5, Pallas kernels, use(): pl.pallas_call(functools.partial(use_kernel, k, first, last, weights is n...  22.6 us
    ppermute x17, waiting for transfers between devices, swap(): return lax.ppermute(x, axis, [(i, i ^ k) for i in range(size)])  20.9 us
    ppermute x17, starting transfers between devices, swap(): return lax.ppermute(x, axis, [(i, i ^ k) for i in range(size)])  18.3 us
    pallas_call x4, Pallas kernels, partial_sums(): pl.pallas_call(functools.partial(sums_kernel, following), in_specs=[WHOLE...  13.9 us
    pallas_call x1, Pallas kernels, load(): pl.pallas_call(functools.partial(load_kernel, k), in_specs=[HOLD] * 3, ou...  3.82 us
  transfers between devices with their start and end apart: 17, of which 11 were waited for; matrix products, arithmetic and copies ran while one was open for 0% of the time, Pallas kernels for 41%

profile of v8, /device:TPU:0, one launch (start us, length us, event | category | flops | bytes accessed | tf_op | source)
XLA Modules:
  0.0 82.3 jit_solution(7196833874111222287)
XLA Ops:
  0.6 0.8 pack.1.refs_0_
  1.4 3.9 %collective-permute-start.2 = (bf16[16,2048]{1,0:T(8,128)(2,1)S(1)}, bf16[16,2048]{1,0:T(8,128)(2,1)S(1)}, u32[]{:S(2)}, u32[]{:S(2)}) collective-permute-start(bf16[16,2048]{1,0:T(8,128)(2,1)S(1)} %pack.1.refs_0_), channel_id=1, source_target_pairs={{0,24},{4,28},{8,16},{12,20},{16,8},{20,12},{24,0},{28,4},{1,25},{... | collective-permute-start | bytes 196616 | tf_op jit(solution)/shard_map/ppermute | solution.py:32
  5.3 0.5 collective-permute-start.1
  5.8 0.1 collective-permute-start
  5.9 0.0 collective-permute-start.3
  5.9 3.8 %load.1 = (bf16[2048,768]{1,0:T(8,128)(2,1)S(1)}, bf16[2048,768]{1,0:T(8,128)(2,1)S(1)}, bf16[768,2048]{1,0:T(8,128)(2,1)S(1)}) custom-call(bf16[2048,3072]{1,0:T(8,128)(2,1)} %refs_0_.7, bf16[2048,3072]{1,0:T(8,128)(2,1)} %refs_1_.7, bf16[3072,2048]{1,0:T(8,128)(2,1)} %refs_2_.7), custom_call_target="tpu_custom_call" | custom-call | bytes 1179648 | tf_op jit(solution)/shard_map/load/pallas_call | solution.py:134
  9.8 0.0 collective-permute-done.2.refs_3_
  9.8 0.0 collective-permute-done.1.refs_2_
  9.8 0.3 collective-permute-done.refs_1_
  10.1 0.3 collective-permute-start.4
  10.4 0.2 collective-permute-start.5
  10.6 0.3 collective-permute-start.6
  10.9 0.4 collective-permute-done.4.refs_5_
  11.3 0.3 collective-permute-done.5.refs_6_
  11.6 0.2 collective-permute-done.6.refs_7_
  11.8 0.2 assemble.1
  12.1 3.9 %partial_sums.4 = (bf16[3,64,768]{2,1,0:T(8,128)(2,1)S(1)}, bf16[2048,768]{1,0:T(8,128)(2,1)S(1)}, bf16[2048,768]{1,0:T(8,128)(2,1)S(1)}, bf16[768,2048]{1,0:T(8,128)(2,1)S(1)}) custom-call(bf16[64,2048]{1,0:T(8,128)(2,1)S(1)} %get-tuple-element.59.tok, bf16[64,2048]{1,0:T(8,128)(2,1)S(1)} %get-tuple-element.60.grad.refs_4_.refs_5_.refs_1_, ...), custom_call_target="tpu_custom_call" | custom-call | flops 75497472 | bytes 1179648 | tf_op jit(solution)/shard_map/partial_sums/pallas_call | solution.py:171
  16.0 1.9 %collective-permute-start.8 = (bf16[3,64,768]{2,1,0:T(8,128)(2,1)S(1)}, bf16[3,64,768]{2,1,0:T(8,128)(2,1)S(1)}, u32[]{:S(2)}, u32[]{:S(2)}) collective-permute-start(bf16[3,64,768]{2,1,0:T(8,128)(2,1)S(1)} %get-tuple-element.75), channel_id=1, source_target_pairs={{0,1},{1,0},{2,3},{3,2},{4,5},{5,4},{6,7},{7,6},{8,9},{9,8},{10,11... | collective-permute-start | bytes 884744 | tf_op jit(solution)/shard_map/ppermute | solution.py:32
  17.9 3.8 %partial_sums.5 = (bf16[3,64,768]{2,1,0:T(8,128)(2,1)S(1)}, bf16[2048,768]{1,0:T(8,128)(2,1)S(1)}, bf16[2048,768]{1,0:T(8,128)(2,1)S(1)}, bf16[768,2048]{1,0:T(8,128)(2,1)S(1)}) custom-call(bf16[64,2048]{1,0:T(8,128)(2,1)S(1)} %get-tuple-element.59.tok, bf16[64,2048]{1,0:T(8,128)(2,1)S(1)} %get-tuple-element.60.grad.refs_4_.refs_5_.refs_1_, ...), custom_call_target="tpu_custom_call" | custom-call | flops 75497472 | bytes 1179648 | tf_op jit(solution)/shard_map/partial_sums/pallas_call | solution.py:171
  21.8 0.2 collective-permute-start.7
  22.0 3.8 %partial_sums.6 = (f32[3,64,768]{2,1,0:T(8,128)S(1)}, bf16[2048,768]{1,0:T(8,128)(2,1)S(1)}, bf16[2048,768]{1,0:T(8,128)(2,1)S(1)}, bf16[768,2048]{1,0:T(8,128)(2,1)S(1)}) custom-call(bf16[64,2048]{1,0:T(8,128)(2,1)S(1)} %get-tuple-element.59.tok, bf16[64,2048]{1,0:T(8,128)(2,1)S(1)} %get-tuple-element.60.grad.refs_4_.refs_5_.refs_1_, ...), custom_call_target="tpu_custom_call" | custom-call | flops 75497472 | bytes 1179648 | tf_op jit(solution)/shard_map/partial_sums/pallas_call | solution.py:171
  25.8 0.1 collective-permute-done.8.other
  25.9 0.1 combine.1
  25.9 3.1 %collective-permute-start.9 = (bf16[3,64,768]{2,1,0:T(8,128)(2,1)S(1)}, bf16[3,64,768]{2,1,0:T(8,128)(2,1)S(1)}, u32[]{:S(2)}, u32[]{:S(2)}) collective-permute-start(bf16[3,64,768]{2,1,0:T(8,128)(2,1)S(1)} %combine.1), channel_id=1, source_target_pairs={{0,2},{1,3},{2,0},{3,1},{4,6},{5,7},{6,4},{7,5},{8,10},{9,11},{10,... | collective-permute-start | bytes 884744 | tf_op jit(solution)/shard_map/ppermute | solution.py:32
  29.0 2.3 %partial_sums.7.own = f32[3,64,768]{2,1,0:T(8,128)S(1)} custom-call(bf16[64,2048]{1,0:T(8,128)(2,1)S(1)} %get-tuple-element.59.tok, bf16[64,2048]{1,0:T(8,128)(2,1)S(1)} %get-tuple-element.60.grad.refs_4_.refs_5_.refs_1_, bf16[2048,768]{1,0:T(8,128)(2,1)S(1)} %get-tuple-element.70.gate_b.refs_0_, bf16[2048,768]{1,0:T(8,128)(2,1)S(1)} %get-tuple-element.71.up_b.refs_1_, ...), custom_call_target="tpu_custom_call" | custom-call | flops 75497472 | bytes 1179648 | tf_op jit(solution)/shard_map/partial_sums/pallas_call | solution.py:171
  31.3 4.9 %collective-permute-done.7.refs_0_ = bf16[3,64,768]{2,1,0:T(8,128)(2,1)S(1)} collective-permute-done((bf16[3,64,768]{2,1,0:T(8,128)(2,1)S(1)}, bf16[3,64,768]{2,1,0:T(8,128)(2,1)S(1)}, u32[]{:S(2)}, u32[]{:S(2)}) %collective-permute-start.7) | collective-permute-done | bytes 294944 | tf_op jit(solution)/shard_map/ppermute | solution.py:32
  36.2 6.1 %collective-permute-done.9.refs_1_ = bf16[3,64,768]{2,1,0:T(8,128)(2,1)S(1)} collective-permute-done((bf16[3,64,768]{2,1,0:T(8,128)(2,1)S(1)}, bf16[3,64,768]{2,1,0:T(8,128)(2,1)S(1)}, u32[]{:S(2)}, u32[]{:S(2)}) %collective-permute-start.9) | collective-permute-done | bytes 294944 | tf_op jit(solution)/shard_map/ppermute | solution.py:32
  42.3 0.2 activate.1.act
  42.5 0.7 collective-permute-start.11
  43.2 3.4 %collective-permute-start.10 = (bf16[3,64,768]{2,1,0:T(8,128)(2,1)S(1)}, bf16[3,64,768]{2,1,0:T(8,128)(2,1)S(1)}, u32[]{:S(2)}, u32[]{:S(2)}) collective-permute-start(bf16[3,64,768]{2,1,0:T(8,128)(2,1)S(1)} %activate.1.act), channel_id=1, source_target_pairs={{0,2},{1,3},{2,0},{3,1},{4,6},{5,7},{6,4},{7,5},{8,10},{9,11},{10,... | collective-permute-start | bytes 884744 | tf_op jit(solution)/shard_map/ppermute | solution.py:32
  46.6 5.3 %productsgrads.3 = (f32[2,64,2048]{2,1,0:T(8,128)S(1)}, bf16[2048,3072]{1,0:T(8,128)(2,1)}, bf16[2048,3072]{1,0:T(8,128)(2,1)}, bf16[3072,2048]{1,0:T(8,128)(2,1)}) custom-call(bf16[3,64,768]{2,1,0:T(8,128)(2,1)S(1)} %activate.1.act, bf16[2048,768]{1,0:T(8,128)(2,1)S(1)} %get-tuple-element.70.gate_b.refs_0_, ...), custom_call_target="tpu_custom_call" | custom-call | flops 150994944 | bytes 2359296 | tf_op jit(solution)/shard_map/productsgrads/pallas_call | solution.py:301
  51.9 4.9 %collective-permute-done.11.act = bf16[3,64,768]{2,1,0:T(8,128)(2,1)S(1)} collective-permute-done((bf16[3,64,768]{2,1,0:T(8,128)(2,1)S(1)}, bf16[3,64,768]{2,1,0:T(8,128)(2,1)S(1)}, u32[]{:S(2)}, u32[]{:S(2)}) %collective-permute-start.11) | collective-permute-done | bytes 294944 | tf_op jit(solution)/shard_map/ppermute | solution.py:32
  56.8 5.3 %productsgrads.4 = (f32[2,64,2048]{2,1,0:T(8,128)S(1)}, bf16[2048,3072]{1,0:T(8,128)(2,1)}, bf16[2048,3072]{1,0:T(8,128)(2,1)}, bf16[3072,2048]{1,0:T(8,128)(2,1)}) custom-call(bf16[3,64,768]{2,1,0:T(8,128)(2,1)S(1)} %collective-permute-done.11.act, ...), custom_call_target="tpu_custom_call", output_to_operand_aliasing={{1}: (7, {}), {2}: (8, {}), {3}: (9, {})} | custom-call | flops 150994944 | bytes 2359296 | tf_op jit(solution)/shard_map/productsgrads/pallas_call | solution.py:301
  62.1 0.1 collective-permute-start.12
  62.2 5.5 %productsgrads.5 = (f32[2,64,2048]{2,1,0:T(8,128)S(1)}, bf16[2048,3072]{1,0:T(8,128)(2,1)}, bf16[2048,3072]{1,0:T(8,128)(2,1)}, bf16[3072,2048]{1,0:T(8,128)(2,1)}) custom-call(bf16[3,64,768]{2,1,0:T(8,128)(2,1)S(1)} %collective-permute-done.10.act, ...), custom_call_target="tpu_custom_call", output_to_operand_aliasing={{1}: (7, {}), {2}: (8, {}), {3}: (9, {})} | custom-call | flops 150994944 | bytes 2359296 | tf_op jit(solution)/shard_map/productsgrads/pallas_call | solution.py:301
  67.7 1.7 %collective-permute-done.12.act = bf16[3,64,768]{2,1,0:T(8,128)(2,1)S(1)} collective-permute-done((bf16[3,64,768]{2,1,0:T(8,128)(2,1)S(1)}, bf16[3,64,768]{2,1,0:T(8,128)(2,1)S(1)}, u32[]{:S(2)}, u32[]{:S(2)}) %collective-permute-start.12) | collective-permute-done | bytes 294944 | tf_op jit(solution)/shard_map/ppermute | solution.py:32
  69.4 2.5 %products.1 = (f32[2,32,2048]{2,1,0:T(8,128)S(1)}, f32[2,32,2048]{2,1,0:T(8,128)S(1)}) custom-call(bf16[3,64,768]{2,1,0:T(8,128)(2,1)S(1)} %collective-permute-done.12.act, bf16[2048,768]{1,0:T(8,128)(2,1)S(1)} %get-tuple-element.61.gate_b.refs_0_, bf16[2048,768]{1,0:T(8,128)(2,1)S(1)} %get-tuple-element.62.up_b.refs_1_, ...), custom_call_target="tpu_custom_call" | custom-call | flops 75497472 | bytes 1179648 | tf_op jit(solution)/shard_map/products/pallas_call | solution.py:301
  72.0 0.1 collective-permute-start.13
  72.0 1.9 %collective-permute-done.13.other = f32[2,32,2048]{2,1,0:T(8,128)S(1)} collective-permute-done((f32[2,32,2048]{2,1,0:T(8,128)S(1)}, f32[2,32,2048]{2,1,0:T(8,128)S(1)}, u32[]{:S(2)}, u32[]{:S(2)}) %collective-permute-start.13) | collective-permute-done | bytes 524320 | tf_op jit(solution)/shard_map/ppermute | solution.py:32
  73.9 0.1 fold.1
  74.0 1.0 %collective-permute-start.14 = (bf16[2,8,2048]{2,1,0:T(8,128)(2,1)S(1)}, bf16[2,8,2048]{2,1,0:T(8,128)(2,1)S(1)}, u32[]{:S(2)}, u32[]{:S(2)}) collective-permute-start(bf16[2,8,2048]{2,1,0:T(8,128)(2,1)S(1)} %get-tuple-element.90), channel_id=1, source_target_pairs={{0,8},{4,12},{8,0},{12,4},{16,24},{20,28},{24,16},{28,20},{1,9},{5... | collective-permute-start | bytes 196616 | tf_op jit(solution)/shard_map/ppermute | solution.py:32
  75.0 1.5 %collective-permute-start.15 = (bf16[2,8,2048]{2,1,0:T(8,128)(2,1)S(1)}, bf16[2,8,2048]{2,1,0:T(8,128)(2,1)S(1)}, u32[]{:S(2)}, u32[]{:S(2)}) collective-permute-start(bf16[2,8,2048]{2,1,0:T(8,128)(2,1)S(1)} %get-tuple-element.91), channel_id=1, source_target_pairs={{0,16},{4,20},{8,24},{12,28},{16,0},{20,4},{24,8},{28,12},{1,17},{... | collective-permute-start | bytes 196616 | tf_op jit(solution)/shard_map/ppermute | solution.py:32
  76.5 1.0 %collective-permute-start.16 = (bf16[2,8,2048]{2,1,0:T(8,128)(2,1)S(1)}, bf16[2,8,2048]{2,1,0:T(8,128)(2,1)S(1)}, u32[]{:S(2)}, u32[]{:S(2)}) collective-permute-start(bf16[2,8,2048]{2,1,0:T(8,128)(2,1)S(1)} %get-tuple-element.92), channel_id=1, source_target_pairs={{0,24},{4,28},{8,16},{12,20},{16,8},{20,12},{24,0},{28,4},{1,25},{... | collective-permute-start | bytes 196616 | tf_op jit(solution)/shard_map/ppermute | solution.py:32
  77.5 4.1 %grads.1 = (bf16[2048,3072]{1,0:T(8,128)(2,1)}, bf16[2048,3072]{1,0:T(8,128)(2,1)}, bf16[3072,2048]{1,0:T(8,128)(2,1)}) custom-call(bf16[3,64,768]{2,1,0:T(8,128)(2,1)S(1)} %collective-permute-done.12.act, bf16[2048,64]{1,0:T(8,128)(2,1)S(1)} %get-tuple-element.76.refs_3_.refs_4_.refs_0_, ...), custom_call_target="tpu_custom_call", output_to_operand_aliasing={{0}: (3, {}), {1}: (4, {}), {2}: (5, {})} | custom-call | flops 75497472 | bytes 1179648 | tf_op jit(solution)/shard_map/grads/pallas_call | solution.py:301
  81.6 0.0 collective-permute-done.14.refs_0_
  81.6 0.0 collective-permute-done.15.refs_1_
  81.6 0.1 collective-permute-done.16.refs_2_
  81.7 0.6 finish.1
  (2 shorter events, 0.0 us)
Async XLA Ops:
  1.4 8.4 %collective-permute-start.2 = (bf16[16,2048]{1,0:T(8,128)(2,1)S(1)}, bf16[16,2048]{1,0:T(8,128)(2,1)S(1)}, u32[]{:S(2)}, u32[]{:S(2)}) collective-permute-start(bf16[16,2048]{1,0:T(8,128)(2,1)S(1)} %pack.1.refs_0_), channel_id=1, source_target_pairs={{0,24},{4,28},{8,16},{12,20},{16,8},{20,12},{24,0},{28,4},{1,25},{... | collective-permute-start | bytes 196616 | tf_op jit(solution)/shard_map/ppermute | solution.py:32
  5.3 4.5 %collective-permute-start.1 = (bf16[16,2048]{1,0:T(8,128)(2,1)S(1)}, bf16[16,2048]{1,0:T(8,128)(2,1)S(1)}, u32[]{:S(2)}, u32[]{:S(2)}) collective-permute-start(bf16[16,2048]{1,0:T(8,128)(2,1)S(1)} %pack.1.refs_0_), channel_id=1, source_target_pairs={{0,16},{4,20},{8,24},{12,28},{16,0},{20,4},{24,8},{28,12},{1,17},{... | collective-permute-start | bytes 196616 | tf_op jit(solution)/shard_map/ppermute | solution.py:32
  5.8 4.3 %collective-permute-start = (bf16[16,2048]{1,0:T(8,128)(2,1)S(1)}, bf16[16,2048]{1,0:T(8,128)(2,1)S(1)}, u32[]{:S(2)}, u32[]{:S(2)}) collective-permute-start(bf16[16,2048]{1,0:T(8,128)(2,1)S(1)} %pack.1.refs_0_), channel_id=1, source_target_pairs={{0,8},{4,12},{8,0},{12,4},{16,24},{20,28},{24,16},{28,20},{1,9},{5... | collective-permute-start | bytes 196616 | tf_op jit(solution)/shard_map/ppermute | solution.py:32
  5.9 5.0 %collective-permute-start.3 = (bf16[16,2048]{1,0:T(8,128)(2,1)S(1)}, bf16[16,2048]{1,0:T(8,128)(2,1)S(1)}, u32[]{:S(2)}, u32[]{:S(2)}) collective-permute-start(bf16[16,2048]{1,0:T(8,128)(2,1)S(1)} %pack.1.refs_0_), channel_id=1, source_target_pairs={{0,4},{4,0},{8,12},{12,8},{16,20},{20,16},{24,28},{28,24},{1,5},{5... | collective-permute-start | bytes 196616 | tf_op jit(solution)/shard_map/ppermute | solution.py:32
  10.1 1.3 %collective-permute-start.4 = (bf16[16,2048]{1,0:T(8,128)(2,1)S(1)}, bf16[16,2048]{1,0:T(8,128)(2,1)S(1)}, u32[]{:S(2)}, u32[]{:S(2)}) collective-permute-start(bf16[16,2048]{1,0:T(8,128)(2,1)S(1)} %collective-permute-done.refs_1_), channel_id=1, source_target_pairs={{0,4},{4,0},{8,12},{12,8},{16,20},{20,16},{24,28},{28,24},{1,5},{5... | collective-permute-start | bytes 196616 | tf_op jit(solution)/shard_map/ppermute | solution.py:32
  10.4 1.3 %collective-permute-start.5 = (bf16[16,2048]{1,0:T(8,128)(2,1)S(1)}, bf16[16,2048]{1,0:T(8,128)(2,1)S(1)}, u32[]{:S(2)}, u32[]{:S(2)}) collective-permute-start(bf16[16,2048]{1,0:T(8,128)(2,1)S(1)} %collective-permute-done.1.refs_2_), channel_id=1, source_target_pairs={{0,4},{4,0},{8,12},{12,8},{16,20},{20,16},{24,28},{28,24},{1,5},{5... | collective-permute-start | bytes 196616 | tf_op jit(solution)/shard_map/ppermute | solution.py:32
  10.6 1.3 %collective-permute-start.6 = (bf16[16,2048]{1,0:T(8,128)(2,1)S(1)}, bf16[16,2048]{1,0:T(8,128)(2,1)S(1)}, u32[]{:S(2)}, u32[]{:S(2)}) collective-permute-start(bf16[16,2048]{1,0:T(8,128)(2,1)S(1)} %collective-permute-done.2.refs_3_), channel_id=1, source_target_pairs={{0,4},{4,0},{8,12},{12,8},{16,20},{20,16},{24,28},{28,24},{1,5},{5... | collective-permute-start | bytes 196616 | tf_op jit(solution)/shard_map/ppermute | solution.py:32
  16.0 9.9 %collective-permute-start.8 = (bf16[3,64,768]{2,1,0:T(8,128)(2,1)S(1)}, bf16[3,64,768]{2,1,0:T(8,128)(2,1)S(1)}, u32[]{:S(2)}, u32[]{:S(2)}) collective-permute-start(bf16[3,64,768]{2,1,0:T(8,128)(2,1)S(1)} %get-tuple-element.75), channel_id=1, source_target_pairs={{0,1},{1,0},{2,3},{3,2},{4,5},{5,4},{6,7},{7,6},{8,9},{9,8},{10,11... | collective-permute-start | bytes 884744 | tf_op jit(solution)/shard_map/ppermute | solution.py:32
  21.8 14.4 %collective-permute-start.7 = (bf16[3,64,768]{2,1,0:T(8,128)(2,1)S(1)}, bf16[3,64,768]{2,1,0:T(8,128)(2,1)S(1)}, u32[]{:S(2)}, u32[]{:S(2)}) collective-permute-start(bf16[3,64,768]{2,1,0:T(8,128)(2,1)S(1)} %get-tuple-element.73), channel_id=1, source_target_pairs={{0,1},{1,0},{2,3},{3,2},{4,5},{5,4},{6,7},{7,6},{8,9},{9,8},{10,11... | collective-permute-start | bytes 884744 | tf_op jit(solution)/shard_map/ppermute | solution.py:32
  25.9 16.4 %collective-permute-start.9 = (bf16[3,64,768]{2,1,0:T(8,128)(2,1)S(1)}, bf16[3,64,768]{2,1,0:T(8,128)(2,1)S(1)}, u32[]{:S(2)}, u32[]{:S(2)}) collective-permute-start(bf16[3,64,768]{2,1,0:T(8,128)(2,1)S(1)} %combine.1), channel_id=1, source_target_pairs={{0,2},{1,3},{2,0},{3,1},{4,6},{5,7},{6,4},{7,5},{8,10},{9,11},{10,... | collective-permute-start | bytes 884744 | tf_op jit(solution)/shard_map/ppermute | solution.py:32
  42.5 14.3 %collective-permute-start.11 = (bf16[3,64,768]{2,1,0:T(8,128)(2,1)S(1)}, bf16[3,64,768]{2,1,0:T(8,128)(2,1)S(1)}, u32[]{:S(2)}, u32[]{:S(2)}) collective-permute-start(bf16[3,64,768]{2,1,0:T(8,128)(2,1)S(1)} %activate.1.act), channel_id=1, source_target_pairs={{0,1},{1,0},{2,3},{3,2},{4,5},{5,4},{6,7},{7,6},{8,9},{9,8},{10,11... | collective-permute-start | bytes 884744 | tf_op jit(solution)/shard_map/ppermute | solution.py:32
  43.2 18.9 %collective-permute-start.10 = (bf16[3,64,768]{2,1,0:T(8,128)(2,1)S(1)}, bf16[3,64,768]{2,1,0:T(8,128)(2,1)S(1)}, u32[]{:S(2)}, u32[]{:S(2)}) collective-permute-start(bf16[3,64,768]{2,1,0:T(8,128)(2,1)S(1)} %activate.1.act), channel_id=1, source_target_pairs={{0,2},{1,3},{2,0},{3,1},{4,6},{5,7},{6,4},{7,5},{8,10},{9,11},{10,... | collective-permute-start | bytes 884744 | tf_op jit(solution)/shard_map/ppermute | solution.py:32
  62.1 7.3 %collective-permute-start.12 = (bf16[3,64,768]{2,1,0:T(8,128)(2,1)S(1)}, bf16[3,64,768]{2,1,0:T(8,128)(2,1)S(1)}, u32[]{:S(2)}, u32[]{:S(2)}) collective-permute-start(bf16[3,64,768]{2,1,0:T(8,128)(2,1)S(1)} %collective-permute-done.10.act), channel_id=1, source_target_pairs={{0,1},{1,0},{2,3},{3,2},{4,5},{5,4},{6,7},{7,6},{8,9},{9,8},{10,11... | collective-permute-start | bytes 884744 | tf_op jit(solution)/shard_map/ppermute | solution.py:32
  72.0 2.0 %collective-permute-start.13 = (f32[2,32,2048]{2,1,0:T(8,128)S(1)}, f32[2,32,2048]{2,1,0:T(8,128)S(1)}, u32[]{:S(2)}, u32[]{:S(2)}) collective-permute-start(f32[2,32,2048]{2,1,0:T(8,128)S(1)} %get-tuple-element.88), channel_id=1, source_target_pairs={{0,4},{4,0},{8,12},{12,8},{16,20},{20,16},{24,28},{28,24},{1,5},{5... | collective-permute-start | bytes 1572872 | tf_op jit(solution)/shard_map/ppermute | solution.py:32
  74.0 7.6 %collective-permute-start.14 = (bf16[2,8,2048]{2,1,0:T(8,128)(2,1)S(1)}, bf16[2,8,2048]{2,1,0:T(8,128)(2,1)S(1)}, u32[]{:S(2)}, u32[]{:S(2)}) collective-permute-start(bf16[2,8,2048]{2,1,0:T(8,128)(2,1)S(1)} %get-tuple-element.90), channel_id=1, source_target_pairs={{0,8},{4,12},{8,0},{12,4},{16,24},{20,28},{24,16},{28,20},{1,9},{5... | collective-permute-start | bytes 196616 | tf_op jit(solution)/shard_map/ppermute | solution.py:32
  75.0 6.6 %collective-permute-start.15 = (bf16[2,8,2048]{2,1,0:T(8,128)(2,1)S(1)}, bf16[2,8,2048]{2,1,0:T(8,128)(2,1)S(1)}, u32[]{:S(2)}, u32[]{:S(2)}) collective-permute-start(bf16[2,8,2048]{2,1,0:T(8,128)(2,1)S(1)} %get-tuple-element.91), channel_id=1, source_target_pairs={{0,16},{4,20},{8,24},{12,28},{16,0},{20,4},{24,8},{28,12},{1,17},{... | collective-permute-start | bytes 196616 | tf_op jit(solution)/shard_map/ppermute | solution.py:32
  76.5 5.2 %collective-permute-start.16 = (bf16[2,8,2048]{2,1,0:T(8,128)(2,1)S(1)}, bf16[2,8,2048]{2,1,0:T(8,128)(2,1)S(1)}, u32[]{:S(2)}, u32[]{:S(2)}) collective-permute-start(bf16[2,8,2048]{2,1,0:T(8,128)(2,1)S(1)} %get-tuple-element.92), channel_id=1, source_target_pairs={{0,24},{4,28},{8,16},{12,20},{16,8},{20,12},{24,0},{28,4},{1,25},{... | collective-permute-start | bytes 196616 | tf_op jit(solution)/shard_map/ppermute | solution.py:32

commit v9 on v8

--- a/solution.py
+++ b/solution.py
@@ -122,25 +122,25 @@
 
 
 def load_kernel(k, *refs):
-    copies = fetches(k, refs[:3], refs[3:6], refs[6])
+    copies = fetches(k, refs[:3], refs[-4:-1], refs[-1])
     for copy in copies:
         copy.start()
     for copy in copies:
         copy.wait()
 
 
-def load(k, weights, units):
+def load(k, weights, units, after=()):
     shapes = block_shapes(units, weights[0].shape[0])
     return pl.pallas_call(
         functools.partial(load_kernel, k),
-        in_specs=[HOLD] * 3,
+        in_specs=[HOLD] * (3 + len(after)),
         out_specs=[WHOLE] * 3,
         scratch_shapes=[pltpu.SemaphoreType.DMA((FETCHES, 3))],
         out_shape=[vmem_array(x) for x in shapes],
         compiler_params=PARAMS,
         cost_estimate=estimate(0, 6 * weights[0].shape[0] * units),
         name="load",
-    )(*in_hbm(weights))
+    )(*in_hbm(weights), *after)
 
 
 def sums_kernel(following, tok, grad, gate_b, up_b, down_b, *refs):
@@ -180,14 +180,15 @@
     )(tok, grad, *in_vmem(block), *(in_hbm(weights) if more else ()))
 
 
-def combine_kernel(own, other, out):
+def combine_kernel(own, other, out, token):
+    token[...] = jnp.zeros_like(token)
     out[...] = (own[...] + other[...].astype(F32)).astype(BF16)
 
 
 def combine(own, other):
     return pl.pallas_call(
         combine_kernel,
-        out_shape=array(own.shape, BF16),
+        out_shape=[array(own.shape, BF16), array((8, 128), F32)],
         compiler_params=PARAMS,
         cost_estimate=estimate(own.size, 8 * own.size),
         name="combine",
@@ -195,7 +196,7 @@
 
 
 def activate_kernel(own, *refs):
-    others, out = refs[:-1], refs[-1]
+    others, (out, hidden, deltas) = refs[:-3], refs[-3:]
     gate, up, hidden_grad = (
         functools.reduce(lambda s, o: s + o[j].astype(F32), others, own[j]) for j in range(3)
     )
@@ -204,20 +205,28 @@
     out[0] = (swish * up).astype(BF16)
     out[1] = (hidden_grad * up * sig * (1.0 + gate * (1.0 - sig))).astype(BF16)
     out[2] = (hidden_grad * swish).astype(BF16)
+    hidden[...] = out[0]
+    deltas[...] = out[1:]
 
 
 def activate(own, others):
     return pl.pallas_call(
         activate_kernel,
-        out_shape=array(own.shape, BF16),
+        out_shape=[array(x, BF16) for x in (own.shape, own.shape[1:], (2, *own.shape[1:]))],
         compiler_params=PARAMS,
         cost_estimate=estimate(8 * own.size, 12 * own.size),
         name="activate",
     )(own, *others)
 
 
-def use_kernel(k, first, last, with_products, with_grads, act, *refs):
+def use_kernel(k, first, last, with_products, with_grads, apart, *refs):
     refs = list(refs)
+    if apart:
+        hidden, deltas = refs.pop(0), refs.pop(0)
+        act = hidden[...], deltas[0], deltas[1]
+    else:
+        whole = refs.pop(0)
+        act = whole[0], whole[1], whole[2]
     leaving = []
     if with_products:
         gate_w, up_w, down_w = (refs.pop(0) for _ in range(3))
@@ -267,9 +276,9 @@
 
 
 def use(k, act, weights=None, terms=None, last=False, sides=None, grads=(), after=()):
-    _, total, units = act.shape
+    total, units = act[-1].shape[1:]
     first = terms is None
-    specs, args = [WHOLE], [act]
+    specs, args = [WHOLE] * len(act), list(act)
     out_specs, out_shape, scratch, aliases = [], [], [], {}
     moved = 0
     if weights is not None:
@@ -299,7 +308,9 @@
         scratch += [pltpu.VMEM((units, width), BF16), pltpu.SemaphoreType.DMA((CHUNKS, 3))]
         moved += 6 * width * units
     return pl.pallas_call(
-        functools.partial(use_kernel, k, first, last, weights is not None, sides is not None),
+        functools.partial(
+            use_kernel, k, first, last, weights is not None, sides is not None, len(act) == 2
+        ),
         in_specs=specs + [HOLD] * len(after),
         out_specs=out_specs,
         scratch_shapes=scratch,
@@ -368,17 +379,25 @@
     near = along_col(there, k=1)
     there, *far_weights = partial_sums(near_weights, tok, grad, BF16, weights, 2)
     from_near = along_col(there, k=1)
-    here, *own_weights = partial_sums(far_weights, tok, grad, F32, weights, 0)
-    from_far = along_col(combine(here, near), k=2)
+    (here,) = partial_sums(far_weights, tok, grad, F32)
+    pair, token = combine(here, near)
+    from_far = along_col(pair, k=2)
+    own_weights = load(0, weights, units, after=(token,))
     (here,) = partial_sums(own_weights, tok, grad, F32)
-    own = activate(here, [from_near, from_far])
+    own, hidden, deltas = activate(here, [from_near, from_far])
 
     near_act = along_col(own, k=1)
-    far_act = along_col(own, k=2)
-    terms, *grads = use(0, own, own_weights, sides=sides)
-    terms, *grads = use(1, near_act, near_weights, terms, sides=sides, grads=grads)
-    held, _ = lax.optimization_barrier((far_act, (terms, grads)))
-    last_act = along_col(held, k=1)
+    (terms,) = use(0, (own,), own_weights)
+    (hidden, deltas, own), _ = lax.optimization_barrier(((hidden, deltas, own), terms))
+    far_deltas = along_col(deltas, k=2)
+    far_hidden = along_col(hidden, k=2)
+    grads = use(0, (own,), sides=sides)
+    terms, *grads = use(1, (near_act,), near_weights, terms, sides=sides, grads=grads)
+    far_deltas, _ = lax.optimization_barrier((far_deltas, (terms, grads)))
+    last_deltas = along_col(far_deltas, k=1)
+    far_hidden, _ = lax.optimization_barrier((far_hidden, (terms, grads)))
+    last_hidden = along_col(far_hidden, k=1)
+    far_act, last_act = (far_hidden, far_deltas), (last_hidden, last_deltas)
     terms, *grads = use(2, far_act, far_weights, terms, sides=sides, grads=grads)
     kept, given = use(3, last_act, last_weights, terms, last=True)
 

time: 82.5 us -> 80.7 us (0.978)
  waiting for transfers between devices: 20.9 us -> 12.5 us
  Pallas kernels: 42.3 us -> 47.2 us
  starting transfers between devices: 18.3 us -> 20 us
    ppermute x17 -> x19, waiting for transfers between devices: 20.9 us -> 12.5 us  [swap(): return lax.ppermute(x, axis, [(i, i ^ k) for i in range(size)])]
    pallas_call x3 -> x4, Pallas kernels: 4.05 us -> 7.93 us  [the longest x2 7.65 us: load(): pl.pallas_call(functools.partial(load_kernel, k), in_specs=[HOLD] * (3 +...]
    pallas_call x5 -> x6, Pallas kernels: 22.6 us -> 25.3 us  [use(): pl.pallas_call(functools.partial(use_kernel, k, first, last, weights is n...]
    ppermute x17 -> x19, starting transfers between devices: 18.3 us -> 20 us  [swap(): return lax.ppermute(x, axis, [(i, i ^ k) for i in range(size)])]
    pallas_call x4, Pallas kernels: 13.9 us -> 12.3 us  [partial_sums(): pl.pallas_call(functools.partial(sums_kernel, following), in_specs=[WHOLE...]
  transfers between devices with their start and end apart: 17 -> 19, of which waited for: 11 -> 11; matrix products, arithmetic and copies ran while one was open for 0% -> 0% of each run, Pallas kernels for 41% -> 48%
where the time goes in v9:
time: 80.7 us; the launch traced here: 80.5 us
  Pallas kernels  47.2 us (58%)
  starting transfers between devices  20 us (25%)
  waiting for transfers between devices  12.5 us (15%)
  between operations  0.82 us (1%)
    pallas_call x6, Pallas kernels, use(): pl.pallas_call(functools.partial(use_kernel, k, first, last, weights is n...  25.3 us
    ppermute x19, starting transfers between devices, swap(): return lax.ppermute(x, axis, [(i, i ^ k) for i in range(size)])  20 us
    ppermute x19, waiting for transfers between devices, swap(): return lax.ppermute(x, axis, [(i, i ^ k) for i in range(size)])  12.5 us
    pallas_call x4, Pallas kernels, partial_sums(): pl.pallas_call(functools.partial(sums_kernel, following), in_specs=[WHOLE...  12.3 us
    pallas_call x2, Pallas kernels, load(): pl.pallas_call(functools.partial(load_kernel, k), in_specs=[HOLD] * (3 +...  7.65 us
  transfers between devices with their start and end apart: 19, of which 11 were waited for; matrix products, arithmetic and copies ran while one was open for 0% of the time, Pallas kernels for 48%

profile of v9, /device:TPU:0, one launch (start us, length us, event | category | flops | bytes accessed | tf_op | source)
XLA Modules:
  0.0 80.5 jit_solution(12089186617616076713)
XLA Ops:
  0.6 0.8 pack.1.refs_0_
  1.4 3.9 %collective-permute-start.2 = (bf16[16,2048]{1,0:T(8,128)(2,1)S(1)}, bf16[16,2048]{1,0:T(8,128)(2,1)S(1)}, u32[]{:S(2)}, u32[]{:S(2)}) collective-permute-start(bf16[16,2048]{1,0:T(8,128)(2,1)S(1)} %pack.1.refs_0_), channel_id=1, source_target_pairs={{0,24},{4,28},{8,16},{12,20},{16,8},{20,12},{24,0},{28,4},{1,25},{... | collective-permute-start | bytes 196616 | tf_op jit(solution)/shard_map/ppermute | solution.py:32
  5.3 0.5 collective-permute-start.1
  5.8 0.1 collective-permute-start
  5.9 3.8 %load.2 = (bf16[2048,768]{1,0:T(8,128)(2,1)S(1)}, bf16[2048,768]{1,0:T(8,128)(2,1)S(1)}, bf16[768,2048]{1,0:T(8,128)(2,1)S(1)}) custom-call(bf16[2048,3072]{1,0:T(8,128)(2,1)} %refs_0_.7, bf16[2048,3072]{1,0:T(8,128)(2,1)} %refs_1_.7, bf16[3072,2048]{1,0:T(8,128)(2,1)} %refs_2_.7), custom_call_target="tpu_custom_call" | custom-call | bytes 1179648 | tf_op jit(solution)/shard_map/load/pallas_call | solution.py:134
  9.8 0.0 collective-permute-done.1.refs_2_
  9.8 0.3 collective-permute-done.refs_1_
  10.1 0.3 collective-permute-start.4
  10.4 0.2 collective-permute-start.5
  10.6 0.3 collective-permute-start.6
  10.9 0.4 collective-permute-done.4.refs_5_
  11.3 0.3 collective-permute-done.5.refs_6_
  11.6 0.2 collective-permute-done.6.refs_7_
  11.8 0.2 assemble.1
  12.1 3.9 %partial_sums.4 = (bf16[3,64,768]{2,1,0:T(8,128)(2,1)S(1)}, bf16[2048,768]{1,0:T(8,128)(2,1)S(1)}, bf16[2048,768]{1,0:T(8,128)(2,1)S(1)}, bf16[768,2048]{1,0:T(8,128)(2,1)S(1)}) custom-call(bf16[64,2048]{1,0:T(8,128)(2,1)S(1)} %get-tuple-element.66.tok, bf16[64,2048]{1,0:T(8,128)(2,1)S(1)} %get-tuple-element.67.grad.refs_2_.refs_6_.refs_7_.refs_3_, ...), custom_call_target="tpu_custom_call" | custom-call | flops 75497472 | bytes 1179648 | tf_op jit(solution)/shard_map/partial_sums/pallas_call | solution.py:171
  16.0 1.9 %collective-permute-start.7 = (bf16[3,64,768]{2,1,0:T(8,128)(2,1)S(1)}, bf16[3,64,768]{2,1,0:T(8,128)(2,1)S(1)}, u32[]{:S(2)}, u32[]{:S(2)}) collective-permute-start(bf16[3,64,768]{2,1,0:T(8,128)(2,1)S(1)} %get-tuple-element.77), channel_id=1, source_target_pairs={{0,1},{1,0},{2,3},{3,2},{4,5},{5,4},{6,7},{7,6},{8,9},{9,8},{10,11... | collective-permute-start | bytes 884744 | tf_op jit(solution)/shard_map/ppermute | solution.py:32
  17.9 3.8 %partial_sums.5 = (bf16[3,64,768]{2,1,0:T(8,128)(2,1)S(1)}, bf16[2048,768]{1,0:T(8,128)(2,1)S(1)}, bf16[2048,768]{1,0:T(8,128)(2,1)S(1)}, bf16[768,2048]{1,0:T(8,128)(2,1)S(1)}) custom-call(bf16[64,2048]{1,0:T(8,128)(2,1)S(1)} %get-tuple-element.66.tok, bf16[64,2048]{1,0:T(8,128)(2,1)S(1)} %get-tuple-element.67.grad.refs_2_.refs_6_.refs_7_.refs_3_, ...), custom_call_target="tpu_custom_call" | custom-call | flops 75497472 | bytes 1179648 | tf_op jit(solution)/shard_map/partial_sums/pallas_call | solution.py:171
  21.8 0.2 collective-permute-start.8
  22.0 2.2 %partial_sums.6.own = f32[3,64,768]{2,1,0:T(8,128)S(1)} custom-call(bf16[64,2048]{1,0:T(8,128)(2,1)S(1)} %get-tuple-element.66.tok, bf16[64,2048]{1,0:T(8,128)(2,1)S(1)} %get-tuple-element.67.grad.refs_2_.refs_6_.refs_7_.refs_3_, bf16[2048,768]{1,0:T(8,128)(2,1)S(1)} %get-tuple-element.74.gate_b.refs_2_, ...), custom_call_target="tpu_custom_call" | custom-call | flops 75497472 | bytes 1179648 | tf_op jit(solution)/shard_map/partial_sums/pallas_call | solution.py:171
  24.1 1.7 %collective-permute-done.7.other = bf16[3,64,768]{2,1,0:T(8,128)(2,1)S(1)} collective-permute-done((bf16[3,64,768]{2,1,0:T(8,128)(2,1)S(1)}, bf16[3,64,768]{2,1,0:T(8,128)(2,1)S(1)}, u32[]{:S(2)}, u32[]{:S(2)}) %collective-permute-start.7) | collective-permute-done | bytes 294944 | tf_op jit(solution)/shard_map/ppermute | solution.py:32
  25.9 0.1 combine.1
  25.9 3.0 %collective-permute-start.9 = (bf16[3,64,768]{2,1,0:T(8,128)(2,1)S(1)}, bf16[3,64,768]{2,1,0:T(8,128)(2,1)S(1)}, u32[]{:S(2)}, u32[]{:S(2)}) collective-permute-start(bf16[3,64,768]{2,1,0:T(8,128)(2,1)S(1)} %get-tuple-element.83), channel_id=1, source_target_pairs={{0,2},{1,3},{2,0},{3,1},{4,6},{5,7},{6,4},{7,5},{8,10},{9,11},{10,... | collective-permute-start | bytes 884744 | tf_op jit(solution)/shard_map/ppermute | solution.py:32
  29.0 3.8 %load.3 = (bf16[2048,768]{1,0:T(8,128)(2,1)S(1)}, bf16[2048,768]{1,0:T(8,128)(2,1)S(1)}, bf16[768,2048]{1,0:T(8,128)(2,1)S(1)}) custom-call(bf16[2048,3072]{1,0:T(8,128)(2,1)} %refs_0_.7, bf16[2048,3072]{1,0:T(8,128)(2,1)} %refs_1_.7, bf16[3072,2048]{1,0:T(8,128)(2,1)} %refs_2_.7, f32[8,128]{1,0:T(8,128)S(1)} %get-tuple-element.78.refs_3_), custom_call_target="tpu_custom_call" | custom-call | bytes 1179648 | tf_op jit(solution)/shard_map/load/pallas_call | solution.py:134
  32.8 2.3 %partial_sums.7.own = f32[3,64,768]{2,1,0:T(8,128)S(1)} custom-call(bf16[64,2048]{1,0:T(8,128)(2,1)S(1)} %get-tuple-element.66.tok, bf16[64,2048]{1,0:T(8,128)(2,1)S(1)} %get-tuple-element.67.grad.refs_2_.refs_6_.refs_7_.refs_3_, bf16[2048,768]{1,0:T(8,128)(2,1)S(1)} %get-tuple-element.79.gate_b.refs_1_, ...), custom_call_target="tpu_custom_call" | custom-call | flops 75497472 | bytes 1179648 | tf_op jit(solution)/shard_map/partial_sums/pallas_call | solution.py:171
  35.1 1.9 %collective-permute-done.8.refs_0_ = bf16[3,64,768]{2,1,0:T(8,128)(2,1)S(1)} collective-permute-done((bf16[3,64,768]{2,1,0:T(8,128)(2,1)S(1)}, bf16[3,64,768]{2,1,0:T(8,128)(2,1)S(1)}, u32[]{:S(2)}, u32[]{:S(2)}) %collective-permute-start.8) | collective-permute-done | bytes 294944 | tf_op jit(solution)/shard_map/ppermute | solution.py:32
  37.1 4.4 %collective-permute-done.9.refs_1_ = bf16[3,64,768]{2,1,0:T(8,128)(2,1)S(1)} collective-permute-done((bf16[3,64,768]{2,1,0:T(8,128)(2,1)S(1)}, bf16[3,64,768]{2,1,0:T(8,128)(2,1)S(1)}, u32[]{:S(2)}, u32[]{:S(2)}) %collective-permute-start.9) | collective-permute-done | bytes 294944 | tf_op jit(solution)/shard_map/ppermute | solution.py:32
  41.5 0.2 activate.1
  41.7 0.8 %collective-permute-start.11 = (bf16[3,64,768]{2,1,0:T(8,128)(2,1)S(1)}, bf16[3,64,768]{2,1,0:T(8,128)(2,1)S(1)}, u32[]{:S(2)}, u32[]{:S(2)}) collective-permute-start(bf16[3,64,768]{2,1,0:T(8,128)(2,1)S(1)} %get-tuple-element.89.refs_0_), channel_id=1, source_target_pairs={{0,1},{1,0},{2,3},{3,2},{4,5},{5,4},{6,7},{7,6},{8,9},{9,8},{10,11... | collective-permute-start | bytes 884744 | tf_op jit(solution)/shard_map/ppermute | solution.py:32
  42.5 2.5 %products.2.refs_4_ = f32[2,64,2048]{2,1,0:T(8,128)S(1)} custom-call(bf16[3,64,768]{2,1,0:T(8,128)(2,1)S(1)} %get-tuple-element.89.refs_0_, bf16[2048,768]{1,0:T(8,128)(2,1)S(1)} %get-tuple-element.79.gate_b.refs_1_, bf16[2048,768]{1,0:T(8,128)(2,1)S(1)} %get-tuple-element.80.up_b.refs_2_, bf16[768,2048]{1,0:T(8,128)(2,1)S(1)} %get-tuple-element.81.down_b.refs_3_), custom_call_target="tpu_custom_call" | custom-call | flops 75497472 | bytes 1179648 | tf_op jit(solution)/shard_map/products/pallas_call | solution.py:310
  45.1 3.4 %collective-permute-start.13 = (bf16[2,64,768]{2,1,0:T(8,128)(2,1)S(1)}, bf16[2,64,768]{2,1,0:T(8,128)(2,1)S(1)}, u32[]{:S(2)}, u32[]{:S(2)}) collective-permute-start(bf16[2,64,768]{2,1,0:T(8,128)(2,1)S(1)} %get-tuple-element.98), channel_id=1, source_target_pairs={{0,2},{1,3},{2,0},{3,1},{4,6},{5,7},{6,4},{7,5},{8,10},{9,11},{10,... | collective-permute-start | bytes 589832 | tf_op jit(solution)/shard_map/ppermute | solution.py:32
  48.5 0.1 collective-permute-start.10
  48.6 4.1 %grads.2 = (bf16[2048,3072]{1,0:T(8,128)(2,1)}, bf16[2048,3072]{1,0:T(8,128)(2,1)}, bf16[3072,2048]{1,0:T(8,128)(2,1)}) custom-call(bf16[3,64,768]{2,1,0:T(8,128)(2,1)S(1)} %get-tuple-element.89.refs_0_, bf16[2048,64]{1,0:T(8,128)(2,1)S(1)} %get-tuple-element.88.refs_1_.refs_5_.refs_6_.refs_2_, ...), custom_call_target="tpu_custom_call" | custom-call | flops 75497472 | bytes 1179648 | tf_op jit(solution)/shard_map/grads/pallas_call | solution.py:310
  52.7 6.0 %productsgrads.2 = (f32[2,64,2048]{2,1,0:T(8,128)S(1)}, bf16[2048,3072]{1,0:T(8,128)(2,1)}, bf16[2048,3072]{1,0:T(8,128)(2,1)}, bf16[3072,2048]{1,0:T(8,128)(2,1)}) custom-call(bf16[3,64,768]{2,1,0:T(8,128)(2,1)S(1)} %collective-permute-done.11.refs_0_, ...), custom_call_target="tpu_custom_call", output_to_operand_aliasing={{1}: (7, {}), {2}: (8, {}), {3}: (9, {})} | custom-call | flops 150994944 | bytes 2359296 | tf_op jit(solution)/shard_map/productsgrads/pallas_call | solution.py:310
  58.7 0.1 collective-permute-done.13.refs_1_
  58.8 0.7 collective-permute-start.14
  59.5 0.5 collective-permute-done.10.refs_0_
  60.0 0.9 %collective-permute-start.12 = (bf16[64,768]{1,0:T(8,128)(2,1)S(1)}, bf16[64,768]{1,0:T(8,128)(2,1)S(1)}, u32[]{:S(2)}, u32[]{:S(2)}) collective-permute-start(bf16[64,768]{1,0:T(8,128)(2,1)S(1)} %collective-permute-done.10.refs_0_), channel_id=1, source_target_pairs={{0,1},{1,0},{2,3},{3,2},{4,5},{5,4},{6,7},{7,6},{8,9},{9,8},{10,11... | collective-permute-start | bytes 294920 | tf_op jit(solution)/shard_map/ppermute | solution.py:32
  60.8 6.2 %productsgrads.3 = (f32[2,64,2048]{2,1,0:T(8,128)S(1)}, bf16[2048,3072]{1,0:T(8,128)(2,1)}, bf16[2048,3072]{1,0:T(8,128)(2,1)}, bf16[3072,2048]{1,0:T(8,128)(2,1)}) custom-call(bf16[64,768]{1,0:T(8,128)(2,1)S(1)} %collective-permute-done.10.refs_0_, ...), custom_call_target="tpu_custom_call", output_to_operand_aliasing={{1}: (8, {}), {2}: (9, {}), {3}: (10, {})} | custom-call | flops 150994944 | bytes 2359296 | tf_op jit(solution)/shard_map/productsgrads/pallas_call | solution.py:310
  67.0 2.5 %products.3 = (f32[2,32,2048]{2,1,0:T(8,128)S(1)}, f32[2,32,2048]{2,1,0:T(8,128)S(1)}) custom-call(bf16[64,768]{1,0:T(8,128)(2,1)S(1)} %collective-permute-done.12.refs_0_, bf16[2,64,768]{2,1,0:T(8,128)(2,1)S(1)} %collective-permute-done.14.refs_1_, bf16[2048,768]{1,0:T(8,128)(2,1)S(1)} %get-tuple-element.68.gate_b.refs_2_, ...), custom_call_target="tpu_custom_call" | custom-call | flops 75497472 | bytes 1179648 | tf_op jit(solution)/shard_map/products/pallas_call | solution.py:310
  69.6 0.1 collective-permute-start.15
  69.7 1.9 %collective-permute-done.15.other = f32[2,32,2048]{2,1,0:T(8,128)S(1)} collective-permute-done((f32[2,32,2048]{2,1,0:T(8,128)S(1)}, f32[2,32,2048]{2,1,0:T(8,128)S(1)}, u32[]{:S(2)}, u32[]{:S(2)}) %collective-permute-start.15) | collective-permute-done | bytes 524320 | tf_op jit(solution)/shard_map/ppermute | solution.py:32
  71.6 0.1 fold.1
  71.6 1.6 %collective-permute-start.16 = (bf16[2,8,2048]{2,1,0:T(8,128)(2,1)S(1)}, bf16[2,8,2048]{2,1,0:T(8,128)(2,1)S(1)}, u32[]{:S(2)}, u32[]{:S(2)}) collective-permute-start(bf16[2,8,2048]{2,1,0:T(8,128)(2,1)S(1)} %get-tuple-element.104), channel_id=1, source_target_pairs={{0,8},{4,12},{8,0},{12,4},{16,24},{20,28},{24,16},{28,20},{1,9},{5... | collective-permute-start | bytes 196616 | tf_op jit(solution)/shard_map/ppermute | solution.py:32
  73.2 1.5 %collective-permute-start.17 = (bf16[2,8,2048]{2,1,0:T(8,128)(2,1)S(1)}, bf16[2,8,2048]{2,1,0:T(8,128)(2,1)S(1)}, u32[]{:S(2)}, u32[]{:S(2)}) collective-permute-start(bf16[2,8,2048]{2,1,0:T(8,128)(2,1)S(1)} %get-tuple-element.105), channel_id=1, source_target_pairs={{0,16},{4,20},{8,24},{12,28},{16,0},{20,4},{24,8},{28,12},{1,17},{... | collective-permute-start | bytes 196616 | tf_op jit(solution)/shard_map/ppermute | solution.py:32
  74.7 0.5 collective-permute-start.18
  75.2 4.1 %grads.3 = (bf16[2048,3072]{1,0:T(8,128)(2,1)}, bf16[2048,3072]{1,0:T(8,128)(2,1)}, bf16[3072,2048]{1,0:T(8,128)(2,1)}) custom-call(bf16[64,768]{1,0:T(8,128)(2,1)S(1)} %collective-permute-done.12.refs_0_, bf16[2,64,768]{2,1,0:T(8,128)(2,1)S(1)} %collective-permute-done.14.refs_1_, ...), custom_call_target="tpu_custom_call", output_to_operand_aliasing={{0}: (4, {}), {1}: (5, {}), {2}: (6, {})} | custom-call | flops 75497472 | bytes 1179648 | tf_op jit(solution)/shard_map/grads/pallas_call | solution.py:310
  79.3 0.6 collective-permute-done.18.refs_2_
  79.9 0.6 finish.1
  (8 shorter events, 0.0 us)
Async XLA Ops:
  1.4 8.4 %collective-permute-start.2 = (bf16[16,2048]{1,0:T(8,128)(2,1)S(1)}, bf16[16,2048]{1,0:T(8,128)(2,1)S(1)}, u32[]{:S(2)}, u32[]{:S(2)}) collective-permute-start(bf16[16,2048]{1,0:T(8,128)(2,1)S(1)} %pack.1.refs_0_), channel_id=1, source_target_pairs={{0,24},{4,28},{8,16},{12,20},{16,8},{20,12},{24,0},{28,4},{1,25},{... | collective-permute-start | bytes 196616 | tf_op jit(solution)/shard_map/ppermute | solution.py:32
  5.3 4.5 %collective-permute-start.1 = (bf16[16,2048]{1,0:T(8,128)(2,1)S(1)}, bf16[16,2048]{1,0:T(8,128)(2,1)S(1)}, u32[]{:S(2)}, u32[]{:S(2)}) collective-permute-start(bf16[16,2048]{1,0:T(8,128)(2,1)S(1)} %pack.1.refs_0_), channel_id=1, source_target_pairs={{0,16},{4,20},{8,24},{12,28},{16,0},{20,4},{24,8},{28,12},{1,17},{... | collective-permute-start | bytes 196616 | tf_op jit(solution)/shard_map/ppermute | solution.py:32
  5.8 4.3 %collective-permute-start = (bf16[16,2048]{1,0:T(8,128)(2,1)S(1)}, bf16[16,2048]{1,0:T(8,128)(2,1)S(1)}, u32[]{:S(2)}, u32[]{:S(2)}) collective-permute-start(bf16[16,2048]{1,0:T(8,128)(2,1)S(1)} %pack.1.refs_0_), channel_id=1, source_target_pairs={{0,8},{4,12},{8,0},{12,4},{16,24},{20,28},{24,16},{28,20},{1,9},{5... | collective-permute-start | bytes 196616 | tf_op jit(solution)/shard_map/ppermute | solution.py:32
  5.9 5.0 %collective-permute-start.3 = (bf16[16,2048]{1,0:T(8,128)(2,1)S(1)}, bf16[16,2048]{1,0:T(8,128)(2,1)S(1)}, u32[]{:S(2)}, u32[]{:S(2)}) collective-permute-start(bf16[16,2048]{1,0:T(8,128)(2,1)S(1)} %pack.1.refs_0_), channel_id=1, source_target_pairs={{0,4},{4,0},{8,12},{12,8},{16,20},{20,16},{24,28},{28,24},{1,5},{5... | collective-permute-start | bytes 196616 | tf_op jit(solution)/shard_map/ppermute | solution.py:32
  10.1 1.3 %collective-permute-start.4 = (bf16[16,2048]{1,0:T(8,128)(2,1)S(1)}, bf16[16,2048]{1,0:T(8,128)(2,1)S(1)}, u32[]{:S(2)}, u32[]{:S(2)}) collective-permute-start(bf16[16,2048]{1,0:T(8,128)(2,1)S(1)} %collective-permute-done.refs_1_), channel_id=1, source_target_pairs={{0,4},{4,0},{8,12},{12,8},{16,20},{20,16},{24,28},{28,24},{1,5},{5... | collective-permute-start | bytes 196616 | tf_op jit(solution)/shard_map/ppermute | solution.py:32
  10.4 1.3 %collective-permute-start.5 = (bf16[16,2048]{1,0:T(8,128)(2,1)S(1)}, bf16[16,2048]{1,0:T(8,128)(2,1)S(1)}, u32[]{:S(2)}, u32[]{:S(2)}) collective-permute-start(bf16[16,2048]{1,0:T(8,128)(2,1)S(1)} %collective-permute-done.1.refs_2_), channel_id=1, source_target_pairs={{0,4},{4,0},{8,12},{12,8},{16,20},{20,16},{24,28},{28,24},{1,5},{5... | collective-permute-start | bytes 196616 | tf_op jit(solution)/shard_map/ppermute | solution.py:32
  10.6 1.3 %collective-permute-start.6 = (bf16[16,2048]{1,0:T(8,128)(2,1)S(1)}, bf16[16,2048]{1,0:T(8,128)(2,1)S(1)}, u32[]{:S(2)}, u32[]{:S(2)}) collective-permute-start(bf16[16,2048]{1,0:T(8,128)(2,1)S(1)} %collective-permute-done.2.refs_3_), channel_id=1, source_target_pairs={{0,4},{4,0},{8,12},{12,8},{16,20},{20,16},{24,28},{28,24},{1,5},{5... | collective-permute-start | bytes 196616 | tf_op jit(solution)/shard_map/ppermute | solution.py:32
  16.0 9.9 %collective-permute-start.7 = (bf16[3,64,768]{2,1,0:T(8,128)(2,1)S(1)}, bf16[3,64,768]{2,1,0:T(8,128)(2,1)S(1)}, u32[]{:S(2)}, u32[]{:S(2)}) collective-permute-start(bf16[3,64,768]{2,1,0:T(8,128)(2,1)S(1)} %get-tuple-element.77), channel_id=1, source_target_pairs={{0,1},{1,0},{2,3},{3,2},{4,5},{5,4},{6,7},{7,6},{8,9},{9,8},{10,11... | collective-permute-start | bytes 884744 | tf_op jit(solution)/shard_map/ppermute | solution.py:32
  21.8 15.3 %collective-permute-start.8 = (bf16[3,64,768]{2,1,0:T(8,128)(2,1)S(1)}, bf16[3,64,768]{2,1,0:T(8,128)(2,1)S(1)}, u32[]{:S(2)}, u32[]{:S(2)}) collective-permute-start(bf16[3,64,768]{2,1,0:T(8,128)(2,1)S(1)} %get-tuple-element.82), channel_id=1, source_target_pairs={{0,1},{1,0},{2,3},{3,2},{4,5},{5,4},{6,7},{7,6},{8,9},{9,8},{10,11... | collective-permute-start | bytes 884744 | tf_op jit(solution)/shard_map/ppermute | solution.py:32
  25.9 15.6 %collective-permute-start.9 = (bf16[3,64,768]{2,1,0:T(8,128)(2,1)S(1)}, bf16[3,64,768]{2,1,0:T(8,128)(2,1)S(1)}, u32[]{:S(2)}, u32[]{:S(2)}) collective-permute-start(bf16[3,64,768]{2,1,0:T(8,128)(2,1)S(1)} %get-tuple-element.83), channel_id=1, source_target_pairs={{0,2},{1,3},{2,0},{3,1},{4,6},{5,7},{6,4},{7,5},{8,10},{9,11},{10,... | collective-permute-start | bytes 884744 | tf_op jit(solution)/shard_map/ppermute | solution.py:32
  41.7 11.0 %collective-permute-start.11 = (bf16[3,64,768]{2,1,0:T(8,128)(2,1)S(1)}, bf16[3,64,768]{2,1,0:T(8,128)(2,1)S(1)}, u32[]{:S(2)}, u32[]{:S(2)}) collective-permute-start(bf16[3,64,768]{2,1,0:T(8,128)(2,1)S(1)} %get-tuple-element.89.refs_0_), channel_id=1, source_target_pairs={{0,1},{1,0},{2,3},{3,2},{4,5},{5,4},{6,7},{7,6},{8,9},{9,8},{10,11... | collective-permute-start | bytes 884744 | tf_op jit(solution)/shard_map/ppermute | solution.py:32
  45.1 13.7 %collective-permute-start.13 = (bf16[2,64,768]{2,1,0:T(8,128)(2,1)S(1)}, bf16[2,64,768]{2,1,0:T(8,128)(2,1)S(1)}, u32[]{:S(2)}, u32[]{:S(2)}) collective-permute-start(bf16[2,64,768]{2,1,0:T(8,128)(2,1)S(1)} %get-tuple-element.98), channel_id=1, source_target_pairs={{0,2},{1,3},{2,0},{3,1},{4,6},{5,7},{6,4},{7,5},{8,10},{9,11},{10,... | collective-permute-start | bytes 589832 | tf_op jit(solution)/shard_map/ppermute | solution.py:32
  48.5 11.4 %collective-permute-start.10 = (bf16[64,768]{1,0:T(8,128)(2,1)S(1)}, bf16[64,768]{1,0:T(8,128)(2,1)S(1)}, u32[]{:S(2)}, u32[]{:S(2)}) collective-permute-start(bf16[64,768]{1,0:T(8,128)(2,1)S(1)} %get-tuple-element.87), channel_id=1, source_target_pairs={{0,2},{1,3},{2,0},{3,1},{4,6},{5,7},{6,4},{7,5},{8,10},{9,11},{10,... | collective-permute-start | bytes 294920 | tf_op jit(solution)/shard_map/ppermute | solution.py:32
  58.8 8.2 %collective-permute-start.14 = (bf16[2,64,768]{2,1,0:T(8,128)(2,1)S(1)}, bf16[2,64,768]{2,1,0:T(8,128)(2,1)S(1)}, u32[]{:S(2)}, u32[]{:S(2)}) collective-permute-start(bf16[2,64,768]{2,1,0:T(8,128)(2,1)S(1)} %collective-permute-done.13.refs_1_), channel_id=1, source_target_pairs={{0,1},{1,0},{2,3},{3,2},{4,5},{5,4},{6,7},{7,6},{8,9},{9,8},{10,11... | collective-permute-start | bytes 589832 | tf_op jit(solution)/shard_map/ppermute | solution.py:32
  60.0 7.0 %collective-permute-start.12 = (bf16[64,768]{1,0:T(8,128)(2,1)S(1)}, bf16[64,768]{1,0:T(8,128)(2,1)S(1)}, u32[]{:S(2)}, u32[]{:S(2)}) collective-permute-start(bf16[64,768]{1,0:T(8,128)(2,1)S(1)} %collective-permute-done.10.refs_0_), channel_id=1, source_target_pairs={{0,1},{1,0},{2,3},{3,2},{4,5},{5,4},{6,7},{7,6},{8,9},{9,8},{10,11... | collective-permute-start | bytes 294920 | tf_op jit(solution)/shard_map/ppermute | solution.py:32
  69.6 2.0 %collective-permute-start.15 = (f32[2,32,2048]{2,1,0:T(8,128)S(1)}, f32[2,32,2048]{2,1,0:T(8,128)S(1)}, u32[]{:S(2)}, u32[]{:S(2)}) collective-permute-start(f32[2,32,2048]{2,1,0:T(8,128)S(1)} %get-tuple-element.102), channel_id=1, source_target_pairs={{0,4},{4,0},{8,12},{12,8},{16,20},{20,16},{24,28},{28,24},{1,5},{5... | collective-permute-start | bytes 1572872 | tf_op jit(solution)/shard_map/ppermute | solution.py:32
  71.6 7.6 %collective-permute-start.16 = (bf16[2,8,2048]{2,1,0:T(8,128)(2,1)S(1)}, bf16[2,8,2048]{2,1,0:T(8,128)(2,1)S(1)}, u32[]{:S(2)}, u32[]{:S(2)}) collective-permute-start(bf16[2,8,2048]{2,1,0:T(8,128)(2,1)S(1)} %get-tuple-element.104), channel_id=1, source_target_pairs={{0,8},{4,12},{8,0},{12,4},{16,24},{20,28},{24,16},{28,20},{1,9},{5... | collective-permute-start | bytes 196616 | tf_op jit(solution)/shard_map/ppermute | solution.py:32
  73.2 6.1 %collective-permute-start.17 = (bf16[2,8,2048]{2,1,0:T(8,128)(2,1)S(1)}, bf16[2,8,2048]{2,1,0:T(8,128)(2,1)S(1)}, u32[]{:S(2)}, u32[]{:S(2)}) collective-permute-start(bf16[2,8,2048]{2,1,0:T(8,128)(2,1)S(1)} %get-tuple-element.105), channel_id=1, source_target_pairs={{0,16},{4,20},{8,24},{12,28},{16,0},{20,4},{24,8},{28,12},{1,17},{... | collective-permute-start | bytes 196616 | tf_op jit(solution)/shard_map/ppermute | solution.py:32
  74.7 5.2 %collective-permute-start.18 = (bf16[2,8,2048]{2,1,0:T(8,128)(2,1)S(1)}, bf16[2,8,2048]{2,1,0:T(8,128)(2,1)S(1)}, u32[]{:S(2)}, u32[]{:S(2)}) collective-permute-start(bf16[2,8,2048]{2,1,0:T(8,128)(2,1)S(1)} %get-tuple-element.106), channel_id=1, source_target_pairs={{0,24},{4,28},{8,16},{12,20},{16,8},{20,12},{24,0},{28,4},{1,25},{... | collective-permute-start | bytes 196616 | tf_op jit(solution)/shard_map/ppermute | solution.py:32

commit v10 on v9

--- a/solution.py
+++ b/solution.py
@@ -143,13 +143,17 @@
     )(*in_hbm(weights), *after)
 
 
-def sums_kernel(following, tok, grad, gate_b, up_b, down_b, *refs):
+def sums_kernel(following, apart, after, tok, grad, gate_b, up_b, down_b, *refs):
     copies = []
     if following is not None:
-        hbm, out, kept, sems = refs[:3], refs[3], refs[4:7], refs[7]
-        copies = fetches(following, hbm, kept, sems)
+        hbm, refs = refs[:3], refs[3:]
+    refs = refs[after:]
+    if apart:
+        out, back = refs[:2]
     else:
-        (out,) = refs
+        out, back = refs[0], refs[0].at[2]
+    if following is not None:
+        copies = fetches(following, hbm, refs[1 + apart : 4 + apart], refs[4 + apart])
     for copy in copies:
         copy.start()
 
@@ -157,49 +161,52 @@
     def _():
         out[0] = dot(tok[...], gate_b[...]).astype(out.dtype)
         out[1] = dot(tok[...], up_b[...]).astype(out.dtype)
-        out[2] = back_dot(grad[...], down_b[...]).astype(out.dtype)
+        back[...] = back_dot(grad[...], down_b[...]).astype(out.dtype)
 
     for copy in copies:
         copy.wait()
 
 
-def partial_sums(block, tok, grad, dtype, weights=None, following=None):
+def partial_sums(
+    block, tok, grad, dtype, weights=None, following=None, apart=False, after=()
+):
     total, width = tok.shape
     units = block[2].shape[0]
     more = following is not None
     shapes = block_shapes(units, width) if more else []
-    return pl.pallas_call(
-        functools.partial(sums_kernel, following),
-        in_specs=[WHOLE] * 5 + [HOLD] * (3 * more),
-        out_specs=[WHOLE] * (1 + 3 * more),
+    sums = [(2, total, units), (total, units)] if apart else [(3, total, units)]
+    return pl.pallas_call(
+        functools.partial(sums_kernel, following, apart, len(after)),
+        in_specs=[WHOLE] * 5 + [HOLD] * (3 * more + len(after)),
+        out_specs=[WHOLE] * (len(sums) + 3 * more),
         scratch_shapes=[pltpu.SemaphoreType.DMA((FETCHES, 3))] * more,
-        out_shape=[array((3, total, units), dtype)] + [vmem_array(x) for x in shapes],
+        out_shape=[array(x, dtype) for x in sums] + [vmem_array(x) for x in shapes],
         compiler_params=PARAMS,
         cost_estimate=estimate(6 * total * width * units, 6 * width * units),
         name="partial_sums",
-    )(tok, grad, *in_vmem(block), *(in_hbm(weights) if more else ()))
-
-
-def combine_kernel(own, other, out, token):
+    )(tok, grad, *in_vmem(block), *(in_hbm(weights) if more else ()), *after)
+
+
+def combine_kernel(own, other, *refs):
+    out, token = refs[-2:]
     token[...] = jnp.zeros_like(token)
     out[...] = (own[...] + other[...].astype(F32)).astype(BF16)
 
 
-def combine(own, other):
+def combine(own, other, after=()):
     return pl.pallas_call(
         combine_kernel,
+        in_specs=[WHOLE, WHOLE] + [HOLD] * len(after),
         out_shape=[array(own.shape, BF16), array((8, 128), F32)],
         compiler_params=PARAMS,
         cost_estimate=estimate(own.size, 8 * own.size),
         name="combine",
-    )(own, other)
-
-
-def activate_kernel(own, *refs):
-    others, (out, hidden, deltas) = refs[:-3], refs[-3:]
-    gate, up, hidden_grad = (
-        functools.reduce(lambda s, o: s + o[j].astype(F32), others, own[j]) for j in range(3)
-    )
+    )(own, other, *after)
+
+
+def activate_kernel(own, near, far, far_back, out, hidden, deltas):
+    gate, up = (own[j] + near[j].astype(F32) + far[j].astype(F32) for j in range(2))
+    hidden_grad = own[2] + near[2].astype(F32) + far_back[...].astype(F32)
     sig = jax.nn.sigmoid(gate)
     swish = gate * sig
     out[0] = (swish * up).astype(BF16)
@@ -223,10 +230,10 @@
     refs = list(refs)
     if apart:
         hidden, deltas = refs.pop(0), refs.pop(0)
-        act = hidden[...], deltas[0], deltas[1]
+        act = hidden, deltas.at[0], deltas.at[1]
     else:
         whole = refs.pop(0)
-        act = whole[0], whole[1], whole[2]
+        act = whole.at[0], whole.at[1], whole.at[2]
     leaving = []
     if with_products:
         gate_w, up_w, down_w = (refs.pop(0) for _ in range(3))
@@ -239,13 +246,13 @@
         refs = refs[:-3]
         units, width = down_s.shape
         part, rows = width // CHUNKS, units // CHUNKS
-        hidden_t = act[0].astype(F32).T.astype(BF16)
+        hidden_t = act[0][...].astype(F32).T.astype(BF16)
         mine = unit_block(k, units)
         start = jnp.bitwise_xor(lax.axis_index("col"), k) * units
         for i in range(CHUNKS):
             here, some = span(i, part), span(i, rows)
-            gate_s[here] = dot(tok_t[here], act[1]).astype(BF16)
-            up_s[here] = dot(tok_t[here], act[2]).astype(BF16)
+            gate_s[here] = dot(tok_t[here], act[1][...]).astype(BF16)
+            up_s[here] = dot(tok_t[here], act[2][...]).astype(BF16)
             down_s[some] = dot(hidden_t[some], grad[...]).astype(BF16)
             there = pl.ds(i * part, part)
             below = pl.ds(pl.multiple_of(start + i * rows, rows), rows)
@@ -262,8 +269,8 @@
         outs = refs[-1 - last :]
         for i in range(down_w.shape[1] // PIECE):
             here = span(i, PIECE)
-            back = back_dot(act[1], gate_w[here]) + back_dot(act[2], up_w[here])
-            for j, term in enumerate((dot(act[0], down_w[:, here]), back)):
+            back = back_dot(act[1][...], gate_w[here]) + back_dot(act[2][...], up_w[here])
+            for j, term in enumerate((dot(act[0][...], down_w[:, here]), back)):
                 term = term if first else before[j, :, here] + term
                 if last:
                     half = term.shape[0] // 2
@@ -375,16 +382,23 @@
     tok, grad, tok_t = assemble(even + odd, rows)
     sides = (tok_t, grad, all_units)
 
-    there, *near_weights = partial_sums(last_weights, tok, grad, BF16, weights, 1)
-    near = along_col(there, k=1)
-    there, *far_weights = partial_sums(near_weights, tok, grad, BF16, weights, 2)
+    sums = functools.partial(partial_sums, tok=tok, grad=grad)
+    there, back, *far_weights = sums(
+        last_weights, dtype=BF16, weights=weights, following=2, apart=True
+    )
+    near_back, near = along_col(back, k=1), along_col(there, k=1)
+    here, back, *near_weights = sums(
+        far_weights, dtype=F32, weights=weights, following=1, apart=True
+    )
+    pair_back, token = combine(back, near_back)
+    far_back = along_col(pair_back, k=2)
+    (there,) = sums(near_weights, dtype=BF16, after=(token,))
     from_near = along_col(there, k=1)
-    (here,) = partial_sums(far_weights, tok, grad, F32)
-    pair, token = combine(here, near)
+    pair, token = combine(here, near, after=(there, far_back))
     from_far = along_col(pair, k=2)
     own_weights = load(0, weights, units, after=(token,))
-    (here,) = partial_sums(own_weights, tok, grad, F32)
-    own, hidden, deltas = activate(here, [from_near, from_far])
+    (here,) = sums(own_weights, dtype=F32)
+    own, hidden, deltas = activate(here, [from_near, from_far, far_back])
 
     near_act = along_col(own, k=1)
     (terms,) = use(0, (own,), own_weights)

time: 80.7 us -> 82.4 us (1.021)
  starting transfers between devices: 20 us -> 24.8 us
  waiting for transfers between devices: 12.5 us -> 10.1 us
    ppermute x19 -> x21, starting transfers between devices: 20 us -> 24.8 us  [swap(): return lax.ppermute(x, axis, [(i, i ^ k) for i in range(size)])]
    ppermute x19 -> x21, waiting for transfers between devices: 12.5 us -> 10.1 us  [swap(): return lax.ppermute(x, axis, [(i, i ^ k) for i in range(size)])]
    pallas_call x5 -> x6, Pallas kernels: 12.3 us -> 12.3 us  [the longest x4 12.3 us: partial_sums(): pl.pallas_call(functools.partial(sums_kernel, following, apart, len(after...]
  transfers between devices with their start and end apart: 19 -> 21, of which waited for: 11 -> 10; matrix products, arithmetic and copies ran while one was open for 0% -> 0% of each run, Pallas kernels for 48% -> 46%
where the time goes in v10:
time: 82.4 us; the launch traced here: 82.3 us
  Pallas kernels  46.6 us (57%)
  starting transfers between devices  24.8 us (30%)
  waiting for transfers between devices  10.1 us (12%)
  between operations  0.83 us (1%)
    ppermute x21, starting transfers between devices, swap(): return lax.ppermute(x, axis, [(i, i ^ k) for i in range(size)])  24.8 us
    pallas_call x6, Pallas kernels, use(): pl.pallas_call(functools.partial(use_kernel, k, first, last, weights is n...  24.7 us
    pallas_call x4, Pallas kernels, partial_sums(): pl.pallas_call(functools.partial(sums_kernel, following, apart, len(after...  12.3 us
    ppermute x21, waiting for transfers between devices, swap(): return lax.ppermute(x, axis, [(i, i ^ k) for i in range(size)])  10.1 us
    pallas_call x2, Pallas kernels, load(): pl.pallas_call(functools.partial(load_kernel, k), in_specs=[HOLD] * (3 +...  7.65 us
  transfers between devices with their start and end apart: 21, of which 10 were waited for; matrix products, arithmetic and copies ran while one was open for 0% of the time, Pallas kernels for 46%

profile of v10, /device:TPU:0, one launch (start us, length us, event | category | flops | bytes accessed | tf_op | source)
XLA Modules:
  0.0 82.3 jit_solution(12068788533765252331)
XLA Ops:
  0.6 0.8 pack.1.refs_0_
  1.4 3.9 %collective-permute-start.2 = (bf16[16,2048]{1,0:T(8,128)(2,1)S(1)}, bf16[16,2048]{1,0:T(8,128)(2,1)S(1)}, u32[]{:S(2)}, u32[]{:S(2)}) collective-permute-start(bf16[16,2048]{1,0:T(8,128)(2,1)S(1)} %pack.1.refs_0_), channel_id=1, source_target_pairs={{0,24},{4,28},{8,16},{12,20},{16,8},{20,12},{24,0},{28,4},{1,25},{... | collective-permute-start | bytes 196616 | tf_op jit(solution)/shard_map/ppermute | solution.py:32
  5.3 0.5 collective-permute-start.1
  5.8 0.1 collective-permute-start
  5.9 0.0 collective-permute-start.3
  5.9 3.8 %load.2 = (bf16[2048,768]{1,0:T(8,128)(2,1)S(1)}, bf16[2048,768]{1,0:T(8,128)(2,1)S(1)}, bf16[768,2048]{1,0:T(8,128)(2,1)S(1)}) custom-call(bf16[2048,3072]{1,0:T(8,128)(2,1)} %refs_0_.7, bf16[2048,3072]{1,0:T(8,128)(2,1)} %refs_1_.7, bf16[3072,2048]{1,0:T(8,128)(2,1)} %refs_2_.7), custom_call_target="tpu_custom_call" | custom-call | bytes 1179648 | tf_op jit(solution)/shard_map/load/pallas_call | solution.py:134
  9.8 0.3 collective-permute-done.refs_1_
  10.1 0.3 collective-permute-start.4
  10.4 0.2 collective-permute-start.5
  10.6 0.3 collective-permute-start.6
  10.9 0.4 collective-permute-done.4.refs_5_
  11.3 0.3 collective-permute-done.5.refs_6_
  11.6 0.2 collective-permute-done.6.refs_7_
  11.8 0.2 assemble.1
  12.1 3.9 %partial_sums.4 = (bf16[2,64,768]{2,1,0:T(8,128)(2,1)S(1)}, bf16[64,768]{1,0:T(8,128)(2,1)S(1)}, bf16[2048,768]{1,0:T(8,128)(2,1)S(1)}, bf16[2048,768]{1,0:T(8,128)(2,1)S(1)}, bf16[768,2048]{1,0:T(8,128)(2,1)S(1)}) custom-call(bf16[64,2048]{1,0:T(8,128)(2,1)S(1)} %get-tuple-element.70.tok, ...), custom_call_target="tpu_custom_call" | custom-call | flops 75497472 | bytes 1179648 | tf_op jit(solution)/shard_map/partial_sums/pallas_call | solution.py:178
  15.9 2.0 %collective-permute-start.8 = (bf16[64,768]{1,0:T(8,128)(2,1)S(1)}, bf16[64,768]{1,0:T(8,128)(2,1)S(1)}, u32[]{:S(2)}, u32[]{:S(2)}) collective-permute-start(bf16[64,768]{1,0:T(8,128)(2,1)S(1)} %get-tuple-element.84), channel_id=1, source_target_pairs={{0,1},{1,0},{2,3},{3,2},{4,5},{5,4},{6,7},{7,6},{8,9},{9,8},{10,11... | collective-permute-start | bytes 294920 | tf_op jit(solution)/shard_map/ppermute | solution.py:32
  17.9 0.1 collective-permute-start.7
  18.0 3.9 %partial_sums.5 = (f32[2,64,768]{2,1,0:T(8,128)S(1)}, f32[64,768]{1,0:T(8,128)S(1)}, bf16[2048,768]{1,0:T(8,128)(2,1)S(1)}, bf16[2048,768]{1,0:T(8,128)(2,1)S(1)}, bf16[768,2048]{1,0:T(8,128)(2,1)S(1)}) custom-call(bf16[64,2048]{1,0:T(8,128)(2,1)S(1)} %get-tuple-element.70.tok, bf16[64,2048]{1,0:T(8,128)(2,1)S(1)} %get-tuple-element.71.grad.refs_2_.refs_6_.refs_7_.refs_3_, ...), custom_call_target="tpu_custom_call" | custom-call | flops 75497472 | bytes 1179648 | tf_op jit(solution)/shard_map/partial_sums/pallas_call | solution.py:178
  22.0 3.0 %collective-permute-start.9 = (bf16[64,768]{1,0:T(8,128)(2,1)S(1)}, bf16[64,768]{1,0:T(8,128)(2,1)S(1)}, u32[]{:S(2)}, u32[]{:S(2)}) collective-permute-start(bf16[64,768]{1,0:T(8,128)(2,1)S(1)} %get-tuple-element.86), channel_id=1, source_target_pairs={{0,2},{1,3},{2,0},{3,1},{4,6},{5,7},{6,4},{7,5},{8,10},{9,11},{10,... | collective-permute-start | bytes 294920 | tf_op jit(solution)/shard_map/ppermute | solution.py:32
  25.0 2.2 %partial_sums.6.refs_0_ = bf16[3,64,768]{2,1,0:T(8,128)(2,1)S(1)} custom-call(bf16[64,2048]{1,0:T(8,128)(2,1)S(1)} %get-tuple-element.70.tok, bf16[64,2048]{1,0:T(8,128)(2,1)S(1)} %get-tuple-element.71.grad.refs_2_.refs_6_.refs_7_.refs_3_, bf16[2048,768]{1,0:T(8,128)(2,1)S(1)} %get-tuple-element.80.gate_b.refs_1_, ...), custom_call_target="tpu_custom_call" | custom-call | flops 75497472 | bytes 1179648 | tf_op jit(solution)/shard_map/partial_sums/pallas_call | solution.py:178
  27.1 1.7 %collective-permute-start.10 = (bf16[3,64,768]{2,1,0:T(8,128)(2,1)S(1)}, bf16[3,64,768]{2,1,0:T(8,128)(2,1)S(1)}, u32[]{:S(2)}, u32[]{:S(2)}) collective-permute-start(bf16[3,64,768]{2,1,0:T(8,128)(2,1)S(1)} %partial_sums.6.refs_0_), channel_id=1, source_target_pairs={{0,1},{1,0},{2,3},{3,2},{4,5},{5,4},{6,7},{7,6},{8,9},{9,8},{10,11... | collective-permute-start | bytes 884744 | tf_op jit(solution)/shard_map/ppermute | solution.py:32
  28.8 0.0 collective-permute-done.7.other
  28.9 1.8 %collective-permute-start.11 = (bf16[2,64,768]{2,1,0:T(8,128)(2,1)S(1)}, bf16[2,64,768]{2,1,0:T(8,128)(2,1)S(1)}, u32[]{:S(2)}, u32[]{:S(2)}) collective-permute-start(bf16[2,64,768]{2,1,0:T(8,128)(2,1)S(1)} %get-tuple-element.91), channel_id=1, source_target_pairs={{0,2},{1,3},{2,0},{3,1},{4,6},{5,7},{6,4},{7,5},{8,10},{9,11},{10,... | collective-permute-start | bytes 589832 | tf_op jit(solution)/shard_map/ppermute | solution.py:32
  30.6 3.8 %load.3 = (bf16[2048,768]{1,0:T(8,128)(2,1)S(1)}, bf16[2048,768]{1,0:T(8,128)(2,1)S(1)}, bf16[768,2048]{1,0:T(8,128)(2,1)S(1)}) custom-call(bf16[2048,3072]{1,0:T(8,128)(2,1)} %refs_0_.7, bf16[2048,3072]{1,0:T(8,128)(2,1)} %refs_1_.7, bf16[3072,2048]{1,0:T(8,128)(2,1)} %refs_2_.7, f32[8,128]{1,0:T(8,128)S(1)} %get-tuple-element.87.refs_3_), custom_call_target="tpu_custom_call" | custom-call | bytes 1179648 | tf_op jit(solution)/shard_map/load/pallas_call | solution.py:134
  34.4 2.3 %partial_sums.7.own = f32[3,64,768]{2,1,0:T(8,128)S(1)} custom-call(bf16[64,2048]{1,0:T(8,128)(2,1)S(1)} %get-tuple-element.70.tok, bf16[64,2048]{1,0:T(8,128)(2,1)S(1)} %get-tuple-element.71.grad.refs_2_.refs_6_.refs_7_.refs_3_, bf16[2048,768]{1,0:T(8,128)(2,1)S(1)} %get-tuple-element.88.gate_b.refs_1_, ...), custom_call_target="tpu_custom_call" | custom-call | flops 75497472 | bytes 1179648 | tf_op jit(solution)/shard_map/partial_sums/pallas_call | solution.py:178
  36.8 2.2 %collective-permute-done.11.far = bf16[2,64,768]{2,1,0:T(8,128)(2,1)S(1)} collective-permute-done((bf16[2,64,768]{2,1,0:T(8,128)(2,1)S(1)}, bf16[2,64,768]{2,1,0:T(8,128)(2,1)S(1)}, u32[]{:S(2)}, u32[]{:S(2)}) %collective-permute-start.11) | collective-permute-done | bytes 196640 | tf_op jit(solution)/shard_map/ppermute | solution.py:32
  39.0 0.8 %collective-permute-done.10.near = bf16[3,64,768]{2,1,0:T(8,128)(2,1)S(1)} collective-permute-done((bf16[3,64,768]{2,1,0:T(8,128)(2,1)S(1)}, bf16[3,64,768]{2,1,0:T(8,128)(2,1)S(1)}, u32[]{:S(2)}, u32[]{:S(2)}) %collective-permute-start.10) | collective-permute-done | bytes 294944 | tf_op jit(solution)/shard_map/ppermute | solution.py:32
  39.8 0.2 activate.1
  40.1 2.9 %collective-permute-start.13 = (bf16[3,64,768]{2,1,0:T(8,128)(2,1)S(1)}, bf16[3,64,768]{2,1,0:T(8,128)(2,1)S(1)}, u32[]{:S(2)}, u32[]{:S(2)}) collective-permute-start(bf16[3,64,768]{2,1,0:T(8,128)(2,1)S(1)} %get-tuple-element.97.refs_0_), channel_id=1, source_target_pairs={{0,1},{1,0},{2,3},{3,2},{4,5},{5,4},{6,7},{7,6},{8,9},{9,8},{10,11... | collective-permute-start | bytes 884744 | tf_op jit(solution)/shard_map/ppermute | solution.py:32
  42.9 2.5 %products.2.refs_4_ = f32[2,64,2048]{2,1,0:T(8,128)S(1)} custom-call(bf16[3,64,768]{2,1,0:T(8,128)(2,1)S(1)} %get-tuple-element.97.refs_0_, bf16[2048,768]{1,0:T(8,128)(2,1)S(1)} %get-tuple-element.88.gate_b.refs_1_, bf16[2048,768]{1,0:T(8,128)(2,1)S(1)} %get-tuple-element.89.up_b.refs_2_, bf16[768,2048]{1,0:T(8,128)(2,1)S(1)} %get-tuple-element.90.down_b.refs_3_), custom_call_target="tpu_custom_call" | custom-call | flops 75497472 | bytes 1179648 | tf_op jit(solution)/shard_map/products/pallas_call | solution.py:317
  45.5 3.4 %collective-permute-start.15 = (bf16[2,64,768]{2,1,0:T(8,128)(2,1)S(1)}, bf16[2,64,768]{2,1,0:T(8,128)(2,1)S(1)}, u32[]{:S(2)}, u32[]{:S(2)}) collective-permute-start(bf16[2,64,768]{2,1,0:T(8,128)(2,1)S(1)} %get-tuple-element.106), channel_id=1, source_target_pairs={{0,2},{1,3},{2,0},{3,1},{4,6},{5,7},{6,4},{7,5},{8,10},{9,11},{10,... | collective-permute-start | bytes 589832 | tf_op jit(solution)/shard_map/ppermute | solution.py:32
  48.9 0.1 collective-permute-start.12
  49.0 4.1 %grads.2 = (bf16[2048,3072]{1,0:T(8,128)(2,1)}, bf16[2048,3072]{1,0:T(8,128)(2,1)}, bf16[3072,2048]{1,0:T(8,128)(2,1)}) custom-call(bf16[3,64,768]{2,1,0:T(8,128)(2,1)S(1)} %get-tuple-element.97.refs_0_, bf16[2048,64]{1,0:T(8,128)(2,1)S(1)} %get-tuple-element.96.refs_1_.refs_5_.refs_6_.refs_2_, ...), custom_call_target="tpu_custom_call" | custom-call | flops 75497472 | bytes 1179648 | tf_op jit(solution)/shard_map/grads/pallas_call | solution.py:317
  53.1 5.3 %productsgrads.2 = (f32[2,64,2048]{2,1,0:T(8,128)S(1)}, bf16[2048,3072]{1,0:T(8,128)(2,1)}, bf16[2048,3072]{1,0:T(8,128)(2,1)}, bf16[3072,2048]{1,0:T(8,128)(2,1)}) custom-call(bf16[3,64,768]{2,1,0:T(8,128)(2,1)S(1)} %collective-permute-done.13.refs_0_, ...), custom_call_target="tpu_custom_call", output_to_operand_aliasing={{1}: (7, {}), {2}: (8, {}), {3}: (9, {})} | custom-call | flops 150994944 | bytes 2359296 | tf_op jit(solution)/shard_map/productsgrads/pallas_call | solution.py:317
  58.4 2.2 %collective-permute-done.15.refs_1_ = bf16[2,64,768]{2,1,0:T(8,128)(2,1)S(1)} collective-permute-done((bf16[2,64,768]{2,1,0:T(8,128)(2,1)S(1)}, bf16[2,64,768]{2,1,0:T(8,128)(2,1)S(1)}, u32[]{:S(2)}, u32[]{:S(2)}) %collective-permute-start.15) | collective-permute-done | bytes 196640 | tf_op jit(solution)/shard_map/ppermute | solution.py:32
  60.6 1.1 %collective-permute-done.12.refs_0_ = bf16[64,768]{1,0:T(8,128)(2,1)S(1)} collective-permute-done((bf16[64,768]{1,0:T(8,128)(2,1)S(1)}, bf16[64,768]{1,0:T(8,128)(2,1)S(1)}, u32[]{:S(2)}, u32[]{:S(2)}) %collective-permute-start.12) | collective-permute-done | bytes 98336 | tf_op jit(solution)/shard_map/ppermute | solution.py:32
  61.6 0.9 %collective-permute-start.14 = (bf16[64,768]{1,0:T(8,128)(2,1)S(1)}, bf16[64,768]{1,0:T(8,128)(2,1)S(1)}, u32[]{:S(2)}, u32[]{:S(2)}) collective-permute-start(bf16[64,768]{1,0:T(8,128)(2,1)S(1)} %collective-permute-done.12.refs_0_), channel_id=1, source_target_pairs={{0,1},{1,0},{2,3},{3,2},{4,5},{5,4},{6,7},{7,6},{8,9},{9,8},{10,11... | collective-permute-start | bytes 294920 | tf_op jit(solution)/shard_map/ppermute | solution.py:32
  62.6 6.2 %productsgrads.3 = (f32[2,64,2048]{2,1,0:T(8,128)S(1)}, bf16[2048,3072]{1,0:T(8,128)(2,1)}, bf16[2048,3072]{1,0:T(8,128)(2,1)}, bf16[3072,2048]{1,0:T(8,128)(2,1)}) custom-call(bf16[64,768]{1,0:T(8,128)(2,1)S(1)} %collective-permute-done.12.refs_0_, ...), custom_call_target="tpu_custom_call", output_to_operand_aliasing={{1}: (8, {}), {2}: (9, {}), {3}: (10, {})} | custom-call | flops 150994944 | bytes 2359296 | tf_op jit(solution)/shard_map/productsgrads/pallas_call | solution.py:317
  68.8 2.5 %products.3 = (f32[2,32,2048]{2,1,0:T(8,128)S(1)}, f32[2,32,2048]{2,1,0:T(8,128)S(1)}) custom-call(bf16[64,768]{1,0:T(8,128)(2,1)S(1)} %collective-permute-done.14.refs_0_, bf16[2,64,768]{2,1,0:T(8,128)(2,1)S(1)} %collective-permute-done.16.refs_1_, bf16[2048,768]{1,0:T(8,128)(2,1)S(1)} %get-tuple-element.72.gate_b.refs_2_, ...), custom_call_target="tpu_custom_call" | custom-call | flops 75497472 | bytes 1179648 | tf_op jit(solution)/shard_map/products/pallas_call | solution.py:317
  71.3 0.1 collective-permute-start.17
  71.4 1.9 %collective-permute-done.17.other = f32[2,32,2048]{2,1,0:T(8,128)S(1)} collective-permute-done((f32[2,32,2048]{2,1,0:T(8,128)S(1)}, f32[2,32,2048]{2,1,0:T(8,128)S(1)}, u32[]{:S(2)}, u32[]{:S(2)}) %collective-permute-start.17) | collective-permute-done | bytes 524320 | tf_op jit(solution)/shard_map/ppermute | solution.py:32
  73.3 0.1 fold.1
  73.4 1.6 %collective-permute-start.18 = (bf16[2,8,2048]{2,1,0:T(8,128)(2,1)S(1)}, bf16[2,8,2048]{2,1,0:T(8,128)(2,1)S(1)}, u32[]{:S(2)}, u32[]{:S(2)}) collective-permute-start(bf16[2,8,2048]{2,1,0:T(8,128)(2,1)S(1)} %get-tuple-element.112), channel_id=1, source_target_pairs={{0,8},{4,12},{8,0},{12,4},{16,24},{20,28},{24,16},{28,20},{1,9},{5... | collective-permute-start | bytes 196616 | tf_op jit(solution)/shard_map/ppermute | solution.py:32
  74.9 1.5 %collective-permute-start.19 = (bf16[2,8,2048]{2,1,0:T(8,128)(2,1)S(1)}, bf16[2,8,2048]{2,1,0:T(8,128)(2,1)S(1)}, u32[]{:S(2)}, u32[]{:S(2)}) collective-permute-start(bf16[2,8,2048]{2,1,0:T(8,128)(2,1)S(1)} %get-tuple-element.113), channel_id=1, source_target_pairs={{0,16},{4,20},{8,24},{12,28},{16,0},{20,4},{24,8},{28,12},{1,17},{... | collective-permute-start | bytes 196616 | tf_op jit(solution)/shard_map/ppermute | solution.py:32
  76.4 0.5 collective-permute-start.20
  76.9 4.1 %grads.3 = (bf16[2048,3072]{1,0:T(8,128)(2,1)}, bf16[2048,3072]{1,0:T(8,128)(2,1)}, bf16[3072,2048]{1,0:T(8,128)(2,1)}) custom-call(bf16[64,768]{1,0:T(8,128)(2,1)S(1)} %collective-permute-done.14.refs_0_, bf16[2,64,768]{2,1,0:T(8,128)(2,1)S(1)} %collective-permute-done.16.refs_1_, ...), custom_call_target="tpu_custom_call", output_to_operand_aliasing={{0}: (4, {}), {1}: (5, {}), {2}: (6, {})} | custom-call | flops 75497472 | bytes 1179648 | tf_op jit(solution)/shard_map/grads/pallas_call | solution.py:317
  81.0 0.6 collective-permute-done.20.refs_2_
  81.6 0.6 finish.1
  (13 shorter events, 0.1 us)
Async XLA Ops:
  1.4 8.4 %collective-permute-start.2 = (bf16[16,2048]{1,0:T(8,128)(2,1)S(1)}, bf16[16,2048]{1,0:T(8,128)(2,1)S(1)}, u32[]{:S(2)}, u32[]{:S(2)}) collective-permute-start(bf16[16,2048]{1,0:T(8,128)(2,1)S(1)} %pack.1.refs_0_), channel_id=1, source_target_pairs={{0,24},{4,28},{8,16},{12,20},{16,8},{20,12},{24,0},{28,4},{1,25},{... | collective-permute-start | bytes 196616 | tf_op jit(solution)/shard_map/ppermute | solution.py:32
  5.3 4.5 %collective-permute-start.1 = (bf16[16,2048]{1,0:T(8,128)(2,1)S(1)}, bf16[16,2048]{1,0:T(8,128)(2,1)S(1)}, u32[]{:S(2)}, u32[]{:S(2)}) collective-permute-start(bf16[16,2048]{1,0:T(8,128)(2,1)S(1)} %pack.1.refs_0_), channel_id=1, source_target_pairs={{0,16},{4,20},{8,24},{12,28},{16,0},{20,4},{24,8},{28,12},{1,17},{... | collective-permute-start | bytes 196616 | tf_op jit(solution)/shard_map/ppermute | solution.py:32
  5.8 4.3 %collective-permute-start = (bf16[16,2048]{1,0:T(8,128)(2,1)S(1)}, bf16[16,2048]{1,0:T(8,128)(2,1)S(1)}, u32[]{:S(2)}, u32[]{:S(2)}) collective-permute-start(bf16[16,2048]{1,0:T(8,128)(2,1)S(1)} %pack.1.refs_0_), channel_id=1, source_target_pairs={{0,8},{4,12},{8,0},{12,4},{16,24},{20,28},{24,16},{28,20},{1,9},{5... | collective-permute-start | bytes 196616 | tf_op jit(solution)/shard_map/ppermute | solution.py:32
  5.9 5.0 %collective-permute-start.3 = (bf16[16,2048]{1,0:T(8,128)(2,1)S(1)}, bf16[16,2048]{1,0:T(8,128)(2,1)S(1)}, u32[]{:S(2)}, u32[]{:S(2)}) collective-permute-start(bf16[16,2048]{1,0:T(8,128)(2,1)S(1)} %pack.1.refs_0_), channel_id=1, source_target_pairs={{0,4},{4,0},{8,12},{12,8},{16,20},{20,16},{24,28},{28,24},{1,5},{5... | collective-permute-start | bytes 196616 | tf_op jit(solution)/shard_map/ppermute | solution.py:32
  10.1 1.3 %collective-permute-start.4 = (bf16[16,2048]{1,0:T(8,128)(2,1)S(1)}, bf16[16,2048]{1,0:T(8,128)(2,1)S(1)}, u32[]{:S(2)}, u32[]{:S(2)}) collective-permute-start(bf16[16,2048]{1,0:T(8,128)(2,1)S(1)} %collective-permute-done.refs_1_), channel_id=1, source_target_pairs={{0,4},{4,0},{8,12},{12,8},{16,20},{20,16},{24,28},{28,24},{1,5},{5... | collective-permute-start | bytes 196616 | tf_op jit(solution)/shard_map/ppermute | solution.py:32
  10.4 1.3 %collective-permute-start.5 = (bf16[16,2048]{1,0:T(8,128)(2,1)S(1)}, bf16[16,2048]{1,0:T(8,128)(2,1)S(1)}, u32[]{:S(2)}, u32[]{:S(2)}) collective-permute-start(bf16[16,2048]{1,0:T(8,128)(2,1)S(1)} %collective-permute-done.1.refs_2_), channel_id=1, source_target_pairs={{0,4},{4,0},{8,12},{12,8},{16,20},{20,16},{24,28},{28,24},{1,5},{5... | collective-permute-start | bytes 196616 | tf_op jit(solution)/shard_map/ppermute | solution.py:32
  10.6 1.3 %collective-permute-start.6 = (bf16[16,2048]{1,0:T(8,128)(2,1)S(1)}, bf16[16,2048]{1,0:T(8,128)(2,1)S(1)}, u32[]{:S(2)}, u32[]{:S(2)}) collective-permute-start(bf16[16,2048]{1,0:T(8,128)(2,1)S(1)} %collective-permute-done.2.refs_3_), channel_id=1, source_target_pairs={{0,4},{4,0},{8,12},{12,8},{16,20},{20,16},{24,28},{28,24},{1,5},{5... | collective-permute-start | bytes 196616 | tf_op jit(solution)/shard_map/ppermute | solution.py:32
  15.9 6.0 %collective-permute-start.8 = (bf16[64,768]{1,0:T(8,128)(2,1)S(1)}, bf16[64,768]{1,0:T(8,128)(2,1)S(1)}, u32[]{:S(2)}, u32[]{:S(2)}) collective-permute-start(bf16[64,768]{1,0:T(8,128)(2,1)S(1)} %get-tuple-element.84), channel_id=1, source_target_pairs={{0,1},{1,0},{2,3},{3,2},{4,5},{5,4},{6,7},{7,6},{8,9},{9,8},{10,11... | collective-permute-start | bytes 294920 | tf_op jit(solution)/shard_map/ppermute | solution.py:32
  17.9 10.9 %collective-permute-start.7 = (bf16[2,64,768]{2,1,0:T(8,128)(2,1)S(1)}, bf16[2,64,768]{2,1,0:T(8,128)(2,1)S(1)}, u32[]{:S(2)}, u32[]{:S(2)}) collective-permute-start(bf16[2,64,768]{2,1,0:T(8,128)(2,1)S(1)} %get-tuple-element.79), channel_id=1, source_target_pairs={{0,1},{1,0},{2,3},{3,2},{4,5},{5,4},{6,7},{7,6},{8,9},{9,8},{10,11... | collective-permute-start | bytes 589832 | tf_op jit(solution)/shard_map/ppermute | solution.py:32
  22.0 6.8 %collective-permute-start.9 = (bf16[64,768]{1,0:T(8,128)(2,1)S(1)}, bf16[64,768]{1,0:T(8,128)(2,1)S(1)}, u32[]{:S(2)}, u32[]{:S(2)}) collective-permute-start(bf16[64,768]{1,0:T(8,128)(2,1)S(1)} %get-tuple-element.86), channel_id=1, source_target_pairs={{0,2},{1,3},{2,0},{3,1},{4,6},{5,7},{6,4},{7,5},{8,10},{9,11},{10,... | collective-permute-start | bytes 294920 | tf_op jit(solution)/shard_map/ppermute | solution.py:32
  27.1 12.7 %collective-permute-start.10 = (bf16[3,64,768]{2,1,0:T(8,128)(2,1)S(1)}, bf16[3,64,768]{2,1,0:T(8,128)(2,1)S(1)}, u32[]{:S(2)}, u32[]{:S(2)}) collective-permute-start(bf16[3,64,768]{2,1,0:T(8,128)(2,1)S(1)} %partial_sums.6.refs_0_), channel_id=1, source_target_pairs={{0,1},{1,0},{2,3},{3,2},{4,5},{5,4},{6,7},{7,6},{8,9},{9,8},{10,11... | collective-permute-start | bytes 884744 | tf_op jit(solution)/shard_map/ppermute | solution.py:32
  28.9 10.1 %collective-permute-start.11 = (bf16[2,64,768]{2,1,0:T(8,128)(2,1)S(1)}, bf16[2,64,768]{2,1,0:T(8,128)(2,1)S(1)}, u32[]{:S(2)}, u32[]{:S(2)}) collective-permute-start(bf16[2,64,768]{2,1,0:T(8,128)(2,1)S(1)} %get-tuple-element.91), channel_id=1, source_target_pairs={{0,2},{1,3},{2,0},{3,1},{4,6},{5,7},{6,4},{7,5},{8,10},{9,11},{10,... | collective-permute-start | bytes 589832 | tf_op jit(solution)/shard_map/ppermute | solution.py:32
  40.1 13.0 %collective-permute-start.13 = (bf16[3,64,768]{2,1,0:T(8,128)(2,1)S(1)}, bf16[3,64,768]{2,1,0:T(8,128)(2,1)S(1)}, u32[]{:S(2)}, u32[]{:S(2)}) collective-permute-start(bf16[3,64,768]{2,1,0:T(8,128)(2,1)S(1)} %get-tuple-element.97.refs_0_), channel_id=1, source_target_pairs={{0,1},{1,0},{2,3},{3,2},{4,5},{5,4},{6,7},{7,6},{8,9},{9,8},{10,11... | collective-permute-start | bytes 884744 | tf_op jit(solution)/shard_map/ppermute | solution.py:32
  45.5 15.1 %collective-permute-start.15 = (bf16[2,64,768]{2,1,0:T(8,128)(2,1)S(1)}, bf16[2,64,768]{2,1,0:T(8,128)(2,1)S(1)}, u32[]{:S(2)}, u32[]{:S(2)}) collective-permute-start(bf16[2,64,768]{2,1,0:T(8,128)(2,1)S(1)} %get-tuple-element.106), channel_id=1, source_target_pairs={{0,2},{1,3},{2,0},{3,1},{4,6},{5,7},{6,4},{7,5},{8,10},{9,11},{10,... | collective-permute-start | bytes 589832 | tf_op jit(solution)/shard_map/ppermute | solution.py:32
  48.9 12.7 %collective-permute-start.12 = (bf16[64,768]{1,0:T(8,128)(2,1)S(1)}, bf16[64,768]{1,0:T(8,128)(2,1)S(1)}, u32[]{:S(2)}, u32[]{:S(2)}) collective-permute-start(bf16[64,768]{1,0:T(8,128)(2,1)S(1)} %get-tuple-element.95), channel_id=1, source_target_pairs={{0,2},{1,3},{2,0},{3,1},{4,6},{5,7},{6,4},{7,5},{8,10},{9,11},{10,... | collective-permute-start | bytes 294920 | tf_op jit(solution)/shard_map/ppermute | solution.py:32
  60.6 8.2 %collective-permute-start.16 = (bf16[2,64,768]{2,1,0:T(8,128)(2,1)S(1)}, bf16[2,64,768]{2,1,0:T(8,128)(2,1)S(1)}, u32[]{:S(2)}, u32[]{:S(2)}) collective-permute-start(bf16[2,64,768]{2,1,0:T(8,128)(2,1)S(1)} %collective-permute-done.15.refs_1_), channel_id=1, source_target_pairs={{0,1},{1,0},{2,3},{3,2},{4,5},{5,4},{6,7},{7,6},{8,9},{9,8},{10,11... | collective-permute-start | bytes 589832 | tf_op jit(solution)/shard_map/ppermute | solution.py:32
  61.6 7.1 %collective-permute-start.14 = (bf16[64,768]{1,0:T(8,128)(2,1)S(1)}, bf16[64,768]{1,0:T(8,128)(2,1)S(1)}, u32[]{:S(2)}, u32[]{:S(2)}) collective-permute-start(bf16[64,768]{1,0:T(8,128)(2,1)S(1)} %collective-permute-done.12.refs_0_), channel_id=1, source_target_pairs={{0,1},{1,0},{2,3},{3,2},{4,5},{5,4},{6,7},{7,6},{8,9},{9,8},{10,11... | collective-permute-start | bytes 294920 | tf_op jit(solution)/shard_map/ppermute | solution.py:32
  71.3 2.0 %collective-permute-start.17 = (f32[2,32,2048]{2,1,0:T(8,128)S(1)}, f32[2,32,2048]{2,1,0:T(8,128)S(1)}, u32[]{:S(2)}, u32[]{:S(2)}) collective-permute-start(f32[2,32,2048]{2,1,0:T(8,128)S(1)} %get-tuple-element.110), channel_id=1, source_target_pairs={{0,4},{4,0},{8,12},{12,8},{16,20},{20,16},{24,28},{28,24},{1,5},{5... | collective-permute-start | bytes 1572872 | tf_op jit(solution)/shard_map/ppermute | solution.py:32
  73.4 7.6 %collective-permute-start.18 = (bf16[2,8,2048]{2,1,0:T(8,128)(2,1)S(1)}, bf16[2,8,2048]{2,1,0:T(8,128)(2,1)S(1)}, u32[]{:S(2)}, u32[]{:S(2)}) collective-permute-start(bf16[2,8,2048]{2,1,0:T(8,128)(2,1)S(1)} %get-tuple-element.112), channel_id=1, source_target_pairs={{0,8},{4,12},{8,0},{12,4},{16,24},{20,28},{24,16},{28,20},{1,9},{5... | collective-permute-start | bytes 196616 | tf_op jit(solution)/shard_map/ppermute | solution.py:32
  74.9 6.1 %collective-permute-start.19 = (bf16[2,8,2048]{2,1,0:T(8,128)(2,1)S(1)}, bf16[2,8,2048]{2,1,0:T(8,128)(2,1)S(1)}, u32[]{:S(2)}, u32[]{:S(2)}) collective-permute-start(bf16[2,8,2048]{2,1,0:T(8,128)(2,1)S(1)} %get-tuple-element.113), channel_id=1, source_target_pairs={{0,16},{4,20},{8,24},{12,28},{16,0},{20,4},{24,8},{28,12},{1,17},{... | collective-permute-start | bytes 196616 | tf_op jit(solution)/shard_map/ppermute | solution.py:32
  76.4 5.2 %collective-permute-start.20 = (bf16[2,8,2048]{2,1,0:T(8,128)(2,1)S(1)}, bf16[2,8,2048]{2,1,0:T(8,128)(2,1)S(1)}, u32[]{:S(2)}, u32[]{:S(2)}) collective-permute-start(bf16[2,8,2048]{2,1,0:T(8,128)(2,1)S(1)} %get-tuple-element.114), channel_id=1, source_target_pairs={{0,24},{4,28},{8,16},{12,20},{16,8},{20,12},{24,0},{28,4},{1,25},{... | collective-permute-start | bytes 196616 | tf_op jit(solution)/shard_map/ppermute | solution.py:32

commit v11 on v9

--- a/solution.py
+++ b/solution.py
@@ -223,10 +223,10 @@
     refs = list(refs)
     if apart:
         hidden, deltas = refs.pop(0), refs.pop(0)
-        act = hidden[...], deltas[0], deltas[1]
+        act = hidden, deltas.at[0], deltas.at[1]
     else:
         whole = refs.pop(0)
-        act = whole[0], whole[1], whole[2]
+        act = whole.at[0], whole.at[1], whole.at[2]
     leaving = []
     if with_products:
         gate_w, up_w, down_w = (refs.pop(0) for _ in range(3))
@@ -239,13 +239,13 @@
         refs = refs[:-3]
         units, width = down_s.shape
         part, rows = width // CHUNKS, units // CHUNKS
-        hidden_t = act[0].astype(F32).T.astype(BF16)
+        hidden_t = act[0][...].astype(F32).T.astype(BF16)
         mine = unit_block(k, units)
         start = jnp.bitwise_xor(lax.axis_index("col"), k) * units
         for i in range(CHUNKS):
             here, some = span(i, part), span(i, rows)
-            gate_s[here] = dot(tok_t[here], act[1]).astype(BF16)
-            up_s[here] = dot(tok_t[here], act[2]).astype(BF16)
+            gate_s[here] = dot(tok_t[here], act[1][...]).astype(BF16)
+            up_s[here] = dot(tok_t[here], act[2][...]).astype(BF16)
             down_s[some] = dot(hidden_t[some], grad[...]).astype(BF16)
             there = pl.ds(i * part, part)
             below = pl.ds(pl.multiple_of(start + i * rows, rows), rows)
@@ -262,8 +262,8 @@
         outs = refs[-1 - last :]
         for i in range(down_w.shape[1] // PIECE):
             here = span(i, PIECE)
-            back = back_dot(act[1], gate_w[here]) + back_dot(act[2], up_w[here])
-            for j, term in enumerate((dot(act[0], down_w[:, here]), back)):
+            back = back_dot(act[1][...], gate_w[here]) + back_dot(act[2][...], up_w[here])
+            for j, term in enumerate((dot(act[0][...], down_w[:, here]), back)):
                 term = term if first else before[j, :, here] + term
                 if last:
                     half = term.shape[0] // 2

time: 80.7 us -> 80.8 us (level)
  waiting for transfers between devices: 12.5 us -> 13.8 us
    ppermute x19, waiting for transfers between devices: 12.5 us -> 13.8 us  [swap(): return lax.ppermute(x, axis, [(i, i ^ k) for i in range(size)])]
  transfers between devices with their start and end apart: 19 -> 19, of which waited for: 11 -> 11; matrix products, arithmetic and copies ran while one was open for 0% -> 0% of each run, Pallas kernels for 48% -> 47%
where the time goes in v11:
time: 80.8 us; the launch traced here: 80.6 us
  Pallas kernels  46.5 us (58%)
  starting transfers between devices  19.4 us (24%)
  waiting for transfers between devices  13.8 us (17%)
  between operations  0.82 us (1%)
    pallas_call x6, Pallas kernels, use(): pl.pallas_call(functools.partial(use_kernel, k, first, last, weights is n...  24.7 us
    ppermute x19, starting transfers between devices, swap(): return lax.ppermute(x, axis, [(i, i ^ k) for i in range(size)])  19.4 us
    ppermute x19, waiting for transfers between devices, swap(): return lax.ppermute(x, axis, [(i, i ^ k) for i in range(size)])  13.8 us
    pallas_call x4, Pallas kernels, partial_sums(): pl.pallas_call(functools.partial(sums_kernel, following), in_specs=[WHOLE...  12.3 us
    pallas_call x2, Pallas kernels, load(): pl.pallas_call(functools.partial(load_kernel, k), in_specs=[HOLD] * (3 +...  7.65 us
  transfers between devices with their start and end apart: 19, of which 11 were waited for; matrix products, arithmetic and copies ran while one was open for 0% of the time, Pallas kernels for 47%

profile of v11, /device:TPU:0, one launch (start us, length us, event | category | flops | bytes accessed | tf_op | source)
XLA Modules:
  0.0 80.6 jit_solution(14080020819102573479)
XLA Ops:
  0.6 0.8 pack.1.refs_0_
  1.4 3.9 %collective-permute-start.2 = (bf16[16,2048]{1,0:T(8,128)(2,1)S(1)}, bf16[16,2048]{1,0:T(8,128)(2,1)S(1)}, u32[]{:S(2)}, u32[]{:S(2)}) collective-permute-start(bf16[16,2048]{1,0:T(8,128)(2,1)S(1)} %pack.1.refs_0_), channel_id=1, source_target_pairs={{0,24},{4,28},{8,16},{12,20},{16,8},{20,12},{24,0},{28,4},{1,25},{... | collective-permute-start | bytes 196616 | tf_op jit(solution)/shard_map/ppermute | solution.py:32
  5.3 0.5 collective-permute-start.1
  5.8 0.1 collective-permute-start
  5.9 3.8 %load.2 = (bf16[2048,768]{1,0:T(8,128)(2,1)S(1)}, bf16[2048,768]{1,0:T(8,128)(2,1)S(1)}, bf16[768,2048]{1,0:T(8,128)(2,1)S(1)}) custom-call(bf16[2048,3072]{1,0:T(8,128)(2,1)} %refs_0_.7, bf16[2048,3072]{1,0:T(8,128)(2,1)} %refs_1_.7, bf16[3072,2048]{1,0:T(8,128)(2,1)} %refs_2_.7), custom_call_target="tpu_custom_call" | custom-call | bytes 1179648 | tf_op jit(solution)/shard_map/load/pallas_call | solution.py:134
  9.8 0.0 collective-permute-done.1.refs_2_
  9.8 0.3 collective-permute-done.refs_1_
  10.1 0.3 collective-permute-start.4
  10.4 0.2 collective-permute-start.5
  10.6 0.3 collective-permute-start.6
  10.9 0.0 collective-permute-done.3.refs_4_
  10.9 0.4 collective-permute-done.4.refs_5_
  11.3 0.3 collective-permute-done.5.refs_6_
  11.6 0.2 collective-permute-done.6.refs_7_
  11.8 0.2 assemble.1
  12.1 3.9 %partial_sums.4 = (bf16[3,64,768]{2,1,0:T(8,128)(2,1)S(1)}, bf16[2048,768]{1,0:T(8,128)(2,1)S(1)}, bf16[2048,768]{1,0:T(8,128)(2,1)S(1)}, bf16[768,2048]{1,0:T(8,128)(2,1)S(1)}) custom-call(bf16[64,2048]{1,0:T(8,128)(2,1)S(1)} %get-tuple-element.66.tok, bf16[64,2048]{1,0:T(8,128)(2,1)S(1)} %get-tuple-element.67.grad.refs_2_.refs_6_.refs_7_.refs_3_, ...), custom_call_target="tpu_custom_call" | custom-call | flops 75497472 | bytes 1179648 | tf_op jit(solution)/shard_map/partial_sums/pallas_call | solution.py:171
  16.0 1.9 %collective-permute-start.7 = (bf16[3,64,768]{2,1,0:T(8,128)(2,1)S(1)}, bf16[3,64,768]{2,1,0:T(8,128)(2,1)S(1)}, u32[]{:S(2)}, u32[]{:S(2)}) collective-permute-start(bf16[3,64,768]{2,1,0:T(8,128)(2,1)S(1)} %get-tuple-element.77), channel_id=1, source_target_pairs={{0,1},{1,0},{2,3},{3,2},{4,5},{5,4},{6,7},{7,6},{8,9},{9,8},{10,11... | collective-permute-start | bytes 884744 | tf_op jit(solution)/shard_map/ppermute | solution.py:32
  17.9 3.8 %partial_sums.5 = (bf16[3,64,768]{2,1,0:T(8,128)(2,1)S(1)}, bf16[2048,768]{1,0:T(8,128)(2,1)S(1)}, bf16[2048,768]{1,0:T(8,128)(2,1)S(1)}, bf16[768,2048]{1,0:T(8,128)(2,1)S(1)}) custom-call(bf16[64,2048]{1,0:T(8,128)(2,1)S(1)} %get-tuple-element.66.tok, bf16[64,2048]{1,0:T(8,128)(2,1)S(1)} %get-tuple-element.67.grad.refs_2_.refs_6_.refs_7_.refs_3_, ...), custom_call_target="tpu_custom_call" | custom-call | flops 75497472 | bytes 1179648 | tf_op jit(solution)/shard_map/partial_sums/pallas_call | solution.py:171
  21.8 0.2 collective-permute-start.8
  22.0 2.2 %partial_sums.6.own = f32[3,64,768]{2,1,0:T(8,128)S(1)} custom-call(bf16[64,2048]{1,0:T(8,128)(2,1)S(1)} %get-tuple-element.66.tok, bf16[64,2048]{1,0:T(8,128)(2,1)S(1)} %get-tuple-element.67.grad.refs_2_.refs_6_.refs_7_.refs_3_, bf16[2048,768]{1,0:T(8,128)(2,1)S(1)} %get-tuple-element.74.gate_b.refs_2_, ...), custom_call_target="tpu_custom_call" | custom-call | flops 75497472 | bytes 1179648 | tf_op jit(solution)/shard_map/partial_sums/pallas_call | solution.py:171
  24.1 1.7 %collective-permute-done.7.other = bf16[3,64,768]{2,1,0:T(8,128)(2,1)S(1)} collective-permute-done((bf16[3,64,768]{2,1,0:T(8,128)(2,1)S(1)}, bf16[3,64,768]{2,1,0:T(8,128)(2,1)S(1)}, u32[]{:S(2)}, u32[]{:S(2)}) %collective-permute-start.7) | collective-permute-done | bytes 294944 | tf_op jit(solution)/shard_map/ppermute | solution.py:32
  25.9 0.1 combine.1
  25.9 3.0 %collective-permute-start.9 = (bf16[3,64,768]{2,1,0:T(8,128)(2,1)S(1)}, bf16[3,64,768]{2,1,0:T(8,128)(2,1)S(1)}, u32[]{:S(2)}, u32[]{:S(2)}) collective-permute-start(bf16[3,64,768]{2,1,0:T(8,128)(2,1)S(1)} %get-tuple-element.83), channel_id=1, source_target_pairs={{0,2},{1,3},{2,0},{3,1},{4,6},{5,7},{6,4},{7,5},{8,10},{9,11},{10,... | collective-permute-start | bytes 884744 | tf_op jit(solution)/shard_map/ppermute | solution.py:32
  29.0 3.8 %load.3 = (bf16[2048,768]{1,0:T(8,128)(2,1)S(1)}, bf16[2048,768]{1,0:T(8,128)(2,1)S(1)}, bf16[768,2048]{1,0:T(8,128)(2,1)S(1)}) custom-call(bf16[2048,3072]{1,0:T(8,128)(2,1)} %refs_0_.7, bf16[2048,3072]{1,0:T(8,128)(2,1)} %refs_1_.7, bf16[3072,2048]{1,0:T(8,128)(2,1)} %refs_2_.7, f32[8,128]{1,0:T(8,128)S(1)} %get-tuple-element.78.refs_3_), custom_call_target="tpu_custom_call" | custom-call | bytes 1179648 | tf_op jit(solution)/shard_map/load/pallas_call | solution.py:134
  32.8 2.3 %partial_sums.7.own = f32[3,64,768]{2,1,0:T(8,128)S(1)} custom-call(bf16[64,2048]{1,0:T(8,128)(2,1)S(1)} %get-tuple-element.66.tok, bf16[64,2048]{1,0:T(8,128)(2,1)S(1)} %get-tuple-element.67.grad.refs_2_.refs_6_.refs_7_.refs_3_, bf16[2048,768]{1,0:T(8,128)(2,1)S(1)} %get-tuple-element.79.gate_b.refs_1_, ...), custom_call_target="tpu_custom_call" | custom-call | flops 75497472 | bytes 1179648 | tf_op jit(solution)/shard_map/partial_sums/pallas_call | solution.py:171
  35.1 1.9 %collective-permute-done.8.refs_0_ = bf16[3,64,768]{2,1,0:T(8,128)(2,1)S(1)} collective-permute-done((bf16[3,64,768]{2,1,0:T(8,128)(2,1)S(1)}, bf16[3,64,768]{2,1,0:T(8,128)(2,1)S(1)}, u32[]{:S(2)}, u32[]{:S(2)}) %collective-permute-start.8) | collective-permute-done | bytes 294944 | tf_op jit(solution)/shard_map/ppermute | solution.py:32
  37.1 4.4 %collective-permute-done.9.refs_1_ = bf16[3,64,768]{2,1,0:T(8,128)(2,1)S(1)} collective-permute-done((bf16[3,64,768]{2,1,0:T(8,128)(2,1)S(1)}, bf16[3,64,768]{2,1,0:T(8,128)(2,1)S(1)}, u32[]{:S(2)}, u32[]{:S(2)}) %collective-permute-start.9) | collective-permute-done | bytes 294944 | tf_op jit(solution)/shard_map/ppermute | solution.py:32
  41.5 0.2 activate.1
  41.7 0.8 %collective-permute-start.11 = (bf16[3,64,768]{2,1,0:T(8,128)(2,1)S(1)}, bf16[3,64,768]{2,1,0:T(8,128)(2,1)S(1)}, u32[]{:S(2)}, u32[]{:S(2)}) collective-permute-start(bf16[3,64,768]{2,1,0:T(8,128)(2,1)S(1)} %get-tuple-element.89.refs_0_), channel_id=1, source_target_pairs={{0,1},{1,0},{2,3},{3,2},{4,5},{5,4},{6,7},{7,6},{8,9},{9,8},{10,11... | collective-permute-start | bytes 884744 | tf_op jit(solution)/shard_map/ppermute | solution.py:32
  42.5 2.5 %products.2.refs_4_ = f32[2,64,2048]{2,1,0:T(8,128)S(1)} custom-call(bf16[3,64,768]{2,1,0:T(8,128)(2,1)S(1)} %get-tuple-element.89.refs_0_, bf16[2048,768]{1,0:T(8,128)(2,1)S(1)} %get-tuple-element.79.gate_b.refs_1_, bf16[2048,768]{1,0:T(8,128)(2,1)S(1)} %get-tuple-element.80.up_b.refs_2_, bf16[768,2048]{1,0:T(8,128)(2,1)S(1)} %get-tuple-element.81.down_b.refs_3_), custom_call_target="tpu_custom_call" | custom-call | flops 75497472 | bytes 1179648 | tf_op jit(solution)/shard_map/products/pallas_call | solution.py:310
  45.1 3.4 %collective-permute-start.13 = (bf16[2,64,768]{2,1,0:T(8,128)(2,1)S(1)}, bf16[2,64,768]{2,1,0:T(8,128)(2,1)S(1)}, u32[]{:S(2)}, u32[]{:S(2)}) collective-permute-start(bf16[2,64,768]{2,1,0:T(8,128)(2,1)S(1)} %get-tuple-element.98), channel_id=1, source_target_pairs={{0,2},{1,3},{2,0},{3,1},{4,6},{5,7},{6,4},{7,5},{8,10},{9,11},{10,... | collective-permute-start | bytes 589832 | tf_op jit(solution)/shard_map/ppermute | solution.py:32
  48.5 0.1 collective-permute-start.10
  48.6 4.1 %grads.2 = (bf16[2048,3072]{1,0:T(8,128)(2,1)}, bf16[2048,3072]{1,0:T(8,128)(2,1)}, bf16[3072,2048]{1,0:T(8,128)(2,1)}) custom-call(bf16[3,64,768]{2,1,0:T(8,128)(2,1)S(1)} %get-tuple-element.89.refs_0_, bf16[2048,64]{1,0:T(8,128)(2,1)S(1)} %get-tuple-element.88.refs_1_.refs_5_.refs_6_.refs_2_, ...), custom_call_target="tpu_custom_call" | custom-call | flops 75497472 | bytes 1179648 | tf_op jit(solution)/shard_map/grads/pallas_call | solution.py:310
  52.7 5.3 %productsgrads.2 = (f32[2,64,2048]{2,1,0:T(8,128)S(1)}, bf16[2048,3072]{1,0:T(8,128)(2,1)}, bf16[2048,3072]{1,0:T(8,128)(2,1)}, bf16[3072,2048]{1,0:T(8,128)(2,1)}) custom-call(bf16[3,64,768]{2,1,0:T(8,128)(2,1)S(1)} %collective-permute-done.11.refs_0_, ...), custom_call_target="tpu_custom_call", output_to_operand_aliasing={{1}: (7, {}), {2}: (8, {}), {3}: (9, {})} | custom-call | flops 150994944 | bytes 2359296 | tf_op jit(solution)/shard_map/productsgrads/pallas_call | solution.py:310
  58.0 0.9 %collective-permute-done.13.refs_1_ = bf16[2,64,768]{2,1,0:T(8,128)(2,1)S(1)} collective-permute-done((bf16[2,64,768]{2,1,0:T(8,128)(2,1)S(1)}, bf16[2,64,768]{2,1,0:T(8,128)(2,1)S(1)}, u32[]{:S(2)}, u32[]{:S(2)}) %collective-permute-start.13) | collective-permute-done | bytes 196640 | tf_op jit(solution)/shard_map/ppermute | solution.py:32
  58.9 1.1 %collective-permute-done.10.refs_0_ = bf16[64,768]{1,0:T(8,128)(2,1)S(1)} collective-permute-done((bf16[64,768]{1,0:T(8,128)(2,1)S(1)}, bf16[64,768]{1,0:T(8,128)(2,1)S(1)}, u32[]{:S(2)}, u32[]{:S(2)}) %collective-permute-start.10) | collective-permute-done | bytes 98336 | tf_op jit(solution)/shard_map/ppermute | solution.py:32
  60.0 0.9 %collective-permute-start.12 = (bf16[64,768]{1,0:T(8,128)(2,1)S(1)}, bf16[64,768]{1,0:T(8,128)(2,1)S(1)}, u32[]{:S(2)}, u32[]{:S(2)}) collective-permute-start(bf16[64,768]{1,0:T(8,128)(2,1)S(1)} %collective-permute-done.10.refs_0_), channel_id=1, source_target_pairs={{0,1},{1,0},{2,3},{3,2},{4,5},{5,4},{6,7},{7,6},{8,9},{9,8},{10,11... | collective-permute-start | bytes 294920 | tf_op jit(solution)/shard_map/ppermute | solution.py:32
  60.9 6.2 %productsgrads.3 = (f32[2,64,2048]{2,1,0:T(8,128)S(1)}, bf16[2048,3072]{1,0:T(8,128)(2,1)}, bf16[2048,3072]{1,0:T(8,128)(2,1)}, bf16[3072,2048]{1,0:T(8,128)(2,1)}) custom-call(bf16[64,768]{1,0:T(8,128)(2,1)S(1)} %collective-permute-done.10.refs_0_, ...), custom_call_target="tpu_custom_call", output_to_operand_aliasing={{1}: (8, {}), {2}: (9, {}), {3}: (10, {})} | custom-call | flops 150994944 | bytes 2359296 | tf_op jit(solution)/shard_map/productsgrads/pallas_call | solution.py:310
  67.1 2.5 %products.3 = (f32[2,32,2048]{2,1,0:T(8,128)S(1)}, f32[2,32,2048]{2,1,0:T(8,128)S(1)}) custom-call(bf16[64,768]{1,0:T(8,128)(2,1)S(1)} %collective-permute-done.12.refs_0_, bf16[2,64,768]{2,1,0:T(8,128)(2,1)S(1)} %collective-permute-done.14.refs_1_, bf16[2048,768]{1,0:T(8,128)(2,1)S(1)} %get-tuple-element.68.gate_b.refs_2_, ...), custom_call_target="tpu_custom_call" | custom-call | flops 75497472 | bytes 1179648 | tf_op jit(solution)/shard_map/products/pallas_call | solution.py:310
  69.7 0.1 collective-permute-start.15
  69.7 1.9 %collective-permute-done.15.other = f32[2,32,2048]{2,1,0:T(8,128)S(1)} collective-permute-done((f32[2,32,2048]{2,1,0:T(8,128)S(1)}, f32[2,32,2048]{2,1,0:T(8,128)S(1)}, u32[]{:S(2)}, u32[]{:S(2)}) %collective-permute-start.15) | collective-permute-done | bytes 524320 | tf_op jit(solution)/shard_map/ppermute | solution.py:32
  71.6 0.1 fold.1
  71.7 1.6 %collective-permute-start.16 = (bf16[2,8,2048]{2,1,0:T(8,128)(2,1)S(1)}, bf16[2,8,2048]{2,1,0:T(8,128)(2,1)S(1)}, u32[]{:S(2)}, u32[]{:S(2)}) collective-permute-start(bf16[2,8,2048]{2,1,0:T(8,128)(2,1)S(1)} %get-tuple-element.104), channel_id=1, source_target_pairs={{0,8},{4,12},{8,0},{12,4},{16,24},{20,28},{24,16},{28,20},{1,9},{5... | collective-permute-start | bytes 196616 | tf_op jit(solution)/shard_map/ppermute | solution.py:32
  73.3 1.5 %collective-permute-start.17 = (bf16[2,8,2048]{2,1,0:T(8,128)(2,1)S(1)}, bf16[2,8,2048]{2,1,0:T(8,128)(2,1)S(1)}, u32[]{:S(2)}, u32[]{:S(2)}) collective-permute-start(bf16[2,8,2048]{2,1,0:T(8,128)(2,1)S(1)} %get-tuple-element.105), channel_id=1, source_target_pairs={{0,16},{4,20},{8,24},{12,28},{16,0},{20,4},{24,8},{28,12},{1,17},{... | collective-permute-start | bytes 196616 | tf_op jit(solution)/shard_map/ppermute | solution.py:32
  74.8 0.5 collective-permute-start.18
  75.2 4.1 %grads.3 = (bf16[2048,3072]{1,0:T(8,128)(2,1)}, bf16[2048,3072]{1,0:T(8,128)(2,1)}, bf16[3072,2048]{1,0:T(8,128)(2,1)}) custom-call(bf16[64,768]{1,0:T(8,128)(2,1)S(1)} %collective-permute-done.12.refs_0_, bf16[2,64,768]{2,1,0:T(8,128)(2,1)S(1)} %collective-permute-done.14.refs_1_, ...), custom_call_target="tpu_custom_call", output_to_operand_aliasing={{0}: (4, {}), {1}: (5, {}), {2}: (6, {})} | custom-call | flops 75497472 | bytes 1179648 | tf_op jit(solution)/shard_map/grads/pallas_call | solution.py:310
  79.3 0.6 collective-permute-done.18.refs_2_
  79.9 0.6 finish.1
  (8 shorter events, 0.0 us)
Async XLA Ops:
  1.4 8.4 %collective-permute-start.2 = (bf16[16,2048]{1,0:T(8,128)(2,1)S(1)}, bf16[16,2048]{1,0:T(8,128)(2,1)S(1)}, u32[]{:S(2)}, u32[]{:S(2)}) collective-permute-start(bf16[16,2048]{1,0:T(8,128)(2,1)S(1)} %pack.1.refs_0_), channel_id=1, source_target_pairs={{0,24},{4,28},{8,16},{12,20},{16,8},{20,12},{24,0},{28,4},{1,25},{... | collective-permute-start | bytes 196616 | tf_op jit(solution)/shard_map/ppermute | solution.py:32
  5.3 4.5 %collective-permute-start.1 = (bf16[16,2048]{1,0:T(8,128)(2,1)S(1)}, bf16[16,2048]{1,0:T(8,128)(2,1)S(1)}, u32[]{:S(2)}, u32[]{:S(2)}) collective-permute-start(bf16[16,2048]{1,0:T(8,128)(2,1)S(1)} %pack.1.refs_0_), channel_id=1, source_target_pairs={{0,16},{4,20},{8,24},{12,28},{16,0},{20,4},{24,8},{28,12},{1,17},{... | collective-permute-start | bytes 196616 | tf_op jit(solution)/shard_map/ppermute | solution.py:32
  5.8 4.3 %collective-permute-start = (bf16[16,2048]{1,0:T(8,128)(2,1)S(1)}, bf16[16,2048]{1,0:T(8,128)(2,1)S(1)}, u32[]{:S(2)}, u32[]{:S(2)}) collective-permute-start(bf16[16,2048]{1,0:T(8,128)(2,1)S(1)} %pack.1.refs_0_), channel_id=1, source_target_pairs={{0,8},{4,12},{8,0},{12,4},{16,24},{20,28},{24,16},{28,20},{1,9},{5... | collective-permute-start | bytes 196616 | tf_op jit(solution)/shard_map/ppermute | solution.py:32
  5.9 5.0 %collective-permute-start.3 = (bf16[16,2048]{1,0:T(8,128)(2,1)S(1)}, bf16[16,2048]{1,0:T(8,128)(2,1)S(1)}, u32[]{:S(2)}, u32[]{:S(2)}) collective-permute-start(bf16[16,2048]{1,0:T(8,128)(2,1)S(1)} %pack.1.refs_0_), channel_id=1, source_target_pairs={{0,4},{4,0},{8,12},{12,8},{16,20},{20,16},{24,28},{28,24},{1,5},{5... | collective-permute-start | bytes 196616 | tf_op jit(solution)/shard_map/ppermute | solution.py:32
  10.1 1.3 %collective-permute-start.4 = (bf16[16,2048]{1,0:T(8,128)(2,1)S(1)}, bf16[16,2048]{1,0:T(8,128)(2,1)S(1)}, u32[]{:S(2)}, u32[]{:S(2)}) collective-permute-start(bf16[16,2048]{1,0:T(8,128)(2,1)S(1)} %collective-permute-done.refs_1_), channel_id=1, source_target_pairs={{0,4},{4,0},{8,12},{12,8},{16,20},{20,16},{24,28},{28,24},{1,5},{5... | collective-permute-start | bytes 196616 | tf_op jit(solution)/shard_map/ppermute | solution.py:32
  10.4 1.3 %collective-permute-start.5 = (bf16[16,2048]{1,0:T(8,128)(2,1)S(1)}, bf16[16,2048]{1,0:T(8,128)(2,1)S(1)}, u32[]{:S(2)}, u32[]{:S(2)}) collective-permute-start(bf16[16,2048]{1,0:T(8,128)(2,1)S(1)} %collective-permute-done.1.refs_2_), channel_id=1, source_target_pairs={{0,4},{4,0},{8,12},{12,8},{16,20},{20,16},{24,28},{28,24},{1,5},{5... | collective-permute-start | bytes 196616 | tf_op jit(solution)/shard_map/ppermute | solution.py:32
  10.6 1.3 %collective-permute-start.6 = (bf16[16,2048]{1,0:T(8,128)(2,1)S(1)}, bf16[16,2048]{1,0:T(8,128)(2,1)S(1)}, u32[]{:S(2)}, u32[]{:S(2)}) collective-permute-start(bf16[16,2048]{1,0:T(8,128)(2,1)S(1)} %collective-permute-done.2.refs_3_), channel_id=1, source_target_pairs={{0,4},{4,0},{8,12},{12,8},{16,20},{20,16},{24,28},{28,24},{1,5},{5... | collective-permute-start | bytes 196616 | tf_op jit(solution)/shard_map/ppermute | solution.py:32
  16.0 9.9 %collective-permute-start.7 = (bf16[3,64,768]{2,1,0:T(8,128)(2,1)S(1)}, bf16[3,64,768]{2,1,0:T(8,128)(2,1)S(1)}, u32[]{:S(2)}, u32[]{:S(2)}) collective-permute-start(bf16[3,64,768]{2,1,0:T(8,128)(2,1)S(1)} %get-tuple-element.77), channel_id=1, source_target_pairs={{0,1},{1,0},{2,3},{3,2},{4,5},{5,4},{6,7},{7,6},{8,9},{9,8},{10,11... | collective-permute-start | bytes 884744 | tf_op jit(solution)/shard_map/ppermute | solution.py:32
  21.8 15.3 %collective-permute-start.8 = (bf16[3,64,768]{2,1,0:T(8,128)(2,1)S(1)}, bf16[3,64,768]{2,1,0:T(8,128)(2,1)S(1)}, u32[]{:S(2)}, u32[]{:S(2)}) collective-permute-start(bf16[3,64,768]{2,1,0:T(8,128)(2,1)S(1)} %get-tuple-element.82), channel_id=1, source_target_pairs={{0,1},{1,0},{2,3},{3,2},{4,5},{5,4},{6,7},{7,6},{8,9},{9,8},{10,11... | collective-permute-start | bytes 884744 | tf_op jit(solution)/shard_map/ppermute | solution.py:32
  25.9 15.6 %collective-permute-start.9 = (bf16[3,64,768]{2,1,0:T(8,128)(2,1)S(1)}, bf16[3,64,768]{2,1,0:T(8,128)(2,1)S(1)}, u32[]{:S(2)}, u32[]{:S(2)}) collective-permute-start(bf16[3,64,768]{2,1,0:T(8,128)(2,1)S(1)} %get-tuple-element.83), channel_id=1, source_target_pairs={{0,2},{1,3},{2,0},{3,1},{4,6},{5,7},{6,4},{7,5},{8,10},{9,11},{10,... | collective-permute-start | bytes 884744 | tf_op jit(solution)/shard_map/ppermute | solution.py:32
  41.7 11.0 %collective-permute-start.11 = (bf16[3,64,768]{2,1,0:T(8,128)(2,1)S(1)}, bf16[3,64,768]{2,1,0:T(8,128)(2,1)S(1)}, u32[]{:S(2)}, u32[]{:S(2)}) collective-permute-start(bf16[3,64,768]{2,1,0:T(8,128)(2,1)S(1)} %get-tuple-element.89.refs_0_), channel_id=1, source_target_pairs={{0,1},{1,0},{2,3},{3,2},{4,5},{5,4},{6,7},{7,6},{8,9},{9,8},{10,11... | collective-permute-start | bytes 884744 | tf_op jit(solution)/shard_map/ppermute | solution.py:32
  45.1 13.8 %collective-permute-start.13 = (bf16[2,64,768]{2,1,0:T(8,128)(2,1)S(1)}, bf16[2,64,768]{2,1,0:T(8,128)(2,1)S(1)}, u32[]{:S(2)}, u32[]{:S(2)}) collective-permute-start(bf16[2,64,768]{2,1,0:T(8,128)(2,1)S(1)} %get-tuple-element.98), channel_id=1, source_target_pairs={{0,2},{1,3},{2,0},{3,1},{4,6},{5,7},{6,4},{7,5},{8,10},{9,11},{10,... | collective-permute-start | bytes 589832 | tf_op jit(solution)/shard_map/ppermute | solution.py:32
  48.5 11.4 %collective-permute-start.10 = (bf16[64,768]{1,0:T(8,128)(2,1)S(1)}, bf16[64,768]{1,0:T(8,128)(2,1)S(1)}, u32[]{:S(2)}, u32[]{:S(2)}) collective-permute-start(bf16[64,768]{1,0:T(8,128)(2,1)S(1)} %get-tuple-element.87), channel_id=1, source_target_pairs={{0,2},{1,3},{2,0},{3,1},{4,6},{5,7},{6,4},{7,5},{8,10},{9,11},{10,... | collective-permute-start | bytes 294920 | tf_op jit(solution)/shard_map/ppermute | solution.py:32
  58.9 8.2 %collective-permute-start.14 = (bf16[2,64,768]{2,1,0:T(8,128)(2,1)S(1)}, bf16[2,64,768]{2,1,0:T(8,128)(2,1)S(1)}, u32[]{:S(2)}, u32[]{:S(2)}) collective-permute-start(bf16[2,64,768]{2,1,0:T(8,128)(2,1)S(1)} %collective-permute-done.13.refs_1_), channel_id=1, source_target_pairs={{0,1},{1,0},{2,3},{3,2},{4,5},{5,4},{6,7},{7,6},{8,9},{9,8},{10,11... | collective-permute-start | bytes 589832 | tf_op jit(solution)/shard_map/ppermute | solution.py:32
  60.0 7.1 %collective-permute-start.12 = (bf16[64,768]{1,0:T(8,128)(2,1)S(1)}, bf16[64,768]{1,0:T(8,128)(2,1)S(1)}, u32[]{:S(2)}, u32[]{:S(2)}) collective-permute-start(bf16[64,768]{1,0:T(8,128)(2,1)S(1)} %collective-permute-done.10.refs_0_), channel_id=1, source_target_pairs={{0,1},{1,0},{2,3},{3,2},{4,5},{5,4},{6,7},{7,6},{8,9},{9,8},{10,11... | collective-permute-start | bytes 294920 | tf_op jit(solution)/shard_map/ppermute | solution.py:32
  69.7 2.0 %collective-permute-start.15 = (f32[2,32,2048]{2,1,0:T(8,128)S(1)}, f32[2,32,2048]{2,1,0:T(8,128)S(1)}, u32[]{:S(2)}, u32[]{:S(2)}) collective-permute-start(f32[2,32,2048]{2,1,0:T(8,128)S(1)} %get-tuple-element.102), channel_id=1, source_target_pairs={{0,4},{4,0},{8,12},{12,8},{16,20},{20,16},{24,28},{28,24},{1,5},{5... | collective-permute-start | bytes 1572872 | tf_op jit(solution)/shard_map/ppermute | solution.py:32
  71.7 7.6 %collective-permute-start.16 = (bf16[2,8,2048]{2,1,0:T(8,128)(2,1)S(1)}, bf16[2,8,2048]{2,1,0:T(8,128)(2,1)S(1)}, u32[]{:S(2)}, u32[]{:S(2)}) collective-permute-start(bf16[2,8,2048]{2,1,0:T(8,128)(2,1)S(1)} %get-tuple-element.104), channel_id=1, source_target_pairs={{0,8},{4,12},{8,0},{12,4},{16,24},{20,28},{24,16},{28,20},{1,9},{5... | collective-permute-start | bytes 196616 | tf_op jit(solution)/shard_map/ppermute | solution.py:32
  73.3 6.1 %collective-permute-start.17 = (bf16[2,8,2048]{2,1,0:T(8,128)(2,1)S(1)}, bf16[2,8,2048]{2,1,0:T(8,128)(2,1)S(1)}, u32[]{:S(2)}, u32[]{:S(2)}) collective-permute-start(bf16[2,8,2048]{2,1,0:T(8,128)(2,1)S(1)} %get-tuple-element.105), channel_id=1, source_target_pairs={{0,16},{4,20},{8,24},{12,28},{16,0},{20,4},{24,8},{28,12},{1,17},{... | collective-permute-start | bytes 196616 | tf_op jit(solution)/shard_map/ppermute | solution.py:32
  74.8 5.2 %collective-permute-start.18 = (bf16[2,8,2048]{2,1,0:T(8,128)(2,1)S(1)}, bf16[2,8,2048]{2,1,0:T(8,128)(2,1)S(1)}, u32[]{:S(2)}, u32[]{:S(2)}) collective-permute-start(bf16[2,8,2048]{2,1,0:T(8,128)(2,1)S(1)} %get-tuple-element.106), channel_id=1, source_target_pairs={{0,24},{4,28},{8,16},{12,20},{16,8},{20,12},{24,0},{28,4},{1,25},{... | collective-permute-start | bytes 196616 | tf_op jit(solution)/shard_map/ppermute | solution.py:32
